TPU v7x, 512 devices: a whole 4x4x16 slice. The times are simulated.
512 devices in a mesh: shard: 128 (over z, y, core), rep: 4 (over x).
Axes of the slice: x: 4, y: 4, z: 16, core: 2. Of those that a mesh axis runs over, the one named last changes fastest.
Arguments:
- queries: bfloat16 [4, 128, 9, 3840], P('rep', 'shard'), may hold values from -2.2 to 2.2
- corpus: bfloat16 [256, 32, 9, 3840], P('shard'), may hold values from -2.2 to 2.2
- cand_shard: int32 [16, 256], replicated, may hold values from 0 to 127, as said below
- cand_clip: int32 [16, 256], replicated, may hold values from 0 to 1
- cand_count: int32 [16], replicated, may hold values from 1 to 256, as said below
- first_kernel: bfloat16 [3, 3, 1, 32], replicated, may hold values from -3 to 3
- first_bias: float32 [32], replicated, may hold values from -3 to 3
- second_kernel: bfloat16 [3, 3, 32, 64], replicated, may hold values from -0.5 to 0.5
- second_bias: float32 [64], replicated, may hold values from -3 to 3
- third_kernel: bfloat16 [3, 3, 64, 128], replicated, may hold values from -0.375 to 0.375
- third_bias: float32 [128], replicated, may hold values from -3 to 3
- score_weight: bfloat16 [128], replicated, may hold values from -0.5 to 0.5
- score_bias: float32 [1], replicated, may hold values from -3 to 3
Outputs:
- scores: float32 [16, 256], P('rep', 'shard')
Inputs may be any that keep to these rules, and one draw needn't show every extreme that they name: `cand_shard`: query q belongs to rep group q // 4. Over the first cand_count[q] slots of every query, at most 8 candidates of one rep group's queries lie on one shard, and at most 20 of all queries lie on one shard; both bounds are reached in every draw. Slots from cand_count[q] on are unused. `cand_count`: some query of every rep group has all 256 slots in use.
All inputs are finite; a program needn't handle non-finite values.
Results may differ from a plain program's by a relative error of at most 0.009.
Values may be sent and summed in bfloat16 or wider, within the bound.
No kernel may reach another device: no remote copies, remote signals or barrier semaphores. Data moves between devices by JAX's collectives and lax.ppermute only.
A program may use at most 128 MiB of HBM per device.

v0:
```python
import jax
import jax.numpy as jnp
from jax import lax
from jax.sharding import PartitionSpec as P

CAP = 8


def convolve(inputs, kernel):
    return lax.conv_general_dilated(
        inputs,
        kernel,
        (1, 1),
        "SAME",
        dimension_numbers=("NHWC", "HWIO", "NHWC"),
        preferred_element_type=jnp.float32,
    )


def shrink(values):
    batch, height, width, chans = values.shape
    return values.reshape(batch, height // 2, 2, width // 2, 2, chans).max(axis=(2, 4))


def frame_rows(query_rows, cand_rows, row_frames, regions):
    region_sim = jnp.einsum("ic,jc->ij", query_rows, cand_rows, preferred_element_type=jnp.float32)
    region_sim = region_sim.reshape(row_frames, regions, cand_rows.shape[0] // regions, regions)
    return region_sim.max(axis=3).mean(axis=1).astype(jnp.bfloat16)


def map_scores(
    frame_sim,
    first_kernel,
    first_bias,
    second_kernel,
    second_bias,
    third_kernel,
    third_bias,
    score_weight,
    score_bias,
):
    first = shrink(jax.nn.relu(convolve(frame_sim[..., None], first_kernel) + first_bias)).astype(
        jnp.bfloat16
    )
    second = shrink(jax.nn.relu(convolve(first, second_kernel) + second_bias)).astype(jnp.bfloat16)
    third = jax.nn.relu(convolve(second, third_kernel) + third_bias).astype(jnp.bfloat16)
    out_map = (
        jnp.einsum("bhwc,c->bhw", third, score_weight, preferred_element_type=jnp.float32)
        + score_bias[0]
    )
    return out_map.max(axis=2).mean(axis=1)


def on_device(
    queries,
    corpus,
    cand_shard,
    cand_clip,
    cand_count,
    first_kernel,
    first_bias,
    second_kernel,
    second_bias,
    third_kernel,
    third_bias,
    score_weight,
    score_bias,
):
    shard_index = lax.axis_index("shard")
    rep_index = lax.axis_index("rep")
    rep_count = lax.axis_size("rep")
    query_count, cand_slots = cand_shard.shape
    group_size = query_count // rep_count
    clip_dev, frames, regions, width = corpus.shape
    block_frames = frames // rep_count
    corpus_rows = corpus.reshape(clip_dev, frames * regions, width)
    block = lax.all_gather(queries, "shard", axis=1, tiled=True)
    cand_pos = jnp.arange(cand_slots, dtype=jnp.int32)
    usable = (cand_pos[None, :] < cand_count[:, None]) & (cand_shard == shard_index)
    slot_count = CAP
    in_group = jnp.arange(query_count, dtype=jnp.int32) // group_size == rep_index
    chosen = usable & in_group[:, None]
    flat_chosen = chosen.reshape(-1)
    slot_rank = jnp.cumsum(flat_chosen.astype(jnp.int32)) - 1
    slot_hit = flat_chosen[:, None] & (
        slot_rank[:, None] == jnp.arange(slot_count, dtype=jnp.int32)[None, :]
    )
    pair_ids = jnp.arange(query_count * cand_slots, dtype=jnp.int32)
    pair_index = jnp.sum(jnp.where(slot_hit, pair_ids[:, None], 0), axis=0)
    query_of = pair_index // cand_slots
    clip_of = cand_clip.reshape(-1)[pair_index]
    split_blocks = block.reshape(rep_count, group_size, 1, block_frames, regions * width)
    grouped = lax.all_to_all(split_blocks, "rep", split_axis=0, concat_axis=2, tiled=True)
    group_rows = grouped.reshape(group_size, frames * regions, width)
    local_query = (query_of - rep_index * group_size) % group_size

    def whole_sim(ids):
        return frame_rows(group_rows[ids[0]], corpus_rows[ids[1]], frames, regions)

    frame_sim = lax.map(whole_sim, (local_query, clip_of))
    slot_scores = map_scores(
        frame_sim,
        first_kernel,
        first_bias,
        second_kernel,
        second_bias,
        third_kernel,
        third_bias,
        score_weight,
        score_bias,
    )
    score_table = jnp.sum(jnp.where(slot_hit, slot_scores[None, :], jnp.float32(0.0)), axis=1)
    score_table = score_table.reshape(query_count, cand_slots)
    group_table = lax.dynamic_slice_in_dim(score_table, rep_index * group_size, group_size, 0)
    return lax.psum_scatter(group_table, "shard", scatter_dimension=1, tiled=True)


def solution(mesh):
    return jax.shard_map(
        on_device,
        mesh=mesh,
        in_specs=(
            P("rep", "shard", None, None),
            P("shard", None, None, None),
            P(),
            P(),
            P(),
            P(),
            P(),
            P(),
            P(),
            P(),
            P(),
            P(),
            P(),
        ),
        out_specs=P("rep", "shard"),
        check_vma=False,
    )
```

profile of v0, /device:TPU:1, one launch (start us, length us, event | category | flops | bytes accessed | tf_op | source)
XLA Modules:
  0.0 771.2 jit_solution(10508498329984835707)
XLA Ops:
  6.5 0.7 all-gather.2.cloned.1.call-update
  7.3 165.8 %all-gather.2.cloned.1.call-done = bf16[1,128,9,3840]{3,2,0,1:T(8,128)(2,1)} async-done(((bf16[1,1,9,3840]{3,2,0,1:T(8,128)(2,1)}), bf16[1,128,9,3840]{3,2,0,1:T(8,128)(2,1)}) %all-gather.2.cloned.1.call-update) | async-done | bytes 8847376 | tf_op jit(solution)/shard_map/all_gather | solution.py:77
  173.0 15.7 %reshape.104 = bf16[4,4,1,8,34560]{4,3,1,0,2:T(8,128)(2,1)} reshape(bf16[1,128,9,3840]{3,2,0,1:T(8,128)(2,1)} %all-gather.2.cloned.1.call-done) | data formatting | bytes 17694720 | tf_op jit(solution)/shard_map/reshape | solution.py:92
  188.7 5.9 all-to-all-start
  195.8 8.9 %copy.48 = bf16[2,32,9,3840]{3,0,2,1:T(2,128)(2,1)} copy(bf16[2,32,9,3840]{3,1,2,0:T(8,128)(2,1)} %param.16) | data formatting | bytes 8847360 | tf_op args[1]
  204.7 4.8 copy.49
  209.5 1.3 dynamic-slice
  212.5 80.7 %all-to-all-done = bf16[4,4,1,8,34560]{4,3,1,2,0:T(8,128)(2,1)} async-done(((bf16[4,4,1,8,34560]{4,3,1,2,0:T(8,128)(2,1)}), bf16[4,4,1,8,34560]{4,3,1,2,0:T(8,128)(2,1)}, u32[]{:S(2)}, u32[]{:S(2)}) %all-to-all-start) | async-done | bytes 8847392 | tf_op jit(solution)/shard_map/all_to_all | solution.py:93
  293.2 7.5 copy.47
  300.7 18.4 %reshape.105 = bf16[4,288,3840]{2,1,0:T(8,128)(2,1)} reshape(bf16[1,4,4,1,8,34560]{5,4,2,1,3,0:T(8,128)(2,1)} %copy.47) | data formatting | bytes 17694720 | tf_op jit(solution)/shard_map/reshape | solution.py:94
  319.1 189.4 %while.10 = (s32[]{:T(128)}, bf16[8,32,32]{2,1,0:T(8,128)(2,1)S(1)}, s32[8]{0:T(128)S(1)}, bf16[4,288,3840]{2,1,0:T(8,128)(2,1)}, s32[8]{0:T(128)S(1)}, /*index=...) while((s32[]{:T(128)}, ...), condition=%wide.region_6.7_spmd, body=%wide.region_3.6_spmd.sunk | while | flops 637093888 | bytes 22221024 | solution.py:100
  321.7 0.7 dynamic_slice.24
  324.2 4.0 constant_dynamic-slice_fusion.5
  328.2 4.6 dot_general.13
  332.8 2.8 dot_general.14
  335.6 7.1 fusion.43
  342.8 0.7 dynamic_slice.25
  345.4 0.7 dynamic_slice.24
  347.9 4.0 constant_dynamic-slice_fusion.5
  351.9 4.6 dot_general.13
  356.5 2.8 dot_general.14
  359.3 7.1 fusion.43
  366.5 0.7 dynamic_slice.25
  369.0 0.7 dynamic_slice.24
  371.6 4.0 constant_dynamic-slice_fusion.5
  375.6 4.6 dot_general.13
  380.2 2.8 dot_general.14
  382.9 7.1 fusion.43
  390.1 0.7 dynamic_slice.25
  392.7 0.7 dynamic_slice.24
  395.3 4.0 constant_dynamic-slice_fusion.5
  399.2 4.6 dot_general.13
  403.8 2.8 dot_general.14
  406.6 7.1 fusion.43
  413.8 0.7 dynamic_slice.25
  416.4 0.7 dynamic_slice.24
  418.9 4.0 constant_dynamic-slice_fusion.5
  422.9 4.6 dot_general.13
  427.5 2.8 dot_general.14
  430.3 7.1 fusion.43
  437.5 0.7 dynamic_slice.25
  440.0 0.7 dynamic_slice.24
  442.6 4.0 constant_dynamic-slice_fusion.5
  446.6 4.6 dot_general.13
  451.2 2.8 dot_general.14
  454.0 7.1 fusion.43
  461.2 0.7 dynamic_slice.25
  463.7 0.7 dynamic_slice.24
  466.3 4.0 constant_dynamic-slice_fusion.5
  470.2 4.6 dot_general.13
  474.9 2.8 dot_general.14
  477.6 7.1 fusion.43
  484.8 0.7 dynamic_slice.25
  487.4 0.7 dynamic_slice.24
  490.0 4.0 constant_dynamic-slice_fusion.5
  493.9 4.6 dot_general.13
  498.5 2.8 dot_general.14
  501.3 7.1 fusion.43
  509.0 3.3 add_maximum_fusion
  512.3 1.1 reduce_max.36
  513.5 1.2 fusion.11
  514.8 1.1 fusion.14
  516.4 247.2 %all-reduce = f32[4,256]{1,0:T(4,128)S(1)} all-reduce(f32[4,256]{1,0:T(4,128)S(1)} %constant_dynamic-slice_fusion.3), channel_id=2, replica_groups=mesh['shard'=128,'rep'=4] {'shard'}, use_global_device_ids=true, to_apply=%region_12.13.clone | all-reduce | flops 1024 | bytes 8192
  763.7 0.7 copy.52
  (64 shorter events, 3.6 us)
Async XLA Ops:
  6.5 508.3 %copy-start = (bf16[3,3,64,128]{3,2,1,0:T(8,128)(2,1)S(1)}, bf16[3,3,64,128]{3,2,1,0:T(8,128)(2,1)}, u32[]{:S(2)}) copy-start(bf16[3,3,64,128]{3,2,1,0:T(8,128)(2,1)} %param.24) | copy-start | bytes 442372
  6.5 166.5 %all-gather.2.cloned.1.call-start = ((), (), s32[]{:S(2)}) async-start(), calls=%async_computation.1 | async-start | bytes 15851520 | tf_op jit(solution)/shard_map/all_gather | solution.py:77
  188.7 6.6 copy-start.2
  188.7 6.6 copy-start.1
  188.7 6.6 copy-start.3
  188.7 104.5 %all-to-all-start = ((bf16[4,4,1,8,34560]{4,3,1,2,0:T(8,128)(2,1)}), bf16[4,4,1,8,34560]{4,3,1,2,0:T(8,128)(2,1)}, u32[]{:S(2)}, u32[]{:S(2)}) async-start(bf16[4,4,1,8,34560]{4,3,1,2,0:T(8,128)(2,1)} %bitcast.65), calls=%async_computation | async-start | bytes 17694720 | tf_op jit(solution)/shard_map/all_to_all | solution.py:93
  319.1 189.8 %copy-start.5 = (bf16[3,3,1,32]{3,1,2,0:T(4,128)(2,1)S(1)}, bf16[3,3,1,32]{3,1,2,0:T(4,128)(2,1)}, u32[]{:S(2)}) copy-start(bf16[3,3,1,32]{3,1,2,0:T(4,128)(2,1)} %param.20) | copy-start | bytes 1732
  319.1 189.8 %copy-start.6 = (f32[32]{0:T(128)S(1)}, f32[32]{0:T(128)}, u32[]{:S(2)}) copy-start(f32[32]{0:T(128)} %param.21) | copy-start | bytes 388
  508.9 4.5 copy-start.4
  508.9 4.5 copy-start.7
  512.3 2.5 copy-start.8
  512.3 2.5 copy-start.9
Sparse Core Ops, SparseCore 0:
  10.5 162.5 all-gather.1
where the time goes:
time: 774 us; the launch traced here: 771 us
  waiting for transfers between devices  247 us (32%)
  blocking collectives  247 us (32%)
  local copies, waits for them, and re-layouts  160 us (21%)
  matrix products  62.6 us (8%)
  loops' own time  30.8 us (4%)
  between operations  14.9 us (2%)
    unnamed x1, blocking collectives  247 us
    all_gather x1, waiting for transfers between devices, on_device(): block = lax.all_gather(queries, 'shard', axis=1, tiled=True)  166 us
    all_to_all x1, waiting for transfers between devices, on_device(): lax.all_to_all(split_blocks, 'rep', split_axis=0, concat_axis=2, tiled=True)  80.7 us
    dot_general x16, local copies, waits for them, and re-layouts, frame_rows(): jnp.einsum('ic,jc->ij', query_rows, cand_rows, preferred_element_type=jnp...  59.1 us
    dot_general x8, matrix products, frame_rows(): jnp.einsum('ic,jc->ij', query_rows, cand_rows, preferred_element_type=jnp...  57 us
    dynamic_slice x8, local copies, waits for them, and re-layouts, whole_sim(): return frame_rows(group_rows[ids[0]], corpus_rows[ids[1]], frames, regions)  31.7 us
    another operation x1, loops' own time, on_device(): frame_sim = lax.map(whole_sim, (local_query, clip_of))  30.8 us
    reshape x1, local copies, waits for them, and re-layouts, on_device(): group_rows = grouped.reshape(group_size, frames * regions, width)  18.4 us
  transfers between devices with their start and end apart: 2, of which 2 were waited for; matrix products, arithmetic and copies ran while one was open for 2% of the time, Pallas kernels for 0%

commit v1 on v0

v1 whole, which is shorter than its diff:
```python
import functools

import jax
import jax.numpy as jnp
import numpy as np
from jax import lax
from jax.experimental import pallas as pl
from jax.experimental.pallas import tpu as pltpu
from jax.sharding import Mesh
from jax.sharding import PartitionSpec as P

NZ, NY, NC, NX = 16, 4, 2, 4
PLANE = ("z", "y", "c")
BACK = (0, 1, -1, 2)


def device_at(z, y, c):
    return ((z % NZ) * NY + y % NY) * NC + c


def shift(values, even, odd):
    pairs = []
    for z in range(NZ):
        for y in range(NY):
            for c, (dz, dy) in ((0, even), (1, odd)):
                pairs.append((device_at(z, y, c), device_at(z + dz, y + dy, c)))
    return lax.ppermute(values, PLANE, pairs)


def gather_queries(block):
    regions, width = block.shape
    flat = block.reshape(regions, width // 128, 128)
    groups = [[j + 4 * k for k in range(4)] for j in range(4)]
    four = lax.all_to_all(
        jnp.broadcast_to(flat, (4,) + flat.shape), "z", 0, 0, axis_index_groups=groups
    )
    four = four.reshape(4, regions, width).transpose(1, 0, 2)
    steps = [four] + [shift(four, (d, 0), (0, d)) for d in BACK[1:]]
    sixteen = jnp.concatenate(steps, axis=1)
    return [sixteen] + [shift(sixteen, (0, d), (d, 0)) for d in BACK[1:]]


def sims_body(regions, frames, own_ref, other_ref, query_ref, out_ref):
    rows = query_ref[...].reshape(-1, query_ref.shape[-1])
    count = rows.shape[0] // regions

    def one(ref):
        sims = lax.dot_general(
            ref[0], rows, (((1,), (1,)), ((), ())), preferred_element_type=jnp.float32
        )
        best = sims[0:frames]
        for j in range(1, regions):
            best = jnp.maximum(best, sims[j * frames : (j + 1) * frames])
        total = best[:, 0:count]
        for i in range(1, regions):
            total = total + best[:, i * count : (i + 1) * count]
        return total * (1.0 / regions)

    step = pl.program_id(0)

    @pl.when(step < 2)
    def _():
        out_ref[0] = one(own_ref)

    @pl.when(step >= 2)
    def _():
        out_ref[0] = one(other_ref)


def frame_sims(own, other, queries):
    clips, rows, width = own.shape
    regions, count = queries.shape[:2]
    frames = rows // regions
    return pl.pallas_call(
        functools.partial(sims_body, regions, frames),
        grid=(4,),
        in_specs=[
            pl.BlockSpec((1, rows, width), lambda s: (jnp.minimum(s, 1), 0, 0)),
            pl.BlockSpec((1, rows, width), lambda s: (jnp.maximum(s, 2) - 2, 0, 0)),
            pl.BlockSpec((regions, count, width), lambda s: (0, 0, 0)),
        ],
        out_specs=pl.BlockSpec((1, frames, count), lambda s: (s, 0, 0)),
        out_shape=jax.ShapeDtypeStruct((4, frames, count), jnp.float32),
        compiler_params=pltpu.CompilerParams(vmem_limit_bytes=40 * 2**20),
        cost_estimate=pl.CostEstimate(
            flops=2 * 4 * rows * regions * count * width,
            bytes_accessed=2 * (4 * rows + regions * count) * width,
            transcendentals=0,
        ),
    )(own, other, queries)


def convolve(inputs, kernel):
    return lax.conv_general_dilated(
        inputs,
        kernel,
        (1, 1),
        "SAME",
        dimension_numbers=("NHWC", "HWIO", "NHWC"),
        preferred_element_type=jnp.float32,
    )


def shrink(values):
    batch, height, width, chans = values.shape
    return values.reshape(batch, height // 2, 2, width // 2, 2, chans).max(axis=(2, 4))


def map_scores(
    frame_sim,
    first_kernel,
    first_bias,
    second_kernel,
    second_bias,
    third_kernel,
    third_bias,
    score_weight,
    score_bias,
):
    first = shrink(jax.nn.relu(convolve(frame_sim[..., None], first_kernel) + first_bias)).astype(
        jnp.bfloat16
    )
    second = shrink(jax.nn.relu(convolve(first, second_kernel) + second_bias)).astype(jnp.bfloat16)
    third = jax.nn.relu(convolve(second, third_kernel) + third_bias).astype(jnp.bfloat16)
    out_map = (
        jnp.einsum("bhwc,c->bhw", third, score_weight, preferred_element_type=jnp.float32)
        + score_bias[0]
    )
    return out_map.max(axis=2).mean(axis=1)


def on_device(
    queries,
    corpus,
    cand_shard,
    cand_clip,
    cand_count,
    *weights,
):
    z, y, c, x = (lax.axis_index(a) for a in ("z", "y", "c", "x"))
    clip_dev, frames, regions, width = corpus.shape
    slots = cand_shard.shape[1]
    group = cand_shard.shape[0] // NX

    own = corpus.transpose(0, 2, 1, 3).reshape(clip_dev, regions * frames, width)
    other = lax.ppermute(own, "c", [(0, 1), (1, 0)])

    blocks = gather_queries(queries[0, 0])
    sims = [frame_sims(own, other, b) for b in blocks]
    sims = jnp.concatenate(sims, axis=2).astype(jnp.bfloat16)
    sims = sims.reshape(NC * clip_dev * frames, NZ * NY)
    sims = jnp.where(c == 0, sims, jnp.roll(sims, clip_dev * frames, axis=0))

    col = jnp.arange(NZ * NY, dtype=jnp.int32)
    back = jnp.array(BACK, jnp.int32)
    far, near = back[col // 16], back[(col // 4) % 4]
    from_z = (z - jnp.where(c == 0, near, far)) % 4 + 4 * (col % 4)
    from_y = (y - jnp.where(c == 0, far, near)) % NY
    place = (from_z * NY + from_y)[:, None] == col[None, :]
    table = lax.dot_general(
        place.astype(jnp.bfloat16),
        sims,
        (((0,), (1,)), ((), ())),
        preferred_element_type=jnp.float32,
    ).astype(jnp.bfloat16)

    parts = lax.all_to_all(
        jnp.concatenate([table, table], axis=0), ("c", "x"), 0, 0, tiled=True
    )
    parts = parts.reshape(NC, NX, group, NY, NC * clip_dev, frames)
    frame_sim = parts.transpose(2, 4, 1, 3, 0, 5).reshape(group * NC * clip_dev, frames, frames)
    scores = map_scores(frame_sim, *weights).reshape(group, NC * clip_dev)

    def mine(listed):
        listed = lax.dynamic_slice_in_dim(listed, x * group, group, 0)
        listed = listed.reshape(group, NZ * NY, NC, slots // (NZ * NY * NC))
        return lax.dynamic_index_in_dim(listed, c, 2, keepdims=False)

    position = jnp.arange(slots, dtype=jnp.int32)
    usable = position[None, :] < cand_count[:, None]
    chip = z * NY + y
    listed = jnp.where(usable & (cand_shard // NC == chip), cand_shard % NC * clip_dev + cand_clip, -1)
    listed = mine(listed)
    hit = listed[..., None] == jnp.arange(NC * clip_dev, dtype=jnp.int32)
    values = jnp.sum(jnp.where(hit, scores[:, None, None, :], 0.0), axis=3)
    values = values.transpose(1, 0, 2).reshape(NZ * NY, -1)
    values = lax.all_to_all(values, ("z", "y"), 0, 0, tiled=True)
    return values.sum(axis=0).reshape(group, -1)


def solution(mesh):
    devices = mesh.devices.reshape(NZ, NY, NC, NX)
    grid = Mesh(devices, ("z", "y", "c", "x"))
    return jax.shard_map(
        on_device,
        mesh=grid,
        in_specs=(P("x", PLANE), P(PLANE)) + (P(),) * 11,
        out_specs=P("x", PLANE),
        check_vma=False,
    )
```

time: 774 us -> 165 us (0.21)
  waiting for transfers between devices: 247 us -> 21.2 us
  blocking collectives: 247 us -> 57.2 us
  local copies, waits for them, and re-layouts: 160 us -> 6.01 us
  matrix products: 62.6 us -> 8.04 us
  starting transfers between devices: 5.87 us -> 39.1 us
  loops' own time: 30.8 us -> 0 us
  Pallas kernels: 0 us -> 24.4 us
  between operations: 14.9 us -> 1.06 us
    unnamed x1 -> x0, blocking collectives: 247 us -> none
    all_gather x1 -> x0, waiting for transfers between devices: 166 us -> none  [on_device(): block = lax.all_gather(queries, 'shard', axis=1, tiled=True)]
    all_to_all x1, waiting for transfers between devices: 80.7 us -> 4.16 us  [on_device(): lax.all_to_all(jnp.concatenate([table, table], axis=0), ('c', 'x'), 0, 0,...]
    dot_general x17 -> x0, local copies, waits for them, and re-layouts: 59.2 us -> none  [the longest x16 59.1 us: frame_rows(): jnp.einsum('ic,jc->ij', query_rows, cand_rows, preferred_element_type=jnp...]
    all_to_all x0 -> x2, blocking collectives: none -> 57.2 us  [the longest x1 31.2 us: on_device(): values = lax.all_to_all(values, ('z', 'y'), 0, 0, tiled=True)]
    dot_general x8 -> x1, matrix products: 57 us -> 0.25 us  [on_device(): lax.dot_general(place.astype(jnp.bfloat16), sims, (((0,), (1,)), ((), ())...]
    dynamic_slice x25 -> x2, local copies, waits for them, and re-layouts: 42.2 us -> 0.88 us  [mine(): listed = lax.dynamic_slice_in_dim(listed, x * group, group, 0)]
    ppermute x0 -> x7, starting transfers between devices: none -> 33.2 us  [the longest x6 24.3 us: shift(): return lax.ppermute(values, PLANE, pairs)]
  transfers between devices with their start and end apart: 2 -> 8, of which waited for: 2 -> 4; matrix products, arithmetic and copies ran while one was open for 2% -> 2% of each run, Pallas kernels for 0% -> 11%
where the time goes in v1:
time: 165 us
  blocking collectives  57.2 us (35%)
  starting transfers between devices  39.1 us (24%)
  Pallas kernels  24.4 us (15%)
  waiting for transfers between devices  21.2 us (13%)
  matrix products  8.04 us (5%)
  other arithmetic  7.47 us (5%)
  local copies, waits for them, and re-layouts  6.01 us (4%)
    all_to_all x1, blocking collectives, on_device(): values = lax.all_to_all(values, ('z', 'y'), 0, 0, tiled=True)  31.2 us
    all_to_all x1, blocking collectives, gather_queries(): lax.all_to_all(jnp.broadcast_to(flat, (4,) + flat.shape), 'z', 0, 0, axis...  26 us
    pallas_call x4, Pallas kernels, frame_sims(): pl.pallas_call(functools.partial(sims_body, regions, frames), grid=(4,),...  24.4 us
    ppermute x6, starting transfers between devices, shift(): return lax.ppermute(values, PLANE, pairs)  24.3 us
    ppermute x6, waiting for transfers between devices, shift(): return lax.ppermute(values, PLANE, pairs)  17.1 us
    ppermute x1, starting transfers between devices, on_device(): other = lax.ppermute(own, 'c', [(0, 1), (1, 0)])  8.91 us
    conv_general_dilated x2, matrix products, convolve(): lax.conv_general_dilated(inputs, kernel, (1, 1), 'SAME', dimension_number...  6.39 us
    all_to_all x1, starting transfers between devices, on_device(): lax.all_to_all(jnp.concatenate([table, table], axis=0), ('c', 'x'), 0, 0,...  5.94 us
  transfers between devices with their start and end apart: 8, of which 4 were waited for; matrix products, arithmetic and copies ran while one was open for 2% of the time, Pallas kernels for 11%

profile of v1, /device:TPU:1, one launch (start us, length us, event | category | flops | bytes accessed | tf_op | source)
XLA Modules:
  0.0 164.6 jit_solution(15700418471126473874)
XLA Ops:
  0.0 0.0 copy-start
  0.0 8.9 %collective-permute-start = (bf16[2,288,3840]{2,1,0:T(8,128)(2,1)}, bf16[2,288,3840]{2,1,0:T(8,128)(2,1)}, u32[]{:S(2)}, u32[]{:S(2)}) collective-permute-start(bf16[2,288,3840]{2,1,0:T(8,128)(2,1)} %bitcast.47), channel_id=1, source_target_pairs={{0,4},{4,0},{1,5},{5,1},{2,6},{6,2},{3,7},{7,3},{8,12},{12,8},{9,1... | collective-permute-start | bytes 13271048 | tf_op jit(solution)/shard_map/ppermute | solution.py:146
  8.9 1.0 reshape_squeeze.3
  9.9 0.0 copy-start.6
  9.9 0.0 copy-start.3
  10.0 26.0 %all_to_all.23 = bf16[4,9,30,128]{3,2,1,0:T(8,128)(2,1)S(1)} all-to-all(bf16[4,9,30,128]{3,2,1,0:T(8,128)(2,1)S(1)} %broadcast_in_dim.12), channel_id=1, replica_groups={{0,128,256,384},{32,160,288,416},{64,192,320,448},{96,224,352,480},{1,1..., dimensions={0} | all-to-all | bytes 552960 | tf_op jit(solution)/shard_map/all_to_all | solution.py:34
  36.0 0.1 reshape.207
  36.1 3.2 %collective-permute-start.1 = (bf16[9,4,3840]{2,1,0:T(4,128)(2,1)S(1)}, bf16[9,4,3840]{2,1,0:T(4,128)(2,1)S(1)}, u32[]{:S(2)}, u32[]{:S(2)}) collective-permute-start(bf16[9,4,3840]{2,1,0:T(4,128)(2,1)S(1)} %bitcast.53), channel_id=1, source_target_pairs={{0,32},{4,12},{8,40},{12,20},{16,48},{20,28},{24,56},{28,4},{32,64... | collective-permute-start | bytes 829448 | tf_op jit(solution)/shard_map/ppermute | solution.py:27
  39.3 3.4 %collective-permute-start.2 = (bf16[9,4,3840]{2,1,0:T(4,128)(2,1)S(1)}, bf16[9,4,3840]{2,1,0:T(4,128)(2,1)S(1)}, u32[]{:S(2)}, u32[]{:S(2)}) collective-permute-start(bf16[9,4,3840]{2,1,0:T(4,128)(2,1)S(1)} %bitcast.54), channel_id=1, source_target_pairs={{0,480},{4,28},{8,488},{12,4},{16,496},{20,12},{24,504},{28,20},{3... | collective-permute-start | bytes 829448 | tf_op jit(solution)/shard_map/ppermute | solution.py:27
  42.7 3.5 %collective-permute-start.3 = (bf16[9,4,3840]{2,1,0:T(4,128)(2,1)S(1)}, bf16[9,4,3840]{2,1,0:T(4,128)(2,1)S(1)}, u32[]{:S(2)}, u32[]{:S(2)}) collective-permute-start(bf16[9,4,3840]{2,1,0:T(4,128)(2,1)S(1)} %bitcast.55), channel_id=1, source_target_pairs={{0,64},{4,20},{8,72},{12,28},{16,80},{20,4},{24,88},{28,12},{32,96... | collective-permute-start | bytes 829448 | tf_op jit(solution)/shard_map/ppermute | solution.py:27
  46.2 0.0 collective-permute-done.1
  46.3 0.6 collective-permute-done.2
  46.9 4.6 %collective-permute-done.3 = bf16[9,4,3840]{2,1,0:T(4,128)(2,1)S(1)} collective-permute-done((bf16[9,4,3840]{2,1,0:T(4,128)(2,1)S(1)}, bf16[9,4,3840]{2,1,0:T(4,128)(2,1)S(1)}, u32[]{:S(2)}, u32[]{:S(2)}) %collective-permute-start.3) | collective-permute-done | bytes 276512 | tf_op jit(solution)/shard_map/ppermute | solution.py:27
  51.5 0.6 pad_maximum_fusion.query_ref
  52.1 8.7 %collective-permute-start.4 = (bf16[9,16,3840]{2,1,0:T(8,128)(2,1)S(1)}, bf16[9,16,3840]{2,1,0:T(8,128)(2,1)S(1)}, u32[]{:S(2)}, u32[]{:S(2)}) collective-permute-start(bf16[9,16,3840]{2,1,0:T(8,128)(2,1)S(1)} %pad_maximum_fusion.query_ref), channel_id=1, source_target_pairs={{0,8},{4,36},{8,16},{12,44},{16,24},{20,52},{24,0},{28,60},{32,40}... | collective-permute-start | bytes 3317768 | tf_op jit(solution)/shard_map/ppermute | solution.py:27
  60.8 1.9 %collective-permute-start.5 = (bf16[9,16,3840]{2,1,0:T(8,128)(2,1)S(1)}, bf16[9,16,3840]{2,1,0:T(8,128)(2,1)S(1)}, u32[]{:S(2)}, u32[]{:S(2)}) collective-permute-start(bf16[9,16,3840]{2,1,0:T(8,128)(2,1)S(1)} %pad_maximum_fusion.query_ref), channel_id=1, source_target_pairs={{0,24},{4,484},{8,0},{12,492},{16,8},{20,500},{24,16},{28,508},{32... | collective-permute-start | bytes 3317768 | tf_op jit(solution)/shard_map/ppermute | solution.py:27
  62.8 0.0 copy-done.6
  62.8 0.1 dynamic-slice
  62.9 3.6 %collective-permute-start.6 = (bf16[9,16,3840]{2,1,0:T(8,128)(2,1)S(1)}, bf16[9,16,3840]{2,1,0:T(8,128)(2,1)}, u32[]{:S(2)}, u32[]{:S(2)}) collective-permute-start(bf16[9,16,3840]{2,1,0:T(8,128)(2,1)S(1)} %pad_maximum_fusion.query_ref), channel_id=1, source_target_pairs={{0,16},{4,68},{8,24},{12,76},{16,0},{20,84},{24,8},{28,92},{32,48}... | collective-permute-start | bytes 3317768 | tf_op jit(solution)/shard_map/ppermute | solution.py:27
  66.4 0.0 copy-done.3
  66.5 0.8 fusion.26
  67.2 0.8 copy.38
  68.1 11.9 %collective-permute-done.4.query_ref = bf16[9,16,3840]{2,1,0:T(8,128)(2,1)S(1)} collective-permute-done((bf16[9,16,3840]{2,1,0:T(8,128)(2,1)S(1)}, bf16[9,16,3840]{2,1,0:T(8,128)(2,1)S(1)}, u32[]{:S(2)}, u32[]{:S(2)}) %collective-permute-start.4) | collective-permute-done | bytes 1105952 | tf_op jit(solution)/shard_map/ppermute | solution.py:27
  79.9 0.0 collective-permute-done.other_ref
  79.9 2.3 %copy-done.1 = bf16[2,32,9,3840]{3,1,2,0:T(8,128)(2,1)S(1)} copy-done((bf16[2,32,9,3840]{3,1,2,0:T(8,128)(2,1)S(1)}, bf16[2,32,9,3840]{3,1,2,0:T(8,128)(2,1)}, u32[]{:S(2)}) %copy-start.1) | copy-done | bytes 4423704
  82.2 6.0 %shard_map.137 = f32[4,32,16]{2,1,0:T(8,128)S(1)} custom-call(bf16[2,288,3840]{2,1,0:T(8,128)(2,1)S(1)} %bitcast.48, bf16[2,288,3840]{2,1,0:T(8,128)(2,1)} %collective-permute-done.other_ref, bf16[9,16,3840]{2,1,0:T(8,128)(2,1)S(1)} %collective-permute-done.4.query_ref), custom_call_target="tpu_custom_call" | custom-call | flops 1274019840 | bytes 9953280 | tf_op jit(solution)/shard_map/pallas_call | solution.py:74
  88.2 6.0 %shard_map.136 = f32[4,32,16]{2,1,0:T(8,128)S(1)} custom-call(bf16[2,288,3840]{2,1,0:T(8,128)(2,1)S(1)} %bitcast.49, bf16[2,288,3840]{2,1,0:T(8,128)(2,1)} %collective-permute-done.other_ref, bf16[9,16,3840]{2,1,0:T(8,128)(2,1)S(1)} %pad_maximum_fusion.query_ref), custom_call_target="tpu_custom_call" | custom-call | flops 1274019840 | bytes 9953280 | tf_op jit(solution)/shard_map/pallas_call | solution.py:74
  94.3 0.0 collective-permute-done.5.query_ref
  94.3 6.0 %shard_map.138 = f32[4,32,16]{2,1,0:T(8,128)S(1)} custom-call(bf16[2,288,3840]{2,1,0:T(8,128)(2,1)S(1)} %bitcast.50, bf16[2,288,3840]{2,1,0:T(8,128)(2,1)} %collective-permute-done.other_ref, bf16[9,16,3840]{2,1,0:T(8,128)(2,1)S(1)} %collective-permute-done.5.query_ref), custom_call_target="tpu_custom_call" | custom-call | flops 1274019840 | bytes 9953280 | tf_op jit(solution)/shard_map/pallas_call | solution.py:74
  100.3 0.0 copy-start.2
  100.3 0.0 copy-start.5
  100.3 0.0 copy-start.7
  100.3 0.0 collective-permute-done.6.query_ref
  100.4 6.3 %shard_map.139 = f32[4,32,16]{2,1,0:T(8,128)S(1)} custom-call(bf16[2,288,3840]{2,1,0:T(8,128)(2,1)S(1)} %bitcast.51, bf16[2,288,3840]{2,1,0:T(8,128)(2,1)} %collective-permute-done.other_ref, bf16[9,16,3840]{2,1,0:T(8,128)(2,1)} %collective-permute-done.6.query_ref), custom_call_target="tpu_custom_call" | custom-call | flops 1274019840 | bytes 9953280 | tf_op jit(solution)/shard_map/pallas_call | solution.py:74
  106.7 0.1 pad_maximum_fusion.1
  106.8 0.3 convolution_convert_fusion
  107.1 0.6 pad_maximum_fusion.2
  107.7 5.9 %all-to-all-start.1 = ((bf16[8,16,128]{2,1,0:T(8,128)(2,1)}), bf16[8,16,128]{2,1,0:T(8,128)(2,1)S(1)}, u32[]{:S(2)}, u32[]{:S(2)}) async-start(bf16[8,16,128]{2,1,0:T(8,128)(2,1)} %bitcast.14), calls=%async_computation.1 | async-start | bytes 65536 | tf_op jit(solution)/shard_map/all_to_all | solution.py:167
  113.7 0.0 copy-done.2
  114.3 0.1 copy.40
  114.4 4.2 %all-to-all-done.1 = bf16[8,16,128]{2,1,0:T(8,128)(2,1)S(1)} async-done(((bf16[8,16,128]{2,1,0:T(8,128)(2,1)}), bf16[8,16,128]{2,1,0:T(8,128)(2,1)S(1)}, u32[]{:S(2)}, u32[]{:S(2)}) %all-to-all-start.1) | async-done | bytes 32800 | tf_op jit(solution)/shard_map/all_to_all | solution.py:167
  118.6 0.1 reshape.208
  118.7 0.1 copy.42
  118.9 0.4 copy.43
  119.3 0.0 copy-done.5
  119.3 0.0 copy-done.7
  119.3 4.9 %add_maximum_fusion = bf16[16,32,32,32]{3,0,2,1:T(8,128)(2,1)} fusion(f32[32]{0:T(128)S(1)} %copy-done.7, bf16[16,32,32,1]{0,3,2,1:T(2,128)(2,1)S(1)} %copy.43, bf16[3,3,1,32]{3,1,2,0:T(4,128)(2,1)S(1)} %copy-done.5), kind=kOutput, calls=%fused_computation | convolution fusion | flops 10620928 | bytes 1082048 | tf_op jit(solution)/shard_map/conv_general_dilated | solution.py:94
  124.2 4.5 %reduce_max.27 = bf16[16,16,16,32]{3,0,2,1:T(8,128)(2,1)S(1)} reduce(bf16[16,16,2,16,2,32]{5,0,4,3,2,1:T(8,128)(2,1)} %bitcast.52, bf16[]{:T(256)} %constant.235), dimensions={2,4}, to_apply=%region_0.1 | reduce | flops 393216 | bytes 1310722 | tf_op jit(solution)/shard_map/reduce_max | solution.py:106
  128.7 0.0 copy-done.4
  128.8 0.0 copy-done.8
  128.8 0.0 copy-start.9
  128.8 0.0 copy-start.10
  128.8 1.5 add_maximum_fusion.1
  130.3 0.5 reduce_max.28
  130.8 0.0 copy-done
  130.8 0.0 copy-done.9
  130.8 1.4 fusion.2
  132.2 0.1 div.34
  132.3 0.1 select_reduce_fusion
  132.4 0.1 copy.45
  132.5 31.2 %all_to_all.24 = f32[64,1,8]{2,1,0:T(1,128)S(1)} all-to-all(f32[64,1,8]{2,1,0:T(1,128)S(1)} %copy.45), channel_id=1, replica_groups=mesh['z'=16,'y'=4,'c'=2,'x'=4] {'z','y'}, dimensions={0} | all-to-all | bytes 4096 | tf_op jit(solution)/shard_map/all_to_all | solution.py:187
  163.7 0.1 reduce_sum.29
  163.8 0.1 reshape.211
  163.9 0.7 copy.46
  (18 shorter events, 0.2 us)
Async XLA Ops:
  0.0 130.8 %copy-start = (bf16[3,3,64,128]{3,2,1,0:T(8,128)(2,1)S(1)}, bf16[3,3,64,128]{3,2,1,0:T(8,128)(2,1)}, u32[]{:S(2)}) copy-start(bf16[3,3,64,128]{3,2,1,0:T(8,128)(2,1)} %param.23) | copy-start | bytes 442372
  0.0 79.9 %collective-permute-start = (bf16[2,288,3840]{2,1,0:T(8,128)(2,1)}, bf16[2,288,3840]{2,1,0:T(8,128)(2,1)}, u32[]{:S(2)}, u32[]{:S(2)}) collective-permute-start(bf16[2,288,3840]{2,1,0:T(8,128)(2,1)} %bitcast.47), channel_id=1, source_target_pairs={{0,4},{4,0},{1,5},{5,1},{2,6},{6,2},{3,7},{7,3},{8,12},{12,8},{9,1... | collective-permute-start | bytes 13271048 | tf_op jit(solution)/shard_map/ppermute | solution.py:146
  9.9 52.9 %copy-start.6 = (s32[16]{0:T(128)S(1)}, s32[16]{0:T(128)}, u32[]{:S(2)}) copy-start(s32[16]{0:T(128)} %param.18) | copy-start | bytes 196
  9.9 56.5 %copy-start.3 = (s32[16,256]{1,0:T(8,128)S(1)}, s32[16,256]{1,0:T(8,128)}, u32[]{:S(2)}) copy-start(s32[16,256]{1,0:T(8,128)} %param.16) | copy-start | bytes 49156
  36.1 10.1 %collective-permute-start.1 = (bf16[9,4,3840]{2,1,0:T(4,128)(2,1)S(1)}, bf16[9,4,3840]{2,1,0:T(4,128)(2,1)S(1)}, u32[]{:S(2)}, u32[]{:S(2)}) collective-permute-start(bf16[9,4,3840]{2,1,0:T(4,128)(2,1)S(1)} %bitcast.53), channel_id=1, source_target_pairs={{0,32},{4,12},{8,40},{12,20},{16,48},{20,28},{24,56},{28,4},{32,64... | collective-permute-start | bytes 829448 | tf_op jit(solution)/shard_map/ppermute | solution.py:27
  39.3 7.6 %collective-permute-start.2 = (bf16[9,4,3840]{2,1,0:T(4,128)(2,1)S(1)}, bf16[9,4,3840]{2,1,0:T(4,128)(2,1)S(1)}, u32[]{:S(2)}, u32[]{:S(2)}) collective-permute-start(bf16[9,4,3840]{2,1,0:T(4,128)(2,1)S(1)} %bitcast.54), channel_id=1, source_target_pairs={{0,480},{4,28},{8,488},{12,4},{16,496},{20,12},{24,504},{28,20},{3... | collective-permute-start | bytes 829448 | tf_op jit(solution)/shard_map/ppermute | solution.py:27
  42.7 8.8 %collective-permute-start.3 = (bf16[9,4,3840]{2,1,0:T(4,128)(2,1)S(1)}, bf16[9,4,3840]{2,1,0:T(4,128)(2,1)S(1)}, u32[]{:S(2)}, u32[]{:S(2)}) collective-permute-start(bf16[9,4,3840]{2,1,0:T(4,128)(2,1)S(1)} %bitcast.55), channel_id=1, source_target_pairs={{0,64},{4,20},{8,72},{12,28},{16,80},{20,4},{24,88},{28,12},{32,96... | collective-permute-start | bytes 829448 | tf_op jit(solution)/shard_map/ppermute | solution.py:27
  52.1 27.8 %collective-permute-start.4 = (bf16[9,16,3840]{2,1,0:T(8,128)(2,1)S(1)}, bf16[9,16,3840]{2,1,0:T(8,128)(2,1)S(1)}, u32[]{:S(2)}, u32[]{:S(2)}) collective-permute-start(bf16[9,16,3840]{2,1,0:T(8,128)(2,1)S(1)} %pad_maximum_fusion.query_ref), channel_id=1, source_target_pairs={{0,8},{4,36},{8,16},{12,44},{16,24},{20,52},{24,0},{28,60},{32,40}... | collective-permute-start | bytes 3317768 | tf_op jit(solution)/shard_map/ppermute | solution.py:27
  60.8 33.4 %collective-permute-start.5 = (bf16[9,16,3840]{2,1,0:T(8,128)(2,1)S(1)}, bf16[9,16,3840]{2,1,0:T(8,128)(2,1)S(1)}, u32[]{:S(2)}, u32[]{:S(2)}) collective-permute-start(bf16[9,16,3840]{2,1,0:T(8,128)(2,1)S(1)} %pad_maximum_fusion.query_ref), channel_id=1, source_target_pairs={{0,24},{4,484},{8,0},{12,492},{16,8},{20,500},{24,16},{28,508},{32... | collective-permute-start | bytes 3317768 | tf_op jit(solution)/shard_map/ppermute | solution.py:27
  62.9 37.5 %collective-permute-start.6 = (bf16[9,16,3840]{2,1,0:T(8,128)(2,1)S(1)}, bf16[9,16,3840]{2,1,0:T(8,128)(2,1)}, u32[]{:S(2)}, u32[]{:S(2)}) collective-permute-start(bf16[9,16,3840]{2,1,0:T(8,128)(2,1)S(1)} %pad_maximum_fusion.query_ref), channel_id=1, source_target_pairs={{0,16},{4,68},{8,24},{12,76},{16,0},{20,84},{24,8},{28,92},{32,48}... | collective-permute-start | bytes 3317768 | tf_op jit(solution)/shard_map/ppermute | solution.py:27
  79.9 2.3 %copy-start.1 = (bf16[2,32,9,3840]{3,1,2,0:T(8,128)(2,1)S(1)}, bf16[2,32,9,3840]{3,1,2,0:T(8,128)(2,1)}, u32[]{:S(2)}) copy-start(bf16[2,32,9,3840]{3,1,2,0:T(8,128)(2,1)} %param.15) | copy-start | bytes 13271044
  100.3 13.4 %copy-start.2 = (s32[4,256]{0,1:T(8,128)S(1)}, s32[4,256]{0,1:T(8,128)}, u32[]{:S(2)}) copy-start(s32[4,256]{0,1:T(8,128)} %copy.38) | copy-start | bytes 12292
  100.3 19.0 %copy-start.5 = (bf16[3,3,1,32]{3,1,2,0:T(4,128)(2,1)S(1)}, bf16[3,3,1,32]{3,1,2,0:T(4,128)(2,1)}, u32[]{:S(2)}) copy-start(bf16[3,3,1,32]{3,1,2,0:T(4,128)(2,1)} %param.19) | copy-start | bytes 1732
  100.3 19.0 %copy-start.7 = (f32[32]{0:T(128)S(1)}, f32[32]{0:T(128)}, u32[]{:S(2)}) copy-start(f32[32]{0:T(128)} %param.20) | copy-start | bytes 388
  107.7 10.9 %all-to-all-start.1 = ((bf16[8,16,128]{2,1,0:T(8,128)(2,1)}), bf16[8,16,128]{2,1,0:T(8,128)(2,1)S(1)}, u32[]{:S(2)}, u32[]{:S(2)}) async-start(bf16[8,16,128]{2,1,0:T(8,128)(2,1)} %bitcast.14), calls=%async_computation.1 | async-start | bytes 65536 | tf_op jit(solution)/shard_map/all_to_all | solution.py:167
  124.2 4.5 %copy-start.4 = (bf16[3,3,32,64]{3,2,1,0:T(8,128)(2,1)S(1)}, bf16[3,3,32,64]{3,2,1,0:T(8,128)(2,1)}, u32[]{:S(2)}) copy-start(bf16[3,3,32,64]{3,2,1,0:T(8,128)(2,1)} %param.21) | copy-start | bytes 110596
  124.2 4.5 %copy-start.8 = (f32[64]{0:T(128)S(1)}, f32[64]{0:T(128)}, u32[]{:S(2)}) copy-start(f32[64]{0:T(128)} %param.22) | copy-start | bytes 772
  128.8 2.0 %copy-start.9 = (f32[128]{0:T(128)S(1)}, f32[128]{0:T(128)}, u32[]{:S(2)}) copy-start(f32[128]{0:T(128)} %param.24) | copy-start | bytes 1540
  128.8 2.0 %copy-start.10 = (bf16[128]{0:T(256)(128)(2,1)S(1)}, bf16[128]{0:T(256)(128)(2,1)}, u32[]{:S(2)}) copy-start(bf16[128]{0:T(256)(128)(2,1)} %param.25) | copy-start | bytes 772

commit v2 on v1

--- a/solution.py
+++ b/solution.py
@@ -27,7 +27,7 @@
     return lax.ppermute(values, PLANE, pairs)
 
 
-def gather_queries(block):
+def gather_stage(block):
     regions, width = block.shape
     flat = block.reshape(regions, width // 128, 128)
     groups = [[j + 4 * k for k in range(4)] for j in range(4)]
@@ -35,59 +35,48 @@
         jnp.broadcast_to(flat, (4,) + flat.shape), "z", 0, 0, axis_index_groups=groups
     )
     four = four.reshape(4, regions, width).transpose(1, 0, 2)
-    steps = [four] + [shift(four, (d, 0), (0, d)) for d in BACK[1:]]
-    sixteen = jnp.concatenate(steps, axis=1)
-    return [sixteen] + [shift(sixteen, (0, d), (d, 0)) for d in BACK[1:]]
-
-
-def sims_body(regions, frames, own_ref, other_ref, query_ref, out_ref):
-    rows = query_ref[...].reshape(-1, query_ref.shape[-1])
-    count = rows.shape[0] // regions
-
-    def one(ref):
-        sims = lax.dot_general(
-            ref[0], rows, (((1,), (1,)), ((), ())), preferred_element_type=jnp.float32
-        )
-        best = sims[0:frames]
-        for j in range(1, regions):
-            best = jnp.maximum(best, sims[j * frames : (j + 1) * frames])
-        total = best[:, 0:count]
-        for i in range(1, regions):
-            total = total + best[:, i * count : (i + 1) * count]
-        return total * (1.0 / regions)
-
-    step = pl.program_id(0)
-
-    @pl.when(step < 2)
-    def _():
-        out_ref[0] = one(own_ref)
-
-    @pl.when(step >= 2)
-    def _():
-        out_ref[0] = one(other_ref)
-
-
-def frame_sims(own, other, queries):
+    behind, ahead, two = (shift(four, (d, 0), (0, d)) for d in BACK[1:])
+    return jnp.concatenate([four, behind], axis=1), jnp.concatenate([ahead, two], axis=1)
+
+
+def sims_body(regions, frames, own_ref, other_ref, *refs):
+    out_ref = refs[-1]
+    rows = jnp.concatenate([ref[...].reshape(-1, ref.shape[-1]) for ref in refs[:-1]], axis=0)
+    count = refs[0].shape[1]
+    pieces = len(refs) - 1
+    for half, corpus_ref in enumerate((own_ref, other_ref)):
+        for clip in range(corpus_ref.shape[0]):
+            sims = lax.dot_general(
+                corpus_ref[clip], rows, (((1,), (1,)), ((), ())), preferred_element_type=jnp.float32
+            )
+            best = sims[0:frames]
+            for j in range(1, regions):
+                best = jnp.maximum(best, sims[j * frames : (j + 1) * frames])
+            for p in range(pieces):
+                total = 0.0
+                for i in range(regions):
+                    at = (p * regions + i) * count
+                    total = total + best[:, at : at + count]
+                out_ref[half * 2 + clip, :, p * count : (p + 1) * count] = total * (1.0 / regions)
+
+
+def frame_sims(own, other, pieces):
     clips, rows, width = own.shape
-    regions, count = queries.shape[:2]
+    regions, count = pieces[0].shape[:2]
     frames = rows // regions
+    total = count * len(pieces)
     return pl.pallas_call(
         functools.partial(sims_body, regions, frames),
-        grid=(4,),
-        in_specs=[
-            pl.BlockSpec((1, rows, width), lambda s: (jnp.minimum(s, 1), 0, 0)),
-            pl.BlockSpec((1, rows, width), lambda s: (jnp.maximum(s, 2) - 2, 0, 0)),
-            pl.BlockSpec((regions, count, width), lambda s: (0, 0, 0)),
-        ],
-        out_specs=pl.BlockSpec((1, frames, count), lambda s: (s, 0, 0)),
-        out_shape=jax.ShapeDtypeStruct((4, frames, count), jnp.float32),
-        compiler_params=pltpu.CompilerParams(vmem_limit_bytes=40 * 2**20),
+        in_specs=[pl.BlockSpec(memory_space=pltpu.VMEM)] * (2 + len(pieces)),
+        out_specs=pl.BlockSpec(memory_space=pltpu.VMEM),
+        out_shape=jax.ShapeDtypeStruct((4, frames, total), jnp.float32),
+        compiler_params=pltpu.CompilerParams(vmem_limit_bytes=24 * 2**20),
         cost_estimate=pl.CostEstimate(
-            flops=2 * 4 * rows * regions * count * width,
-            bytes_accessed=2 * (4 * rows + regions * count) * width,
+            flops=2 * 4 * rows * regions * total * width,
+            bytes_accessed=2 * (4 * rows + regions * total) * width,
             transcendentals=0,
         ),
-    )(own, other, queries)
+    )(own, other, *pieces)
 
 
 def convolve(inputs, kernel):
@@ -145,8 +134,20 @@
     own = corpus.transpose(0, 2, 1, 3).reshape(clip_dev, regions * frames, width)
     other = lax.ppermute(own, "c", [(0, 1), (1, 0)])
 
-    blocks = gather_queries(queries[0, 0])
-    sims = [frame_sims(own, other, b) for b in blocks]
+    first, last = gather_stage(queries[0, 0])
+    behind_first = shift(first, (0, 1), (1, 0))
+    ahead_last = shift(last, (0, -1), (-1, 0))
+    behind_last = shift(last, (0, 1), (1, 0))
+    ahead_first = shift(first, (0, -1), (-1, 0))
+    two_first = shift(behind_first, (0, 1), (1, 0))
+    two_last = shift(ahead_last, (0, -1), (-1, 0))
+    sims = [frame_sims(own, other, [first, last])]
+    near, sims[0] = lax.optimization_barrier(
+        ((behind_first, behind_last, ahead_first, ahead_last), sims[0])
+    )
+    sims.append(frame_sims(own, other, near))
+    two, sims[1] = lax.optimization_barrier(((two_first, two_last), sims[1]))
+    sims.append(frame_sims(own, other, two))
     sims = jnp.concatenate(sims, axis=2).astype(jnp.bfloat16)
     sims = sims.reshape(NC * clip_dev * frames, NZ * NY)
     sims = jnp.where(c == 0, sims, jnp.roll(sims, clip_dev * frames, axis=0))

time: 165 us -> 147 us (0.89)
  waiting for transfers between devices: 21.2 us -> 8.18 us
  starting transfers between devices: 39.1 us -> 51.7 us
  blocking collectives: 57.2 us -> 46.5 us
  Pallas kernels: 24.4 us -> 17.3 us
    ppermute x6 -> x9, waiting for transfers between devices: 17.1 us -> 4.02 us  [shift(): return lax.ppermute(values, PLANE, pairs)]
    all_to_all x1, blocking collectives: 31.2 us -> 20.5 us  [on_device(): values = lax.all_to_all(values, ('z', 'y'), 0, 0, tiled=True)]
    ppermute x6 -> x9, starting transfers between devices: 24.3 us -> 32.4 us  [shift(): return lax.ppermute(values, PLANE, pairs)]
    pallas_call x4 -> x3, Pallas kernels: 24.4 us -> 17.3 us  [frame_sims(): pl.pallas_call(functools.partial(sims_body, regions, frames), in_specs=[p...]
    all_to_all x1, starting transfers between devices: 5.94 us -> 10.4 us  [on_device(): lax.all_to_all(jnp.concatenate([table, table], axis=0), ('c', 'x'), 0, 0,...]
  transfers between devices with their start and end apart: 8 -> 11, of which waited for: 4 -> 2; matrix products, arithmetic and copies ran while one was open for 2% -> 2% of each run, Pallas kernels for 11% -> 8%
where the time goes in v2:
time: 147 us; the launch traced here: 146 us
  starting transfers between devices  51.7 us (35%)
  blocking collectives  46.5 us (32%)
  Pallas kernels  17.3 us (12%)
  waiting for transfers between devices  8.18 us (6%)
  matrix products  8.15 us (6%)
  other arithmetic  7.37 us (5%)
  local copies, waits for them, and re-layouts  6 us (4%)
    ppermute x9, starting transfers between devices, shift(): return lax.ppermute(values, PLANE, pairs)  32.4 us
    all_to_all x1, blocking collectives, gather_stage(): lax.all_to_all(jnp.broadcast_to(flat, (4,) + flat.shape), 'z', 0, 0, axis...  26 us
    all_to_all x1, blocking collectives, on_device(): values = lax.all_to_all(values, ('z', 'y'), 0, 0, tiled=True)  20.5 us
    pallas_call x3, Pallas kernels, frame_sims(): pl.pallas_call(functools.partial(sims_body, regions, frames), in_specs=[p...  17.3 us
    all_to_all x1, starting transfers between devices, on_device(): lax.all_to_all(jnp.concatenate([table, table], axis=0), ('c', 'x'), 0, 0,...  10.4 us
    ppermute x1, starting transfers between devices, on_device(): other = lax.ppermute(own, 'c', [(0, 1), (1, 0)])  8.91 us
    conv_general_dilated x2, matrix products, convolve(): lax.conv_general_dilated(inputs, kernel, (1, 1), 'SAME', dimension_number...  6.51 us
    reduce_max x2, other arithmetic, shrink(): values.reshape(batch, height // 2, 2, width // 2, 2, chans).max(axis=(2, 4))  5.02 us
  transfers between devices with their start and end apart: 11, of which 2 were waited for; matrix products, arithmetic and copies ran while one was open for 2% of the time, Pallas kernels for 8%

profile of v2, /device:TPU:1, one launch (start us, length us, event | category | flops | bytes accessed | tf_op | source)
XLA Modules:
  0.0 146.2 jit_solution(12885653961394522180)
XLA Ops:
  0.0 0.0 copy-start
  0.0 8.9 %collective-permute-start.7 = (bf16[2,288,3840]{2,1,0:T(8,128)(2,1)}, bf16[2,288,3840]{2,1,0:T(8,128)(2,1)}, u32[]{:S(2)}, u32[]{:S(2)}) collective-permute-start(bf16[2,288,3840]{2,1,0:T(8,128)(2,1)} %bitcast.46), channel_id=1, source_target_pairs={{0,4},{4,0},{1,5},{5,1},{2,6},{6,2},{3,7},{7,3},{8,12},{12,8},{9,1... | collective-permute-start | bytes 13271048 | tf_op jit(solution)/shard_map/ppermute | solution.py:135
  8.9 1.0 reshape_squeeze.3
  9.9 0.0 copy-start.3
  10.0 0.0 copy-start.6
  10.0 26.0 %all_to_all.23 = bf16[4,9,30,128]{3,2,1,0:T(8,128)(2,1)S(1)} all-to-all(bf16[4,9,30,128]{3,2,1,0:T(8,128)(2,1)S(1)} %broadcast_in_dim.12), channel_id=1, replica_groups={{0,128,256,384},{32,160,288,416},{64,192,320,448},{96,224,352,480},{1,1..., dimensions={0} | all-to-all | bytes 552960 | tf_op jit(solution)/shard_map/all_to_all | solution.py:34
  36.0 0.1 reshape.204
  36.1 4.6 %collective-permute-start.2 = (bf16[9,4,3840]{2,1,0:T(4,128)(2,1)S(1)}, bf16[9,4,3840]{2,1,0:T(4,128)(2,1)S(1)}, u32[]{:S(2)}, u32[]{:S(2)}) collective-permute-start(bf16[9,4,3840]{2,1,0:T(4,128)(2,1)S(1)} %bitcast.51), channel_id=1, source_target_pairs={{0,480},{4,28},{8,488},{12,4},{16,496},{20,12},{24,504},{28,20},{3... | collective-permute-start | bytes 829448 | tf_op jit(solution)/shard_map/ppermute | solution.py:27
  40.8 2.3 %collective-permute-start.3 = (bf16[9,4,3840]{2,1,0:T(4,128)(2,1)S(1)}, bf16[9,4,3840]{2,1,0:T(4,128)(2,1)S(1)}, u32[]{:S(2)}, u32[]{:S(2)}) collective-permute-start(bf16[9,4,3840]{2,1,0:T(4,128)(2,1)S(1)} %bitcast.52), channel_id=1, source_target_pairs={{0,64},{4,20},{8,72},{12,28},{16,80},{20,4},{24,88},{28,12},{32,96... | collective-permute-start | bytes 829448 | tf_op jit(solution)/shard_map/ppermute | solution.py:27
  43.0 2.6 %collective-permute-start = (bf16[9,4,3840]{2,1,0:T(4,128)(2,1)S(1)}, bf16[9,4,3840]{2,1,0:T(4,128)(2,1)S(1)}, u32[]{:S(2)}, u32[]{:S(2)}) collective-permute-start(bf16[9,4,3840]{2,1,0:T(4,128)(2,1)S(1)} %bitcast.53), channel_id=1, source_target_pairs={{0,32},{4,12},{8,40},{12,20},{16,48},{20,28},{24,56},{28,4},{32,64... | collective-permute-start | bytes 829448 | tf_op jit(solution)/shard_map/ppermute | solution.py:27
  45.6 0.0 collective-permute-done.2
  45.6 4.0 %collective-permute-done.3 = bf16[9,4,3840]{2,1,0:T(4,128)(2,1)S(1)} collective-permute-done((bf16[9,4,3840]{2,1,0:T(4,128)(2,1)S(1)}, bf16[9,4,3840]{2,1,0:T(4,128)(2,1)S(1)}, u32[]{:S(2)}, u32[]{:S(2)}) %collective-permute-start.3) | collective-permute-done | bytes 276512 | tf_op jit(solution)/shard_map/ppermute | solution.py:27
  49.6 0.3 pad_maximum_fusion.1.refs_1_
  49.9 5.6 %collective-permute-start.6 = (bf16[9,8,3840]{2,1,0:T(8,128)(2,1)S(1)}, bf16[9,8,3840]{2,1,0:T(8,128)(2,1)S(1)}, u32[]{:S(2)}, u32[]{:S(2)}) collective-permute-start(bf16[9,8,3840]{2,1,0:T(8,128)(2,1)S(1)} %pad_maximum_fusion.1.refs_1_), channel_id=1, source_target_pairs={{0,24},{4,484},{8,0},{12,492},{16,8},{20,500},{24,16},{28,508},{32... | collective-permute-start | bytes 1658888 | tf_op jit(solution)/shard_map/ppermute | solution.py:27
  55.5 0.0 collective-permute-done
  55.5 0.3 pad_maximum_fusion.refs_0_
  55.8 5.5 %collective-permute-start.1 = (bf16[9,8,3840]{2,1,0:T(8,128)(2,1)S(1)}, bf16[9,8,3840]{2,1,0:T(8,128)(2,1)S(1)}, u32[]{:S(2)}, u32[]{:S(2)}) collective-permute-start(bf16[9,8,3840]{2,1,0:T(8,128)(2,1)S(1)} %pad_maximum_fusion.refs_0_), channel_id=1, source_target_pairs={{0,8},{4,36},{8,16},{12,44},{16,24},{20,52},{24,0},{28,60},{32,40}... | collective-permute-start | bytes 1658888 | tf_op jit(solution)/shard_map/ppermute | solution.py:27
  61.4 0.0 copy-done.3
  61.4 2.7 %collective-permute-start.4 = (bf16[9,8,3840]{2,1,0:T(8,128)(2,1)S(1)}, bf16[9,8,3840]{2,1,0:T(8,128)(2,1)S(1)}, u32[]{:S(2)}, u32[]{:S(2)}) collective-permute-start(bf16[9,8,3840]{2,1,0:T(8,128)(2,1)S(1)} %pad_maximum_fusion.1.refs_1_), channel_id=1, source_target_pairs={{0,8},{4,36},{8,16},{12,44},{16,24},{20,52},{24,0},{28,60},{32,40}... | collective-permute-start | bytes 1658888 | tf_op jit(solution)/shard_map/ppermute | solution.py:27
  64.1 3.8 %collective-permute-start.5 = (bf16[9,8,3840]{2,1,0:T(8,128)(2,1)S(1)}, bf16[9,8,3840]{2,1,0:T(8,128)(2,1)S(1)}, u32[]{:S(2)}, u32[]{:S(2)}) collective-permute-start(bf16[9,8,3840]{2,1,0:T(8,128)(2,1)S(1)} %pad_maximum_fusion.refs_0_), channel_id=1, source_target_pairs={{0,24},{4,484},{8,0},{12,492},{16,8},{20,500},{24,16},{28,508},{32... | collective-permute-start | bytes 1658888 | tf_op jit(solution)/shard_map/ppermute | solution.py:27
  67.9 0.0 copy-done.6
  67.9 0.1 dynamic-slice
  68.0 0.0 collective-permute-done.6.refs_3_
  68.0 1.9 %collective-permute-start.9 = (bf16[9,8,3840]{2,1,0:T(8,128)(2,1)S(1)}, bf16[9,8,3840]{2,1,0:T(8,128)(2,1)}, u32[]{:S(2)}, u32[]{:S(2)}) collective-permute-start(bf16[9,8,3840]{2,1,0:T(8,128)(2,1)S(1)} %collective-permute-done.6.refs_3_), channel_id=1, source_target_pairs={{0,24},{4,484},{8,0},{12,492},{16,8},{20,500},{24,16},{28,508},{32... | collective-permute-start | bytes 1658888 | tf_op jit(solution)/shard_map/ppermute | solution.py:27
  69.9 0.0 collective-permute-done.1.refs_0_
  69.9 3.4 %collective-permute-start.8 = (bf16[9,8,3840]{2,1,0:T(8,128)(2,1)S(1)}, bf16[9,8,3840]{2,1,0:T(8,128)(2,1)}, u32[]{:S(2)}, u32[]{:S(2)}) collective-permute-start(bf16[9,8,3840]{2,1,0:T(8,128)(2,1)S(1)} %collective-permute-done.1.refs_0_), channel_id=1, source_target_pairs={{0,8},{4,36},{8,16},{12,44},{16,24},{20,52},{24,0},{28,60},{32,40}... | collective-permute-start | bytes 1658888 | tf_op jit(solution)/shard_map/ppermute | solution.py:27
  73.3 0.8 fusion.24
  74.1 0.8 copy.38
  74.9 0.0 collective-permute-done.7.other_ref
  74.9 0.0 copy-start.1
  74.9 2.2 %copy-done.1 = bf16[2,32,9,3840]{3,1,2,0:T(8,128)(2,1)S(1)} copy-done((bf16[2,32,9,3840]{3,1,2,0:T(8,128)(2,1)S(1)}, bf16[2,32,9,3840]{3,1,2,0:T(8,128)(2,1)}, u32[]{:S(2)}) %copy-start.1) | copy-done | bytes 4423704
  77.2 4.9 %shard_map.136 = f32[4,32,16]{2,1,0:T(8,128)S(1)} custom-call(bf16[2,288,3840]{2,1,0:T(8,128)(2,1)S(1)} %bitcast.47, bf16[2,288,3840]{2,1,0:T(8,128)(2,1)} %collective-permute-done.7.other_ref, bf16[9,8,3840]{2,1,0:T(8,128)(2,1)S(1)} %pad_maximum_fusion.refs_0_, bf16[9,8,3840]{2,1,0:T(8,128)(2,1)S(1)} %pad_maximum_fusion.1.refs_1_), custom_call_target="tpu_custom_call" | custom-call | flops 1274019840 | bytes 9953280 | tf_op jit(solution)/shard_map/pallas_call | solution.py:68
  82.1 0.0 collective-permute-done.4.refs_1_
  82.1 0.0 collective-permute-done.5.refs_2_
  82.1 7.1 %shard_map.137 = f32[4,32,32]{2,1,0:T(8,128)S(1)} custom-call(bf16[2,288,3840]{2,1,0:T(8,128)(2,1)S(1)} %bitcast.48, bf16[2,288,3840]{2,1,0:T(8,128)(2,1)} %collective-permute-done.7.other_ref, bf16[9,8,3840]{2,1,0:T(8,128)(2,1)S(1)} %collective-permute-done.1.refs_0_, bf16[9,8,3840]{2,1,0:T(8,128)(2,1)S(1)} %collective-permute-done.4.refs_1_, ...), custom_call_target="tpu_custom_call" | custom-call | flops 2548039680 | bytes 11059200 | tf_op jit(solution)/shard_map/pallas_call | solution.py:68
  89.2 0.0 collective-permute-done.9.refs_1_
  89.2 0.0 collective-permute-done.8.refs_0_
  89.3 5.2 %shard_map.138 = f32[4,32,16]{2,1,0:T(8,128)S(1)} custom-call(bf16[2,288,3840]{2,1,0:T(8,128)(2,1)S(1)} %bitcast.49, bf16[2,288,3840]{2,1,0:T(8,128)(2,1)} %collective-permute-done.7.other_ref, bf16[9,8,3840]{2,1,0:T(8,128)(2,1)} %collective-permute-done.8.refs_0_, bf16[9,8,3840]{2,1,0:T(8,128)(2,1)} %collective-permute-done.9.refs_1_), custom_call_target="tpu_custom_call" | custom-call | flops 1274019840 | bytes 9953280 | tf_op jit(solution)/shard_map/pallas_call | solution.py:68
  94.5 0.1 pad_maximum_fusion.2
  94.6 0.2 convolution_convert_fusion
  94.9 0.6 pad_maximum_fusion.3
  95.5 10.4 %all-to-all-start.1 = ((bf16[8,16,128]{2,1,0:T(8,128)(2,1)}), bf16[8,16,128]{2,1,0:T(8,128)(2,1)S(1)}, u32[]{:S(2)}, u32[]{:S(2)}) async-start(bf16[8,16,128]{2,1,0:T(8,128)(2,1)} %bitcast.13), calls=%async_computation.1 | async-start | bytes 65536 | tf_op jit(solution)/shard_map/all_to_all | solution.py:168
  106.6 0.1 copy.40
  106.7 4.2 %all-to-all-done.1 = bf16[8,16,128]{2,1,0:T(8,128)(2,1)S(1)} async-done(((bf16[8,16,128]{2,1,0:T(8,128)(2,1)}), bf16[8,16,128]{2,1,0:T(8,128)(2,1)S(1)}, u32[]{:S(2)}, u32[]{:S(2)}) %all-to-all-start.1) | async-done | bytes 32800 | tf_op jit(solution)/shard_map/all_to_all | solution.py:168
  110.8 0.1 reshape.206
  111.0 0.1 copy.42
  111.1 0.4 copy.43
  111.5 5.0 %add_maximum_fusion = bf16[16,32,32,32]{3,0,2,1:T(8,128)(2,1)} fusion(f32[32]{0:T(128)S(1)} %copy-done.7, bf16[16,32,32,1]{0,3,2,1:T(2,128)(2,1)S(1)} %copy.43, bf16[3,3,1,32]{3,1,2,0:T(4,128)(2,1)S(1)} %copy-done.5), kind=kOutput, calls=%fused_computation | convolution fusion | flops 10620928 | bytes 1082048 | tf_op jit(solution)/shard_map/conv_general_dilated | solution.py:83
  116.6 4.5 %reduce_max.27 = bf16[16,16,16,32]{3,0,2,1:T(8,128)(2,1)S(1)} reduce(bf16[16,16,2,16,2,32]{5,0,4,3,2,1:T(8,128)(2,1)} %bitcast.50, bf16[]{:T(256)} %constant.235), dimensions={2,4}, to_apply=%region_0.1 | reduce | flops 393216 | bytes 1310722 | tf_op jit(solution)/shard_map/reduce_max | solution.py:95
  121.1 0.0 copy-start.9
  121.1 0.0 copy-start.10
  121.1 1.5 %add_maximum_fusion.1 = bf16[16,16,16,64]{3,0,2,1:T(8,128)(2,1)S(1)} fusion(bf16[3,3,32,64]{3,2,1,0:T(8,128)(2,1)S(1)} %copy-done.4, f32[64]{0:T(128)S(1)} %copy-done.8, bf16[16,16,16,32]{3,0,2,1:T(8,128)(2,1)S(1)} %reduce_max.27), kind=kOutput, calls=%fused_computation.1 | convolution fusion | flops 139460608 | bytes 823552 | tf_op jit(solution)/shard_map/conv_general_dilated | solution.py:83
  122.6 0.5 reduce_max.28
  123.1 0.0 copy-done
  123.1 0.0 copy-done.9
  123.2 0.0 copy-done.10
  123.2 1.4 fusion.2
  124.6 0.1 div.34
  124.7 0.1 select_reduce_fusion
  124.8 0.1 copy.45
  124.9 20.5 %all_to_all.24 = f32[64,1,8]{2,1,0:T(1,128)S(1)} all-to-all(f32[64,1,8]{2,1,0:T(1,128)S(1)} %copy.45), channel_id=1, replica_groups=mesh['z'=16,'y'=4,'c'=2,'x'=4] {'z','y'}, dimensions={0} | all-to-all | bytes 4096 | tf_op jit(solution)/shard_map/all_to_all | solution.py:188
  145.4 0.1 reduce_sum.29
  145.5 0.1 reshape.209
  145.5 0.7 copy.46
  (23 shorter events, 0.2 us)
Async XLA Ops:
  0.0 123.1 %copy-start = (bf16[3,3,64,128]{3,2,1,0:T(8,128)(2,1)S(1)}, bf16[3,3,64,128]{3,2,1,0:T(8,128)(2,1)}, u32[]{:S(2)}) copy-start(bf16[3,3,64,128]{3,2,1,0:T(8,128)(2,1)} %param.23) | copy-start | bytes 442372
  0.0 74.9 %collective-permute-start.7 = (bf16[2,288,3840]{2,1,0:T(8,128)(2,1)}, bf16[2,288,3840]{2,1,0:T(8,128)(2,1)}, u32[]{:S(2)}, u32[]{:S(2)}) collective-permute-start(bf16[2,288,3840]{2,1,0:T(8,128)(2,1)} %bitcast.46), channel_id=1, source_target_pairs={{0,4},{4,0},{1,5},{5,1},{2,6},{6,2},{3,7},{7,3},{8,12},{12,8},{9,1... | collective-permute-start | bytes 13271048 | tf_op jit(solution)/shard_map/ppermute | solution.py:135
  9.9 51.5 %copy-start.3 = (s32[16,256]{1,0:T(8,128)S(1)}, s32[16,256]{1,0:T(8,128)}, u32[]{:S(2)}) copy-start(s32[16,256]{1,0:T(8,128)} %param.16) | copy-start | bytes 49156
  10.0 58.0 %copy-start.6 = (s32[16]{0:T(128)S(1)}, s32[16]{0:T(128)}, u32[]{:S(2)}) copy-start(s32[16]{0:T(128)} %param.18) | copy-start | bytes 196
  36.1 9.5 %collective-permute-start.2 = (bf16[9,4,3840]{2,1,0:T(4,128)(2,1)S(1)}, bf16[9,4,3840]{2,1,0:T(4,128)(2,1)S(1)}, u32[]{:S(2)}, u32[]{:S(2)}) collective-permute-start(bf16[9,4,3840]{2,1,0:T(4,128)(2,1)S(1)} %bitcast.51), channel_id=1, source_target_pairs={{0,480},{4,28},{8,488},{12,4},{16,496},{20,12},{24,504},{28,20},{3... | collective-permute-start | bytes 829448 | tf_op jit(solution)/shard_map/ppermute | solution.py:27
  40.8 8.9 %collective-permute-start.3 = (bf16[9,4,3840]{2,1,0:T(4,128)(2,1)S(1)}, bf16[9,4,3840]{2,1,0:T(4,128)(2,1)S(1)}, u32[]{:S(2)}, u32[]{:S(2)}) collective-permute-start(bf16[9,4,3840]{2,1,0:T(4,128)(2,1)S(1)} %bitcast.52), channel_id=1, source_target_pairs={{0,64},{4,20},{8,72},{12,28},{16,80},{20,4},{24,88},{28,12},{32,96... | collective-permute-start | bytes 829448 | tf_op jit(solution)/shard_map/ppermute | solution.py:27
  43.0 12.5 %collective-permute-start = (bf16[9,4,3840]{2,1,0:T(4,128)(2,1)S(1)}, bf16[9,4,3840]{2,1,0:T(4,128)(2,1)S(1)}, u32[]{:S(2)}, u32[]{:S(2)}) collective-permute-start(bf16[9,4,3840]{2,1,0:T(4,128)(2,1)S(1)} %bitcast.53), channel_id=1, source_target_pairs={{0,32},{4,12},{8,40},{12,20},{16,48},{20,28},{24,56},{28,4},{32,64... | collective-permute-start | bytes 829448 | tf_op jit(solution)/shard_map/ppermute | solution.py:27
  49.9 18.1 %collective-permute-start.6 = (bf16[9,8,3840]{2,1,0:T(8,128)(2,1)S(1)}, bf16[9,8,3840]{2,1,0:T(8,128)(2,1)S(1)}, u32[]{:S(2)}, u32[]{:S(2)}) collective-permute-start(bf16[9,8,3840]{2,1,0:T(8,128)(2,1)S(1)} %pad_maximum_fusion.1.refs_1_), channel_id=1, source_target_pairs={{0,24},{4,484},{8,0},{12,492},{16,8},{20,500},{24,16},{28,508},{32... | collective-permute-start | bytes 1658888 | tf_op jit(solution)/shard_map/ppermute | solution.py:27
  55.8 14.1 %collective-permute-start.1 = (bf16[9,8,3840]{2,1,0:T(8,128)(2,1)S(1)}, bf16[9,8,3840]{2,1,0:T(8,128)(2,1)S(1)}, u32[]{:S(2)}, u32[]{:S(2)}) collective-permute-start(bf16[9,8,3840]{2,1,0:T(8,128)(2,1)S(1)} %pad_maximum_fusion.refs_0_), channel_id=1, source_target_pairs={{0,8},{4,36},{8,16},{12,44},{16,24},{20,52},{24,0},{28,60},{32,40}... | collective-permute-start | bytes 1658888 | tf_op jit(solution)/shard_map/ppermute | solution.py:27
  61.4 20.7 %collective-permute-start.4 = (bf16[9,8,3840]{2,1,0:T(8,128)(2,1)S(1)}, bf16[9,8,3840]{2,1,0:T(8,128)(2,1)S(1)}, u32[]{:S(2)}, u32[]{:S(2)}) collective-permute-start(bf16[9,8,3840]{2,1,0:T(8,128)(2,1)S(1)} %pad_maximum_fusion.1.refs_1_), channel_id=1, source_target_pairs={{0,8},{4,36},{8,16},{12,44},{16,24},{20,52},{24,0},{28,60},{32,40}... | collective-permute-start | bytes 1658888 | tf_op jit(solution)/shard_map/ppermute | solution.py:27
  64.1 18.0 %collective-permute-start.5 = (bf16[9,8,3840]{2,1,0:T(8,128)(2,1)S(1)}, bf16[9,8,3840]{2,1,0:T(8,128)(2,1)S(1)}, u32[]{:S(2)}, u32[]{:S(2)}) collective-permute-start(bf16[9,8,3840]{2,1,0:T(8,128)(2,1)S(1)} %pad_maximum_fusion.refs_0_), channel_id=1, source_target_pairs={{0,24},{4,484},{8,0},{12,492},{16,8},{20,500},{24,16},{28,508},{32... | collective-permute-start | bytes 1658888 | tf_op jit(solution)/shard_map/ppermute | solution.py:27
  68.0 21.2 %collective-permute-start.9 = (bf16[9,8,3840]{2,1,0:T(8,128)(2,1)S(1)}, bf16[9,8,3840]{2,1,0:T(8,128)(2,1)}, u32[]{:S(2)}, u32[]{:S(2)}) collective-permute-start(bf16[9,8,3840]{2,1,0:T(8,128)(2,1)S(1)} %collective-permute-done.6.refs_3_), channel_id=1, source_target_pairs={{0,24},{4,484},{8,0},{12,492},{16,8},{20,500},{24,16},{28,508},{32... | collective-permute-start | bytes 1658888 | tf_op jit(solution)/shard_map/ppermute | solution.py:27
  69.9 19.3 %collective-permute-start.8 = (bf16[9,8,3840]{2,1,0:T(8,128)(2,1)S(1)}, bf16[9,8,3840]{2,1,0:T(8,128)(2,1)}, u32[]{:S(2)}, u32[]{:S(2)}) collective-permute-start(bf16[9,8,3840]{2,1,0:T(8,128)(2,1)S(1)} %collective-permute-done.1.refs_0_), channel_id=1, source_target_pairs={{0,8},{4,36},{8,16},{12,44},{16,24},{20,52},{24,0},{28,60},{32,40}... | collective-permute-start | bytes 1658888 | tf_op jit(solution)/shard_map/ppermute | solution.py:27
  74.9 2.3 %copy-start.1 = (bf16[2,32,9,3840]{3,1,2,0:T(8,128)(2,1)S(1)}, bf16[2,32,9,3840]{3,1,2,0:T(8,128)(2,1)}, u32[]{:S(2)}) copy-start(bf16[2,32,9,3840]{3,1,2,0:T(8,128)(2,1)} %param.15) | copy-start | bytes 13271044
  89.2 16.7 %copy-start.2 = (s32[4,256]{0,1:T(8,128)S(1)}, s32[4,256]{0,1:T(8,128)}, u32[]{:S(2)}) copy-start(s32[4,256]{0,1:T(8,128)} %copy.38) | copy-start | bytes 12292
  94.5 17.0 %copy-start.5 = (bf16[3,3,1,32]{3,1,2,0:T(4,128)(2,1)S(1)}, bf16[3,3,1,32]{3,1,2,0:T(4,128)(2,1)}, u32[]{:S(2)}) copy-start(bf16[3,3,1,32]{3,1,2,0:T(4,128)(2,1)} %param.19) | copy-start | bytes 1732
  94.5 17.1 %copy-start.7 = (f32[32]{0:T(128)S(1)}, f32[32]{0:T(128)}, u32[]{:S(2)}) copy-start(f32[32]{0:T(128)} %param.20) | copy-start | bytes 388
  95.5 15.3 %all-to-all-start.1 = ((bf16[8,16,128]{2,1,0:T(8,128)(2,1)}), bf16[8,16,128]{2,1,0:T(8,128)(2,1)S(1)}, u32[]{:S(2)}, u32[]{:S(2)}) async-start(bf16[8,16,128]{2,1,0:T(8,128)(2,1)} %bitcast.13), calls=%async_computation.1 | async-start | bytes 65536 | tf_op jit(solution)/shard_map/all_to_all | solution.py:168
  116.6 4.5 %copy-start.4 = (bf16[3,3,32,64]{3,2,1,0:T(8,128)(2,1)S(1)}, bf16[3,3,32,64]{3,2,1,0:T(8,128)(2,1)}, u32[]{:S(2)}) copy-start(bf16[3,3,32,64]{3,2,1,0:T(8,128)(2,1)} %param.21) | copy-start | bytes 110596
  116.6 4.5 %copy-start.8 = (f32[64]{0:T(128)S(1)}, f32[64]{0:T(128)}, u32[]{:S(2)}) copy-start(f32[64]{0:T(128)} %param.22) | copy-start | bytes 772
  121.1 2.0 %copy-start.9 = (f32[128]{0:T(128)S(1)}, f32[128]{0:T(128)}, u32[]{:S(2)}) copy-start(f32[128]{0:T(128)} %param.24) | copy-start | bytes 1540
  121.1 2.0 %copy-start.10 = (bf16[128]{0:T(256)(128)(2,1)S(1)}, bf16[128]{0:T(256)(128)(2,1)}, u32[]{:S(2)}) copy-start(bf16[128]{0:T(256)(128)(2,1)} %param.25) | copy-start | bytes 772

commit v3 on v2

v3 whole, which is shorter than its diff:
```python
import functools

import jax
import jax.numpy as jnp
import numpy as np
from jax import lax
from jax.experimental import pallas as pl
from jax.experimental.pallas import tpu as pltpu
from jax.sharding import Mesh
from jax.sharding import PartitionSpec as P

NZ, NY, NC, NX = 16, 4, 2, 4
PLANE = ("z", "y", "c")
BACK = (0, 1, -1, 2)


def device_at(z, y, c):
    return ((z % NZ) * NY + y % NY) * NC + c


def shift(values, even, odd):
    pairs = []
    for z in range(NZ):
        for y in range(NY):
            for c, (dz, dy) in ((0, even), (1, odd)):
                pairs.append((device_at(z, y, c), device_at(z + dz, y + dy, c)))
    return lax.ppermute(values, PLANE, pairs)


def gather_stage(block):
    regions, width = block.shape
    flat = block.reshape(regions, width // 128, 128)
    groups = [[j + 4 * k for k in range(4)] for j in range(4)]
    four = lax.all_to_all(
        jnp.broadcast_to(flat, (4,) + flat.shape), "z", 0, 0, axis_index_groups=groups
    )
    four = four.reshape(4, regions, width).transpose(1, 0, 2)
    behind, ahead, two = (shift(four, (d, 0), (0, d)) for d in BACK[1:])
    return jnp.concatenate([four, behind], axis=1), jnp.concatenate([ahead, two], axis=1)


def best_means(regions, frames, corpus_ref, clip, rows, count):
    sims = lax.dot_general(
        corpus_ref[clip], rows, (((1,), (1,)), ((), ())), preferred_element_type=jnp.float32
    )
    best = sims[0:frames]
    for j in range(1, regions):
        best = jnp.maximum(best, sims[j * frames : (j + 1) * frames])
    totals = []
    for p in range(rows.shape[0] // (regions * count)):
        total = 0.0
        for i in range(regions):
            at = (p * regions + i) * count
            total = total + best[:, at : at + count]
        totals.append(total * (1.0 / regions))
    return totals


def stacked(refs):
    return jnp.concatenate([ref[...].reshape(-1, ref.shape[-1]) for ref in refs], axis=0)


def sims_body(regions, frames, own_ref, other_ref, *refs):
    out_ref = refs[-1]
    count = refs[0].shape[1]
    rows = stacked(refs[:-1])
    for half, corpus_ref in enumerate((own_ref, other_ref)):
        for clip in range(2):
            at = (half * 2 + clip) * frames
            totals = best_means(regions, frames, corpus_ref, clip, rows, count)
            for p, total in enumerate(totals):
                out_ref[at : at + frames, p * count : (p + 1) * count] = total


def table_body(regions, frames, own_ref, other_ref, prev_ref, place_ref, *refs):
    out_ref, last_ref = refs[-2:]
    sims_body(regions, frames, own_ref, other_ref, *refs[:-2], last_ref)
    prev = prev_ref[...].astype(jnp.bfloat16)
    last = last_ref[...].astype(jnp.bfloat16)
    done = prev.shape[1]
    dims = (((1,), (1,)), ((), ()))
    table = lax.dot_general(
        place_ref[:, :done], prev, dims, preferred_element_type=jnp.float32
    ) + lax.dot_general(place_ref[:, done:], last, dims, preferred_element_type=jnp.float32)
    table = table.astype(jnp.bfloat16)
    out_ref[0 : table.shape[0], :] = table
    out_ref[table.shape[0] :, :] = table


def kernel_call(body, shape, dtype, operands, scratch, flops):
    return pl.pallas_call(
        body,
        in_specs=[pl.BlockSpec(memory_space=pltpu.VMEM)] * len(operands),
        out_specs=pl.BlockSpec(memory_space=pltpu.VMEM),
        out_shape=jax.ShapeDtypeStruct(shape, dtype),
        scratch_shapes=scratch,
        compiler_params=pltpu.CompilerParams(vmem_limit_bytes=24 * 2**20),
        cost_estimate=pl.CostEstimate(
            flops=flops,
            bytes_accessed=sum(o.size * o.dtype.itemsize for o in operands),
            transcendentals=0,
        ),
    )(*operands)


def frame_sims(own, other, pieces):
    clips, rows, width = own.shape
    regions, count = pieces[0].shape[:2]
    frames = rows // regions
    total = count * len(pieces)
    body = functools.partial(sims_body, regions, frames)
    flops = 4 * clips * rows * regions * total * width
    return kernel_call(body, (2 * clips * frames, total), jnp.float32, [own, other, *pieces], [], flops)


def frame_table(own, other, prev, place, pieces):
    clips, rows, width = own.shape
    regions, count = pieces[0].shape[:2]
    frames = rows // regions
    total = count * len(pieces)
    body = functools.partial(table_body, regions, frames)
    flops = 4 * clips * rows * regions * total * width
    return kernel_call(
        body,
        (NC * NZ * NY, 2 * clips * frames),
        jnp.bfloat16,
        [own, other, prev, place, *pieces],
        [pltpu.VMEM((2 * clips * frames, total), jnp.float32)],
        flops,
    )


def row_order():
    group = 4
    order = np.zeros((4, 2, group, 8, NC, NX, group, NY), np.float32)
    for k in range(4):
        for f in range(16):
            frame = 2 * f - 1 + k
            if 0 <= frame < 32:
                for q in range(group):
                    order[k, f % 2, q, f // 2, frame % 2, frame // 8, q, frame % 8 // 2] = 1
    return order.reshape(4 * 64, 128)


def weights_body(first_ref, second_ref, third_ref, t1_ref, t2_ref, t3_ref):
    lanes = t1_ref.shape[1]
    row = lax.broadcasted_iota(jnp.int32, (128, lanes), 0) % 32
    lane = lax.broadcasted_iota(jnp.int32, (128, lanes), 1)
    column = (lane // 32) % 16 * 2 + lane // 512
    for dy in range(3):
        block = jnp.zeros((128, lanes), jnp.float32)
        for dx in range(3):
            tap = first_ref[dy * 3 + dx : dy * 3 + dx + 1, :]
            block = jnp.where(row == column + (dx - 1), tap, block)
        t1_ref[dy * 128 : (dy + 1) * 128, :] = block.astype(jnp.bfloat16)
    left = lax.broadcasted_iota(jnp.int32, (384, 128), 1) < 64

    def placed(tap, before, total):
        rows, width = tap.shape
        parts = [jnp.zeros((before, width), jnp.float32), tap]
        parts.append(jnp.zeros((total - before - rows, width), jnp.float32))
        return jnp.concatenate(parts, axis=0)

    for dy in range(3):
        tap = second_ref[dy * 96 : (dy + 1) * 96, :]
        for odd in range(2):
            one = placed(tap, 96 + 32 * odd, 384)
            two = placed(tap, 160 + 32 * odd, 384)
            t2_ref[dy * 384 : (dy + 1) * 384, odd * 128 : (odd + 1) * 128] = jnp.where(
                left, one, two
            ).astype(jnp.bfloat16)
    for dy in range(3):
        tap = third_ref[dy * 192 : (dy + 1) * 192, :]
        for w in range(2):
            t3_ref[dy * 384 : (dy + 1) * 384, w * 128 : (w + 1) * 128] = placed(
                tap, 64 + 64 * w, 384
            ).astype(jnp.bfloat16)


def spread_weights(first_kernel, second_kernel, third_kernel):
    first = jnp.tile(first_kernel.reshape(9, 32), (1, 32)).astype(jnp.float32)
    second = jnp.tile(second_kernel.reshape(288, 64), (1, 2)).astype(jnp.float32)
    third = third_kernel.reshape(576, 128).astype(jnp.float32)
    return pl.pallas_call(
        weights_body,
        in_specs=[pl.BlockSpec(memory_space=pltpu.VMEM)] * 3,
        out_specs=[pl.BlockSpec(memory_space=pltpu.VMEM)] * 3,
        out_shape=[
            jax.ShapeDtypeStruct((384, 1024), jnp.bfloat16),
            jax.ShapeDtypeStruct((1152, 256), jnp.bfloat16),
            jax.ShapeDtypeStruct((1152, 256), jnp.bfloat16),
        ],
        compiler_params=pltpu.CompilerParams(vmem_limit_bytes=24 * 2**20),
        cost_estimate=pl.CostEstimate(flops=4000000, bytes_accessed=4000000, transcendentals=0),
    )(first, second, third)


def dot(a, b):
    return jnp.dot(a, b, preferred_element_type=jnp.float32)


def rows_beside(values):
    rows = values.shape[0]
    at = lax.broadcasted_iota(jnp.int32, values.shape, 0) % 8
    before = jnp.where(at == 0, 0.0, pltpu.roll(values, 1, 0))
    after = jnp.where(at == 7, 0.0, pltpu.roll(values, rows - 1, 0))
    return before, after


def windows(layers, blocks):
    zero = jnp.zeros((layers[0].shape[0], 128), layers[0].dtype)
    out = []
    for t in range(blocks):
        parts = []
        for layer in layers:
            for b in (t - 1, t, t + 1):
                parts.append(layer[:, b * 128 : (b + 1) * 128] if 0 <= b < blocks else zero)
        out.append(jnp.concatenate(parts, axis=1))
    return out


def score_body(
    parts_ref, order_ref, t1_ref, b1_ref, t2_ref, b2_ref, t3_ref, b3_ref, weight_ref, bias_ref, listed_ref, out_ref
):
    bf16 = jnp.bfloat16
    maps = dot(order_ref[...], parts_ref[...])
    x = [maps[k * 64 : (k + 1) * 64] for k in range(4)]
    x = [(pltpu.roll(v, 64, 1) if k % 2 == 0 else v).astype(bf16) for k, v in enumerate(x)]
    both = jnp.concatenate(
        [jnp.concatenate(x[0:3], axis=1), jnp.concatenate(x[1:4], axis=1)], axis=0
    )
    clip = lax.broadcasted_iota(jnp.int32, both.shape, 1) // 32 % 4
    wide = both.astype(jnp.float32)
    lhs = jnp.concatenate([jnp.where(clip == k, wide, 0.0).astype(bf16) for k in range(4)], axis=0)
    first = dot(lhs, t1_ref[...])
    first = jnp.maximum(first[:, :512], first[:, 512:])
    first = jnp.concatenate(
        [jnp.maximum(first[k * 128 : k * 128 + 64], first[k * 128 + 64 : k * 128 + 128]) for k in range(4)],
        axis=0,
    )
    first = jnp.maximum(first + b1_ref[...], 0.0)
    even = jnp.concatenate([first[k * 64 : k * 64 + 32] for k in range(4)], axis=0)
    odd = jnp.concatenate([first[k * 64 + 32 : k * 64 + 64] for k in range(4)], axis=0)
    odd_before = rows_beside(odd)[0]
    even_after = rows_beside(even)[1]
    layers = [v.astype(bf16) for v in (odd_before, even, odd, even_after)]
    lhs = jnp.concatenate(windows(layers[0:3], 4) + windows(layers[1:4], 4), axis=0)
    second = dot(lhs, t2_ref[...])
    second = jnp.maximum(second[:, :128], second[:, 128:])
    second = jnp.maximum(second[:512], second[512:])
    second = jnp.maximum(second + b2_ref[...], 0.0)
    second = jnp.concatenate([second[t * 128 : (t + 1) * 128] for t in range(4)], axis=1)
    before, after = rows_beside(second)
    lhs = jnp.concatenate(windows([v.astype(bf16) for v in (before, second, after)], 4), axis=0)
    third = jnp.maximum(dot(lhs, t3_ref[...]) + b3_ref[...], 0.0).astype(bf16)
    score = dot(third, weight_ref[...])
    score = jnp.maximum(
        jnp.maximum(score[0:128], score[128:256]), jnp.maximum(score[256:384], score[384:512])
    )
    score = jnp.max(score, axis=1, keepdims=True) + bias_ref[...]
    score = score.reshape(16, 8, score.shape[1]).sum(axis=1) * 0.125
    listed = listed_ref[...]
    slot_query = lax.broadcasted_iota(jnp.int32, (1, listed.shape[1]), 1) // 2
    total = jnp.zeros(listed.shape, jnp.float32)
    for k in range(4):
        line = jnp.zeros((1, listed.shape[1]), jnp.float32)
        for q in range(4):
            line = jnp.where(slot_query == q, score[k * 4 + q : k * 4 + q + 1, : listed.shape[1]], line)
        total = jnp.where(listed == k, line, total)
    out_ref[...] = total


def slot_scores(parts, listed, spread, first_bias, second_bias, third_bias, score_weight, score_bias):
    lanes = jnp.arange(128, dtype=jnp.int32)[None, :] % 2
    half = jnp.arange(256, dtype=jnp.int32)[:, None] // 128
    weight = jnp.where(lanes == half, jnp.tile(score_weight, 2)[:, None], 0).astype(jnp.bfloat16)
    operands = [
        parts,
        jnp.asarray(row_order(), jnp.bfloat16),
        spread[0],
        jnp.tile(first_bias, 16)[None, :],
        spread[1],
        jnp.tile(second_bias, 2)[None, :],
        spread[2],
        jnp.tile(third_bias, 2)[None, :],
        weight,
        jnp.broadcast_to(score_bias[None, :], (1, 128)),
        listed,
    ]
    return kernel_call(score_body, listed.shape, jnp.float32, operands, [], 2 * 10**9)


def on_device(
    queries,
    corpus,
    cand_shard,
    cand_clip,
    cand_count,
    first_kernel,
    first_bias,
    second_kernel,
    second_bias,
    third_kernel,
    third_bias,
    score_weight,
    score_bias,
):
    z, y, c, x = (lax.axis_index(a) for a in ("z", "y", "c", "x"))
    clip_dev, frames, regions, width = corpus.shape
    slots = cand_shard.shape[1]
    group = cand_shard.shape[0] // NX

    own = corpus.transpose(0, 2, 1, 3).reshape(clip_dev, regions * frames, width)
    other = lax.ppermute(own, "c", [(0, 1), (1, 0)])

    first, last = gather_stage(queries[0, 0])
    behind_first = shift(first, (0, 1), (1, 0))
    ahead_last = shift(last, (0, -1), (-1, 0))
    behind_last = shift(last, (0, 1), (1, 0))
    ahead_first = shift(first, (0, -1), (-1, 0))
    two_first = shift(behind_first, (0, 1), (1, 0))
    two_last = shift(ahead_last, (0, -1), (-1, 0))
    col = jnp.arange(NZ * NY, dtype=jnp.int32)
    back = jnp.array(BACK, jnp.int32)
    far, near = back[col // 16], back[(col // 4) % 4]
    from_z = (z - jnp.where(c == 0, near, far)) % 4 + 4 * (col % 4)
    from_y = (y - jnp.where(c == 0, far, near)) % NY
    place = ((from_z * NY + from_y)[None, :] == col[:, None]).astype(jnp.bfloat16)

    def mine(listed):
        listed = lax.dynamic_slice_in_dim(listed, x * group, group, 0)
        listed = listed.reshape(group, NZ * NY, NC, slots // (NZ * NY * NC))
        return lax.dynamic_index_in_dim(listed, c, 2, keepdims=False)

    position = jnp.arange(slots, dtype=jnp.int32)
    usable = position[None, :] < cand_count[:, None]
    chip = z * NY + y
    listed = jnp.where(usable & (cand_shard // NC == chip), cand_shard % NC * clip_dev + cand_clip, -1)
    listed = mine(listed).transpose(1, 0, 2).reshape(NZ * NY, -1)

    spread = spread_weights(first_kernel, second_kernel, third_kernel)

    near = [first, last, behind_first, behind_last, ahead_first, ahead_last]
    prev = frame_sims(own, other, near)
    two, prev = lax.optimization_barrier(((two_first, two_last), prev))
    table = frame_table(own, other, prev, place, two)

    parts = lax.all_to_all(table, ("c", "x"), 0, 0, tiled=True)
    values = slot_scores(
        parts, listed, spread, first_bias, second_bias, third_bias, score_weight, score_bias
    )
    values = lax.all_to_all(values, ("z", "y"), 0, 0, tiled=True)
    return values.sum(axis=0).reshape(group, -1)


def solution(mesh):
    devices = mesh.devices.reshape(NZ, NY, NC, NX)
    grid = Mesh(devices, ("z", "y", "c", "x"))
    return jax.shard_map(
        on_device,
        mesh=grid,
        in_specs=(P("x", PLANE), P(PLANE)) + (P(),) * 11,
        out_specs=P("x", PLANE),
        check_vma=False,
    )
```

time: 147 us -> 132 us (0.90)
  blocking collectives: 46.5 us -> 19.7 us
  waiting for transfers between devices: 8.18 us -> 23.9 us
  starting transfers between devices: 51.7 us -> 62 us
  matrix products: 8.15 us -> 0 us
  other arithmetic: 7.37 us -> 1.65 us
    all_to_all x1 -> x0, blocking collectives: 26 us -> none  [gather_stage(): lax.all_to_all(jnp.broadcast_to(flat, (4,) + flat.shape), 'z', 0, 0, axis...]
    all_to_all x1 -> x2, waiting for transfers between devices: 4.16 us -> 18.7 us  [the longest x1 15.9 us: gather_stage(): lax.all_to_all(jnp.broadcast_to(flat, (4,) + flat.shape), 'z', 0, 0, axis...]
    all_to_all x1 -> x2, starting transfers between devices: 10.4 us -> 21.5 us  [the longest x1 11.9 us: on_device(): parts = lax.all_to_all(table, ('c', 'x'), 0, 0, tiled=True)]
    conv_general_dilated x2 -> x0, matrix products: 6.51 us -> none  [convolve(): lax.conv_general_dilated(inputs, kernel, (1, 1), 'SAME', dimension_number...]
    reduce_max x3 -> x0, other arithmetic: 5.06 us -> none  [the longest x2 5.02 us: shrink(): values.reshape(batch, height // 2, 2, width // 2, 2, chans).max(axis=(2, 4))]
    dot_general x2 -> x0, matrix products: 1.64 us -> none  [the longest x1 1.39 us: map_scores(): jnp.einsum('bhwc,c->bhw', third, score_weight, preferred_element_type=jnp...]
    pallas_call x3 -> x4, Pallas kernels: 17.3 us -> 16.5 us  [the longest x3 15.9 us: kernel_call(): pl.pallas_call(body, in_specs=[pl.BlockSpec(memory_space=pltpu.VMEM)] * l...]
  transfers between devices with their start and end apart: 11 -> 12, of which waited for: 2 -> 5; matrix products, arithmetic and copies ran while one was open for 2% -> 3% of each run, Pallas kernels for 8% -> 6%
where the time goes in v3:
time: 132 us; the launch traced here: 131 us
  starting transfers between devices  62 us (47%)
  waiting for transfers between devices  23.9 us (18%)
  blocking collectives  19.7 us (15%)
  Pallas kernels  16.5 us (12%)
  local copies, waits for them, and re-layouts  5.86 us (4%)
  other arithmetic  1.65 us (1%)
    ppermute x9, starting transfers between devices, shift(): return lax.ppermute(values, PLANE, pairs)  31.7 us
    all_to_all x1, blocking collectives, on_device(): values = lax.all_to_all(values, ('z', 'y'), 0, 0, tiled=True)  19.7 us
    pallas_call x3, Pallas kernels, kernel_call(): pl.pallas_call(body, in_specs=[pl.BlockSpec(memory_space=pltpu.VMEM)] * l...  15.9 us
    all_to_all x1, waiting for transfers between devices, gather_stage(): lax.all_to_all(jnp.broadcast_to(flat, (4,) + flat.shape), 'z', 0, 0, axis...  15.9 us
    all_to_all x1, starting transfers between devices, on_device(): parts = lax.all_to_all(table, ('c', 'x'), 0, 0, tiled=True)  11.9 us
    all_to_all x1, starting transfers between devices, gather_stage(): lax.all_to_all(jnp.broadcast_to(flat, (4,) + flat.shape), 'z', 0, 0, axis...  9.58 us
    ppermute x1, starting transfers between devices, on_device(): other = lax.ppermute(own, 'c', [(0, 1), (1, 0)])  8.91 us
    ppermute x9, waiting for transfers between devices, shift(): return lax.ppermute(values, PLANE, pairs)  5.16 us
  transfers between devices with their start and end apart: 12, of which 5 were waited for; matrix products, arithmetic and copies ran while one was open for 3% of the time, Pallas kernels for 6%

profile of v3, /device:TPU:1, one launch (start us, length us, event | category | flops | bytes accessed | tf_op | source)
XLA Modules:
  0.0 130.7 jit_solution(16672783847483254384)
XLA Ops:
  0.0 0.0 copy-start
  0.0 0.0 copy-start.8
  0.0 0.0 copy-start.5
  0.0 8.9 %collective-permute-start = (bf16[2,288,3840]{2,1,0:T(8,128)(2,1)}, bf16[2,288,3840]{2,1,0:T(8,128)(2,1)}, u32[]{:S(2)}, u32[]{:S(2)}) collective-permute-start(bf16[2,288,3840]{2,1,0:T(8,128)(2,1)} %bitcast.40), channel_id=1, source_target_pairs={{0,4},{4,0},{1,5},{5,1},{2,6},{6,2},{3,7},{7,3},{8,12},{12,8},{9,1... | collective-permute-start | bytes 13271048 | tf_op jit(solution)/shard_map/ppermute | solution.py:314
  8.9 1.0 reshape_squeeze.3
  9.9 0.8 broadcast_in_dim.22
  10.7 9.6 %all-to-all-start = ((bf16[4,9,30,128]{3,2,1,0:T(8,128)(2,1)}), bf16[4,9,30,128]{3,2,1,0:T(8,128)(2,1)S(1)}, u32[]{:S(2)}, u32[]{:S(2)}) async-start(bf16[4,9,30,128]{3,2,1,0:T(8,128)(2,1)} %broadcast_in_dim.22), calls=%async_computation | async-start | bytes 589824 | tf_op jit(solution)/shard_map/all_to_all | solution.py:34
  20.2 0.0 copy-done
  20.3 0.0 copy-done.8
  20.3 0.1 dynamic-slice
  20.4 0.0 copy-done.5
  20.4 0.8 fusion.5
  21.2 15.9 %all-to-all-done = bf16[4,9,30,128]{3,2,1,0:T(8,128)(2,1)S(1)} async-done(((bf16[4,9,30,128]{3,2,1,0:T(8,128)(2,1)}), bf16[4,9,30,128]{3,2,1,0:T(8,128)(2,1)S(1)}, u32[]{:S(2)}, u32[]{:S(2)}) %all-to-all-start) | async-done | bytes 276512 | tf_op jit(solution)/shard_map/all_to_all | solution.py:34
  37.1 0.1 reshape.251
  37.2 4.6 %collective-permute-start.4 = (bf16[9,4,3840]{2,1,0:T(4,128)(2,1)S(1)}, bf16[9,4,3840]{2,1,0:T(4,128)(2,1)S(1)}, u32[]{:S(2)}, u32[]{:S(2)}) collective-permute-start(bf16[9,4,3840]{2,1,0:T(4,128)(2,1)S(1)} %bitcast.46), channel_id=1, source_target_pairs={{0,480},{4,28},{8,488},{12,4},{16,496},{20,12},{24,504},{28,20},{3... | collective-permute-start | bytes 829448 | tf_op jit(solution)/shard_map/ppermute | solution.py:27
  41.8 2.3 %collective-permute-start.5 = (bf16[9,4,3840]{2,1,0:T(4,128)(2,1)S(1)}, bf16[9,4,3840]{2,1,0:T(4,128)(2,1)S(1)}, u32[]{:S(2)}, u32[]{:S(2)}) collective-permute-start(bf16[9,4,3840]{2,1,0:T(4,128)(2,1)S(1)} %bitcast.47), channel_id=1, source_target_pairs={{0,64},{4,20},{8,72},{12,28},{16,80},{20,4},{24,88},{28,12},{32,96... | collective-permute-start | bytes 829448 | tf_op jit(solution)/shard_map/ppermute | solution.py:27
  44.1 0.1 copy.32
  44.2 0.0 copy-done.4
  44.3 0.0 copy-start.3
  44.3 2.7 %collective-permute-start.1 = (bf16[9,4,3840]{2,1,0:T(4,128)(2,1)S(1)}, bf16[9,4,3840]{2,1,0:T(4,128)(2,1)S(1)}, u32[]{:S(2)}, u32[]{:S(2)}) collective-permute-start(bf16[9,4,3840]{2,1,0:T(4,128)(2,1)S(1)} %bitcast.48), channel_id=1, source_target_pairs={{0,32},{4,12},{8,40},{12,20},{16,48},{20,28},{24,56},{28,4},{32,64... | collective-permute-start | bytes 829448 | tf_op jit(solution)/shard_map/ppermute | solution.py:27
  47.0 0.0 collective-permute-done.4
  47.0 3.6 %collective-permute-done.5 = bf16[9,4,3840]{2,1,0:T(4,128)(2,1)S(1)} collective-permute-done((bf16[9,4,3840]{2,1,0:T(4,128)(2,1)S(1)}, bf16[9,4,3840]{2,1,0:T(4,128)(2,1)S(1)}, u32[]{:S(2)}, u32[]{:S(2)}) %collective-permute-start.5) | collective-permute-done | bytes 276512 | tf_op jit(solution)/shard_map/ppermute | solution.py:27
  50.7 0.3 pad_maximum_fusion.1.refs_1_
  50.9 5.7 %collective-permute-start.6 = (bf16[9,8,3840]{2,1,0:T(8,128)(2,1)S(1)}, bf16[9,8,3840]{2,1,0:T(8,128)(2,1)S(1)}, u32[]{:S(2)}, u32[]{:S(2)}) collective-permute-start(bf16[9,8,3840]{2,1,0:T(8,128)(2,1)S(1)} %pad_maximum_fusion.1.refs_1_), channel_id=1, source_target_pairs={{0,24},{4,484},{8,0},{12,492},{16,8},{20,500},{24,16},{28,508},{32... | collective-permute-start | bytes 1658888 | tf_op jit(solution)/shard_map/ppermute | solution.py:27
  56.6 0.0 collective-permute-done.1
  56.6 0.3 pad_maximum_fusion.refs_0_
  56.9 4.6 %collective-permute-start.2 = (bf16[9,8,3840]{2,1,0:T(8,128)(2,1)S(1)}, bf16[9,8,3840]{2,1,0:T(8,128)(2,1)S(1)}, u32[]{:S(2)}, u32[]{:S(2)}) collective-permute-start(bf16[9,8,3840]{2,1,0:T(8,128)(2,1)S(1)} %pad_maximum_fusion.refs_0_), channel_id=1, source_target_pairs={{0,8},{4,36},{8,16},{12,44},{16,24},{20,52},{24,0},{28,60},{32,40}... | collective-permute-start | bytes 1658888 | tf_op jit(solution)/shard_map/ppermute | solution.py:27
  61.5 0.1 compare_select_fusion.weight_ref
  61.6 2.9 %collective-permute-start.8 = (bf16[9,8,3840]{2,1,0:T(8,128)(2,1)S(1)}, bf16[9,8,3840]{2,1,0:T(8,128)(2,1)S(1)}, u32[]{:S(2)}, u32[]{:S(2)}) collective-permute-start(bf16[9,8,3840]{2,1,0:T(8,128)(2,1)S(1)} %pad_maximum_fusion.1.refs_1_), channel_id=1, source_target_pairs={{0,8},{4,36},{8,16},{12,44},{16,24},{20,52},{24,0},{28,60},{32,40}... | collective-permute-start | bytes 1658888 | tf_op jit(solution)/shard_map/ppermute | solution.py:27
  64.6 3.6 %collective-permute-start.9 = (bf16[9,8,3840]{2,1,0:T(8,128)(2,1)S(1)}, bf16[9,8,3840]{2,1,0:T(8,128)(2,1)S(1)}, u32[]{:S(2)}, u32[]{:S(2)}) collective-permute-start(bf16[9,8,3840]{2,1,0:T(8,128)(2,1)S(1)} %pad_maximum_fusion.refs_0_), channel_id=1, source_target_pairs={{0,24},{4,484},{8,0},{12,492},{16,8},{20,500},{24,16},{28,508},{32... | collective-permute-start | bytes 1658888 | tf_op jit(solution)/shard_map/ppermute | solution.py:27
  68.2 0.0 copy-done.3
  68.2 0.0 collective-permute-done.6.refs_5_
  68.2 1.9 %collective-permute-start.7 = (bf16[9,8,3840]{2,1,0:T(8,128)(2,1)S(1)}, bf16[9,8,3840]{2,1,0:T(8,128)(2,1)S(1)}, u32[]{:S(2)}, u32[]{:S(2)}) collective-permute-start(bf16[9,8,3840]{2,1,0:T(8,128)(2,1)S(1)} %collective-permute-done.6.refs_5_), channel_id=1, source_target_pairs={{0,24},{4,484},{8,0},{12,492},{16,8},{20,500},{24,16},{28,508},{32... | collective-permute-start | bytes 1658888 | tf_op jit(solution)/shard_map/ppermute | solution.py:27
  70.2 0.0 collective-permute-done.2.refs_2_
  70.2 3.4 %collective-permute-start.3 = (bf16[9,8,3840]{2,1,0:T(8,128)(2,1)S(1)}, bf16[9,8,3840]{2,1,0:T(8,128)(2,1)S(1)}, u32[]{:S(2)}, u32[]{:S(2)}) collective-permute-start(bf16[9,8,3840]{2,1,0:T(8,128)(2,1)S(1)} %collective-permute-done.2.refs_2_), channel_id=1, source_target_pairs={{0,8},{4,36},{8,16},{12,44},{16,24},{20,52},{24,0},{28,60},{32,40}... | collective-permute-start | bytes 1658888 | tf_op jit(solution)/shard_map/ppermute | solution.py:27
  73.6 1.0 collective-permute-done.8.refs_3_
  74.6 0.5 collective-permute-done.9.refs_4_
  75.1 0.0 collective-permute-done.other_ref
  75.1 2.3 %copy-done.1 = bf16[2,32,9,3840]{3,1,2,0:T(8,128)(2,1)S(1)} copy-done((bf16[2,32,9,3840]{3,1,2,0:T(8,128)(2,1)S(1)}, bf16[2,32,9,3840]{3,1,2,0:T(8,128)(2,1)}, u32[]{:S(2)}) %copy-start.1) | copy-done | bytes 4423704
  77.4 7.2 %shard_map.145.prev_ref = f32[128,48]{1,0:T(8,128)S(1)} custom-call(bf16[2,288,3840]{2,1,0:T(8,128)(2,1)S(1)} %bitcast.41, bf16[2,288,3840]{2,1,0:T(8,128)(2,1)} %collective-permute-done.other_ref, bf16[9,8,3840]{2,1,0:T(8,128)(2,1)S(1)} %pad_maximum_fusion.refs_0_, bf16[9,8,3840]{2,1,0:T(8,128)(2,1)S(1)} %pad_maximum_fusion.1.refs_1_, ...), custom_call_target="tpu_custom_call" | custom-call | flops 3822059520 | bytes 12165120 | tf_op jit(solution)/shard_map/pallas_call | solution.py:91
  84.6 0.0 collective-permute-done.7.refs_1_
  84.6 0.0 collective-permute-done.3.refs_0_
  84.6 5.7 %shard_map.146 = bf16[128,128]{1,0:T(8,128)(2,1)} custom-call(bf16[2,288,3840]{2,1,0:T(8,128)(2,1)S(1)} %bitcast.42, bf16[2,288,3840]{2,1,0:T(8,128)(2,1)} %collective-permute-done.other_ref, f32[128,48]{1,0:T(8,128)S(1)} %shard_map.145.prev_ref, bf16[64,64]{1,0:T(8,128)(2,1)S(1)} %fusion.place_ref, bf16[9,8,3840]{2,1,0:T(8,128)(2,1)S(1)} %collective-permute-done.3.refs_0_, ...), custom_call_target="tpu_custom_call" | custom-call | flops 1274019840 | bytes 9986048 | tf_op jit(solution)/shard_map/pallas_call | solution.py:91
  90.3 0.0 copy-start.2
  90.3 11.9 %all-to-all-start.1 = ((bf16[8,16,128]{2,1,0:T(8,128)(2,1)}), bf16[8,16,128]{2,1,0:T(8,128)(2,1)S(1)}, u32[]{:S(2)}, u32[]{:S(2)}) async-start(bf16[8,16,128]{2,1,0:T(8,128)(2,1)} %bitcast.6), calls=%async_computation.1 | async-start | bytes 65536 | tf_op jit(solution)/shard_map/all_to_all | solution.py:348
  102.2 0.1 copy.33
  102.3 0.1 copy.35.listed_ref
  102.4 0.1 copy.30
  102.5 0.1 copy.31.second_ref
  102.6 0.0 copy-done.6
  102.7 0.1 convert_element_type.27.first_ref
  102.8 0.0 copy-done.7
  102.8 0.1 broadcast_in_dim_tile.10.b1_ref
  102.9 0.0 copy-done.9
  102.9 0.1 broadcast_in_dim_tile.11.b2_ref
  103.6 0.6 shard_map.147
  104.2 2.9 %all-to-all-done.1 = bf16[8,16,128]{2,1,0:T(8,128)(2,1)S(1)} async-done(((bf16[8,16,128]{2,1,0:T(8,128)(2,1)}), bf16[8,16,128]{2,1,0:T(8,128)(2,1)S(1)}, u32[]{:S(2)}, u32[]{:S(2)}) %all-to-all-start.1) | async-done | bytes 32800 | tf_op jit(solution)/shard_map/all_to_all | solution.py:348
  107.1 0.0 copy-done.10
  107.1 0.0 copy-done.2
  107.1 3.0 %shard_map.148 = f32[64,8]{1,0:T(8,128)S(1)} custom-call(bf16[128,128]{1,0:T(8,128)(2,1)S(1)} %bitcast.43, bf16[256,128]{1,0:T(8,128)(2,1)S(1)} %copy-done.2, bf16[384,1024]{1,0:T(8,128)(2,1)S(1)} %get-tuple-element.14.t1_ref, f32[1,512]{1,0:T(1,128)S(1)} %broadcast_in_dim_tile.10.b1_ref, bf16[1152,256]{1,0:T(8,128)(2,1)S(1)} %get-tuple-element.15.t2_ref, ...), custom_call_target="tpu_custom_call" | custom-call | flops 2000000000 | bytes 2136064 | tf_op jit(solution)/shard_map/pallas_call | solution.py:91
  110.2 19.7 %all_to_all.25 = f32[64,1,8]{2,1,0:T(1,128)S(1)} all-to-all(f32[64,1,8]{2,1,0:T(1,128)S(1)} %bitcast.44), channel_id=1, replica_groups=mesh['z'=16,'y'=4,'c'=2,'x'=4] {'z','y'}, dimensions={0} | all-to-all | bytes 4096 | tf_op jit(solution)/shard_map/all_to_all | solution.py:352
  129.9 0.1 reduce_sum.9
  130.0 0.1 reshape.254
  130.1 0.7 copy.37
  (25 shorter events, 0.2 us)
Async XLA Ops:
  0.0 20.3 %copy-start = (bf16[128]{0:T(256)(128)(2,1)S(1)}, bf16[128]{0:T(256)(128)(2,1)}, u32[]{:S(2)}) copy-start(bf16[128]{0:T(256)(128)(2,1)} %param.26) | copy-start | bytes 772
  0.0 20.3 %copy-start.8 = (s32[16]{0:T(128)S(1)}, s32[16]{0:T(128)}, u32[]{:S(2)}) copy-start(s32[16]{0:T(128)} %param.19) | copy-start | bytes 196
  0.0 20.4 %copy-start.5 = (s32[16,256]{1,0:T(8,128)S(1)}, s32[16,256]{1,0:T(8,128)}, u32[]{:S(2)}) copy-start(s32[16,256]{1,0:T(8,128)} %param.17) | copy-start | bytes 49156
  0.0 75.1 %collective-permute-start = (bf16[2,288,3840]{2,1,0:T(8,128)(2,1)}, bf16[2,288,3840]{2,1,0:T(8,128)(2,1)}, u32[]{:S(2)}, u32[]{:S(2)}) collective-permute-start(bf16[2,288,3840]{2,1,0:T(8,128)(2,1)} %bitcast.40), channel_id=1, source_target_pairs={{0,4},{4,0},{1,5},{5,1},{2,6},{6,2},{3,7},{7,3},{8,12},{12,8},{9,1... | collective-permute-start | bytes 13271048 | tf_op jit(solution)/shard_map/ppermute | solution.py:314
  10.7 33.6 %copy-start.4 = (bf16[3,3,32,64]{3,2,1,0:T(8,128)(2,1)S(1)}, bf16[3,3,32,64]{3,2,1,0:T(8,128)(2,1)}, u32[]{:S(2)}) copy-start(bf16[3,3,32,64]{3,2,1,0:T(8,128)(2,1)} %param.22) | copy-start | bytes 110596
  10.7 26.4 %all-to-all-start = ((bf16[4,9,30,128]{3,2,1,0:T(8,128)(2,1)}), bf16[4,9,30,128]{3,2,1,0:T(8,128)(2,1)S(1)}, u32[]{:S(2)}, u32[]{:S(2)}) async-start(bf16[4,9,30,128]{3,2,1,0:T(8,128)(2,1)} %broadcast_in_dim.22), calls=%async_computation | async-start | bytes 589824 | tf_op jit(solution)/shard_map/all_to_all | solution.py:34
  37.2 9.9 %collective-permute-start.4 = (bf16[9,4,3840]{2,1,0:T(4,128)(2,1)S(1)}, bf16[9,4,3840]{2,1,0:T(4,128)(2,1)S(1)}, u32[]{:S(2)}, u32[]{:S(2)}) collective-permute-start(bf16[9,4,3840]{2,1,0:T(4,128)(2,1)S(1)} %bitcast.46), channel_id=1, source_target_pairs={{0,480},{4,28},{8,488},{12,4},{16,496},{20,12},{24,504},{28,20},{3... | collective-permute-start | bytes 829448 | tf_op jit(solution)/shard_map/ppermute | solution.py:27
  41.8 8.8 %collective-permute-start.5 = (bf16[9,4,3840]{2,1,0:T(4,128)(2,1)S(1)}, bf16[9,4,3840]{2,1,0:T(4,128)(2,1)S(1)}, u32[]{:S(2)}, u32[]{:S(2)}) collective-permute-start(bf16[9,4,3840]{2,1,0:T(4,128)(2,1)S(1)} %bitcast.47), channel_id=1, source_target_pairs={{0,64},{4,20},{8,72},{12,28},{16,80},{20,4},{24,88},{28,12},{32,96... | collective-permute-start | bytes 829448 | tf_op jit(solution)/shard_map/ppermute | solution.py:27
  44.3 23.9 %copy-start.3 = (bf16[3,3,64,128]{3,2,1,0:T(8,128)(2,1)S(1)}, bf16[3,3,64,128]{3,2,1,0:T(8,128)(2,1)}, u32[]{:S(2)}) copy-start(bf16[3,3,64,128]{3,2,1,0:T(8,128)(2,1)} %param.24) | copy-start | bytes 442372
  44.3 12.3 %collective-permute-start.1 = (bf16[9,4,3840]{2,1,0:T(4,128)(2,1)S(1)}, bf16[9,4,3840]{2,1,0:T(4,128)(2,1)S(1)}, u32[]{:S(2)}, u32[]{:S(2)}) collective-permute-start(bf16[9,4,3840]{2,1,0:T(4,128)(2,1)S(1)} %bitcast.48), channel_id=1, source_target_pairs={{0,32},{4,12},{8,40},{12,20},{16,48},{20,28},{24,56},{28,4},{32,64... | collective-permute-start | bytes 829448 | tf_op jit(solution)/shard_map/ppermute | solution.py:27
  50.9 17.3 %collective-permute-start.6 = (bf16[9,8,3840]{2,1,0:T(8,128)(2,1)S(1)}, bf16[9,8,3840]{2,1,0:T(8,128)(2,1)S(1)}, u32[]{:S(2)}, u32[]{:S(2)}) collective-permute-start(bf16[9,8,3840]{2,1,0:T(8,128)(2,1)S(1)} %pad_maximum_fusion.1.refs_1_), channel_id=1, source_target_pairs={{0,24},{4,484},{8,0},{12,492},{16,8},{20,500},{24,16},{28,508},{32... | collective-permute-start | bytes 1658888 | tf_op jit(solution)/shard_map/ppermute | solution.py:27
  56.9 13.3 %collective-permute-start.2 = (bf16[9,8,3840]{2,1,0:T(8,128)(2,1)S(1)}, bf16[9,8,3840]{2,1,0:T(8,128)(2,1)S(1)}, u32[]{:S(2)}, u32[]{:S(2)}) collective-permute-start(bf16[9,8,3840]{2,1,0:T(8,128)(2,1)S(1)} %pad_maximum_fusion.refs_0_), channel_id=1, source_target_pairs={{0,8},{4,36},{8,16},{12,44},{16,24},{20,52},{24,0},{28,60},{32,40}... | collective-permute-start | bytes 1658888 | tf_op jit(solution)/shard_map/ppermute | solution.py:27
  61.6 12.9 %collective-permute-start.8 = (bf16[9,8,3840]{2,1,0:T(8,128)(2,1)S(1)}, bf16[9,8,3840]{2,1,0:T(8,128)(2,1)S(1)}, u32[]{:S(2)}, u32[]{:S(2)}) collective-permute-start(bf16[9,8,3840]{2,1,0:T(8,128)(2,1)S(1)} %pad_maximum_fusion.1.refs_1_), channel_id=1, source_target_pairs={{0,8},{4,36},{8,16},{12,44},{16,24},{20,52},{24,0},{28,60},{32,40}... | collective-permute-start | bytes 1658888 | tf_op jit(solution)/shard_map/ppermute | solution.py:27
  64.6 10.5 %collective-permute-start.9 = (bf16[9,8,3840]{2,1,0:T(8,128)(2,1)S(1)}, bf16[9,8,3840]{2,1,0:T(8,128)(2,1)S(1)}, u32[]{:S(2)}, u32[]{:S(2)}) collective-permute-start(bf16[9,8,3840]{2,1,0:T(8,128)(2,1)S(1)} %pad_maximum_fusion.refs_0_), channel_id=1, source_target_pairs={{0,24},{4,484},{8,0},{12,492},{16,8},{20,500},{24,16},{28,508},{32... | collective-permute-start | bytes 1658888 | tf_op jit(solution)/shard_map/ppermute | solution.py:27
  68.2 16.4 %collective-permute-start.7 = (bf16[9,8,3840]{2,1,0:T(8,128)(2,1)S(1)}, bf16[9,8,3840]{2,1,0:T(8,128)(2,1)S(1)}, u32[]{:S(2)}, u32[]{:S(2)}) collective-permute-start(bf16[9,8,3840]{2,1,0:T(8,128)(2,1)S(1)} %collective-permute-done.6.refs_5_), channel_id=1, source_target_pairs={{0,24},{4,484},{8,0},{12,492},{16,8},{20,500},{24,16},{28,508},{32... | collective-permute-start | bytes 1658888 | tf_op jit(solution)/shard_map/ppermute | solution.py:27
  70.2 14.4 %collective-permute-start.3 = (bf16[9,8,3840]{2,1,0:T(8,128)(2,1)S(1)}, bf16[9,8,3840]{2,1,0:T(8,128)(2,1)S(1)}, u32[]{:S(2)}, u32[]{:S(2)}) collective-permute-start(bf16[9,8,3840]{2,1,0:T(8,128)(2,1)S(1)} %collective-permute-done.2.refs_2_), channel_id=1, source_target_pairs={{0,8},{4,36},{8,16},{12,44},{16,24},{20,52},{24,0},{28,60},{32,40}... | collective-permute-start | bytes 1658888 | tf_op jit(solution)/shard_map/ppermute | solution.py:27
  75.1 2.3 %copy-start.1 = (bf16[2,32,9,3840]{3,1,2,0:T(8,128)(2,1)S(1)}, bf16[2,32,9,3840]{3,1,2,0:T(8,128)(2,1)}, u32[]{:S(2)}) copy-start(bf16[2,32,9,3840]{3,1,2,0:T(8,128)(2,1)} %param.16) | copy-start | bytes 13271044
  90.3 12.4 %copy-start.6 = (bf16[3,3,1,32]{3,1,2,0:T(4,128)(2,1)S(1)}, bf16[3,3,1,32]{3,1,2,0:T(4,128)(2,1)}, u32[]{:S(2)}) copy-start(bf16[3,3,1,32]{3,1,2,0:T(4,128)(2,1)} %param.20) | copy-start | bytes 1732
  90.3 12.5 %copy-start.7 = (f32[32]{0:T(128)S(1)}, f32[32]{0:T(128)}, u32[]{:S(2)}) copy-start(f32[32]{0:T(128)} %param.21) | copy-start | bytes 388
  90.3 12.6 %copy-start.9 = (f32[64]{0:T(128)S(1)}, f32[64]{0:T(128)}, u32[]{:S(2)}) copy-start(f32[64]{0:T(128)} %param.23) | copy-start | bytes 772
  90.3 16.8 %copy-start.10 = (f32[128]{0:T(128)S(1)}, f32[128]{0:T(128)}, u32[]{:S(2)}) copy-start(f32[128]{0:T(128)} %param.25) | copy-start | bytes 1540
  90.3 16.8 %copy-start.2 = (bf16[256,128]{1,0:T(8,128)(2,1)S(1)}, bf16[256,128]{1,0:T(8,128)(2,1)}, u32[]{:S(2)}) copy-start(bf16[256,128]{1,0:T(8,128)(2,1)} %constant.141.clone.order_ref) | copy-start | bytes 196612
  90.3 16.8 %all-to-all-start.1 = ((bf16[8,16,128]{2,1,0:T(8,128)(2,1)}), bf16[8,16,128]{2,1,0:T(8,128)(2,1)S(1)}, u32[]{:S(2)}, u32[]{:S(2)}) async-start(bf16[8,16,128]{2,1,0:T(8,128)(2,1)} %bitcast.6), calls=%async_computation.1 | async-start | bytes 65536 | tf_op jit(solution)/shard_map/all_to_all | solution.py:348

commit v4 on v3

v4 whole, which is shorter than its diff:
```python
import functools

import jax
import jax.numpy as jnp
import numpy as np
from jax import lax
from jax.experimental import pallas as pl
from jax.experimental.pallas import tpu as pltpu
from jax.sharding import Mesh
from jax.sharding import PartitionSpec as P

NZ, NY, NC, NX = 16, 4, 2, 4
PLANE = ("z", "y", "c")


def device_at(z, y, c):
    return ((z % NZ) * NY + y % NY) * NC + c


def send(values, even, odd):
    pairs = []
    for z in range(NZ):
        for y in range(NY):
            for c, to in ((0, even), (1, odd)):
                pairs.append((device_at(z, y, c), device_at(*to(z, y), c)))
    return lax.ppermute(values, PLANE, pairs)


def shift(values, d):
    return send(values, lambda z, y: (z, y + d), lambda z, y: (z + d, y))


def paired(values, side):
    return send(values, lambda z, y: (partner(z, side), y), lambda z, y: (z, partner(y, side)))


def partner(at, side):
    return at + 1 if at % 2 == side else at - 1


def gather_classes(block):
    regions, width = block.shape
    flat = block.reshape(regions, width // 128, 128)
    groups = [[j + 4 * k for k in range(4)] for j in range(4)]
    four = lax.all_to_all(
        jnp.broadcast_to(flat, (4,) + flat.shape), "z", 0, 0, axis_index_groups=groups
    )
    return four.reshape(4, regions, width).transpose(1, 0, 2)


def best_means(regions, frames, corpus_ref, clip, rows, count):
    sims = lax.dot_general(
        corpus_ref[clip], rows, (((1,), (1,)), ((), ())), preferred_element_type=jnp.float32
    )
    best = sims[0:frames]
    for j in range(1, regions):
        best = jnp.maximum(best, sims[j * frames : (j + 1) * frames])
    totals = []
    for p in range(rows.shape[0] // (regions * count)):
        total = 0.0
        for i in range(regions):
            at = (p * regions + i) * count
            total = total + best[:, at : at + count]
        totals.append(total * (1.0 / regions))
    return totals


def stacked(refs):
    return jnp.concatenate([ref[...].reshape(-1, ref.shape[-1]) for ref in refs], axis=0)


def sims_body(regions, frames, own_ref, other_ref, *refs):
    out_ref = refs[-1]
    count = refs[0].shape[1]
    rows = stacked(refs[:-1])
    for half, corpus_ref in enumerate((own_ref, other_ref)):
        for clip in range(2):
            at = (half * 2 + clip) * frames
            totals = best_means(regions, frames, corpus_ref, clip, rows, count)
            for p, total in enumerate(totals):
                out_ref[at : at + frames, p * count : (p + 1) * count] = total


def column_places(z, y, c):
    shape = (NZ * NY, NZ * NY)
    col = lax.broadcasted_iota(jnp.int32, shape, 1)
    row = lax.broadcasted_iota(jnp.int32, shape, 0)
    far = col // 16
    far = jnp.where(far == 2, -1, jnp.where(far == 3, 2, far))
    step = col // 4 % 4

    def near(at):
        beside = jnp.where(at % 2 == 0, at - 1, at + 1)
        start = jnp.where(step < 2, at, (beside + NZ) % NZ)
        return jnp.where(step % 2 == 0, start, start + 1 - start % 2 * 2)

    from_z = jnp.where(c == 0, near(z), z - far + NZ) % 4 + 4 * (col % 4)
    from_y = jnp.where(c == 0, y - far + NZ, near(y)) % NY
    return jnp.where(from_z * NY + from_y == row, 1.0, 0.0).astype(jnp.bfloat16)


def table_body(regions, frames, at_ref, own_ref, other_ref, prev_ref, *refs):
    out_ref, last_ref = refs[-2:]
    place = column_places(at_ref[0], at_ref[1], at_ref[2])
    sims_body(regions, frames, own_ref, other_ref, *refs[:-2], last_ref)
    prev = prev_ref[...].astype(jnp.bfloat16)
    last = last_ref[...].astype(jnp.bfloat16)
    done = prev.shape[1]
    dims = (((1,), (1,)), ((), ()))
    table = lax.dot_general(
        place[:, :done], prev, dims, preferred_element_type=jnp.float32
    ) + lax.dot_general(place[:, done:], last, dims, preferred_element_type=jnp.float32)
    table = table.astype(jnp.bfloat16)
    out_ref[0 : table.shape[0], :] = table
    out_ref[table.shape[0] :, :] = table


def kernel_call(body, outs, operands, scratch, flops, scalars=0):
    spaces = [pltpu.SMEM] * scalars + [pltpu.VMEM] * (len(operands) - scalars)
    return pl.pallas_call(
        body,
        in_specs=[pl.BlockSpec(memory_space=space) for space in spaces],
        out_specs=[pl.BlockSpec(memory_space=pltpu.VMEM)] * len(outs),
        out_shape=[jax.ShapeDtypeStruct(*out) for out in outs],
        scratch_shapes=scratch,
        compiler_params=pltpu.CompilerParams(vmem_limit_bytes=24 * 2**20),
        cost_estimate=pl.CostEstimate(
            flops=flops,
            bytes_accessed=sum(o.size * o.dtype.itemsize for o in operands),
            transcendentals=0,
        ),
    )(*operands)


def frame_sims(own, other, pieces):
    clips, rows, width = own.shape
    regions, count = pieces[0].shape[:2]
    frames = rows // regions
    total = count * len(pieces)
    body = functools.partial(sims_body, regions, frames)
    flops = 4 * clips * rows * regions * total * width
    outs = [((2 * clips * frames, total), jnp.float32)]
    return kernel_call(body, outs, [own, other, *pieces], [], flops)[0]


def frame_table(at, own, other, prev, pieces):
    clips, rows, width = own.shape
    regions, count = pieces[0].shape[:2]
    frames = rows // regions
    total = count * len(pieces)
    return kernel_call(
        functools.partial(table_body, regions, frames),
        [((NC * NZ * NY, 2 * clips * frames), jnp.bfloat16)],
        [at, own, other, prev, *pieces],
        [pltpu.VMEM((2 * clips * frames, total), jnp.float32)],
        4 * clips * rows * regions * total * width,
        scalars=1,
    )[0]


def row_order():
    group = 4
    order = np.zeros((4, 2, group, 8, NC, NX, group, NY), np.float32)
    for k in range(4):
        for f in range(16):
            frame = 2 * f - 1 + k
            if 0 <= frame < 32:
                for q in range(group):
                    order[k, f % 2, q, f // 2, frame % 2, frame // 8, q, frame % 8 // 2] = 1
    return order.reshape(4 * 64, 128)


def prepare_body(
    at_ref, count_ref, shard_ref, clip_ref, first_ref, second_ref, third_ref, listed_ref, t1_ref, t2_ref, t3_ref
):
    f32, bf16 = jnp.float32, jnp.bfloat16
    group, slots = 4, shard_ref.shape[1]
    chip, core, x = at_ref[0] * NY + at_ref[1], at_ref[2], at_ref[3]
    shards = shard_ref[...]
    names = jnp.where(shards // NC == chip, shards % NC * 2 + clip_ref[...], -1)
    line = lax.broadcasted_iota(jnp.int32, names.shape, 0)
    slot = lax.broadcasted_iota(jnp.int32, (1, slots), 1)
    chips = slots // 4
    to_chip = lax.broadcasted_iota(jnp.int32, (chips, slots), 0)
    of_slot = lax.broadcasted_iota(jnp.int32, (chips, slots), 1)
    pick_slot = lax.broadcasted_iota(jnp.int32, (slots, 2 * group), 0) % 4
    pick_to = lax.broadcasted_iota(jnp.int32, (slots, 2 * group), 1)
    listed = jnp.zeros((chips, 2 * group), f32)
    for q in range(group):
        query = x * group + q
        names_q = jnp.sum(jnp.where(line == query, names, 0), axis=0, keepdims=True)
        names_q = jnp.where(slot < count_ref[query], names_q, -1).astype(f32)
        spread = jnp.where(of_slot // 4 == to_chip, names_q, 0.0).astype(bf16)
        pick = jnp.where((pick_to // 2 == q) & (pick_slot == core * 2 + pick_to % 2), 1.0, 0.0)
        listed = listed + dot(spread, pick.astype(bf16))
    listed_ref[...] = listed.astype(jnp.int32)

    lanes = t1_ref.shape[1]
    row = lax.broadcasted_iota(jnp.int32, (128, lanes), 0) % 32
    lane = lax.broadcasted_iota(jnp.int32, (128, lanes), 1)
    column = (lane // 32) % 16 * 2 + lane // 512
    channel = lax.broadcasted_iota(jnp.int32, (32, lanes), 1) % 32
    each = lax.broadcasted_iota(jnp.int32, (32, lanes), 0)
    taps = dot(first_ref[...], jnp.where(channel == each, 1.0, 0.0).astype(bf16))
    for dy in range(3):
        block = jnp.zeros((128, lanes), f32)
        for dx in range(3):
            tap = taps[dy * 3 + dx : dy * 3 + dx + 1, :]
            block = jnp.where(row == column + (dx - 1), tap, block)
        t1_ref[dy * 128 : (dy + 1) * 128, :] = block.astype(bf16)

    def placed(tap, before, total):
        rows, width = tap.shape
        parts = [jnp.zeros((before, width), f32), tap]
        parts.append(jnp.zeros((total - before - rows, width), f32))
        return jnp.concatenate(parts, axis=0)

    left = lax.broadcasted_iota(jnp.int32, (384, 128), 1) < 64
    for dy in range(3):
        tap = second_ref[dy * 96 : (dy + 1) * 96, :].astype(f32)
        tap = jnp.concatenate([tap, tap], axis=1)
        for odd in range(2):
            one = placed(tap, 96 + 32 * odd, 384)
            two = placed(tap, 160 + 32 * odd, 384)
            block = jnp.where(left, one, two).astype(bf16)
            t2_ref[dy * 384 : (dy + 1) * 384, odd * 128 : (odd + 1) * 128] = block
    for dy in range(3):
        tap = third_ref[dy * 192 : (dy + 1) * 192, :].astype(f32)
        for w in range(2):
            block = placed(tap, 64 + 64 * w, 384).astype(bf16)
            t3_ref[dy * 384 : (dy + 1) * 384, w * 128 : (w + 1) * 128] = block


def prepare(at, cand_count, cand_shard, cand_clip, first_kernel, second_kernel, third_kernel):
    operands = [
        at,
        cand_count,
        cand_shard,
        cand_clip,
        first_kernel.reshape(9, 32),
        second_kernel.reshape(288, 64),
        third_kernel.reshape(576, 128),
    ]
    outs = [
        ((cand_shard.shape[1] // 4, 8), jnp.int32),
        ((384, 1024), jnp.bfloat16),
        ((1152, 256), jnp.bfloat16),
        ((1152, 256), jnp.bfloat16),
    ]
    return kernel_call(prepare_body, outs, operands, [], 10**9, scalars=2)


def dot(a, b):
    return jnp.dot(a, b, preferred_element_type=jnp.float32)


def rows_beside(values):
    rows = values.shape[0]
    at = lax.broadcasted_iota(jnp.int32, values.shape, 0) % 8
    before = jnp.where(at == 0, 0.0, pltpu.roll(values, 1, 0))
    after = jnp.where(at == 7, 0.0, pltpu.roll(values, rows - 1, 0))
    return before, after


def windows(layers, blocks):
    zero = jnp.zeros((layers[0].shape[0], 128), layers[0].dtype)
    out = []
    for t in range(blocks):
        parts = []
        for layer in layers:
            for b in (t - 1, t, t + 1):
                parts.append(layer[:, b * 128 : (b + 1) * 128] if 0 <= b < blocks else zero)
        out.append(jnp.concatenate(parts, axis=1))
    return out


def score_body(
    bias_ref, parts_ref, order_ref, t1_ref, b1_ref, t2_ref, b2_ref, t3_ref, b3_ref, weight_ref, listed_ref, out_ref
):
    b1 = jnp.concatenate([b1_ref[...]] * 16, axis=1)
    b2 = jnp.concatenate([b2_ref[...]] * 2, axis=1)
    b3 = jnp.concatenate([b3_ref[...]] * 2, axis=1)
    weight = jnp.concatenate([weight_ref[...].astype(jnp.float32)] * 2, axis=1)
    lane = lax.broadcasted_iota(jnp.int32, (128, 256), 1) // 128
    even_row = lax.broadcasted_iota(jnp.int32, (128, 256), 0) % 2
    weight = jnp.where(lane == even_row, weight, 0.0).astype(jnp.bfloat16)
    bf16 = jnp.bfloat16
    maps = dot(order_ref[...], parts_ref[...])
    x = [maps[k * 64 : (k + 1) * 64] for k in range(4)]
    x = [(pltpu.roll(v, 64, 1) if k % 2 == 0 else v).astype(bf16) for k, v in enumerate(x)]
    both = jnp.concatenate(
        [jnp.concatenate(x[0:3], axis=1), jnp.concatenate(x[1:4], axis=1)], axis=0
    )
    clip = lax.broadcasted_iota(jnp.int32, both.shape, 1) // 32 % 4
    wide = both.astype(jnp.float32)
    lhs = jnp.concatenate([jnp.where(clip == k, wide, 0.0).astype(bf16) for k in range(4)], axis=0)
    first = dot(lhs, t1_ref[...])
    first = jnp.maximum(first[:, :512], first[:, 512:])
    first = jnp.concatenate(
        [jnp.maximum(first[k * 128 : k * 128 + 64], first[k * 128 + 64 : k * 128 + 128]) for k in range(4)],
        axis=0,
    )
    first = jnp.maximum(first + b1, 0.0)
    even = jnp.concatenate([first[k * 64 : k * 64 + 32] for k in range(4)], axis=0)
    odd = jnp.concatenate([first[k * 64 + 32 : k * 64 + 64] for k in range(4)], axis=0)
    odd_before = rows_beside(odd)[0]
    even_after = rows_beside(even)[1]
    layers = [v.astype(bf16) for v in (odd_before, even, odd, even_after)]
    lhs = jnp.concatenate(windows(layers[0:3], 4) + windows(layers[1:4], 4), axis=0)
    second = dot(lhs, t2_ref[...])
    second = jnp.maximum(second[:, :128], second[:, 128:])
    second = jnp.maximum(second[:512], second[512:])
    second = jnp.maximum(second + b2, 0.0)
    second = jnp.concatenate([second[t * 128 : (t + 1) * 128] for t in range(4)], axis=1)
    before, after = rows_beside(second)
    lhs = jnp.concatenate(windows([v.astype(bf16) for v in (before, second, after)], 4), axis=0)
    third = jnp.maximum(dot(lhs, t3_ref[...]) + b3, 0.0).astype(bf16)
    score = lax.dot_general(
        third, weight, (((1,), (1,)), ((), ())), preferred_element_type=jnp.float32
    )
    score = jnp.maximum(
        jnp.maximum(score[0:128], score[128:256]), jnp.maximum(score[256:384], score[384:512])
    )
    score = jnp.max(score, axis=1, keepdims=True) + jnp.broadcast_to(bias_ref[0], (1, 128))
    score = score.reshape(16, 8, score.shape[1]).sum(axis=1) * 0.125
    listed = listed_ref[...]
    slot_query = lax.broadcasted_iota(jnp.int32, (1, listed.shape[1]), 1) // 2
    total = jnp.zeros(listed.shape, jnp.float32)
    for k in range(4):
        line = jnp.zeros((1, listed.shape[1]), jnp.float32)
        for q in range(4):
            line = jnp.where(slot_query == q, score[k * 4 + q : k * 4 + q + 1, : listed.shape[1]], line)
        total = jnp.where(listed == k, line, total)
    out_ref[...] = total


def slot_scores(parts, listed, spread, first_bias, second_bias, third_bias, score_weight, score_bias):
    operands = [
        score_bias,
        parts,
        jnp.asarray(row_order(), jnp.bfloat16),
        spread[0],
        first_bias[None, :],
        spread[1],
        second_bias[None, :],
        spread[2],
        third_bias[None, :],
        score_weight[None, :],
        listed,
    ]
    outs = [(listed.shape, jnp.float32)]
    return kernel_call(score_body, outs, operands, [], 2 * 10**9, scalars=1)[0]


def on_device(
    queries,
    corpus,
    cand_shard,
    cand_clip,
    cand_count,
    first_kernel,
    first_bias,
    second_kernel,
    second_bias,
    third_kernel,
    third_bias,
    score_weight,
    score_bias,
):
    at = jnp.stack([lax.axis_index(a) for a in ("z", "y", "c", "x")]).astype(jnp.int32)
    clip_dev, frames, regions, width = corpus.shape
    group = cand_shard.shape[0] // NX

    own = corpus.transpose(0, 2, 1, 3).reshape(clip_dev, regions * frames, width)
    four = gather_classes(queries[0, 0])
    beside = paired(four, 0)
    kernels = (first_kernel, second_kernel, third_kernel)
    kernels, four = lax.optimization_barrier((kernels, four))
    listed, *spread = prepare(at, cand_count, cand_shard, cand_clip, *kernels)
    first = jnp.concatenate([four, beside], axis=1)
    own, first, listed = lax.optimization_barrier((own, first, listed))
    other = lax.ppermute(own, "c", [(0, 1), (1, 0)])
    last = paired(first, 1)
    behind_first = shift(first, 1)
    ahead_first = shift(first, -1)
    two_first = shift(behind_first, 1)
    behind_last = shift(last, 1)
    ahead_last = shift(last, -1)
    two_last = shift(ahead_last, -1)

    near = [first, last, behind_first, behind_last, ahead_first, ahead_last]
    prev = frame_sims(own, other, near)
    two, prev = lax.optimization_barrier(((two_first, two_last), prev))
    table = frame_table(at, own, other, prev, two)

    parts = lax.all_to_all(table, ("c", "x"), 0, 0, tiled=True)
    values = slot_scores(
        parts, listed, spread, first_bias, second_bias, third_bias, score_weight, score_bias
    )
    values = lax.all_to_all(values, ("z", "y"), 0, 0, tiled=True)
    return values.sum(axis=0).reshape(group, -1)


def solution(mesh):
    devices = mesh.devices.reshape(NZ, NY, NC, NX)
    grid = Mesh(devices, ("z", "y", "c", "x"))
    return jax.shard_map(
        on_device,
        mesh=grid,
        in_specs=(P("x", PLANE), P(PLANE)) + (P(),) * 11,
        out_specs=P("x", PLANE),
        check_vma=False,
    )
```

time: 132 us -> 131 us (level)
  blocking collectives: 19.7 us -> 49.7 us
  starting transfers between devices: 62 us -> 46.5 us
  waiting for transfers between devices: 23.9 us -> 17.2 us
  local copies, waits for them, and re-layouts: 5.86 us -> 1.97 us
  Pallas kernels: 16.5 us -> 13.3 us
    all_to_all x0 -> x1, blocking collectives: none -> 30.2 us  [gather_classes(): lax.all_to_all(jnp.broadcast_to(flat, (4,) + flat.shape), 'z', 0, 0, axis...]
    all_to_all x1 -> x0, waiting for transfers between devices: 15.9 us -> none  [gather_stage(): lax.all_to_all(jnp.broadcast_to(flat, (4,) + flat.shape), 'z', 0, 0, axis...]
    all_to_all x1 -> x0, starting transfers between devices: 9.58 us -> none  [gather_stage(): lax.all_to_all(jnp.broadcast_to(flat, (4,) + flat.shape), 'z', 0, 0, axis...]
    ppermute x9 -> x8, waiting for transfers between devices: 5.16 us -> 13 us  [send(): return lax.ppermute(values, PLANE, pairs)]
    ppermute x9 -> x8, starting transfers between devices: 31.7 us -> 25.3 us  [send(): return lax.ppermute(values, PLANE, pairs)]
    pallas_call x4, Pallas kernels: 16.5 us -> 13.3 us  [kernel_call(): pl.pallas_call(body, in_specs=[pl.BlockSpec(memory_space=space) for space...]
    ppermute x1, starting transfers between devices: 8.91 us -> 11.5 us  [on_device(): other = lax.ppermute(own, 'c', [(0, 1), (1, 0)])]
    all_to_all x1, starting transfers between devices: 11.9 us -> 9.63 us  [on_device(): parts = lax.all_to_all(table, ('c', 'x'), 0, 0, tiled=True)]
  transfers between devices with their start and end apart: 12 -> 10, of which waited for: 5 -> 6; matrix products, arithmetic and copies ran while one was open for 3% -> 0% of each run, Pallas kernels for 6% -> 5%
where the time goes in v4:
time: 131 us; the launch traced here: 130 us
  blocking collectives  49.7 us (38%)
  starting transfers between devices  46.5 us (35%)
  waiting for transfers between devices  17.2 us (13%)
  Pallas kernels  13.3 us (10%)
  local copies, waits for them, and re-layouts  1.97 us (2%)
    all_to_all x1, blocking collectives, gather_classes(): lax.all_to_all(jnp.broadcast_to(flat, (4,) + flat.shape), 'z', 0, 0, axis...  30.2 us
    ppermute x8, starting transfers between devices, send(): return lax.ppermute(values, PLANE, pairs)  25.3 us
    all_to_all x1, blocking collectives, on_device(): values = lax.all_to_all(values, ('z', 'y'), 0, 0, tiled=True)  19.5 us
    pallas_call x4, Pallas kernels, kernel_call(): pl.pallas_call(body, in_specs=[pl.BlockSpec(memory_space=space) for space...  13.3 us
    ppermute x8, waiting for transfers between devices, send(): return lax.ppermute(values, PLANE, pairs)  13 us
    ppermute x1, starting transfers between devices, on_device(): other = lax.ppermute(own, 'c', [(0, 1), (1, 0)])  11.5 us
    all_to_all x1, starting transfers between devices, on_device(): parts = lax.all_to_all(table, ('c', 'x'), 0, 0, tiled=True)  9.63 us
    all_to_all x1, waiting for transfers between devices, on_device(): parts = lax.all_to_all(table, ('c', 'x'), 0, 0, tiled=True)  4.27 us
  transfers between devices with their start and end apart: 10, of which 6 were waited for; matrix products, arithmetic and copies ran while one was open for 0% of the time, Pallas kernels for 5%

profile of v4, /device:TPU:1, one launch (start us, length us, event | category | flops | bytes accessed | tf_op | source)
XLA Modules:
  0.0 130.0 jit_solution(10345622088579228124)
XLA Ops:
  0.0 1.0 reshape_squeeze.3
  1.0 0.0 copy-start.11
  1.0 0.0 copy-start.1
  1.0 0.0 copy-start.2
  1.0 0.0 copy-start.3
  1.0 0.0 copy-start.4
  1.0 0.0 copy-start.5
  1.1 30.2 %all_to_all.25 = bf16[4,9,30,128]{3,2,1,0:T(8,128)(2,1)S(1)} all-to-all(bf16[4,9,30,128]{3,2,1,0:T(8,128)(2,1)S(1)} %broadcast_in_dim.15), channel_id=1, replica_groups={{0,128,256,384},{32,160,288,416},{64,192,320,448},{96,224,352,480},{1,1..., dimensions={0} | all-to-all | bytes 552960 | tf_op jit(solution)/shard_map/all_to_all | solution.py:45
  31.3 0.1 reshape.23
  31.4 3.2 %collective-permute-start = (bf16[9,4,3840]{2,1,0:T(4,128)(2,1)S(1)}, bf16[9,4,3840]{2,1,0:T(4,128)(2,1)S(1)}, u32[]{:S(2)}, u32[]{:S(2)}) collective-permute-start(bf16[9,4,3840]{2,1,0:T(4,128)(2,1)S(1)} %bitcast.34), channel_id=1, source_target_pairs={{0,32},{4,12},{8,40},{12,4},{16,48},{20,28},{24,56},{28,20},{32,0}... | collective-permute-start | bytes 829448 | tf_op jit(solution)/shard_map/ppermute | solution.py:26
  34.6 0.1 pad_add_fusion.at_ref
  34.7 0.0 copy-done.11
  34.7 0.0 copy-done.1
  34.7 0.0 copy-done.2
  34.7 0.0 copy-done.3
  34.7 0.0 copy-done.4
  34.7 0.0 copy-done.5
  34.8 0.0 copy-start
  34.8 1.3 %shard_map.136 = (s32[64,8]{1,0:T(8,128)S(1)}, bf16[384,1024]{1,0:T(8,128)(2,1)S(1)}, bf16[1152,256]{1,0:T(8,128)(2,1)S(1)}, bf16[1152,256]{1,0:T(8,128)(2,1)S(1)}) custom-call(s32[4]{0:T(128)S(1)} %pad_add_fusion.at_ref, s32[16]{0:T(128)S(1)} %copy-done.5, s32[16,256]{1,0:T(8,128)S(1)} %copy-done.3, s32[16,256]{1,0:T(8,128)S(1)} %copy-done.4, ...), custom_call_target="tpu_custom_call" | custom-call | flops 1000000000 | bytes 217744 | tf_op jit(solution)/shard_map/pallas_call | solution.py:120
  36.1 2.6 %collective-permute-done = bf16[9,4,3840]{2,1,0:T(4,128)(2,1)S(1)} collective-permute-done((bf16[9,4,3840]{2,1,0:T(4,128)(2,1)S(1)}, bf16[9,4,3840]{2,1,0:T(4,128)(2,1)S(1)}, u32[]{:S(2)}, u32[]{:S(2)}) %collective-permute-start) | collective-permute-done | bytes 276512 | tf_op jit(solution)/shard_map/ppermute | solution.py:26
  38.7 0.3 pad_maximum_fusion.refs_0_
  38.9 0.0 copy-done
  39.0 11.5 %collective-permute-start.1 = (bf16[2,288,3840]{2,1,0:T(8,128)(2,1)S(1)}, bf16[2,288,3840]{2,1,0:T(8,128)(2,1)S(1)}, u32[]{:S(2)}, u32[]{:S(2)}) collective-permute-start(bf16[2,288,3840]{2,1,0:T(8,128)(2,1)S(1)} %bitcast.23), channel_id=1, source_target_pairs={{0,4},{4,0},{1,5},{5,1},{2,6},{6,2},{3,7},{7,3},{8,12},{12,8},{9,1... | collective-permute-start | bytes 13271048 | tf_op jit(solution)/shard_map/ppermute | solution.py:382
  50.5 4.6 %collective-permute-start.4 = (bf16[9,8,3840]{2,1,0:T(8,128)(2,1)S(1)}, bf16[9,8,3840]{2,1,0:T(8,128)(2,1)S(1)}, u32[]{:S(2)}, u32[]{:S(2)}) collective-permute-start(bf16[9,8,3840]{2,1,0:T(8,128)(2,1)S(1)} %pad_maximum_fusion.refs_0_), channel_id=1, source_target_pairs={{0,480},{4,28},{8,488},{12,20},{16,496},{20,12},{24,504},{28,4},{3... | collective-permute-start | bytes 1658888 | tf_op jit(solution)/shard_map/ppermute | solution.py:26
  55.1 3.6 %collective-permute-start.2 = (bf16[9,8,3840]{2,1,0:T(8,128)(2,1)S(1)}, bf16[9,8,3840]{2,1,0:T(8,128)(2,1)S(1)}, u32[]{:S(2)}, u32[]{:S(2)}) collective-permute-start(bf16[9,8,3840]{2,1,0:T(8,128)(2,1)S(1)} %pad_maximum_fusion.refs_0_), channel_id=1, source_target_pairs={{0,8},{4,36},{8,16},{12,44},{16,24},{20,52},{24,0},{28,60},{32,40}... | collective-permute-start | bytes 1658888 | tf_op jit(solution)/shard_map/ppermute | solution.py:26
  58.8 6.2 %collective-permute-done.4.refs_1_ = bf16[9,8,3840]{2,1,0:T(8,128)(2,1)S(1)} collective-permute-done((bf16[9,8,3840]{2,1,0:T(8,128)(2,1)S(1)}, bf16[9,8,3840]{2,1,0:T(8,128)(2,1)S(1)}, u32[]{:S(2)}, u32[]{:S(2)}) %collective-permute-start.4) | collective-permute-done | bytes 552992 | tf_op jit(solution)/shard_map/ppermute | solution.py:26
  65.0 1.9 %collective-permute-start.5 = (bf16[9,8,3840]{2,1,0:T(8,128)(2,1)S(1)}, bf16[9,8,3840]{2,1,0:T(8,128)(2,1)S(1)}, u32[]{:S(2)}, u32[]{:S(2)}) collective-permute-start(bf16[9,8,3840]{2,1,0:T(8,128)(2,1)S(1)} %collective-permute-done.4.refs_1_), channel_id=1, source_target_pairs={{0,24},{4,484},{8,0},{12,492},{16,8},{20,500},{24,16},{28,508},{32... | collective-permute-start | bytes 1658888 | tf_op jit(solution)/shard_map/ppermute | solution.py:26
  66.9 3.5 %collective-permute-start.8 = (bf16[9,8,3840]{2,1,0:T(8,128)(2,1)S(1)}, bf16[9,8,3840]{2,1,0:T(8,128)(2,1)S(1)}, u32[]{:S(2)}, u32[]{:S(2)}) collective-permute-start(bf16[9,8,3840]{2,1,0:T(8,128)(2,1)S(1)} %pad_maximum_fusion.refs_0_), channel_id=1, source_target_pairs={{0,24},{4,484},{8,0},{12,492},{16,8},{20,500},{24,16},{28,508},{32... | collective-permute-start | bytes 1658888 | tf_op jit(solution)/shard_map/ppermute | solution.py:26
  70.4 1.9 %collective-permute-start.7 = (bf16[9,8,3840]{2,1,0:T(8,128)(2,1)S(1)}, bf16[9,8,3840]{2,1,0:T(8,128)(2,1)S(1)}, u32[]{:S(2)}, u32[]{:S(2)}) collective-permute-start(bf16[9,8,3840]{2,1,0:T(8,128)(2,1)S(1)} %collective-permute-done.4.refs_1_), channel_id=1, source_target_pairs={{0,8},{4,36},{8,16},{12,44},{16,24},{20,52},{24,0},{28,60},{32,40}... | collective-permute-start | bytes 1658888 | tf_op jit(solution)/shard_map/ppermute | solution.py:26
  72.4 0.0 collective-permute-done.2.refs_2_
  72.4 3.3 %collective-permute-start.3 = (bf16[9,8,3840]{2,1,0:T(8,128)(2,1)S(1)}, bf16[9,8,3840]{2,1,0:T(8,128)(2,1)S(1)}, u32[]{:S(2)}, u32[]{:S(2)}) collective-permute-start(bf16[9,8,3840]{2,1,0:T(8,128)(2,1)S(1)} %collective-permute-done.2.refs_2_), channel_id=1, source_target_pairs={{0,8},{4,36},{8,16},{12,44},{16,24},{20,52},{24,0},{28,60},{32,40}... | collective-permute-start | bytes 1658888 | tf_op jit(solution)/shard_map/ppermute | solution.py:26
  75.7 0.0 collective-permute-done.5.refs_5_
  75.7 3.2 %collective-permute-start.6 = (bf16[9,8,3840]{2,1,0:T(8,128)(2,1)S(1)}, bf16[9,8,3840]{2,1,0:T(8,128)(2,1)S(1)}, u32[]{:S(2)}, u32[]{:S(2)}) collective-permute-start(bf16[9,8,3840]{2,1,0:T(8,128)(2,1)S(1)} %collective-permute-done.5.refs_5_), channel_id=1, source_target_pairs={{0,24},{4,484},{8,0},{12,492},{16,8},{20,500},{24,16},{28,508},{32... | collective-permute-start | bytes 1658888 | tf_op jit(solution)/shard_map/ppermute | solution.py:26
  78.9 2.6 %collective-permute-done.8.refs_4_ = bf16[9,8,3840]{2,1,0:T(8,128)(2,1)S(1)} collective-permute-done((bf16[9,8,3840]{2,1,0:T(8,128)(2,1)S(1)}, bf16[9,8,3840]{2,1,0:T(8,128)(2,1)S(1)}, u32[]{:S(2)}, u32[]{:S(2)}) %collective-permute-start.8) | collective-permute-done | bytes 552992 | tf_op jit(solution)/shard_map/ppermute | solution.py:26
  81.5 0.7 collective-permute-done.7.refs_3_
  82.2 0.0 collective-permute-done.1.other_ref
  82.2 5.0 %shard_map.137.prev_ref = f32[128,48]{1,0:T(8,128)S(1)} custom-call(bf16[2,288,3840]{2,1,0:T(8,128)(2,1)S(1)} %bitcast.24, bf16[2,288,3840]{2,1,0:T(8,128)(2,1)S(1)} %collective-permute-done.1.other_ref, bf16[9,8,3840]{2,1,0:T(8,128)(2,1)S(1)} %pad_maximum_fusion.refs_0_, bf16[9,8,3840]{2,1,0:T(8,128)(2,1)S(1)} %collective-permute-done.4.refs_1_, ...), custom_call_target="tpu_custom_call" | custom-call | flops 3822059520 | bytes 12165120 | tf_op jit(solution)/shard_map/pallas_call | solution.py:120
  87.2 0.0 copy-start.6
  87.2 0.0 copy-start.7
  87.2 0.0 copy-start.8
  87.2 0.0 copy-start.9
  87.2 0.0 copy-start.10
  87.2 0.9 collective-permute-done.3.refs_0_
  88.1 0.0 collective-permute-done.6.refs_1_
  88.1 3.9 %shard_map.138 = bf16[128,128]{1,0:T(8,128)(2,1)} custom-call(s32[4]{0:T(128)S(1)} %pad_add_fusion.at_ref, bf16[2,288,3840]{2,1,0:T(8,128)(2,1)S(1)} %bitcast.25, bf16[2,288,3840]{2,1,0:T(8,128)(2,1)S(1)} %collective-permute-done.1.other_ref, f32[128,48]{1,0:T(8,128)S(1)} %shard_map.137.prev_ref, bf16[9,8,3840]{2,1,0:T(8,128)(2,1)S(1)} %collective-permute-done.3.refs_0_, ...), custom_call_target="tpu_custom_call" | custom-call | flops 1274019840 | bytes 9977872 | tf_op jit(solution)/shard_map/pallas_call | solution.py:120
  92.0 9.6 %all-to-all-start.1 = ((bf16[8,16,128]{2,1,0:T(8,128)(2,1)}), bf16[8,16,128]{2,1,0:T(8,128)(2,1)S(1)}, u32[]{:S(2)}, u32[]{:S(2)}) async-start(bf16[8,16,128]{2,1,0:T(8,128)(2,1)} %bitcast.9), calls=%async_computation.1 | async-start | bytes 65536 | tf_op jit(solution)/shard_map/all_to_all | solution.py:396
  102.3 4.3 %all-to-all-done.1 = bf16[8,16,128]{2,1,0:T(8,128)(2,1)S(1)} async-done(((bf16[8,16,128]{2,1,0:T(8,128)(2,1)}), bf16[8,16,128]{2,1,0:T(8,128)(2,1)S(1)}, u32[]{:S(2)}, u32[]{:S(2)}) %all-to-all-start.1) | async-done | bytes 32800 | tf_op jit(solution)/shard_map/all_to_all | solution.py:396
  106.6 0.0 copy-done.6
  106.6 0.0 copy-done.7
  106.6 0.0 copy-done.8
  106.6 0.0 copy-done.9
  106.6 0.0 copy-done.10
  106.6 3.0 %shard_map.139 = f32[64,8]{1,0:T(8,128)S(1)} custom-call(f32[1]{0:T(128)S(6)} %copy.20.bias_ref, bf16[128,128]{1,0:T(8,128)(2,1)S(1)} %bitcast.26, bf16[256,128]{1,0:T(8,128)(2,1)S(1)} %copy-done.10, bf16[384,1024]{1,0:T(8,128)(2,1)S(1)} %get-tuple-element.29.t1_ref, f32[1,32]{1,0:T(1,128)S(1)} %bitcast.30, bf16[1152,256]{1,0:T(8,128)(2,1)S(1)} %get-tuple-element.30.t2_ref, ...), custom_call_target="tpu_custom_call" | custom-call | flops 2000000000 | bytes 2067588 | tf_op jit(solution)/shard_map/pallas_call | solution.py:120
  109.7 19.5 %all_to_all.26 = f32[64,1,8]{2,1,0:T(1,128)S(1)} all-to-all(f32[64,1,8]{2,1,0:T(1,128)S(1)} %bitcast.27), channel_id=1, replica_groups=mesh['z'=16,'y'=4,'c'=2,'x'=4] {'z','y'}, dimensions={0} | all-to-all | bytes 4096 | tf_op jit(solution)/shard_map/all_to_all | solution.py:400
  129.2 0.1 reduce_sum.9
  129.3 0.1 reshape.27
  129.3 0.7 copy.19
  (3 shorter events, 0.1 us)
Async XLA Ops:
  1.0 33.7 %copy-start.11 = (bf16[3,3,1,32]{3,1,2,0:T(4,128)(2,1)S(1)}, bf16[3,3,1,32]{3,1,2,0:T(4,128)(2,1)}, u32[]{:S(2)}) copy-start(bf16[3,3,1,32]{3,1,2,0:T(4,128)(2,1)} %param.19) | copy-start | bytes 1732
  1.0 33.7 %copy-start.1 = (bf16[3,3,64,128]{3,2,1,0:T(8,128)(2,1)S(1)}, bf16[3,3,64,128]{3,2,1,0:T(8,128)(2,1)}, u32[]{:S(2)}) copy-start(bf16[3,3,64,128]{3,2,1,0:T(8,128)(2,1)} %param.23) | copy-start | bytes 442372
  1.0 33.7 %copy-start.2 = (bf16[3,3,32,64]{3,2,1,0:T(8,128)(2,1)S(1)}, bf16[3,3,32,64]{3,2,1,0:T(8,128)(2,1)}, u32[]{:S(2)}) copy-start(bf16[3,3,32,64]{3,2,1,0:T(8,128)(2,1)} %param.21) | copy-start | bytes 110596
  1.0 33.7 %copy-start.3 = (s32[16,256]{1,0:T(8,128)S(1)}, s32[16,256]{1,0:T(8,128)}, u32[]{:S(2)}) copy-start(s32[16,256]{1,0:T(8,128)} %shard_ref.1) | copy-start | bytes 49156
  1.0 33.7 %copy-start.4 = (s32[16,256]{1,0:T(8,128)S(1)}, s32[16,256]{1,0:T(8,128)}, u32[]{:S(2)}) copy-start(s32[16,256]{1,0:T(8,128)} %clip_ref.1) | copy-start | bytes 49156
  1.0 33.7 %copy-start.5 = (s32[16]{0:T(128)S(1)}, s32[16]{0:T(128)}, u32[]{:S(2)}) copy-start(s32[16]{0:T(128)} %count_ref.1) | copy-start | bytes 196
  31.4 7.3 %collective-permute-start = (bf16[9,4,3840]{2,1,0:T(4,128)(2,1)S(1)}, bf16[9,4,3840]{2,1,0:T(4,128)(2,1)S(1)}, u32[]{:S(2)}, u32[]{:S(2)}) collective-permute-start(bf16[9,4,3840]{2,1,0:T(4,128)(2,1)S(1)} %bitcast.34), channel_id=1, source_target_pairs={{0,32},{4,12},{8,40},{12,4},{16,48},{20,28},{24,56},{28,20},{32,0}... | collective-permute-start | bytes 829448 | tf_op jit(solution)/shard_map/ppermute | solution.py:26
  34.8 4.2 %copy-start = (bf16[2,32,9,3840]{3,1,2,0:T(8,128)(2,1)S(1)}, bf16[2,32,9,3840]{3,1,2,0:T(8,128)(2,1)}, u32[]{:S(2)}) copy-start(bf16[2,32,9,3840]{3,1,2,0:T(8,128)(2,1)} %param.15) | copy-start | bytes 13271044
  39.0 43.2 %collective-permute-start.1 = (bf16[2,288,3840]{2,1,0:T(8,128)(2,1)S(1)}, bf16[2,288,3840]{2,1,0:T(8,128)(2,1)S(1)}, u32[]{:S(2)}, u32[]{:S(2)}) collective-permute-start(bf16[2,288,3840]{2,1,0:T(8,128)(2,1)S(1)} %bitcast.23), channel_id=1, source_target_pairs={{0,4},{4,0},{1,5},{5,1},{2,6},{6,2},{3,7},{7,3},{8,12},{12,8},{9,1... | collective-permute-start | bytes 13271048 | tf_op jit(solution)/shard_map/ppermute | solution.py:382
  50.5 14.5 %collective-permute-start.4 = (bf16[9,8,3840]{2,1,0:T(8,128)(2,1)S(1)}, bf16[9,8,3840]{2,1,0:T(8,128)(2,1)S(1)}, u32[]{:S(2)}, u32[]{:S(2)}) collective-permute-start(bf16[9,8,3840]{2,1,0:T(8,128)(2,1)S(1)} %pad_maximum_fusion.refs_0_), channel_id=1, source_target_pairs={{0,480},{4,28},{8,488},{12,20},{16,496},{20,12},{24,504},{28,4},{3... | collective-permute-start | bytes 1658888 | tf_op jit(solution)/shard_map/ppermute | solution.py:26
  55.1 17.2 %collective-permute-start.2 = (bf16[9,8,3840]{2,1,0:T(8,128)(2,1)S(1)}, bf16[9,8,3840]{2,1,0:T(8,128)(2,1)S(1)}, u32[]{:S(2)}, u32[]{:S(2)}) collective-permute-start(bf16[9,8,3840]{2,1,0:T(8,128)(2,1)S(1)} %pad_maximum_fusion.refs_0_), channel_id=1, source_target_pairs={{0,8},{4,36},{8,16},{12,44},{16,24},{20,52},{24,0},{28,60},{32,40}... | collective-permute-start | bytes 1658888 | tf_op jit(solution)/shard_map/ppermute | solution.py:26
  65.0 10.7 %collective-permute-start.5 = (bf16[9,8,3840]{2,1,0:T(8,128)(2,1)S(1)}, bf16[9,8,3840]{2,1,0:T(8,128)(2,1)S(1)}, u32[]{:S(2)}, u32[]{:S(2)}) collective-permute-start(bf16[9,8,3840]{2,1,0:T(8,128)(2,1)S(1)} %collective-permute-done.4.refs_1_), channel_id=1, source_target_pairs={{0,24},{4,484},{8,0},{12,492},{16,8},{20,500},{24,16},{28,508},{32... | collective-permute-start | bytes 1658888 | tf_op jit(solution)/shard_map/ppermute | solution.py:26
  66.9 14.6 %collective-permute-start.8 = (bf16[9,8,3840]{2,1,0:T(8,128)(2,1)S(1)}, bf16[9,8,3840]{2,1,0:T(8,128)(2,1)S(1)}, u32[]{:S(2)}, u32[]{:S(2)}) collective-permute-start(bf16[9,8,3840]{2,1,0:T(8,128)(2,1)S(1)} %pad_maximum_fusion.refs_0_), channel_id=1, source_target_pairs={{0,24},{4,484},{8,0},{12,492},{16,8},{20,500},{24,16},{28,508},{32... | collective-permute-start | bytes 1658888 | tf_op jit(solution)/shard_map/ppermute | solution.py:26
  70.4 11.7 %collective-permute-start.7 = (bf16[9,8,3840]{2,1,0:T(8,128)(2,1)S(1)}, bf16[9,8,3840]{2,1,0:T(8,128)(2,1)S(1)}, u32[]{:S(2)}, u32[]{:S(2)}) collective-permute-start(bf16[9,8,3840]{2,1,0:T(8,128)(2,1)S(1)} %collective-permute-done.4.refs_1_), channel_id=1, source_target_pairs={{0,8},{4,36},{8,16},{12,44},{16,24},{20,52},{24,0},{28,60},{32,40}... | collective-permute-start | bytes 1658888 | tf_op jit(solution)/shard_map/ppermute | solution.py:26
  72.4 15.7 %collective-permute-start.3 = (bf16[9,8,3840]{2,1,0:T(8,128)(2,1)S(1)}, bf16[9,8,3840]{2,1,0:T(8,128)(2,1)S(1)}, u32[]{:S(2)}, u32[]{:S(2)}) collective-permute-start(bf16[9,8,3840]{2,1,0:T(8,128)(2,1)S(1)} %collective-permute-done.2.refs_2_), channel_id=1, source_target_pairs={{0,8},{4,36},{8,16},{12,44},{16,24},{20,52},{24,0},{28,60},{32,40}... | collective-permute-start | bytes 1658888 | tf_op jit(solution)/shard_map/ppermute | solution.py:26
  75.7 12.4 %collective-permute-start.6 = (bf16[9,8,3840]{2,1,0:T(8,128)(2,1)S(1)}, bf16[9,8,3840]{2,1,0:T(8,128)(2,1)S(1)}, u32[]{:S(2)}, u32[]{:S(2)}) collective-permute-start(bf16[9,8,3840]{2,1,0:T(8,128)(2,1)S(1)} %collective-permute-done.5.refs_5_), channel_id=1, source_target_pairs={{0,24},{4,484},{8,0},{12,492},{16,8},{20,500},{24,16},{28,508},{32... | collective-permute-start | bytes 1658888 | tf_op jit(solution)/shard_map/ppermute | solution.py:26
  87.2 19.4 %copy-start.6 = (f32[32]{0:T(128)S(1)}, f32[32]{0:T(128)}, u32[]{:S(2)}) copy-start(f32[32]{0:T(128)} %param.20) | copy-start | bytes 388
  87.2 19.4 %copy-start.7 = (f32[64]{0:T(128)S(1)}, f32[64]{0:T(128)}, u32[]{:S(2)}) copy-start(f32[64]{0:T(128)} %param.22) | copy-start | bytes 772
  87.2 19.4 %copy-start.8 = (f32[128]{0:T(128)S(1)}, f32[128]{0:T(128)}, u32[]{:S(2)}) copy-start(f32[128]{0:T(128)} %param.24) | copy-start | bytes 1540
  87.2 19.4 %copy-start.9 = (bf16[128]{0:T(256)(128)(2,1)S(1)}, bf16[128]{0:T(256)(128)(2,1)}, u32[]{:S(2)}) copy-start(bf16[128]{0:T(256)(128)(2,1)} %param.25) | copy-start | bytes 772
  87.2 19.4 %copy-start.10 = (bf16[256,128]{1,0:T(8,128)(2,1)S(1)}, bf16[256,128]{1,0:T(8,128)(2,1)}, u32[]{:S(2)}) copy-start(bf16[256,128]{1,0:T(8,128)(2,1)} %constant.22.clone.order_ref) | copy-start | bytes 196612
  92.0 14.6 %all-to-all-start.1 = ((bf16[8,16,128]{2,1,0:T(8,128)(2,1)}), bf16[8,16,128]{2,1,0:T(8,128)(2,1)S(1)}, u32[]{:S(2)}, u32[]{:S(2)}) async-start(bf16[8,16,128]{2,1,0:T(8,128)(2,1)} %bitcast.9), calls=%async_computation.1 | async-start | bytes 65536 | tf_op jit(solution)/shard_map/all_to_all | solution.py:396

commit v5 on v4

--- a/solution.py
+++ b/solution.py
@@ -30,12 +30,8 @@
     return send(values, lambda z, y: (z, y + d), lambda z, y: (z + d, y))
 
 
-def paired(values, side):
-    return send(values, lambda z, y: (partner(z, side), y), lambda z, y: (z, partner(y, side)))
-
-
-def partner(at, side):
-    return at + 1 if at % 2 == side else at - 1
+def near_shift(values, d):
+    return send(values, lambda z, y: (z + d, y), lambda z, y: (z, y + d))
 
 
 def gather_classes(block):
@@ -85,17 +81,13 @@
     shape = (NZ * NY, NZ * NY)
     col = lax.broadcasted_iota(jnp.int32, shape, 1)
     row = lax.broadcasted_iota(jnp.int32, shape, 0)
-    far = col // 16
-    far = jnp.where(far == 2, -1, jnp.where(far == 3, 2, far))
-    step = col // 4 % 4
-
-    def near(at):
-        beside = jnp.where(at % 2 == 0, at - 1, at + 1)
-        start = jnp.where(step < 2, at, (beside + NZ) % NZ)
-        return jnp.where(step % 2 == 0, start, start + 1 - start % 2 * 2)
-
-    from_z = jnp.where(c == 0, near(z), z - far + NZ) % 4 + 4 * (col % 4)
-    from_y = jnp.where(c == 0, y - far + NZ, near(y)) % NY
+
+    def back(k):
+        return jnp.where(k == 2, -1, jnp.where(k == 3, 2, k))
+
+    far, near = back(col // 16), back(col // 4 % 4)
+    from_z = (z + NZ - jnp.where(c == 0, near, far)) % 4 + 4 * (col % 4)
+    from_y = (y + NY - jnp.where(c == 0, far, near)) % NY
     return jnp.where(from_z * NY + from_y == row, 1.0, 0.0).astype(jnp.bfloat16)
 
 
@@ -373,14 +365,14 @@
 
     own = corpus.transpose(0, 2, 1, 3).reshape(clip_dev, regions * frames, width)
     four = gather_classes(queries[0, 0])
-    beside = paired(four, 0)
+    ahead = near_shift(four, -1)
+    two = near_shift(four, 2)
+    behind = near_shift(four, 1)
+    first = jnp.concatenate([four, behind], axis=1)
+    last = jnp.concatenate([ahead, two], axis=1)
     kernels = (first_kernel, second_kernel, third_kernel)
-    kernels, four = lax.optimization_barrier((kernels, four))
     listed, *spread = prepare(at, cand_count, cand_shard, cand_clip, *kernels)
-    first = jnp.concatenate([four, beside], axis=1)
-    own, first, listed = lax.optimization_barrier((own, first, listed))
     other = lax.ppermute(own, "c", [(0, 1), (1, 0)])
-    last = paired(first, 1)
     behind_first = shift(first, 1)
     ahead_first = shift(first, -1)
     two_first = shift(behind_first, 1)

time: 131 us -> 131 us (level)
  waiting for transfers between devices: 17.2 us -> 8.21 us
  starting transfers between devices: 46.5 us -> 52.6 us
  Pallas kernels: 13.3 us -> 17.6 us
  blocking collectives: 49.7 us -> 46 us
  local copies, waits for them, and re-layouts: 1.97 us -> 4.22 us
    ppermute x8 -> x9, waiting for transfers between devices: 13 us -> 5.35 us  [send(): return lax.ppermute(values, PLANE, pairs)]
    ppermute x8 -> x9, starting transfers between devices: 25.3 us -> 32.4 us  [send(): return lax.ppermute(values, PLANE, pairs)]
    pallas_call x4, Pallas kernels: 13.3 us -> 17.6 us  [kernel_call(): pl.pallas_call(body, in_specs=[pl.BlockSpec(memory_space=space) for space...]
    all_to_all x1, blocking collectives: 30.2 us -> 26 us  [gather_classes(): lax.all_to_all(jnp.broadcast_to(flat, (4,) + flat.shape), 'z', 0, 0, axis...]
    ppermute x1, starting transfers between devices: 11.5 us -> 8.78 us  [on_device(): other = lax.ppermute(own, 'c', [(0, 1), (1, 0)])]
    unnamed x24, local copies, waits for them, and re-layouts: 0.07 us -> 2.32 us
    all_to_all x1, starting transfers between devices: 9.63 us -> 11.4 us  [on_device(): parts = lax.all_to_all(table, ('c', 'x'), 0, 0, tiled=True)]
    all_to_all x1, waiting for transfers between devices: 4.27 us -> 2.86 us  [on_device(): parts = lax.all_to_all(table, ('c', 'x'), 0, 0, tiled=True)]
  transfers between devices with their start and end apart: 10 -> 11, of which waited for: 6 -> 4; matrix products, arithmetic and copies ran while one was open for 0% -> 1% of each run, Pallas kernels for 5% -> 7%
where the time goes in v5:
time: 131 us; the launch traced here: 130 us
  starting transfers between devices  52.6 us (40%)
  blocking collectives  46 us (35%)
  Pallas kernels  17.6 us (13%)
  waiting for transfers between devices  8.21 us (6%)
  local copies, waits for them, and re-layouts  4.22 us (3%)
    ppermute x9, starting transfers between devices, send(): return lax.ppermute(values, PLANE, pairs)  32.4 us
    all_to_all x1, blocking collectives, gather_classes(): lax.all_to_all(jnp.broadcast_to(flat, (4,) + flat.shape), 'z', 0, 0, axis...  26 us
    all_to_all x1, blocking collectives, on_device(): values = lax.all_to_all(values, ('z', 'y'), 0, 0, tiled=True)  20 us
    pallas_call x4, Pallas kernels, kernel_call(): pl.pallas_call(body, in_specs=[pl.BlockSpec(memory_space=space) for space...  17.6 us
    all_to_all x1, starting transfers between devices, on_device(): parts = lax.all_to_all(table, ('c', 'x'), 0, 0, tiled=True)  11.4 us
    ppermute x1, starting transfers between devices, on_device(): other = lax.ppermute(own, 'c', [(0, 1), (1, 0)])  8.78 us
    ppermute x9, waiting for transfers between devices, send(): return lax.ppermute(values, PLANE, pairs)  5.35 us
    all_to_all x1, waiting for transfers between devices, on_device(): parts = lax.all_to_all(table, ('c', 'x'), 0, 0, tiled=True)  2.86 us
  transfers between devices with their start and end apart: 11, of which 4 were waited for; matrix products, arithmetic and copies ran while one was open for 1% of the time, Pallas kernels for 7%

profile of v5, /device:TPU:1, one launch (start us, length us, event | category | flops | bytes accessed | tf_op | source)
XLA Modules:
  0.0 130.3 jit_solution(16357261964347934087)
XLA Ops:
  0.0 8.8 %collective-permute-start = (bf16[2,288,3840]{2,1,0:T(8,128)(2,1)}, bf16[2,288,3840]{2,1,0:T(8,128)(2,1)}, u32[]{:S(2)}, u32[]{:S(2)}) collective-permute-start(bf16[2,288,3840]{2,1,0:T(8,128)(2,1)} %bitcast.23), channel_id=1, source_target_pairs={{0,4},{4,0},{1,5},{5,1},{2,6},{6,2},{3,7},{7,3},{8,12},{12,8},{9,1... | collective-permute-start | bytes 13271048 | tf_op jit(solution)/shard_map/ppermute | solution.py:375
  8.8 1.0 reshape_squeeze.3
  9.8 26.0 %all_to_all.25 = bf16[4,9,30,128]{3,2,1,0:T(8,128)(2,1)S(1)} all-to-all(bf16[4,9,30,128]{3,2,1,0:T(8,128)(2,1)S(1)} %broadcast_in_dim.15), channel_id=1, replica_groups={{0,128,256,384},{32,160,288,416},{64,192,320,448},{96,224,352,480},{1,1..., dimensions={0} | all-to-all | bytes 552960 | tf_op jit(solution)/shard_map/all_to_all | solution.py:41
  35.8 0.1 reshape.23
  36.0 0.0 copy-start.11
  36.0 4.6 %collective-permute-start.4 = (bf16[9,4,3840]{2,1,0:T(4,128)(2,1)S(1)}, bf16[9,4,3840]{2,1,0:T(4,128)(2,1)S(1)}, u32[]{:S(2)}, u32[]{:S(2)}) collective-permute-start(bf16[9,4,3840]{2,1,0:T(4,128)(2,1)S(1)} %bitcast.34), channel_id=1, source_target_pairs={{0,480},{4,28},{8,488},{12,4},{16,496},{20,12},{24,504},{28,20},{3... | collective-permute-start | bytes 829448 | tf_op jit(solution)/shard_map/ppermute | solution.py:26
  40.6 2.3 %collective-permute-start.5 = (bf16[9,4,3840]{2,1,0:T(4,128)(2,1)S(1)}, bf16[9,4,3840]{2,1,0:T(4,128)(2,1)S(1)}, u32[]{:S(2)}, u32[]{:S(2)}) collective-permute-start(bf16[9,4,3840]{2,1,0:T(4,128)(2,1)S(1)} %bitcast.35), channel_id=1, source_target_pairs={{0,64},{4,20},{8,72},{12,28},{16,80},{20,4},{24,88},{28,12},{32,96... | collective-permute-start | bytes 829448 | tf_op jit(solution)/shard_map/ppermute | solution.py:26
  42.9 2.6 %collective-permute-start.1 = (bf16[9,4,3840]{2,1,0:T(4,128)(2,1)S(1)}, bf16[9,4,3840]{2,1,0:T(4,128)(2,1)S(1)}, u32[]{:S(2)}, u32[]{:S(2)}) collective-permute-start(bf16[9,4,3840]{2,1,0:T(4,128)(2,1)S(1)} %bitcast.36), channel_id=1, source_target_pairs={{0,32},{4,12},{8,40},{12,20},{16,48},{20,28},{24,56},{28,4},{32,64... | collective-permute-start | bytes 829448 | tf_op jit(solution)/shard_map/ppermute | solution.py:26
  45.5 0.0 collective-permute-done.4
  45.5 4.0 %collective-permute-done.5 = bf16[9,4,3840]{2,1,0:T(4,128)(2,1)S(1)} collective-permute-done((bf16[9,4,3840]{2,1,0:T(4,128)(2,1)S(1)}, bf16[9,4,3840]{2,1,0:T(4,128)(2,1)S(1)}, u32[]{:S(2)}, u32[]{:S(2)}) %collective-permute-start.5) | collective-permute-done | bytes 276512 | tf_op jit(solution)/shard_map/ppermute | solution.py:26
  49.5 0.3 pad_maximum_fusion.1.refs_1_
  49.8 5.6 %collective-permute-start.6 = (bf16[9,8,3840]{2,1,0:T(8,128)(2,1)S(1)}, bf16[9,8,3840]{2,1,0:T(8,128)(2,1)S(1)}, u32[]{:S(2)}, u32[]{:S(2)}) collective-permute-start(bf16[9,8,3840]{2,1,0:T(8,128)(2,1)S(1)} %pad_maximum_fusion.1.refs_1_), channel_id=1, source_target_pairs={{0,24},{4,484},{8,0},{12,492},{16,8},{20,500},{24,16},{28,508},{32... | collective-permute-start | bytes 1658888 | tf_op jit(solution)/shard_map/ppermute | solution.py:26
  55.4 0.0 collective-permute-done.1
  55.4 0.3 pad_maximum_fusion.refs_0_
  55.7 5.5 %collective-permute-start.2 = (bf16[9,8,3840]{2,1,0:T(8,128)(2,1)S(1)}, bf16[9,8,3840]{2,1,0:T(8,128)(2,1)S(1)}, u32[]{:S(2)}, u32[]{:S(2)}) collective-permute-start(bf16[9,8,3840]{2,1,0:T(8,128)(2,1)S(1)} %pad_maximum_fusion.refs_0_), channel_id=1, source_target_pairs={{0,8},{4,36},{8,16},{12,44},{16,24},{20,52},{24,0},{28,60},{32,40}... | collective-permute-start | bytes 1658888 | tf_op jit(solution)/shard_map/ppermute | solution.py:26
  61.2 2.7 %collective-permute-start.8 = (bf16[9,8,3840]{2,1,0:T(8,128)(2,1)S(1)}, bf16[9,8,3840]{2,1,0:T(8,128)(2,1)}, u32[]{:S(2)}, u32[]{:S(2)}) collective-permute-start(bf16[9,8,3840]{2,1,0:T(8,128)(2,1)S(1)} %pad_maximum_fusion.1.refs_1_), channel_id=1, source_target_pairs={{0,8},{4,36},{8,16},{12,44},{16,24},{20,52},{24,0},{28,60},{32,40}... | collective-permute-start | bytes 1658888 | tf_op jit(solution)/shard_map/ppermute | solution.py:26
  64.0 3.8 %collective-permute-start.9 = (bf16[9,8,3840]{2,1,0:T(8,128)(2,1)S(1)}, bf16[9,8,3840]{2,1,0:T(8,128)(2,1)}, u32[]{:S(2)}, u32[]{:S(2)}) collective-permute-start(bf16[9,8,3840]{2,1,0:T(8,128)(2,1)S(1)} %pad_maximum_fusion.refs_0_), channel_id=1, source_target_pairs={{0,24},{4,484},{8,0},{12,492},{16,8},{20,500},{24,16},{28,508},{32... | collective-permute-start | bytes 1658888 | tf_op jit(solution)/shard_map/ppermute | solution.py:26
  67.7 0.0 collective-permute-done.6.refs_5_
  67.7 1.9 %collective-permute-start.7 = (bf16[9,8,3840]{2,1,0:T(8,128)(2,1)S(1)}, bf16[9,8,3840]{2,1,0:T(8,128)(2,1)S(1)}, u32[]{:S(2)}, u32[]{:S(2)}) collective-permute-start(bf16[9,8,3840]{2,1,0:T(8,128)(2,1)S(1)} %collective-permute-done.6.refs_5_), channel_id=1, source_target_pairs={{0,24},{4,484},{8,0},{12,492},{16,8},{20,500},{24,16},{28,508},{32... | collective-permute-start | bytes 1658888 | tf_op jit(solution)/shard_map/ppermute | solution.py:26
  69.7 0.0 collective-permute-done.2.refs_2_
  69.7 3.4 %collective-permute-start.3 = (bf16[9,8,3840]{2,1,0:T(8,128)(2,1)S(1)}, bf16[9,8,3840]{2,1,0:T(8,128)(2,1)S(1)}, u32[]{:S(2)}, u32[]{:S(2)}) collective-permute-start(bf16[9,8,3840]{2,1,0:T(8,128)(2,1)S(1)} %collective-permute-done.2.refs_2_), channel_id=1, source_target_pairs={{0,8},{4,36},{8,16},{12,44},{16,24},{20,52},{24,0},{28,60},{32,40}... | collective-permute-start | bytes 1658888 | tf_op jit(solution)/shard_map/ppermute | solution.py:26
  73.1 0.0 copy-done.11
  73.1 0.1 pad_add_fusion.at_ref
  73.2 0.4 collective-permute-done.8.refs_3_
  73.6 0.9 collective-permute-done.9.refs_4_
  74.5 0.0 collective-permute-done.other_ref
  74.5 0.0 copy-start
  74.5 2.3 %copy-done = bf16[2,32,9,3840]{3,1,2,0:T(8,128)(2,1)S(1)} copy-done((bf16[2,32,9,3840]{3,1,2,0:T(8,128)(2,1)S(1)}, bf16[2,32,9,3840]{3,1,2,0:T(8,128)(2,1)}, u32[]{:S(2)}) %copy-start) | copy-done | bytes 4423704
  76.8 7.5 %shard_map.136.prev_ref = f32[128,48]{1,0:T(8,128)S(1)} custom-call(bf16[2,288,3840]{2,1,0:T(8,128)(2,1)S(1)} %bitcast.24, bf16[2,288,3840]{2,1,0:T(8,128)(2,1)} %collective-permute-done.other_ref, bf16[9,8,3840]{2,1,0:T(8,128)(2,1)S(1)} %pad_maximum_fusion.refs_0_, bf16[9,8,3840]{2,1,0:T(8,128)(2,1)S(1)} %pad_maximum_fusion.1.refs_1_, ...), custom_call_target="tpu_custom_call" | custom-call | flops 3822059520 | bytes 12165120 | tf_op jit(solution)/shard_map/pallas_call | solution.py:112
  84.3 0.0 copy-start.1
  84.3 0.0 copy-start.2
  84.3 0.0 copy-start.3
  84.3 0.0 copy-start.4
  84.3 0.0 copy-start.5
  84.3 0.0 collective-permute-done.7.refs_1_
  84.3 0.0 collective-permute-done.3.refs_0_
  84.3 5.7 %shard_map.137 = bf16[128,128]{1,0:T(8,128)(2,1)} custom-call(s32[4]{0:T(128)S(1)} %pad_add_fusion.at_ref, bf16[2,288,3840]{2,1,0:T(8,128)(2,1)S(1)} %bitcast.25, bf16[2,288,3840]{2,1,0:T(8,128)(2,1)} %collective-permute-done.other_ref, f32[128,48]{1,0:T(8,128)S(1)} %shard_map.136.prev_ref, bf16[9,8,3840]{2,1,0:T(8,128)(2,1)S(1)} %collective-permute-done.3.refs_0_, ...), custom_call_target="tpu_custom_call" | custom-call | flops 1274019840 | bytes 9977872 | tf_op jit(solution)/shard_map/pallas_call | solution.py:112
  90.1 11.4 %all-to-all-start.1 = ((bf16[8,16,128]{2,1,0:T(8,128)(2,1)}), bf16[8,16,128]{2,1,0:T(8,128)(2,1)S(1)}, u32[]{:S(2)}, u32[]{:S(2)}) async-start(bf16[8,16,128]{2,1,0:T(8,128)(2,1)} %bitcast.8), calls=%async_computation.1 | async-start | bytes 65536 | tf_op jit(solution)/shard_map/all_to_all | solution.py:388
  101.5 0.0 copy-done.1
  101.5 0.0 copy-done.2
  101.5 0.0 copy-done.3
  101.5 0.0 copy-done.4
  101.5 0.0 copy-done.5
  101.5 0.0 copy-start.6
  101.5 0.0 copy-start.7
  101.5 0.0 copy-start.8
  101.5 0.0 copy-start.9
  101.5 0.0 copy-start.10
  101.6 1.3 %shard_map.138 = (s32[64,8]{1,0:T(8,128)S(1)}, bf16[384,1024]{1,0:T(8,128)(2,1)S(1)}, bf16[1152,256]{1,0:T(8,128)(2,1)S(1)}, bf16[1152,256]{1,0:T(8,128)(2,1)S(1)}) custom-call(s32[4]{0:T(128)S(1)} %pad_add_fusion.at_ref, s32[16]{0:T(128)S(1)} %copy-done.5, s32[16,256]{1,0:T(8,128)S(1)} %copy-done.3, s32[16,256]{1,0:T(8,128)S(1)} %copy-done.4, ...), custom_call_target="tpu_custom_call" | custom-call | flops 1000000000 | bytes 217744 | tf_op jit(solution)/shard_map/pallas_call | solution.py:112
  103.5 2.9 %all-to-all-done.1 = bf16[8,16,128]{2,1,0:T(8,128)(2,1)S(1)} async-done(((bf16[8,16,128]{2,1,0:T(8,128)(2,1)}), bf16[8,16,128]{2,1,0:T(8,128)(2,1)S(1)}, u32[]{:S(2)}, u32[]{:S(2)}) %all-to-all-start.1) | async-done | bytes 32800 | tf_op jit(solution)/shard_map/all_to_all | solution.py:388
  106.4 0.0 copy-done.6
  106.4 0.0 copy-done.7
  106.4 0.0 copy-done.8
  106.4 0.0 copy-done.9
  106.4 0.0 copy-done.10
  106.4 3.0 %shard_map.139 = f32[64,8]{1,0:T(8,128)S(1)} custom-call(f32[1]{0:T(128)S(6)} %copy.20.bias_ref, bf16[128,128]{1,0:T(8,128)(2,1)S(1)} %bitcast.26, bf16[256,128]{1,0:T(8,128)(2,1)S(1)} %copy-done.10, bf16[384,1024]{1,0:T(8,128)(2,1)S(1)} %get-tuple-element.15.t1_ref, f32[1,32]{1,0:T(1,128)S(1)} %bitcast.30, bf16[1152,256]{1,0:T(8,128)(2,1)S(1)} %get-tuple-element.16.t2_ref, ...), custom_call_target="tpu_custom_call" | custom-call | flops 2000000000 | bytes 2067588 | tf_op jit(solution)/shard_map/pallas_call | solution.py:112
  109.4 20.0 %all_to_all.26 = f32[64,1,8]{2,1,0:T(1,128)S(1)} all-to-all(f32[64,1,8]{2,1,0:T(1,128)S(1)} %bitcast.27), channel_id=1, replica_groups=mesh['z'=16,'y'=4,'c'=2,'x'=4] {'z','y'}, dimensions={0} | all-to-all | bytes 4096 | tf_op jit(solution)/shard_map/all_to_all | solution.py:392
  129.5 0.1 reduce_sum.9
  129.5 0.1 reshape.27
  129.6 0.7 copy.19
  (3 shorter events, 0.1 us)
Async XLA Ops:
  0.0 74.5 %collective-permute-start = (bf16[2,288,3840]{2,1,0:T(8,128)(2,1)}, bf16[2,288,3840]{2,1,0:T(8,128)(2,1)}, u32[]{:S(2)}, u32[]{:S(2)}) collective-permute-start(bf16[2,288,3840]{2,1,0:T(8,128)(2,1)} %bitcast.23), channel_id=1, source_target_pairs={{0,4},{4,0},{1,5},{5,1},{2,6},{6,2},{3,7},{7,3},{8,12},{12,8},{9,1... | collective-permute-start | bytes 13271048 | tf_op jit(solution)/shard_map/ppermute | solution.py:375
  36.0 37.1 %copy-start.11 = (bf16[3,3,1,32]{3,1,2,0:T(4,128)(2,1)S(1)}, bf16[3,3,1,32]{3,1,2,0:T(4,128)(2,1)}, u32[]{:S(2)}) copy-start(bf16[3,3,1,32]{3,1,2,0:T(4,128)(2,1)} %param.19) | copy-start | bytes 1732
  36.0 9.5 %collective-permute-start.4 = (bf16[9,4,3840]{2,1,0:T(4,128)(2,1)S(1)}, bf16[9,4,3840]{2,1,0:T(4,128)(2,1)S(1)}, u32[]{:S(2)}, u32[]{:S(2)}) collective-permute-start(bf16[9,4,3840]{2,1,0:T(4,128)(2,1)S(1)} %bitcast.34), channel_id=1, source_target_pairs={{0,480},{4,28},{8,488},{12,4},{16,496},{20,12},{24,504},{28,20},{3... | collective-permute-start | bytes 829448 | tf_op jit(solution)/shard_map/ppermute | solution.py:26
  40.6 8.9 %collective-permute-start.5 = (bf16[9,4,3840]{2,1,0:T(4,128)(2,1)S(1)}, bf16[9,4,3840]{2,1,0:T(4,128)(2,1)S(1)}, u32[]{:S(2)}, u32[]{:S(2)}) collective-permute-start(bf16[9,4,3840]{2,1,0:T(4,128)(2,1)S(1)} %bitcast.35), channel_id=1, source_target_pairs={{0,64},{4,20},{8,72},{12,28},{16,80},{20,4},{24,88},{28,12},{32,96... | collective-permute-start | bytes 829448 | tf_op jit(solution)/shard_map/ppermute | solution.py:26
  42.9 12.5 %collective-permute-start.1 = (bf16[9,4,3840]{2,1,0:T(4,128)(2,1)S(1)}, bf16[9,4,3840]{2,1,0:T(4,128)(2,1)S(1)}, u32[]{:S(2)}, u32[]{:S(2)}) collective-permute-start(bf16[9,4,3840]{2,1,0:T(4,128)(2,1)S(1)} %bitcast.36), channel_id=1, source_target_pairs={{0,32},{4,12},{8,40},{12,20},{16,48},{20,28},{24,56},{28,4},{32,64... | collective-permute-start | bytes 829448 | tf_op jit(solution)/shard_map/ppermute | solution.py:26
  49.8 18.0 %collective-permute-start.6 = (bf16[9,8,3840]{2,1,0:T(8,128)(2,1)S(1)}, bf16[9,8,3840]{2,1,0:T(8,128)(2,1)S(1)}, u32[]{:S(2)}, u32[]{:S(2)}) collective-permute-start(bf16[9,8,3840]{2,1,0:T(8,128)(2,1)S(1)} %pad_maximum_fusion.1.refs_1_), channel_id=1, source_target_pairs={{0,24},{4,484},{8,0},{12,492},{16,8},{20,500},{24,16},{28,508},{32... | collective-permute-start | bytes 1658888 | tf_op jit(solution)/shard_map/ppermute | solution.py:26
  55.7 14.0 %collective-permute-start.2 = (bf16[9,8,3840]{2,1,0:T(8,128)(2,1)S(1)}, bf16[9,8,3840]{2,1,0:T(8,128)(2,1)S(1)}, u32[]{:S(2)}, u32[]{:S(2)}) collective-permute-start(bf16[9,8,3840]{2,1,0:T(8,128)(2,1)S(1)} %pad_maximum_fusion.refs_0_), channel_id=1, source_target_pairs={{0,8},{4,36},{8,16},{12,44},{16,24},{20,52},{24,0},{28,60},{32,40}... | collective-permute-start | bytes 1658888 | tf_op jit(solution)/shard_map/ppermute | solution.py:26
  61.2 12.3 %collective-permute-start.8 = (bf16[9,8,3840]{2,1,0:T(8,128)(2,1)S(1)}, bf16[9,8,3840]{2,1,0:T(8,128)(2,1)}, u32[]{:S(2)}, u32[]{:S(2)}) collective-permute-start(bf16[9,8,3840]{2,1,0:T(8,128)(2,1)S(1)} %pad_maximum_fusion.1.refs_1_), channel_id=1, source_target_pairs={{0,8},{4,36},{8,16},{12,44},{16,24},{20,52},{24,0},{28,60},{32,40}... | collective-permute-start | bytes 1658888 | tf_op jit(solution)/shard_map/ppermute | solution.py:26
  64.0 10.5 %collective-permute-start.9 = (bf16[9,8,3840]{2,1,0:T(8,128)(2,1)S(1)}, bf16[9,8,3840]{2,1,0:T(8,128)(2,1)}, u32[]{:S(2)}, u32[]{:S(2)}) collective-permute-start(bf16[9,8,3840]{2,1,0:T(8,128)(2,1)S(1)} %pad_maximum_fusion.refs_0_), channel_id=1, source_target_pairs={{0,24},{4,484},{8,0},{12,492},{16,8},{20,500},{24,16},{28,508},{32... | collective-permute-start | bytes 1658888 | tf_op jit(solution)/shard_map/ppermute | solution.py:26
  67.7 16.6 %collective-permute-start.7 = (bf16[9,8,3840]{2,1,0:T(8,128)(2,1)S(1)}, bf16[9,8,3840]{2,1,0:T(8,128)(2,1)S(1)}, u32[]{:S(2)}, u32[]{:S(2)}) collective-permute-start(bf16[9,8,3840]{2,1,0:T(8,128)(2,1)S(1)} %collective-permute-done.6.refs_5_), channel_id=1, source_target_pairs={{0,24},{4,484},{8,0},{12,492},{16,8},{20,500},{24,16},{28,508},{32... | collective-permute-start | bytes 1658888 | tf_op jit(solution)/shard_map/ppermute | solution.py:26
  69.7 14.6 %collective-permute-start.3 = (bf16[9,8,3840]{2,1,0:T(8,128)(2,1)S(1)}, bf16[9,8,3840]{2,1,0:T(8,128)(2,1)S(1)}, u32[]{:S(2)}, u32[]{:S(2)}) collective-permute-start(bf16[9,8,3840]{2,1,0:T(8,128)(2,1)S(1)} %collective-permute-done.2.refs_2_), channel_id=1, source_target_pairs={{0,8},{4,36},{8,16},{12,44},{16,24},{20,52},{24,0},{28,60},{32,40}... | collective-permute-start | bytes 1658888 | tf_op jit(solution)/shard_map/ppermute | solution.py:26
  74.5 2.3 %copy-start = (bf16[2,32,9,3840]{3,1,2,0:T(8,128)(2,1)S(1)}, bf16[2,32,9,3840]{3,1,2,0:T(8,128)(2,1)}, u32[]{:S(2)}) copy-start(bf16[2,32,9,3840]{3,1,2,0:T(8,128)(2,1)} %param.15) | copy-start | bytes 13271044
  84.3 17.2 %copy-start.1 = (bf16[3,3,64,128]{3,2,1,0:T(8,128)(2,1)S(1)}, bf16[3,3,64,128]{3,2,1,0:T(8,128)(2,1)}, u32[]{:S(2)}) copy-start(bf16[3,3,64,128]{3,2,1,0:T(8,128)(2,1)} %param.23) | copy-start | bytes 442372
  84.3 17.2 %copy-start.2 = (bf16[3,3,32,64]{3,2,1,0:T(8,128)(2,1)S(1)}, bf16[3,3,32,64]{3,2,1,0:T(8,128)(2,1)}, u32[]{:S(2)}) copy-start(bf16[3,3,32,64]{3,2,1,0:T(8,128)(2,1)} %param.21) | copy-start | bytes 110596
  84.3 17.2 %copy-start.3 = (s32[16,256]{1,0:T(8,128)S(1)}, s32[16,256]{1,0:T(8,128)}, u32[]{:S(2)}) copy-start(s32[16,256]{1,0:T(8,128)} %shard_ref.1) | copy-start | bytes 49156
  84.3 17.2 %copy-start.4 = (s32[16,256]{1,0:T(8,128)S(1)}, s32[16,256]{1,0:T(8,128)}, u32[]{:S(2)}) copy-start(s32[16,256]{1,0:T(8,128)} %clip_ref.1) | copy-start | bytes 49156
  84.3 17.2 %copy-start.5 = (s32[16]{0:T(128)S(1)}, s32[16]{0:T(128)}, u32[]{:S(2)}) copy-start(s32[16]{0:T(128)} %count_ref.1) | copy-start | bytes 196
  90.1 16.3 %all-to-all-start.1 = ((bf16[8,16,128]{2,1,0:T(8,128)(2,1)}), bf16[8,16,128]{2,1,0:T(8,128)(2,1)S(1)}, u32[]{:S(2)}, u32[]{:S(2)}) async-start(bf16[8,16,128]{2,1,0:T(8,128)(2,1)} %bitcast.8), calls=%async_computation.1 | async-start | bytes 65536 | tf_op jit(solution)/shard_map/all_to_all | solution.py:388
  101.5 4.9 %copy-start.6 = (f32[32]{0:T(128)S(1)}, f32[32]{0:T(128)}, u32[]{:S(2)}) copy-start(f32[32]{0:T(128)} %param.20) | copy-start | bytes 388
  101.5 4.9 %copy-start.7 = (f32[64]{0:T(128)S(1)}, f32[64]{0:T(128)}, u32[]{:S(2)}) copy-start(f32[64]{0:T(128)} %param.22) | copy-start | bytes 772
  101.5 4.9 %copy-start.8 = (f32[128]{0:T(128)S(1)}, f32[128]{0:T(128)}, u32[]{:S(2)}) copy-start(f32[128]{0:T(128)} %param.24) | copy-start | bytes 1540
  101.5 4.9 %copy-start.9 = (bf16[128]{0:T(256)(128)(2,1)S(1)}, bf16[128]{0:T(256)(128)(2,1)}, u32[]{:S(2)}) copy-start(bf16[128]{0:T(256)(128)(2,1)} %param.25) | copy-start | bytes 772
  101.5 4.9 %copy-start.10 = (bf16[256,128]{1,0:T(8,128)(2,1)S(1)}, bf16[256,128]{1,0:T(8,128)(2,1)}, u32[]{:S(2)}) copy-start(bf16[256,128]{1,0:T(8,128)(2,1)} %constant.22.clone.order_ref) | copy-start | bytes 196612

commit v6 on v5

--- a/solution.py
+++ b/solution.py
@@ -372,6 +372,7 @@
     last = jnp.concatenate([ahead, two], axis=1)
     kernels = (first_kernel, second_kernel, third_kernel)
     listed, *spread = prepare(at, cand_count, cand_shard, cand_clip, *kernels)
+    own, first, last = lax.optimization_barrier((own, first, last))
     other = lax.ppermute(own, "c", [(0, 1), (1, 0)])
     behind_first = shift(first, 1)
     ahead_first = shift(first, -1)

time: 131 us -> 133 us (1.015)
  blocking collectives: 46 us -> 51.3 us
  starting transfers between devices: 52.6 us -> 49.2 us
    all_to_all x1, starting transfers between devices: 11.4 us -> 5.39 us  [on_device(): parts = lax.all_to_all(table, ('c', 'x'), 0, 0, tiled=True)]
    ppermute x1, starting transfers between devices: 8.78 us -> 14.2 us  [on_device(): other = lax.ppermute(own, 'c', [(0, 1), (1, 0)])]
    all_to_all x1, blocking collectives: 26 us -> 30 us  [gather_classes(): lax.all_to_all(jnp.broadcast_to(flat, (4,) + flat.shape), 'z', 0, 0, axis...]
    ppermute x9, starting transfers between devices: 32.4 us -> 29.6 us  [send(): return lax.ppermute(values, PLANE, pairs)]
  transfers between devices with their start and end apart: 11 -> 11, of which waited for: 4 -> 4; matrix products, arithmetic and copies ran while one was open for 1% -> 0% of each run, Pallas kernels for 7% -> 7%
where the time goes in v6:
time: 133 us; the launch traced here: 132 us
  blocking collectives  51.3 us (39%)
  starting transfers between devices  49.2 us (37%)
  Pallas kernels  17.6 us (13%)
  waiting for transfers between devices  8.41 us (6%)
  local copies, waits for them, and re-layouts  4.21 us (3%)
    all_to_all x1, blocking collectives, gather_classes(): lax.all_to_all(jnp.broadcast_to(flat, (4,) + flat.shape), 'z', 0, 0, axis...  30 us
    ppermute x9, starting transfers between devices, send(): return lax.ppermute(values, PLANE, pairs)  29.6 us
    all_to_all x1, blocking collectives, on_device(): values = lax.all_to_all(values, ('z', 'y'), 0, 0, tiled=True)  21.3 us
    pallas_call x4, Pallas kernels, kernel_call(): pl.pallas_call(body, in_specs=[pl.BlockSpec(memory_space=space) for space...  17.6 us
    ppermute x1, starting transfers between devices, on_device(): other = lax.ppermute(own, 'c', [(0, 1), (1, 0)])  14.2 us
    ppermute x9, waiting for transfers between devices, send(): return lax.ppermute(values, PLANE, pairs)  5.55 us
    all_to_all x1, starting transfers between devices, on_device(): parts = lax.all_to_all(table, ('c', 'x'), 0, 0, tiled=True)  5.39 us
    all_to_all x1, waiting for transfers between devices, on_device(): parts = lax.all_to_all(table, ('c', 'x'), 0, 0, tiled=True)  2.86 us
  transfers between devices with their start and end apart: 11, of which 4 were waited for; matrix products, arithmetic and copies ran while one was open for 0% of the time, Pallas kernels for 7%

profile of v6, /device:TPU:1, one launch (start us, length us, event | category | flops | bytes accessed | tf_op | source)
XLA Modules:
  0.0 132.4 jit_solution(1623349261877080091)
XLA Ops:
  0.0 1.0 reshape_squeeze.3
  1.0 30.0 %all_to_all.25 = bf16[4,9,30,128]{3,2,1,0:T(8,128)(2,1)S(1)} all-to-all(bf16[4,9,30,128]{3,2,1,0:T(8,128)(2,1)S(1)} %broadcast_in_dim.15), channel_id=1, replica_groups={{0,128,256,384},{32,160,288,416},{64,192,320,448},{96,224,352,480},{1,1..., dimensions={0} | all-to-all | bytes 552960 | tf_op jit(solution)/shard_map/all_to_all | solution.py:41
  31.1 0.1 reshape.23
  31.2 0.0 copy-start.11
  31.2 3.2 %collective-permute-start = (bf16[9,4,3840]{2,1,0:T(4,128)(2,1)S(1)}, bf16[9,4,3840]{2,1,0:T(4,128)(2,1)S(1)}, u32[]{:S(2)}, u32[]{:S(2)}) collective-permute-start(bf16[9,4,3840]{2,1,0:T(4,128)(2,1)S(1)} %bitcast.34), channel_id=1, source_target_pairs={{0,32},{4,12},{8,40},{12,20},{16,48},{20,28},{24,56},{28,4},{32,64... | collective-permute-start | bytes 829448 | tf_op jit(solution)/shard_map/ppermute | solution.py:26
  34.4 3.4 %collective-permute-start.1 = (bf16[9,4,3840]{2,1,0:T(4,128)(2,1)S(1)}, bf16[9,4,3840]{2,1,0:T(4,128)(2,1)S(1)}, u32[]{:S(2)}, u32[]{:S(2)}) collective-permute-start(bf16[9,4,3840]{2,1,0:T(4,128)(2,1)S(1)} %bitcast.35), channel_id=1, source_target_pairs={{0,480},{4,28},{8,488},{12,4},{16,496},{20,12},{24,504},{28,20},{3... | collective-permute-start | bytes 829448 | tf_op jit(solution)/shard_map/ppermute | solution.py:26
  37.8 3.5 %collective-permute-start.2 = (bf16[9,4,3840]{2,1,0:T(4,128)(2,1)S(1)}, bf16[9,4,3840]{2,1,0:T(4,128)(2,1)S(1)}, u32[]{:S(2)}, u32[]{:S(2)}) collective-permute-start(bf16[9,4,3840]{2,1,0:T(4,128)(2,1)S(1)} %bitcast.36), channel_id=1, source_target_pairs={{0,64},{4,20},{8,72},{12,28},{16,80},{20,4},{24,88},{28,12},{32,96... | collective-permute-start | bytes 829448 | tf_op jit(solution)/shard_map/ppermute | solution.py:26
  41.3 0.0 collective-permute-done
  41.3 0.3 pad_maximum_fusion.refs_0_
  41.6 0.1 collective-permute-done.1
  41.7 4.9 %collective-permute-done.2 = bf16[9,4,3840]{2,1,0:T(4,128)(2,1)S(1)} collective-permute-done((bf16[9,4,3840]{2,1,0:T(4,128)(2,1)S(1)}, bf16[9,4,3840]{2,1,0:T(4,128)(2,1)S(1)}, u32[]{:S(2)}, u32[]{:S(2)}) %collective-permute-start.2) | collective-permute-done | bytes 276512 | tf_op jit(solution)/shard_map/ppermute | solution.py:26
  46.6 0.3 pad_maximum_fusion.1.refs_1_
  46.8 14.2 %collective-permute-start.3 = (bf16[2,288,3840]{2,1,0:T(8,128)(2,1)}, bf16[2,288,3840]{2,1,0:T(8,128)(2,1)}, u32[]{:S(2)}, u32[]{:S(2)}) collective-permute-start(bf16[2,288,3840]{2,1,0:T(8,128)(2,1)} %bitcast.23), channel_id=1, source_target_pairs={{0,4},{4,0},{1,5},{5,1},{2,6},{6,2},{3,7},{7,3},{8,12},{12,8},{9,1... | collective-permute-start | bytes 13271048 | tf_op jit(solution)/shard_map/ppermute | solution.py:376
  61.1 3.7 %collective-permute-start.4 = (bf16[9,8,3840]{2,1,0:T(8,128)(2,1)S(1)}, bf16[9,8,3840]{2,1,0:T(8,128)(2,1)S(1)}, u32[]{:S(2)}, u32[]{:S(2)}) collective-permute-start(bf16[9,8,3840]{2,1,0:T(8,128)(2,1)S(1)} %pad_maximum_fusion.refs_0_), channel_id=1, source_target_pairs={{0,8},{4,36},{8,16},{12,44},{16,24},{20,52},{24,0},{28,60},{32,40}... | collective-permute-start | bytes 1658888 | tf_op jit(solution)/shard_map/ppermute | solution.py:26
  64.8 2.8 %collective-permute-start.6 = (bf16[9,8,3840]{2,1,0:T(8,128)(2,1)S(1)}, bf16[9,8,3840]{2,1,0:T(8,128)(2,1)S(1)}, u32[]{:S(2)}, u32[]{:S(2)}) collective-permute-start(bf16[9,8,3840]{2,1,0:T(8,128)(2,1)S(1)} %pad_maximum_fusion.1.refs_1_), channel_id=1, source_target_pairs={{0,24},{4,484},{8,0},{12,492},{16,8},{20,500},{24,16},{28,508},{32... | collective-permute-start | bytes 1658888 | tf_op jit(solution)/shard_map/ppermute | solution.py:26
  67.6 2.5 %collective-permute-start.8 = (bf16[9,8,3840]{2,1,0:T(8,128)(2,1)S(1)}, bf16[9,8,3840]{2,1,0:T(8,128)(2,1)}, u32[]{:S(2)}, u32[]{:S(2)}) collective-permute-start(bf16[9,8,3840]{2,1,0:T(8,128)(2,1)S(1)} %pad_maximum_fusion.1.refs_1_), channel_id=1, source_target_pairs={{0,8},{4,36},{8,16},{12,44},{16,24},{20,52},{24,0},{28,60},{32,40}... | collective-permute-start | bytes 1658888 | tf_op jit(solution)/shard_map/ppermute | solution.py:26
  70.1 4.0 %collective-permute-start.9 = (bf16[9,8,3840]{2,1,0:T(8,128)(2,1)S(1)}, bf16[9,8,3840]{2,1,0:T(8,128)(2,1)}, u32[]{:S(2)}, u32[]{:S(2)}) collective-permute-start(bf16[9,8,3840]{2,1,0:T(8,128)(2,1)S(1)} %pad_maximum_fusion.refs_0_), channel_id=1, source_target_pairs={{0,24},{4,484},{8,0},{12,492},{16,8},{20,500},{24,16},{28,508},{32... | collective-permute-start | bytes 1658888 | tf_op jit(solution)/shard_map/ppermute | solution.py:26
  74.1 0.0 collective-permute-done.4.refs_2_
  74.1 1.9 %collective-permute-start.5 = (bf16[9,8,3840]{2,1,0:T(8,128)(2,1)S(1)}, bf16[9,8,3840]{2,1,0:T(8,128)(2,1)S(1)}, u32[]{:S(2)}, u32[]{:S(2)}) collective-permute-start(bf16[9,8,3840]{2,1,0:T(8,128)(2,1)S(1)} %collective-permute-done.4.refs_2_), channel_id=1, source_target_pairs={{0,8},{4,36},{8,16},{12,44},{16,24},{20,52},{24,0},{28,60},{32,40}... | collective-permute-start | bytes 1658888 | tf_op jit(solution)/shard_map/ppermute | solution.py:26
  76.0 0.0 collective-permute-done.6.refs_5_
  76.1 4.6 %collective-permute-start.7 = (bf16[9,8,3840]{2,1,0:T(8,128)(2,1)S(1)}, bf16[9,8,3840]{2,1,0:T(8,128)(2,1)S(1)}, u32[]{:S(2)}, u32[]{:S(2)}) collective-permute-start(bf16[9,8,3840]{2,1,0:T(8,128)(2,1)S(1)} %collective-permute-done.6.refs_5_), channel_id=1, source_target_pairs={{0,24},{4,484},{8,0},{12,492},{16,8},{20,500},{24,16},{28,508},{32... | collective-permute-start | bytes 1658888 | tf_op jit(solution)/shard_map/ppermute | solution.py:26
  80.6 0.0 copy-done.11
  80.7 0.1 pad_add_fusion.at_ref
  80.7 0.0 collective-permute-done.8.refs_3_
  80.8 0.6 collective-permute-done.9.refs_4_
  81.4 0.0 collective-permute-done.3.other_ref
  81.4 0.0 copy-start
  81.4 2.3 %copy-done = bf16[2,32,9,3840]{3,1,2,0:T(8,128)(2,1)S(1)} copy-done((bf16[2,32,9,3840]{3,1,2,0:T(8,128)(2,1)S(1)}, bf16[2,32,9,3840]{3,1,2,0:T(8,128)(2,1)}, u32[]{:S(2)}) %copy-start) | copy-done | bytes 4423704
  83.6 7.5 %shard_map.136.prev_ref = f32[128,48]{1,0:T(8,128)S(1)} custom-call(bf16[2,288,3840]{2,1,0:T(8,128)(2,1)S(1)} %bitcast.24, bf16[2,288,3840]{2,1,0:T(8,128)(2,1)} %collective-permute-done.3.other_ref, bf16[9,8,3840]{2,1,0:T(8,128)(2,1)S(1)} %pad_maximum_fusion.refs_0_, bf16[9,8,3840]{2,1,0:T(8,128)(2,1)S(1)} %pad_maximum_fusion.1.refs_1_, ...), custom_call_target="tpu_custom_call" | custom-call | flops 3822059520 | bytes 12165120 | tf_op jit(solution)/shard_map/pallas_call | solution.py:112
  91.1 0.0 copy-start.1
  91.1 0.0 copy-start.2
  91.1 0.0 copy-start.3
  91.1 0.0 copy-start.4
  91.2 0.0 copy-start.5
  91.2 0.0 collective-permute-done.5.refs_0_
  91.2 0.0 collective-permute-done.7.refs_1_
  91.2 5.7 %shard_map.137 = bf16[128,128]{1,0:T(8,128)(2,1)} custom-call(s32[4]{0:T(128)S(1)} %pad_add_fusion.at_ref, bf16[2,288,3840]{2,1,0:T(8,128)(2,1)S(1)} %bitcast.25, bf16[2,288,3840]{2,1,0:T(8,128)(2,1)} %collective-permute-done.3.other_ref, f32[128,48]{1,0:T(8,128)S(1)} %shard_map.136.prev_ref, bf16[9,8,3840]{2,1,0:T(8,128)(2,1)S(1)} %collective-permute-done.5.refs_0_, ...), custom_call_target="tpu_custom_call" | custom-call | flops 1274019840 | bytes 9977872 | tf_op jit(solution)/shard_map/pallas_call | solution.py:112
  96.9 5.4 %all-to-all-start.1 = ((bf16[8,16,128]{2,1,0:T(8,128)(2,1)}), bf16[8,16,128]{2,1,0:T(8,128)(2,1)S(1)}, u32[]{:S(2)}, u32[]{:S(2)}) async-start(bf16[8,16,128]{2,1,0:T(8,128)(2,1)} %bitcast.7), calls=%async_computation.1 | async-start | bytes 65536 | tf_op jit(solution)/shard_map/all_to_all | solution.py:389
  102.3 0.0 copy-done.1
  102.3 0.0 copy-done.2
  102.3 0.0 copy-done.3
  102.3 0.0 copy-done.4
  102.4 0.0 copy-done.5
  102.4 0.0 copy-start.6
  102.4 0.0 copy-start.7
  102.4 0.0 copy-start.8
  102.4 0.0 copy-start.9
  102.4 0.0 copy-start.10
  102.4 1.3 shard_map.138
  104.4 2.9 %all-to-all-done.1 = bf16[8,16,128]{2,1,0:T(8,128)(2,1)S(1)} async-done(((bf16[8,16,128]{2,1,0:T(8,128)(2,1)}), bf16[8,16,128]{2,1,0:T(8,128)(2,1)S(1)}, u32[]{:S(2)}, u32[]{:S(2)}) %all-to-all-start.1) | async-done | bytes 32800 | tf_op jit(solution)/shard_map/all_to_all | solution.py:389
  107.2 0.0 copy-done.6
  107.3 0.0 copy-done.7
  107.3 0.0 copy-done.8
  107.3 0.0 copy-done.9
  107.3 0.0 copy-done.10
  107.3 3.0 %shard_map.139 = f32[64,8]{1,0:T(8,128)S(1)} custom-call(f32[1]{0:T(128)S(6)} %copy.20.bias_ref, bf16[128,128]{1,0:T(8,128)(2,1)S(1)} %bitcast.26, bf16[256,128]{1,0:T(8,128)(2,1)S(1)} %copy-done.10, bf16[384,1024]{1,0:T(8,128)(2,1)S(1)} %get-tuple-element.21.t1_ref, f32[1,32]{1,0:T(1,128)S(1)} %bitcast.30, bf16[1152,256]{1,0:T(8,128)(2,1)S(1)} %get-tuple-element.22.t2_ref, ...), custom_call_target="tpu_custom_call" | custom-call | flops 2000000000 | bytes 2067588 | tf_op jit(solution)/shard_map/pallas_call | solution.py:112
  110.3 21.3 %all_to_all.26 = f32[64,1,8]{2,1,0:T(1,128)S(1)} all-to-all(f32[64,1,8]{2,1,0:T(1,128)S(1)} %bitcast.27), channel_id=1, replica_groups=mesh['z'=16,'y'=4,'c'=2,'x'=4] {'z','y'}, dimensions={0} | all-to-all | bytes 4096 | tf_op jit(solution)/shard_map/all_to_all | solution.py:393
  131.6 0.1 reduce_sum.9
  131.7 0.1 reshape.27
  131.8 0.7 copy.19
  (3 shorter events, 0.1 us)
Async XLA Ops:
  31.2 49.5 %copy-start.11 = (bf16[3,3,1,32]{3,1,2,0:T(4,128)(2,1)S(1)}, bf16[3,3,1,32]{3,1,2,0:T(4,128)(2,1)}, u32[]{:S(2)}) copy-start(bf16[3,3,1,32]{3,1,2,0:T(4,128)(2,1)} %param.19) | copy-start | bytes 1732
  31.2 10.1 %collective-permute-start = (bf16[9,4,3840]{2,1,0:T(4,128)(2,1)S(1)}, bf16[9,4,3840]{2,1,0:T(4,128)(2,1)S(1)}, u32[]{:S(2)}, u32[]{:S(2)}) collective-permute-start(bf16[9,4,3840]{2,1,0:T(4,128)(2,1)S(1)} %bitcast.34), channel_id=1, source_target_pairs={{0,32},{4,12},{8,40},{12,20},{16,48},{20,28},{24,56},{28,4},{32,64... | collective-permute-start | bytes 829448 | tf_op jit(solution)/shard_map/ppermute | solution.py:26
  34.4 7.3 %collective-permute-start.1 = (bf16[9,4,3840]{2,1,0:T(4,128)(2,1)S(1)}, bf16[9,4,3840]{2,1,0:T(4,128)(2,1)S(1)}, u32[]{:S(2)}, u32[]{:S(2)}) collective-permute-start(bf16[9,4,3840]{2,1,0:T(4,128)(2,1)S(1)} %bitcast.35), channel_id=1, source_target_pairs={{0,480},{4,28},{8,488},{12,4},{16,496},{20,12},{24,504},{28,20},{3... | collective-permute-start | bytes 829448 | tf_op jit(solution)/shard_map/ppermute | solution.py:26
  37.8 8.8 %collective-permute-start.2 = (bf16[9,4,3840]{2,1,0:T(4,128)(2,1)S(1)}, bf16[9,4,3840]{2,1,0:T(4,128)(2,1)S(1)}, u32[]{:S(2)}, u32[]{:S(2)}) collective-permute-start(bf16[9,4,3840]{2,1,0:T(4,128)(2,1)S(1)} %bitcast.36), channel_id=1, source_target_pairs={{0,64},{4,20},{8,72},{12,28},{16,80},{20,4},{24,88},{28,12},{32,96... | collective-permute-start | bytes 829448 | tf_op jit(solution)/shard_map/ppermute | solution.py:26
  46.8 34.5 %collective-permute-start.3 = (bf16[2,288,3840]{2,1,0:T(8,128)(2,1)}, bf16[2,288,3840]{2,1,0:T(8,128)(2,1)}, u32[]{:S(2)}, u32[]{:S(2)}) collective-permute-start(bf16[2,288,3840]{2,1,0:T(8,128)(2,1)} %bitcast.23), channel_id=1, source_target_pairs={{0,4},{4,0},{1,5},{5,1},{2,6},{6,2},{3,7},{7,3},{8,12},{12,8},{9,1... | collective-permute-start | bytes 13271048 | tf_op jit(solution)/shard_map/ppermute | solution.py:376
  61.1 13.0 %collective-permute-start.4 = (bf16[9,8,3840]{2,1,0:T(8,128)(2,1)S(1)}, bf16[9,8,3840]{2,1,0:T(8,128)(2,1)S(1)}, u32[]{:S(2)}, u32[]{:S(2)}) collective-permute-start(bf16[9,8,3840]{2,1,0:T(8,128)(2,1)S(1)} %pad_maximum_fusion.refs_0_), channel_id=1, source_target_pairs={{0,8},{4,36},{8,16},{12,44},{16,24},{20,52},{24,0},{28,60},{32,40}... | collective-permute-start | bytes 1658888 | tf_op jit(solution)/shard_map/ppermute | solution.py:26
  64.8 11.2 %collective-permute-start.6 = (bf16[9,8,3840]{2,1,0:T(8,128)(2,1)S(1)}, bf16[9,8,3840]{2,1,0:T(8,128)(2,1)S(1)}, u32[]{:S(2)}, u32[]{:S(2)}) collective-permute-start(bf16[9,8,3840]{2,1,0:T(8,128)(2,1)S(1)} %pad_maximum_fusion.1.refs_1_), channel_id=1, source_target_pairs={{0,24},{4,484},{8,0},{12,492},{16,8},{20,500},{24,16},{28,508},{32... | collective-permute-start | bytes 1658888 | tf_op jit(solution)/shard_map/ppermute | solution.py:26
  67.6 13.2 %collective-permute-start.8 = (bf16[9,8,3840]{2,1,0:T(8,128)(2,1)S(1)}, bf16[9,8,3840]{2,1,0:T(8,128)(2,1)}, u32[]{:S(2)}, u32[]{:S(2)}) collective-permute-start(bf16[9,8,3840]{2,1,0:T(8,128)(2,1)S(1)} %pad_maximum_fusion.1.refs_1_), channel_id=1, source_target_pairs={{0,8},{4,36},{8,16},{12,44},{16,24},{20,52},{24,0},{28,60},{32,40}... | collective-permute-start | bytes 1658888 | tf_op jit(solution)/shard_map/ppermute | solution.py:26
  70.1 11.3 %collective-permute-start.9 = (bf16[9,8,3840]{2,1,0:T(8,128)(2,1)S(1)}, bf16[9,8,3840]{2,1,0:T(8,128)(2,1)}, u32[]{:S(2)}, u32[]{:S(2)}) collective-permute-start(bf16[9,8,3840]{2,1,0:T(8,128)(2,1)S(1)} %pad_maximum_fusion.refs_0_), channel_id=1, source_target_pairs={{0,24},{4,484},{8,0},{12,492},{16,8},{20,500},{24,16},{28,508},{32... | collective-permute-start | bytes 1658888 | tf_op jit(solution)/shard_map/ppermute | solution.py:26
  74.1 17.1 %collective-permute-start.5 = (bf16[9,8,3840]{2,1,0:T(8,128)(2,1)S(1)}, bf16[9,8,3840]{2,1,0:T(8,128)(2,1)S(1)}, u32[]{:S(2)}, u32[]{:S(2)}) collective-permute-start(bf16[9,8,3840]{2,1,0:T(8,128)(2,1)S(1)} %collective-permute-done.4.refs_2_), channel_id=1, source_target_pairs={{0,8},{4,36},{8,16},{12,44},{16,24},{20,52},{24,0},{28,60},{32,40}... | collective-permute-start | bytes 1658888 | tf_op jit(solution)/shard_map/ppermute | solution.py:26
  76.1 15.1 %collective-permute-start.7 = (bf16[9,8,3840]{2,1,0:T(8,128)(2,1)S(1)}, bf16[9,8,3840]{2,1,0:T(8,128)(2,1)S(1)}, u32[]{:S(2)}, u32[]{:S(2)}) collective-permute-start(bf16[9,8,3840]{2,1,0:T(8,128)(2,1)S(1)} %collective-permute-done.6.refs_5_), channel_id=1, source_target_pairs={{0,24},{4,484},{8,0},{12,492},{16,8},{20,500},{24,16},{28,508},{32... | collective-permute-start | bytes 1658888 | tf_op jit(solution)/shard_map/ppermute | solution.py:26
  81.4 2.3 %copy-start = (bf16[2,32,9,3840]{3,1,2,0:T(8,128)(2,1)S(1)}, bf16[2,32,9,3840]{3,1,2,0:T(8,128)(2,1)}, u32[]{:S(2)}) copy-start(bf16[2,32,9,3840]{3,1,2,0:T(8,128)(2,1)} %param.15) | copy-start | bytes 13271044
  91.1 11.2 %copy-start.1 = (bf16[3,3,64,128]{3,2,1,0:T(8,128)(2,1)S(1)}, bf16[3,3,64,128]{3,2,1,0:T(8,128)(2,1)}, u32[]{:S(2)}) copy-start(bf16[3,3,64,128]{3,2,1,0:T(8,128)(2,1)} %param.23) | copy-start | bytes 442372
  91.1 11.2 %copy-start.2 = (bf16[3,3,32,64]{3,2,1,0:T(8,128)(2,1)S(1)}, bf16[3,3,32,64]{3,2,1,0:T(8,128)(2,1)}, u32[]{:S(2)}) copy-start(bf16[3,3,32,64]{3,2,1,0:T(8,128)(2,1)} %param.21) | copy-start | bytes 110596
  91.1 11.2 %copy-start.3 = (s32[16,256]{1,0:T(8,128)S(1)}, s32[16,256]{1,0:T(8,128)}, u32[]{:S(2)}) copy-start(s32[16,256]{1,0:T(8,128)} %shard_ref.1) | copy-start | bytes 49156
  91.1 11.2 %copy-start.4 = (s32[16,256]{1,0:T(8,128)S(1)}, s32[16,256]{1,0:T(8,128)}, u32[]{:S(2)}) copy-start(s32[16,256]{1,0:T(8,128)} %clip_ref.1) | copy-start | bytes 49156
  91.2 11.2 %copy-start.5 = (s32[16]{0:T(128)S(1)}, s32[16]{0:T(128)}, u32[]{:S(2)}) copy-start(s32[16]{0:T(128)} %count_ref.1) | copy-start | bytes 196
  96.9 10.3 %all-to-all-start.1 = ((bf16[8,16,128]{2,1,0:T(8,128)(2,1)}), bf16[8,16,128]{2,1,0:T(8,128)(2,1)S(1)}, u32[]{:S(2)}, u32[]{:S(2)}) async-start(bf16[8,16,128]{2,1,0:T(8,128)(2,1)} %bitcast.7), calls=%async_computation.1 | async-start | bytes 65536 | tf_op jit(solution)/shard_map/all_to_all | solution.py:389
  102.4 4.9 %copy-start.6 = (f32[32]{0:T(128)S(1)}, f32[32]{0:T(128)}, u32[]{:S(2)}) copy-start(f32[32]{0:T(128)} %param.20) | copy-start | bytes 388
  102.4 4.9 %copy-start.7 = (f32[64]{0:T(128)S(1)}, f32[64]{0:T(128)}, u32[]{:S(2)}) copy-start(f32[64]{0:T(128)} %param.22) | copy-start | bytes 772
  102.4 4.9 %copy-start.8 = (f32[128]{0:T(128)S(1)}, f32[128]{0:T(128)}, u32[]{:S(2)}) copy-start(f32[128]{0:T(128)} %param.24) | copy-start | bytes 1540
  102.4 4.9 %copy-start.9 = (bf16[128]{0:T(256)(128)(2,1)S(1)}, bf16[128]{0:T(256)(128)(2,1)}, u32[]{:S(2)}) copy-start(bf16[128]{0:T(256)(128)(2,1)} %param.25) | copy-start | bytes 772
  102.4 4.9 %copy-start.10 = (bf16[256,128]{1,0:T(8,128)(2,1)S(1)}, bf16[256,128]{1,0:T(8,128)(2,1)}, u32[]{:S(2)}) copy-start(bf16[256,128]{1,0:T(8,128)(2,1)} %constant.22.clone.order_ref) | copy-start | bytes 196612

commit v7 on v5

--- a/solution.py
+++ b/solution.py
@@ -368,10 +368,12 @@
     ahead = near_shift(four, -1)
     two = near_shift(four, 2)
     behind = near_shift(four, 1)
+    kernels = (first_kernel, second_kernel, third_kernel)
+    kernels, behind = lax.optimization_barrier((kernels, behind))
+    listed, *spread = prepare(at, cand_count, cand_shard, cand_clip, *kernels)
     first = jnp.concatenate([four, behind], axis=1)
     last = jnp.concatenate([ahead, two], axis=1)
-    kernels = (first_kernel, second_kernel, third_kernel)
-    listed, *spread = prepare(at, cand_count, cand_shard, cand_clip, *kernels)
+    own, listed, first, last = lax.optimization_barrier((own, listed, first, last))
     other = lax.ppermute(own, "c", [(0, 1), (1, 0)])
     behind_first = shift(first, 1)
     ahead_first = shift(first, -1)

time: 131 us -> 129 us (0.985)
  blocking collectives: 46 us -> 51.4 us
  Pallas kernels: 17.6 us -> 13.2 us
  starting transfers between devices: 52.6 us -> 50.2 us
  local copies, waits for them, and re-layouts: 4.22 us -> 1.95 us
    ppermute x1, starting transfers between devices: 8.78 us -> 14.2 us  [on_device(): other = lax.ppermute(own, 'c', [(0, 1), (1, 0)])]
    all_to_all x1, starting transfers between devices: 11.4 us -> 6.43 us  [on_device(): parts = lax.all_to_all(table, ('c', 'x'), 0, 0, tiled=True)]
    pallas_call x4, Pallas kernels: 17.6 us -> 13.2 us  [kernel_call(): pl.pallas_call(body, in_specs=[pl.BlockSpec(memory_space=space) for space...]
    all_to_all x1, blocking collectives: 26 us -> 30 us  [gather_classes(): lax.all_to_all(jnp.broadcast_to(flat, (4,) + flat.shape), 'z', 0, 0, axis...]
    ppermute x9, starting transfers between devices: 32.4 us -> 29.6 us  [send(): return lax.ppermute(values, PLANE, pairs)]
    unnamed x24, local copies, waits for them, and re-layouts: 2.32 us -> 0.06 us
    all_to_all x1, waiting for transfers between devices: 2.86 us -> 4.27 us  [on_device(): parts = lax.all_to_all(table, ('c', 'x'), 0, 0, tiled=True)]
    all_to_all x1, blocking collectives: 20 us -> 21.4 us  [on_device(): values = lax.all_to_all(values, ('z', 'y'), 0, 0, tiled=True)]
  transfers between devices with their start and end apart: 11 -> 11, of which waited for: 4 -> 4; matrix products, arithmetic and copies ran while one was open for 1% -> 0% of each run, Pallas kernels for 7% -> 5%
where the time goes in v7:
time: 129 us
  blocking collectives  51.4 us (40%)
  starting transfers between devices  50.2 us (39%)
  Pallas kernels  13.2 us (10%)
  waiting for transfers between devices  9.41 us (7%)
  local copies, waits for them, and re-layouts  1.95 us (2%)
  other arithmetic  1.66 us (1%)
    all_to_all x1, blocking collectives, gather_classes(): lax.all_to_all(jnp.broadcast_to(flat, (4,) + flat.shape), 'z', 0, 0, axis...  30 us
    ppermute x9, starting transfers between devices, send(): return lax.ppermute(values, PLANE, pairs)  29.6 us
    all_to_all x1, blocking collectives, on_device(): values = lax.all_to_all(values, ('z', 'y'), 0, 0, tiled=True)  21.4 us
    ppermute x1, starting transfers between devices, on_device(): other = lax.ppermute(own, 'c', [(0, 1), (1, 0)])  14.2 us
    pallas_call x4, Pallas kernels, kernel_call(): pl.pallas_call(body, in_specs=[pl.BlockSpec(memory_space=space) for space...  13.2 us
    all_to_all x1, starting transfers between devices, on_device(): parts = lax.all_to_all(table, ('c', 'x'), 0, 0, tiled=True)  6.43 us
    ppermute x9, waiting for transfers between devices, send(): return lax.ppermute(values, PLANE, pairs)  5.14 us
    all_to_all x1, waiting for transfers between devices, on_device(): parts = lax.all_to_all(table, ('c', 'x'), 0, 0, tiled=True)  4.27 us
  transfers between devices with their start and end apart: 11, of which 4 were waited for; matrix products, arithmetic and copies ran while one was open for 0% of the time, Pallas kernels for 5%

profile of v7, /device:TPU:1, one launch (start us, length us, event | category | flops | bytes accessed | tf_op | source)
XLA Modules:
  0.0 128.9 jit_solution(11829447539942027473)
XLA Ops:
  0.0 1.0 reshape_squeeze.3
  1.0 30.0 %all_to_all.25 = bf16[4,9,30,128]{3,2,1,0:T(8,128)(2,1)S(1)} all-to-all(bf16[4,9,30,128]{3,2,1,0:T(8,128)(2,1)S(1)} %broadcast_in_dim.15), channel_id=1, replica_groups={{0,128,256,384},{32,160,288,416},{64,192,320,448},{96,224,352,480},{1,1..., dimensions={0} | all-to-all | bytes 552960 | tf_op jit(solution)/shard_map/all_to_all | solution.py:41
  31.0 0.0 copy-start.11
  31.0 0.0 copy-start.1
  31.0 0.0 copy-start.2
  31.1 0.0 copy-start.3
  31.1 0.0 copy-start.4
  31.1 0.0 copy-start.5
  31.1 0.1 reshape.23
  31.2 3.2 %collective-permute-start = (bf16[9,4,3840]{2,1,0:T(4,128)(2,1)S(1)}, bf16[9,4,3840]{2,1,0:T(4,128)(2,1)S(1)}, u32[]{:S(2)}, u32[]{:S(2)}) collective-permute-start(bf16[9,4,3840]{2,1,0:T(4,128)(2,1)S(1)} %bitcast.34), channel_id=1, source_target_pairs={{0,32},{4,12},{8,40},{12,20},{16,48},{20,28},{24,56},{28,4},{32,64... | collective-permute-start | bytes 829448 | tf_op jit(solution)/shard_map/ppermute | solution.py:26
  34.4 0.1 pad_add_fusion.at_ref
  34.5 3.3 %collective-permute-start.1 = (bf16[9,4,3840]{2,1,0:T(4,128)(2,1)S(1)}, bf16[9,4,3840]{2,1,0:T(4,128)(2,1)S(1)}, u32[]{:S(2)}, u32[]{:S(2)}) collective-permute-start(bf16[9,4,3840]{2,1,0:T(4,128)(2,1)S(1)} %bitcast.35), channel_id=1, source_target_pairs={{0,480},{4,28},{8,488},{12,4},{16,496},{20,12},{24,504},{28,20},{3... | collective-permute-start | bytes 829448 | tf_op jit(solution)/shard_map/ppermute | solution.py:26
  37.9 3.5 %collective-permute-start.2 = (bf16[9,4,3840]{2,1,0:T(4,128)(2,1)S(1)}, bf16[9,4,3840]{2,1,0:T(4,128)(2,1)}, u32[]{:S(2)}, u32[]{:S(2)}) collective-permute-start(bf16[9,4,3840]{2,1,0:T(4,128)(2,1)S(1)} %bitcast.36), channel_id=1, source_target_pairs={{0,64},{4,20},{8,72},{12,28},{16,80},{20,4},{24,88},{28,12},{32,96... | collective-permute-start | bytes 829448 | tf_op jit(solution)/shard_map/ppermute | solution.py:26
  41.4 0.0 collective-permute-done
  41.4 0.3 pad_maximum_fusion.refs_0_
  41.7 0.0 copy-done.11
  41.7 0.0 copy-done.1
  41.8 0.0 copy-done.2
  41.8 0.0 copy-done.3
  41.8 0.0 copy-done.4
  41.8 0.0 copy-done.5
  41.8 0.0 copy-start
  41.8 1.3 %shard_map.136 = (s32[64,8]{1,0:T(8,128)S(1)}, bf16[384,1024]{1,0:T(8,128)(2,1)S(1)}, bf16[1152,256]{1,0:T(8,128)(2,1)S(1)}, bf16[1152,256]{1,0:T(8,128)(2,1)S(1)}) custom-call(s32[4]{0:T(128)S(1)} %pad_add_fusion.at_ref, s32[16]{0:T(128)S(1)} %copy-done.5, s32[16,256]{1,0:T(8,128)S(1)} %copy-done.3, s32[16,256]{1,0:T(8,128)S(1)} %copy-done.4, ...), custom_call_target="tpu_custom_call" | custom-call | flops 1000000000 | bytes 217744 | tf_op jit(solution)/shard_map/pallas_call | solution.py:112
  43.1 0.0 collective-permute-done.1
  43.1 3.6 %collective-permute-done.2 = bf16[9,4,3840]{2,1,0:T(4,128)(2,1)} collective-permute-done((bf16[9,4,3840]{2,1,0:T(4,128)(2,1)S(1)}, bf16[9,4,3840]{2,1,0:T(4,128)(2,1)}, u32[]{:S(2)}, u32[]{:S(2)}) %collective-permute-start.2) | collective-permute-done | bytes 276512 | tf_op jit(solution)/shard_map/ppermute | solution.py:26
  46.8 1.2 pad_maximum_fusion.1.refs_1_
  48.0 0.0 copy-done
  48.0 14.2 %collective-permute-start.3 = (bf16[2,288,3840]{2,1,0:T(8,128)(2,1)S(1)}, bf16[2,288,3840]{2,1,0:T(8,128)(2,1)S(1)}, u32[]{:S(2)}, u32[]{:S(2)}) collective-permute-start(bf16[2,288,3840]{2,1,0:T(8,128)(2,1)S(1)} %bitcast.23), channel_id=1, source_target_pairs={{0,4},{4,0},{1,5},{5,1},{2,6},{6,2},{3,7},{7,3},{8,12},{12,8},{9,1... | collective-permute-start | bytes 13271048 | tf_op jit(solution)/shard_map/ppermute | solution.py:377
  62.3 3.7 %collective-permute-start.4 = (bf16[9,8,3840]{2,1,0:T(8,128)(2,1)S(1)}, bf16[9,8,3840]{2,1,0:T(8,128)(2,1)S(1)}, u32[]{:S(2)}, u32[]{:S(2)}) collective-permute-start(bf16[9,8,3840]{2,1,0:T(8,128)(2,1)S(1)} %pad_maximum_fusion.refs_0_), channel_id=1, source_target_pairs={{0,8},{4,36},{8,16},{12,44},{16,24},{20,52},{24,0},{28,60},{32,40}... | collective-permute-start | bytes 1658888 | tf_op jit(solution)/shard_map/ppermute | solution.py:26
  66.0 2.8 %collective-permute-start.6 = (bf16[9,8,3840]{2,1,0:T(8,128)(2,1)S(1)}, bf16[9,8,3840]{2,1,0:T(8,128)(2,1)S(1)}, u32[]{:S(2)}, u32[]{:S(2)}) collective-permute-start(bf16[9,8,3840]{2,1,0:T(8,128)(2,1)S(1)} %pad_maximum_fusion.1.refs_1_), channel_id=1, source_target_pairs={{0,24},{4,484},{8,0},{12,492},{16,8},{20,500},{24,16},{28,508},{32... | collective-permute-start | bytes 1658888 | tf_op jit(solution)/shard_map/ppermute | solution.py:26
  68.8 2.5 %collective-permute-start.8 = (bf16[9,8,3840]{2,1,0:T(8,128)(2,1)S(1)}, bf16[9,8,3840]{2,1,0:T(8,128)(2,1)S(1)}, u32[]{:S(2)}, u32[]{:S(2)}) collective-permute-start(bf16[9,8,3840]{2,1,0:T(8,128)(2,1)S(1)} %pad_maximum_fusion.1.refs_1_), channel_id=1, source_target_pairs={{0,8},{4,36},{8,16},{12,44},{16,24},{20,52},{24,0},{28,60},{32,40}... | collective-permute-start | bytes 1658888 | tf_op jit(solution)/shard_map/ppermute | solution.py:26
  71.3 4.0 %collective-permute-start.9 = (bf16[9,8,3840]{2,1,0:T(8,128)(2,1)S(1)}, bf16[9,8,3840]{2,1,0:T(8,128)(2,1)S(1)}, u32[]{:S(2)}, u32[]{:S(2)}) collective-permute-start(bf16[9,8,3840]{2,1,0:T(8,128)(2,1)S(1)} %pad_maximum_fusion.refs_0_), channel_id=1, source_target_pairs={{0,24},{4,484},{8,0},{12,492},{16,8},{20,500},{24,16},{28,508},{32... | collective-permute-start | bytes 1658888 | tf_op jit(solution)/shard_map/ppermute | solution.py:26
  75.3 0.0 collective-permute-done.4.refs_2_
  75.3 1.9 %collective-permute-start.5 = (bf16[9,8,3840]{2,1,0:T(8,128)(2,1)S(1)}, bf16[9,8,3840]{2,1,0:T(8,128)(2,1)S(1)}, u32[]{:S(2)}, u32[]{:S(2)}) collective-permute-start(bf16[9,8,3840]{2,1,0:T(8,128)(2,1)S(1)} %collective-permute-done.4.refs_2_), channel_id=1, source_target_pairs={{0,8},{4,36},{8,16},{12,44},{16,24},{20,52},{24,0},{28,60},{32,40}... | collective-permute-start | bytes 1658888 | tf_op jit(solution)/shard_map/ppermute | solution.py:26
  77.2 0.0 collective-permute-done.6.refs_5_
  77.2 4.6 %collective-permute-start.7 = (bf16[9,8,3840]{2,1,0:T(8,128)(2,1)S(1)}, bf16[9,8,3840]{2,1,0:T(8,128)(2,1)S(1)}, u32[]{:S(2)}, u32[]{:S(2)}) collective-permute-start(bf16[9,8,3840]{2,1,0:T(8,128)(2,1)S(1)} %collective-permute-done.6.refs_5_), channel_id=1, source_target_pairs={{0,24},{4,484},{8,0},{12,492},{16,8},{20,500},{24,16},{28,508},{32... | collective-permute-start | bytes 1658888 | tf_op jit(solution)/shard_map/ppermute | solution.py:26
  81.8 0.0 collective-permute-done.8.refs_3_
  81.8 0.6 collective-permute-done.9.refs_4_
  82.4 0.0 collective-permute-done.3.other_ref
  82.4 5.0 %shard_map.137.prev_ref = f32[128,48]{1,0:T(8,128)S(1)} custom-call(bf16[2,288,3840]{2,1,0:T(8,128)(2,1)S(1)} %bitcast.24, bf16[2,288,3840]{2,1,0:T(8,128)(2,1)S(1)} %collective-permute-done.3.other_ref, bf16[9,8,3840]{2,1,0:T(8,128)(2,1)S(1)} %pad_maximum_fusion.refs_0_, bf16[9,8,3840]{2,1,0:T(8,128)(2,1)S(1)} %pad_maximum_fusion.1.refs_1_, ...), custom_call_target="tpu_custom_call" | custom-call | flops 3822059520 | bytes 12165120 | tf_op jit(solution)/shard_map/pallas_call | solution.py:112
  87.4 0.0 copy-start.6
  87.4 0.0 copy-start.7
  87.4 0.0 copy-start.8
  87.4 0.0 copy-start.9
  87.4 0.0 copy-start.10
  87.4 0.0 collective-permute-done.5.refs_0_
  87.4 0.9 collective-permute-done.7.refs_1_
  88.3 3.9 %shard_map.138 = bf16[128,128]{1,0:T(8,128)(2,1)} custom-call(s32[4]{0:T(128)S(1)} %pad_add_fusion.at_ref, bf16[2,288,3840]{2,1,0:T(8,128)(2,1)S(1)} %bitcast.25, bf16[2,288,3840]{2,1,0:T(8,128)(2,1)S(1)} %collective-permute-done.3.other_ref, f32[128,48]{1,0:T(8,128)S(1)} %shard_map.137.prev_ref, bf16[9,8,3840]{2,1,0:T(8,128)(2,1)S(1)} %collective-permute-done.5.refs_0_, ...), custom_call_target="tpu_custom_call" | custom-call | flops 1274019840 | bytes 9977872 | tf_op jit(solution)/shard_map/pallas_call | solution.py:112
  92.3 6.4 %all-to-all-start.1 = ((bf16[8,16,128]{2,1,0:T(8,128)(2,1)}), bf16[8,16,128]{2,1,0:T(8,128)(2,1)S(1)}, u32[]{:S(2)}, u32[]{:S(2)}) async-start(bf16[8,16,128]{2,1,0:T(8,128)(2,1)} %bitcast.9), calls=%async_computation.1 | async-start | bytes 65536 | tf_op jit(solution)/shard_map/all_to_all | solution.py:390
  99.3 4.3 %all-to-all-done.1 = bf16[8,16,128]{2,1,0:T(8,128)(2,1)S(1)} async-done(((bf16[8,16,128]{2,1,0:T(8,128)(2,1)}), bf16[8,16,128]{2,1,0:T(8,128)(2,1)S(1)}, u32[]{:S(2)}, u32[]{:S(2)}) %all-to-all-start.1) | async-done | bytes 32800 | tf_op jit(solution)/shard_map/all_to_all | solution.py:390
  103.6 0.0 copy-done.6
  103.6 0.0 copy-done.7
  103.6 0.0 copy-done.8
  103.6 0.0 copy-done.9
  103.6 0.0 copy-done.10
  103.7 3.0 %shard_map.139 = f32[64,8]{1,0:T(8,128)S(1)} custom-call(f32[1]{0:T(128)S(6)} %copy.20.bias_ref, bf16[128,128]{1,0:T(8,128)(2,1)S(1)} %bitcast.26, bf16[256,128]{1,0:T(8,128)(2,1)S(1)} %copy-done.10, bf16[384,1024]{1,0:T(8,128)(2,1)S(1)} %get-tuple-element.31.t1_ref, f32[1,32]{1,0:T(1,128)S(1)} %bitcast.30, bf16[1152,256]{1,0:T(8,128)(2,1)S(1)} %get-tuple-element.32.t2_ref, ...), custom_call_target="tpu_custom_call" | custom-call | flops 2000000000 | bytes 2067588 | tf_op jit(solution)/shard_map/pallas_call | solution.py:112
  106.7 21.4 %all_to_all.26 = f32[64,1,8]{2,1,0:T(1,128)S(1)} all-to-all(f32[64,1,8]{2,1,0:T(1,128)S(1)} %bitcast.27), channel_id=1, replica_groups=mesh['z'=16,'y'=4,'c'=2,'x'=4] {'z','y'}, dimensions={0} | all-to-all | bytes 4096 | tf_op jit(solution)/shard_map/all_to_all | solution.py:394
  128.1 0.1 reduce_sum.9
  128.2 0.1 reshape.27
  128.2 0.7 copy.19
  (3 shorter events, 0.1 us)
Async XLA Ops:
  31.0 10.7 %copy-start.11 = (bf16[3,3,1,32]{3,1,2,0:T(4,128)(2,1)S(1)}, bf16[3,3,1,32]{3,1,2,0:T(4,128)(2,1)}, u32[]{:S(2)}) copy-start(bf16[3,3,1,32]{3,1,2,0:T(4,128)(2,1)} %param.19) | copy-start | bytes 1732
  31.0 10.7 %copy-start.1 = (bf16[3,3,64,128]{3,2,1,0:T(8,128)(2,1)S(1)}, bf16[3,3,64,128]{3,2,1,0:T(8,128)(2,1)}, u32[]{:S(2)}) copy-start(bf16[3,3,64,128]{3,2,1,0:T(8,128)(2,1)} %param.23) | copy-start | bytes 442372
  31.0 10.7 %copy-start.2 = (bf16[3,3,32,64]{3,2,1,0:T(8,128)(2,1)S(1)}, bf16[3,3,32,64]{3,2,1,0:T(8,128)(2,1)}, u32[]{:S(2)}) copy-start(bf16[3,3,32,64]{3,2,1,0:T(8,128)(2,1)} %param.21) | copy-start | bytes 110596
  31.1 10.7 %copy-start.3 = (s32[16,256]{1,0:T(8,128)S(1)}, s32[16,256]{1,0:T(8,128)}, u32[]{:S(2)}) copy-start(s32[16,256]{1,0:T(8,128)} %shard_ref.1) | copy-start | bytes 49156
  31.1 10.7 %copy-start.4 = (s32[16,256]{1,0:T(8,128)S(1)}, s32[16,256]{1,0:T(8,128)}, u32[]{:S(2)}) copy-start(s32[16,256]{1,0:T(8,128)} %clip_ref.1) | copy-start | bytes 49156
  31.1 10.7 %copy-start.5 = (s32[16]{0:T(128)S(1)}, s32[16]{0:T(128)}, u32[]{:S(2)}) copy-start(s32[16]{0:T(128)} %count_ref.1) | copy-start | bytes 196
  31.2 10.2 %collective-permute-start = (bf16[9,4,3840]{2,1,0:T(4,128)(2,1)S(1)}, bf16[9,4,3840]{2,1,0:T(4,128)(2,1)S(1)}, u32[]{:S(2)}, u32[]{:S(2)}) collective-permute-start(bf16[9,4,3840]{2,1,0:T(4,128)(2,1)S(1)} %bitcast.34), channel_id=1, source_target_pairs={{0,32},{4,12},{8,40},{12,20},{16,48},{20,28},{24,56},{28,4},{32,64... | collective-permute-start | bytes 829448 | tf_op jit(solution)/shard_map/ppermute | solution.py:26
  34.5 8.6 %collective-permute-start.1 = (bf16[9,4,3840]{2,1,0:T(4,128)(2,1)S(1)}, bf16[9,4,3840]{2,1,0:T(4,128)(2,1)S(1)}, u32[]{:S(2)}, u32[]{:S(2)}) collective-permute-start(bf16[9,4,3840]{2,1,0:T(4,128)(2,1)S(1)} %bitcast.35), channel_id=1, source_target_pairs={{0,480},{4,28},{8,488},{12,4},{16,496},{20,12},{24,504},{28,20},{3... | collective-permute-start | bytes 829448 | tf_op jit(solution)/shard_map/ppermute | solution.py:26
  37.9 8.9 %collective-permute-start.2 = (bf16[9,4,3840]{2,1,0:T(4,128)(2,1)S(1)}, bf16[9,4,3840]{2,1,0:T(4,128)(2,1)}, u32[]{:S(2)}, u32[]{:S(2)}) collective-permute-start(bf16[9,4,3840]{2,1,0:T(4,128)(2,1)S(1)} %bitcast.36), channel_id=1, source_target_pairs={{0,64},{4,20},{8,72},{12,28},{16,80},{20,4},{24,88},{28,12},{32,96... | collective-permute-start | bytes 829448 | tf_op jit(solution)/shard_map/ppermute | solution.py:26
  41.8 6.2 %copy-start = (bf16[2,32,9,3840]{3,1,2,0:T(8,128)(2,1)S(1)}, bf16[2,32,9,3840]{3,1,2,0:T(8,128)(2,1)}, u32[]{:S(2)}) copy-start(bf16[2,32,9,3840]{3,1,2,0:T(8,128)(2,1)} %param.15) | copy-start | bytes 13271044
  48.0 34.4 %collective-permute-start.3 = (bf16[2,288,3840]{2,1,0:T(8,128)(2,1)S(1)}, bf16[2,288,3840]{2,1,0:T(8,128)(2,1)S(1)}, u32[]{:S(2)}, u32[]{:S(2)}) collective-permute-start(bf16[2,288,3840]{2,1,0:T(8,128)(2,1)S(1)} %bitcast.23), channel_id=1, source_target_pairs={{0,4},{4,0},{1,5},{5,1},{2,6},{6,2},{3,7},{7,3},{8,12},{12,8},{9,1... | collective-permute-start | bytes 13271048 | tf_op jit(solution)/shard_map/ppermute | solution.py:377
  62.3 13.0 %collective-permute-start.4 = (bf16[9,8,3840]{2,1,0:T(8,128)(2,1)S(1)}, bf16[9,8,3840]{2,1,0:T(8,128)(2,1)S(1)}, u32[]{:S(2)}, u32[]{:S(2)}) collective-permute-start(bf16[9,8,3840]{2,1,0:T(8,128)(2,1)S(1)} %pad_maximum_fusion.refs_0_), channel_id=1, source_target_pairs={{0,8},{4,36},{8,16},{12,44},{16,24},{20,52},{24,0},{28,60},{32,40}... | collective-permute-start | bytes 1658888 | tf_op jit(solution)/shard_map/ppermute | solution.py:26
  66.0 11.2 %collective-permute-start.6 = (bf16[9,8,3840]{2,1,0:T(8,128)(2,1)S(1)}, bf16[9,8,3840]{2,1,0:T(8,128)(2,1)S(1)}, u32[]{:S(2)}, u32[]{:S(2)}) collective-permute-start(bf16[9,8,3840]{2,1,0:T(8,128)(2,1)S(1)} %pad_maximum_fusion.1.refs_1_), channel_id=1, source_target_pairs={{0,24},{4,484},{8,0},{12,492},{16,8},{20,500},{24,16},{28,508},{32... | collective-permute-start | bytes 1658888 | tf_op jit(solution)/shard_map/ppermute | solution.py:26
  68.8 13.0 %collective-permute-start.8 = (bf16[9,8,3840]{2,1,0:T(8,128)(2,1)S(1)}, bf16[9,8,3840]{2,1,0:T(8,128)(2,1)S(1)}, u32[]{:S(2)}, u32[]{:S(2)}) collective-permute-start(bf16[9,8,3840]{2,1,0:T(8,128)(2,1)S(1)} %pad_maximum_fusion.1.refs_1_), channel_id=1, source_target_pairs={{0,8},{4,36},{8,16},{12,44},{16,24},{20,52},{24,0},{28,60},{32,40}... | collective-permute-start | bytes 1658888 | tf_op jit(solution)/shard_map/ppermute | solution.py:26
  71.3 11.2 %collective-permute-start.9 = (bf16[9,8,3840]{2,1,0:T(8,128)(2,1)S(1)}, bf16[9,8,3840]{2,1,0:T(8,128)(2,1)S(1)}, u32[]{:S(2)}, u32[]{:S(2)}) collective-permute-start(bf16[9,8,3840]{2,1,0:T(8,128)(2,1)S(1)} %pad_maximum_fusion.refs_0_), channel_id=1, source_target_pairs={{0,24},{4,484},{8,0},{12,492},{16,8},{20,500},{24,16},{28,508},{32... | collective-permute-start | bytes 1658888 | tf_op jit(solution)/shard_map/ppermute | solution.py:26
  75.3 12.2 %collective-permute-start.5 = (bf16[9,8,3840]{2,1,0:T(8,128)(2,1)S(1)}, bf16[9,8,3840]{2,1,0:T(8,128)(2,1)S(1)}, u32[]{:S(2)}, u32[]{:S(2)}) collective-permute-start(bf16[9,8,3840]{2,1,0:T(8,128)(2,1)S(1)} %collective-permute-done.4.refs_2_), channel_id=1, source_target_pairs={{0,8},{4,36},{8,16},{12,44},{16,24},{20,52},{24,0},{28,60},{32,40}... | collective-permute-start | bytes 1658888 | tf_op jit(solution)/shard_map/ppermute | solution.py:26
  77.2 11.1 %collective-permute-start.7 = (bf16[9,8,3840]{2,1,0:T(8,128)(2,1)S(1)}, bf16[9,8,3840]{2,1,0:T(8,128)(2,1)S(1)}, u32[]{:S(2)}, u32[]{:S(2)}) collective-permute-start(bf16[9,8,3840]{2,1,0:T(8,128)(2,1)S(1)} %collective-permute-done.6.refs_5_), channel_id=1, source_target_pairs={{0,24},{4,484},{8,0},{12,492},{16,8},{20,500},{24,16},{28,508},{32... | collective-permute-start | bytes 1658888 | tf_op jit(solution)/shard_map/ppermute | solution.py:26
  87.4 16.2 %copy-start.6 = (f32[32]{0:T(128)S(1)}, f32[32]{0:T(128)}, u32[]{:S(2)}) copy-start(f32[32]{0:T(128)} %param.20) | copy-start | bytes 388
  87.4 16.2 %copy-start.7 = (f32[64]{0:T(128)S(1)}, f32[64]{0:T(128)}, u32[]{:S(2)}) copy-start(f32[64]{0:T(128)} %param.22) | copy-start | bytes 772
  87.4 16.2 %copy-start.8 = (f32[128]{0:T(128)S(1)}, f32[128]{0:T(128)}, u32[]{:S(2)}) copy-start(f32[128]{0:T(128)} %param.24) | copy-start | bytes 1540
  87.4 16.2 %copy-start.9 = (bf16[128]{0:T(256)(128)(2,1)S(1)}, bf16[128]{0:T(256)(128)(2,1)}, u32[]{:S(2)}) copy-start(bf16[128]{0:T(256)(128)(2,1)} %param.25) | copy-start | bytes 772
  87.4 16.2 %copy-start.10 = (bf16[256,128]{1,0:T(8,128)(2,1)S(1)}, bf16[256,128]{1,0:T(8,128)(2,1)}, u32[]{:S(2)}) copy-start(bf16[256,128]{1,0:T(8,128)(2,1)} %constant.22.clone.order_ref) | copy-start | bytes 196612
  92.3 11.4 %all-to-all-start.1 = ((bf16[8,16,128]{2,1,0:T(8,128)(2,1)}), bf16[8,16,128]{2,1,0:T(8,128)(2,1)S(1)}, u32[]{:S(2)}, u32[]{:S(2)}) async-start(bf16[8,16,128]{2,1,0:T(8,128)(2,1)} %bitcast.9), calls=%async_computation.1 | async-start | bytes 65536 | tf_op jit(solution)/shard_map/all_to_all | solution.py:390

commit v8 on v7

--- a/solution.py
+++ b/solution.py
@@ -11,6 +11,7 @@
 
 NZ, NY, NC, NX = 16, 4, 2, 4
 PLANE = ("z", "y", "c")
+CLASS_STEPS = (6, -6, 2, -2)
 
 
 def device_at(z, y, c):
@@ -37,11 +38,8 @@
 def gather_classes(block):
     regions, width = block.shape
     flat = block.reshape(regions, width // 128, 128)
-    groups = [[j + 4 * k for k in range(4)] for j in range(4)]
-    four = lax.all_to_all(
-        jnp.broadcast_to(flat, (4,) + flat.shape), "z", 0, 0, axis_index_groups=groups
-    )
-    return four.reshape(4, regions, width).transpose(1, 0, 2)
+    four = [send(flat, lambda z, y: (z + d, y), lambda z, y: (z + d, y)) for d in CLASS_STEPS]
+    return jnp.stack([v.reshape(regions, width) for v in four], axis=1)
 
 
 def best_means(regions, frames, corpus_ref, clip, rows, count):
@@ -85,8 +83,12 @@
     def back(k):
         return jnp.where(k == 2, -1, jnp.where(k == 3, 2, k))
 
-    far, near = back(col // 16), back(col // 4 % 4)
-    from_z = (z + NZ - jnp.where(c == 0, near, far)) % 4 + 4 * (col % 4)
+    far, step = back(col // 16), col // 4 % 4
+    near = jnp.where(step == 1, 2, jnp.where(step == 2, 1, jnp.where(step == 3, -1, 0)))
+    far_z = jnp.where((far == 2) & (step >= 2), -2, far)
+    kind = col % 4
+    first = jnp.where(kind < 2, 6, 2) * (1 - kind % 2 * 2)
+    from_z = (z + NZ - jnp.where(c == 0, near, far_z) - first) % NZ
     from_y = (y + NY - jnp.where(c == 0, far, near)) % NY
     return jnp.where(from_z * NY + from_y == row, 1.0, 0.0).astype(jnp.bfloat16)
 
@@ -369,10 +371,10 @@
     two = near_shift(four, 2)
     behind = near_shift(four, 1)
     kernels = (first_kernel, second_kernel, third_kernel)
-    kernels, behind = lax.optimization_barrier((kernels, behind))
+    kernels, two = lax.optimization_barrier((kernels, two))
     listed, *spread = prepare(at, cand_count, cand_shard, cand_clip, *kernels)
-    first = jnp.concatenate([four, behind], axis=1)
-    last = jnp.concatenate([ahead, two], axis=1)
+    first = jnp.concatenate([four, two], axis=1)
+    last = jnp.concatenate([behind, ahead], axis=1)
     own, listed, first, last = lax.optimization_barrier((own, listed, first, last))
     other = lax.ppermute(own, "c", [(0, 1), (1, 0)])
     behind_first = shift(first, 1)

time: 129 us -> 126 us (0.977)
  blocking collectives: 51.4 us -> 20.9 us
  starting transfers between devices: 50.2 us -> 68.3 us
  waiting for transfers between devices: 9.41 us -> 16 us
  local copies, waits for them, and re-layouts: 1.95 us -> 3.43 us
    all_to_all x1 -> x0, blocking collectives: 30 us -> none  [gather_classes(): lax.all_to_all(jnp.broadcast_to(flat, (4,) + flat.shape), 'z', 0, 0, axis...]
    ppermute x9 -> x13, starting transfers between devices: 29.6 us -> 55.7 us  [send(): return lax.ppermute(values, PLANE, pairs)]
    ppermute x1, starting transfers between devices: 14.2 us -> 6.83 us  [on_device(): other = lax.ppermute(own, 'c', [(0, 1), (1, 0)])]
    ppermute x9 -> x13, waiting for transfers between devices: 5.14 us -> 11.8 us  [send(): return lax.ppermute(values, PLANE, pairs)]
  transfers between devices with their start and end apart: 11 -> 15, of which waited for: 4 -> 6; matrix products, arithmetic and copies ran while one was open for 0% -> 1% of each run, Pallas kernels for 5% -> 5%
where the time goes in v8:
time: 126 us; the launch traced here: 125 us
  starting transfers between devices  68.3 us (54%)
  blocking collectives  20.9 us (17%)
  waiting for transfers between devices  16 us (13%)
  Pallas kernels  13.3 us (11%)
  local copies, waits for them, and re-layouts  3.43 us (3%)
  other arithmetic  2.04 us (2%)
    ppermute x13, starting transfers between devices, send(): return lax.ppermute(values, PLANE, pairs)  55.7 us
    all_to_all x1, blocking collectives, on_device(): values = lax.all_to_all(values, ('z', 'y'), 0, 0, tiled=True)  20.9 us
    pallas_call x4, Pallas kernels, kernel_call(): pl.pallas_call(body, in_specs=[pl.BlockSpec(memory_space=space) for space...  13.3 us
    ppermute x13, waiting for transfers between devices, send(): return lax.ppermute(values, PLANE, pairs)  11.8 us
    ppermute x1, starting transfers between devices, on_device(): other = lax.ppermute(own, 'c', [(0, 1), (1, 0)])  6.83 us
    all_to_all x1, starting transfers between devices, on_device(): parts = lax.all_to_all(table, ('c', 'x'), 0, 0, tiled=True)  5.76 us
    all_to_all x1, waiting for transfers between devices, on_device(): parts = lax.all_to_all(table, ('c', 'x'), 0, 0, tiled=True)  4.27 us
  transfers between devices with their start and end apart: 15, of which 6 were waited for; matrix products, arithmetic and copies ran while one was open for 1% of the time, Pallas kernels for 5%

profile of v8, /device:TPU:1, one launch (start us, length us, event | category | flops | bytes accessed | tf_op | source)
XLA Modules:
  0.0 125.0 jit_solution(14402347639050819872)
XLA Ops:
  0.0 1.0 reshape_squeeze.3
  1.0 12.4 %collective-permute-start = (bf16[9,30,128]{2,1,0:T(8,128)(2,1)S(1)}, bf16[9,30,128]{2,1,0:T(8,128)(2,1)S(1)}, u32[]{:S(2)}, u32[]{:S(2)}) collective-permute-start(bf16[9,30,128]{2,1,0:T(8,128)(2,1)S(1)} %reshape_squeeze.3), channel_id=1, source_target_pairs={{0,192},{4,196},{8,200},{12,204},{16,208},{20,212},{24,216},{28,22... | collective-permute-start | bytes 207368 | tf_op jit(solution)/shard_map/ppermute | solution.py:27
  13.4 5.0 %collective-permute-start.1 = (bf16[9,30,128]{2,1,0:T(8,128)(2,1)S(1)}, bf16[9,30,128]{2,1,0:T(8,128)(2,1)S(1)}, u32[]{:S(2)}, u32[]{:S(2)}) collective-permute-start(bf16[9,30,128]{2,1,0:T(8,128)(2,1)S(1)} %reshape_squeeze.3), channel_id=1, source_target_pairs={{0,320},{4,324},{8,328},{12,332},{16,336},{20,340},{24,344},{28,34... | collective-permute-start | bytes 207368 | tf_op jit(solution)/shard_map/ppermute | solution.py:27
  18.3 3.1 %collective-permute-start.2 = (bf16[9,30,128]{2,1,0:T(8,128)(2,1)S(1)}, bf16[9,30,128]{2,1,0:T(8,128)(2,1)S(1)}, u32[]{:S(2)}, u32[]{:S(2)}) collective-permute-start(bf16[9,30,128]{2,1,0:T(8,128)(2,1)S(1)} %reshape_squeeze.3), channel_id=1, source_target_pairs={{0,64},{4,68},{8,72},{12,76},{16,80},{20,84},{24,88},{28,92},{32,9... | collective-permute-start | bytes 207368 | tf_op jit(solution)/shard_map/ppermute | solution.py:27
  21.4 4.9 %collective-permute-start.3 = (bf16[9,30,128]{2,1,0:T(8,128)(2,1)S(1)}, bf16[9,30,128]{2,1,0:T(8,128)(2,1)S(1)}, u32[]{:S(2)}, u32[]{:S(2)}) collective-permute-start(bf16[9,30,128]{2,1,0:T(8,128)(2,1)S(1)} %reshape_squeeze.3), channel_id=1, source_target_pairs={{0,448},{4,452},{8,456},{12,460},{16,464},{20,468},{24,472},{28,47... | collective-permute-start | bytes 207368 | tf_op jit(solution)/shard_map/ppermute | solution.py:27
  26.3 0.0 collective-permute-done
  26.3 0.1 stack_reshape.16
  26.5 0.0 collective-permute-done.1
  26.5 0.1 stack_reshape.17
  26.6 0.3 collective-permute-done.2
  26.9 0.1 stack_reshape.18
  27.1 5.8 %collective-permute-done.3 = bf16[9,30,128]{2,1,0:T(8,128)(2,1)S(1)} collective-permute-done((bf16[9,30,128]{2,1,0:T(8,128)(2,1)S(1)}, bf16[9,30,128]{2,1,0:T(8,128)(2,1)S(1)}, u32[]{:S(2)}, u32[]{:S(2)}) %collective-permute-start.3) | collective-permute-done | bytes 69152 | tf_op jit(solution)/shard_map/ppermute | solution.py:27
  32.9 0.1 stack_reshape.19
  33.0 0.0 copy-start.1
  33.0 0.0 copy-start.2
  33.0 0.0 copy-start.3
  33.0 0.0 copy-start.4
  33.1 0.0 copy-start.5
  33.1 0.6 pad_maximum_fusion.1
  33.7 4.8 %collective-permute-start.4 = (bf16[9,4,3840]{2,1,0:T(4,128)(2,1)S(1)}, bf16[9,4,3840]{2,1,0:T(4,128)(2,1)S(1)}, u32[]{:S(2)}, u32[]{:S(2)}) collective-permute-start(bf16[9,4,3840]{2,1,0:T(4,128)(2,1)S(1)} %pad_maximum_fusion.1), channel_id=1, source_target_pairs={{0,64},{4,20},{8,72},{12,28},{16,80},{20,4},{24,88},{28,12},{32,96... | collective-permute-start | bytes 829448 | tf_op jit(solution)/shard_map/ppermute | solution.py:27
  38.6 2.3 %collective-permute-start.5 = (bf16[9,4,3840]{2,1,0:T(4,128)(2,1)S(1)}, bf16[9,4,3840]{2,1,0:T(4,128)(2,1)S(1)}, u32[]{:S(2)}, u32[]{:S(2)}) collective-permute-start(bf16[9,4,3840]{2,1,0:T(4,128)(2,1)S(1)} %pad_maximum_fusion.1), channel_id=1, source_target_pairs={{0,32},{4,12},{8,40},{12,20},{16,48},{20,28},{24,56},{28,4},{32,64... | collective-permute-start | bytes 829448 | tf_op jit(solution)/shard_map/ppermute | solution.py:27
  40.9 4.2 %collective-permute-start.6 = (bf16[9,4,3840]{2,1,0:T(4,128)(2,1)S(1)}, bf16[9,4,3840]{2,1,0:T(4,128)(2,1)}, u32[]{:S(2)}, u32[]{:S(2)}) collective-permute-start(bf16[9,4,3840]{2,1,0:T(4,128)(2,1)S(1)} %pad_maximum_fusion.1), channel_id=1, source_target_pairs={{0,480},{4,28},{8,488},{12,4},{16,496},{20,12},{24,504},{28,20},{3... | collective-permute-start | bytes 829448 | tf_op jit(solution)/shard_map/ppermute | solution.py:27
  45.1 0.1 pad_add_fusion.at_ref
  45.1 0.0 collective-permute-done.4
  45.2 0.0 copy-done.11
  45.2 1.1 concatenate.7.refs_0_
  46.3 0.0 copy-done.1
  46.3 0.0 copy-done.2
  46.3 0.0 copy-done.3
  46.3 0.0 copy-done.4
  46.3 0.0 copy-done.5
  46.3 0.0 copy-start
  46.3 1.3 %shard_map.136 = (s32[64,8]{1,0:T(8,128)S(1)}, bf16[384,1024]{1,0:T(8,128)(2,1)S(1)}, bf16[1152,256]{1,0:T(8,128)(2,1)S(1)}, bf16[1152,256]{1,0:T(8,128)(2,1)S(1)}) custom-call(s32[4]{0:T(128)S(1)} %pad_add_fusion.at_ref, s32[16]{0:T(128)S(1)} %copy-done.5, s32[16,256]{1,0:T(8,128)S(1)} %copy-done.3, s32[16,256]{1,0:T(8,128)S(1)} %copy-done.4, ...), custom_call_target="tpu_custom_call" | custom-call | flops 1000000000 | bytes 217744 | tf_op jit(solution)/shard_map/pallas_call | solution.py:114
  47.6 0.0 collective-permute-done.5
  47.6 0.9 collective-permute-done.6
  48.5 1.2 pad_maximum_fusion.refs_1_
  49.8 6.8 %collective-permute-start.7 = (bf16[2,288,3840]{2,1,0:T(8,128)(2,1)S(1)}, bf16[2,288,3840]{2,1,0:T(8,128)(2,1)S(1)}, u32[]{:S(2)}, u32[]{:S(2)}) collective-permute-start(bf16[2,288,3840]{2,1,0:T(8,128)(2,1)S(1)} %bitcast.20), channel_id=1, source_target_pairs={{0,4},{4,0},{1,5},{5,1},{2,6},{6,2},{3,7},{7,3},{8,12},{12,8},{9,1... | collective-permute-start | bytes 13271048 | tf_op jit(solution)/shard_map/ppermute | solution.py:379
  56.6 5.4 %collective-permute-start.10 = (bf16[9,8,3840]{2,1,0:T(8,128)(2,1)S(1)}, bf16[9,8,3840]{2,1,0:T(8,128)(2,1)S(1)}, u32[]{:S(2)}, u32[]{:S(2)}) collective-permute-start(bf16[9,8,3840]{2,1,0:T(8,128)(2,1)S(1)} %pad_maximum_fusion.refs_1_), channel_id=1, source_target_pairs={{0,24},{4,484},{8,0},{12,492},{16,8},{20,500},{24,16},{28,508},{32... | collective-permute-start | bytes 1658888 | tf_op jit(solution)/shard_map/ppermute | solution.py:27
  62.0 1.9 %collective-permute-start.8 = (bf16[9,8,3840]{2,1,0:T(8,128)(2,1)S(1)}, bf16[9,8,3840]{2,1,0:T(8,128)(2,1)S(1)}, u32[]{:S(2)}, u32[]{:S(2)}) collective-permute-start(bf16[9,8,3840]{2,1,0:T(8,128)(2,1)S(1)} %concatenate.7.refs_0_), channel_id=1, source_target_pairs={{0,8},{4,36},{8,16},{12,44},{16,24},{20,52},{24,0},{28,60},{32,40}... | collective-permute-start | bytes 1658888 | tf_op jit(solution)/shard_map/ppermute | solution.py:27
  63.9 1.9 %collective-permute-start.12 = (bf16[9,8,3840]{2,1,0:T(8,128)(2,1)S(1)}, bf16[9,8,3840]{2,1,0:T(8,128)(2,1)S(1)}, u32[]{:S(2)}, u32[]{:S(2)}) collective-permute-start(bf16[9,8,3840]{2,1,0:T(8,128)(2,1)S(1)} %pad_maximum_fusion.refs_1_), channel_id=1, source_target_pairs={{0,8},{4,36},{8,16},{12,44},{16,24},{20,52},{24,0},{28,60},{32,40}... | collective-permute-start | bytes 1658888 | tf_op jit(solution)/shard_map/ppermute | solution.py:27
  65.9 4.6 %collective-permute-start.13 = (bf16[9,8,3840]{2,1,0:T(8,128)(2,1)S(1)}, bf16[9,8,3840]{2,1,0:T(8,128)(2,1)S(1)}, u32[]{:S(2)}, u32[]{:S(2)}) collective-permute-start(bf16[9,8,3840]{2,1,0:T(8,128)(2,1)S(1)} %concatenate.7.refs_0_), channel_id=1, source_target_pairs={{0,24},{4,484},{8,0},{12,492},{16,8},{20,500},{24,16},{28,508},{32... | collective-permute-start | bytes 1658888 | tf_op jit(solution)/shard_map/ppermute | solution.py:27
  70.5 0.0 collective-permute-done.10.refs_5_
  70.5 3.4 %collective-permute-start.11 = (bf16[9,8,3840]{2,1,0:T(8,128)(2,1)S(1)}, bf16[9,8,3840]{2,1,0:T(8,128)(2,1)S(1)}, u32[]{:S(2)}, u32[]{:S(2)}) collective-permute-start(bf16[9,8,3840]{2,1,0:T(8,128)(2,1)S(1)} %collective-permute-done.10.refs_5_), channel_id=1, source_target_pairs={{0,24},{4,484},{8,0},{12,492},{16,8},{20,500},{24,16},{28,508},{32... | collective-permute-start | bytes 1658888 | tf_op jit(solution)/shard_map/ppermute | solution.py:27
  73.8 0.0 collective-permute-done.8.refs_2_
  73.8 1.9 %collective-permute-start.9 = (bf16[9,8,3840]{2,1,0:T(8,128)(2,1)S(1)}, bf16[9,8,3840]{2,1,0:T(8,128)(2,1)S(1)}, u32[]{:S(2)}, u32[]{:S(2)}) collective-permute-start(bf16[9,8,3840]{2,1,0:T(8,128)(2,1)S(1)} %collective-permute-done.8.refs_2_), channel_id=1, source_target_pairs={{0,8},{4,36},{8,16},{12,44},{16,24},{20,52},{24,0},{28,60},{32,40}... | collective-permute-start | bytes 1658888 | tf_op jit(solution)/shard_map/ppermute | solution.py:27
  75.8 3.9 %collective-permute-done.12.refs_3_ = bf16[9,8,3840]{2,1,0:T(8,128)(2,1)S(1)} collective-permute-done((bf16[9,8,3840]{2,1,0:T(8,128)(2,1)S(1)}, bf16[9,8,3840]{2,1,0:T(8,128)(2,1)S(1)}, u32[]{:S(2)}, u32[]{:S(2)}) %collective-permute-start.12) | collective-permute-done | bytes 552992 | tf_op jit(solution)/shard_map/ppermute | solution.py:27
  79.7 0.0 collective-permute-done.13.refs_4_
  79.7 0.0 collective-permute-done.7.other_ref
  79.7 5.0 %shard_map.137.prev_ref = f32[128,48]{1,0:T(8,128)S(1)} custom-call(bf16[2,288,3840]{2,1,0:T(8,128)(2,1)S(1)} %bitcast.21, bf16[2,288,3840]{2,1,0:T(8,128)(2,1)S(1)} %collective-permute-done.7.other_ref, bf16[9,8,3840]{2,1,0:T(8,128)(2,1)S(1)} %concatenate.7.refs_0_, bf16[9,8,3840]{2,1,0:T(8,128)(2,1)S(1)} %pad_maximum_fusion.refs_1_, ...), custom_call_target="tpu_custom_call" | custom-call | flops 3822059520 | bytes 12165120 | tf_op jit(solution)/shard_map/pallas_call | solution.py:114
  84.6 0.0 copy-start.8
  84.7 0.0 copy-start.9
  84.7 0.0 copy-start.10
  84.7 0.0 collective-permute-done.11.refs_1_
  84.7 0.9 collective-permute-done.9.refs_0_
  85.6 3.9 %shard_map.138 = bf16[128,128]{1,0:T(8,128)(2,1)} custom-call(s32[4]{0:T(128)S(1)} %pad_add_fusion.at_ref, bf16[2,288,3840]{2,1,0:T(8,128)(2,1)S(1)} %bitcast.22, bf16[2,288,3840]{2,1,0:T(8,128)(2,1)S(1)} %collective-permute-done.7.other_ref, f32[128,48]{1,0:T(8,128)S(1)} %shard_map.137.prev_ref, bf16[9,8,3840]{2,1,0:T(8,128)(2,1)S(1)} %collective-permute-done.9.refs_0_, ...), custom_call_target="tpu_custom_call" | custom-call | flops 1274019840 | bytes 9977872 | tf_op jit(solution)/shard_map/pallas_call | solution.py:114
  89.5 5.8 %all-to-all-start = ((bf16[8,16,128]{2,1,0:T(8,128)(2,1)}), bf16[8,16,128]{2,1,0:T(8,128)(2,1)S(1)}, u32[]{:S(2)}, u32[]{:S(2)}) async-start(bf16[8,16,128]{2,1,0:T(8,128)(2,1)} %bitcast.8), calls=%async_computation | async-start | bytes 65536 | tf_op jit(solution)/shard_map/all_to_all | solution.py:392
  96.0 4.3 %all-to-all-done = bf16[8,16,128]{2,1,0:T(8,128)(2,1)S(1)} async-done(((bf16[8,16,128]{2,1,0:T(8,128)(2,1)}), bf16[8,16,128]{2,1,0:T(8,128)(2,1)S(1)}, u32[]{:S(2)}, u32[]{:S(2)}) %all-to-all-start) | async-done | bytes 32800 | tf_op jit(solution)/shard_map/all_to_all | solution.py:392
  100.2 0.0 copy-done.6
  100.2 0.0 copy-done.8
  100.3 3.0 %shard_map.139 = f32[64,8]{1,0:T(8,128)S(1)} custom-call(f32[1]{0:T(128)S(6)} %copy.35.bias_ref, bf16[128,128]{1,0:T(8,128)(2,1)S(1)} %bitcast.23, bf16[256,128]{1,0:T(8,128)(2,1)S(1)} %copy-done.10, bf16[384,1024]{1,0:T(8,128)(2,1)S(1)} %get-tuple-element.31.t1_ref, f32[1,32]{1,0:T(1,128)S(1)} %bitcast.27, bf16[1152,256]{1,0:T(8,128)(2,1)S(1)} %get-tuple-element.32.t2_ref, ...), custom_call_target="tpu_custom_call" | custom-call | flops 2000000000 | bytes 2067588 | tf_op jit(solution)/shard_map/pallas_call | solution.py:114
  103.3 20.9 %all_to_all.20 = f32[64,1,8]{2,1,0:T(1,128)S(1)} all-to-all(f32[64,1,8]{2,1,0:T(1,128)S(1)} %bitcast.24), channel_id=1, replica_groups=mesh['z'=16,'y'=4,'c'=2,'x'=4] {'z','y'}, dimensions={0} | all-to-all | bytes 4096 | tf_op jit(solution)/shard_map/all_to_all | solution.py:396
  124.2 0.1 reduce_sum.9
  124.3 0.1 reshape.23
  124.3 0.7 copy.34
  (8 shorter events, 0.0 us)
Async XLA Ops:
  0.0 45.2 %copy-start.11 = (bf16[3,3,1,32]{3,1,2,0:T(4,128)(2,1)S(1)}, bf16[3,3,1,32]{3,1,2,0:T(4,128)(2,1)}, u32[]{:S(2)}) copy-start(bf16[3,3,1,32]{3,1,2,0:T(4,128)(2,1)} %param.19) | copy-start | bytes 1732
  1.0 25.3 %collective-permute-start = (bf16[9,30,128]{2,1,0:T(8,128)(2,1)S(1)}, bf16[9,30,128]{2,1,0:T(8,128)(2,1)S(1)}, u32[]{:S(2)}, u32[]{:S(2)}) collective-permute-start(bf16[9,30,128]{2,1,0:T(8,128)(2,1)S(1)} %reshape_squeeze.3), channel_id=1, source_target_pairs={{0,192},{4,196},{8,200},{12,204},{16,208},{20,212},{24,216},{28,22... | collective-permute-start | bytes 207368 | tf_op jit(solution)/shard_map/ppermute | solution.py:27
  13.4 13.1 %collective-permute-start.1 = (bf16[9,30,128]{2,1,0:T(8,128)(2,1)S(1)}, bf16[9,30,128]{2,1,0:T(8,128)(2,1)S(1)}, u32[]{:S(2)}, u32[]{:S(2)}) collective-permute-start(bf16[9,30,128]{2,1,0:T(8,128)(2,1)S(1)} %reshape_squeeze.3), channel_id=1, source_target_pairs={{0,320},{4,324},{8,328},{12,332},{16,336},{20,340},{24,344},{28,34... | collective-permute-start | bytes 207368 | tf_op jit(solution)/shard_map/ppermute | solution.py:27
  18.3 8.6 %collective-permute-start.2 = (bf16[9,30,128]{2,1,0:T(8,128)(2,1)S(1)}, bf16[9,30,128]{2,1,0:T(8,128)(2,1)S(1)}, u32[]{:S(2)}, u32[]{:S(2)}) collective-permute-start(bf16[9,30,128]{2,1,0:T(8,128)(2,1)S(1)} %reshape_squeeze.3), channel_id=1, source_target_pairs={{0,64},{4,68},{8,72},{12,76},{16,80},{20,84},{24,88},{28,92},{32,9... | collective-permute-start | bytes 207368 | tf_op jit(solution)/shard_map/ppermute | solution.py:27
  21.4 11.5 %collective-permute-start.3 = (bf16[9,30,128]{2,1,0:T(8,128)(2,1)S(1)}, bf16[9,30,128]{2,1,0:T(8,128)(2,1)S(1)}, u32[]{:S(2)}, u32[]{:S(2)}) collective-permute-start(bf16[9,30,128]{2,1,0:T(8,128)(2,1)S(1)} %reshape_squeeze.3), channel_id=1, source_target_pairs={{0,448},{4,452},{8,456},{12,460},{16,464},{20,468},{24,472},{28,47... | collective-permute-start | bytes 207368 | tf_op jit(solution)/shard_map/ppermute | solution.py:27
  33.0 13.3 %copy-start.1 = (bf16[3,3,64,128]{3,2,1,0:T(8,128)(2,1)S(1)}, bf16[3,3,64,128]{3,2,1,0:T(8,128)(2,1)}, u32[]{:S(2)}) copy-start(bf16[3,3,64,128]{3,2,1,0:T(8,128)(2,1)} %param.23) | copy-start | bytes 442372
  33.0 13.3 %copy-start.2 = (bf16[3,3,32,64]{3,2,1,0:T(8,128)(2,1)S(1)}, bf16[3,3,32,64]{3,2,1,0:T(8,128)(2,1)}, u32[]{:S(2)}) copy-start(bf16[3,3,32,64]{3,2,1,0:T(8,128)(2,1)} %param.21) | copy-start | bytes 110596
  33.0 13.3 %copy-start.3 = (s32[16,256]{1,0:T(8,128)S(1)}, s32[16,256]{1,0:T(8,128)}, u32[]{:S(2)}) copy-start(s32[16,256]{1,0:T(8,128)} %shard_ref.1) | copy-start | bytes 49156
  33.0 13.2 %copy-start.4 = (s32[16,256]{1,0:T(8,128)S(1)}, s32[16,256]{1,0:T(8,128)}, u32[]{:S(2)}) copy-start(s32[16,256]{1,0:T(8,128)} %clip_ref.1) | copy-start | bytes 49156
  33.1 13.2 %copy-start.5 = (s32[16]{0:T(128)S(1)}, s32[16]{0:T(128)}, u32[]{:S(2)}) copy-start(s32[16]{0:T(128)} %count_ref.1) | copy-start | bytes 196
  33.7 11.4 %collective-permute-start.4 = (bf16[9,4,3840]{2,1,0:T(4,128)(2,1)S(1)}, bf16[9,4,3840]{2,1,0:T(4,128)(2,1)S(1)}, u32[]{:S(2)}, u32[]{:S(2)}) collective-permute-start(bf16[9,4,3840]{2,1,0:T(4,128)(2,1)S(1)} %pad_maximum_fusion.1), channel_id=1, source_target_pairs={{0,64},{4,20},{8,72},{12,28},{16,80},{20,4},{24,88},{28,12},{32,96... | collective-permute-start | bytes 829448 | tf_op jit(solution)/shard_map/ppermute | solution.py:27
  38.6 9.1 %collective-permute-start.5 = (bf16[9,4,3840]{2,1,0:T(4,128)(2,1)S(1)}, bf16[9,4,3840]{2,1,0:T(4,128)(2,1)S(1)}, u32[]{:S(2)}, u32[]{:S(2)}) collective-permute-start(bf16[9,4,3840]{2,1,0:T(4,128)(2,1)S(1)} %pad_maximum_fusion.1), channel_id=1, source_target_pairs={{0,32},{4,12},{8,40},{12,20},{16,48},{20,28},{24,56},{28,4},{32,64... | collective-permute-start | bytes 829448 | tf_op jit(solution)/shard_map/ppermute | solution.py:27
  40.9 7.6 %collective-permute-start.6 = (bf16[9,4,3840]{2,1,0:T(4,128)(2,1)S(1)}, bf16[9,4,3840]{2,1,0:T(4,128)(2,1)}, u32[]{:S(2)}, u32[]{:S(2)}) collective-permute-start(bf16[9,4,3840]{2,1,0:T(4,128)(2,1)S(1)} %pad_maximum_fusion.1), channel_id=1, source_target_pairs={{0,480},{4,28},{8,488},{12,4},{16,496},{20,12},{24,504},{28,20},{3... | collective-permute-start | bytes 829448 | tf_op jit(solution)/shard_map/ppermute | solution.py:27
  46.3 3.4 %copy-start = (bf16[2,32,9,3840]{3,1,2,0:T(8,128)(2,1)S(1)}, bf16[2,32,9,3840]{3,1,2,0:T(8,128)(2,1)}, u32[]{:S(2)}) copy-start(bf16[2,32,9,3840]{3,1,2,0:T(8,128)(2,1)} %param.15) | copy-start | bytes 13271044
  49.8 29.9 %collective-permute-start.7 = (bf16[2,288,3840]{2,1,0:T(8,128)(2,1)S(1)}, bf16[2,288,3840]{2,1,0:T(8,128)(2,1)S(1)}, u32[]{:S(2)}, u32[]{:S(2)}) collective-permute-start(bf16[2,288,3840]{2,1,0:T(8,128)(2,1)S(1)} %bitcast.20), channel_id=1, source_target_pairs={{0,4},{4,0},{1,5},{5,1},{2,6},{6,2},{3,7},{7,3},{8,12},{12,8},{9,1... | collective-permute-start | bytes 13271048 | tf_op jit(solution)/shard_map/ppermute | solution.py:379
  56.6 13.9 %collective-permute-start.10 = (bf16[9,8,3840]{2,1,0:T(8,128)(2,1)S(1)}, bf16[9,8,3840]{2,1,0:T(8,128)(2,1)S(1)}, u32[]{:S(2)}, u32[]{:S(2)}) collective-permute-start(bf16[9,8,3840]{2,1,0:T(8,128)(2,1)S(1)} %pad_maximum_fusion.refs_1_), channel_id=1, source_target_pairs={{0,24},{4,484},{8,0},{12,492},{16,8},{20,500},{24,16},{28,508},{32... | collective-permute-start | bytes 1658888 | tf_op jit(solution)/shard_map/ppermute | solution.py:27
  62.0 11.8 %collective-permute-start.8 = (bf16[9,8,3840]{2,1,0:T(8,128)(2,1)S(1)}, bf16[9,8,3840]{2,1,0:T(8,128)(2,1)S(1)}, u32[]{:S(2)}, u32[]{:S(2)}) collective-permute-start(bf16[9,8,3840]{2,1,0:T(8,128)(2,1)S(1)} %concatenate.7.refs_0_), channel_id=1, source_target_pairs={{0,8},{4,36},{8,16},{12,44},{16,24},{20,52},{24,0},{28,60},{32,40}... | collective-permute-start | bytes 1658888 | tf_op jit(solution)/shard_map/ppermute | solution.py:27
  63.9 15.7 %collective-permute-start.12 = (bf16[9,8,3840]{2,1,0:T(8,128)(2,1)S(1)}, bf16[9,8,3840]{2,1,0:T(8,128)(2,1)S(1)}, u32[]{:S(2)}, u32[]{:S(2)}) collective-permute-start(bf16[9,8,3840]{2,1,0:T(8,128)(2,1)S(1)} %pad_maximum_fusion.refs_1_), channel_id=1, source_target_pairs={{0,8},{4,36},{8,16},{12,44},{16,24},{20,52},{24,0},{28,60},{32,40}... | collective-permute-start | bytes 1658888 | tf_op jit(solution)/shard_map/ppermute | solution.py:27
  65.9 13.8 %collective-permute-start.13 = (bf16[9,8,3840]{2,1,0:T(8,128)(2,1)S(1)}, bf16[9,8,3840]{2,1,0:T(8,128)(2,1)S(1)}, u32[]{:S(2)}, u32[]{:S(2)}) collective-permute-start(bf16[9,8,3840]{2,1,0:T(8,128)(2,1)S(1)} %concatenate.7.refs_0_), channel_id=1, source_target_pairs={{0,24},{4,484},{8,0},{12,492},{16,8},{20,500},{24,16},{28,508},{32... | collective-permute-start | bytes 1658888 | tf_op jit(solution)/shard_map/ppermute | solution.py:27
  70.5 14.2 %collective-permute-start.11 = (bf16[9,8,3840]{2,1,0:T(8,128)(2,1)S(1)}, bf16[9,8,3840]{2,1,0:T(8,128)(2,1)S(1)}, u32[]{:S(2)}, u32[]{:S(2)}) collective-permute-start(bf16[9,8,3840]{2,1,0:T(8,128)(2,1)S(1)} %collective-permute-done.10.refs_5_), channel_id=1, source_target_pairs={{0,24},{4,484},{8,0},{12,492},{16,8},{20,500},{24,16},{28,508},{32... | collective-permute-start | bytes 1658888 | tf_op jit(solution)/shard_map/ppermute | solution.py:27
  73.8 11.8 %collective-permute-start.9 = (bf16[9,8,3840]{2,1,0:T(8,128)(2,1)S(1)}, bf16[9,8,3840]{2,1,0:T(8,128)(2,1)S(1)}, u32[]{:S(2)}, u32[]{:S(2)}) collective-permute-start(bf16[9,8,3840]{2,1,0:T(8,128)(2,1)S(1)} %collective-permute-done.8.refs_2_), channel_id=1, source_target_pairs={{0,8},{4,36},{8,16},{12,44},{16,24},{20,52},{24,0},{28,60},{32,40}... | collective-permute-start | bytes 1658888 | tf_op jit(solution)/shard_map/ppermute | solution.py:27
  84.6 15.6 %copy-start.6 = (f32[32]{0:T(128)S(1)}, f32[32]{0:T(128)}, u32[]{:S(2)}) copy-start(f32[32]{0:T(128)} %param.20) | copy-start | bytes 388
  84.6 15.6 %copy-start.7 = (f32[64]{0:T(128)S(1)}, f32[64]{0:T(128)}, u32[]{:S(2)}) copy-start(f32[64]{0:T(128)} %param.22) | copy-start | bytes 772
  84.6 15.6 %copy-start.8 = (f32[128]{0:T(128)S(1)}, f32[128]{0:T(128)}, u32[]{:S(2)}) copy-start(f32[128]{0:T(128)} %param.24) | copy-start | bytes 1540
  84.7 15.6 %copy-start.9 = (bf16[128]{0:T(256)(128)(2,1)S(1)}, bf16[128]{0:T(256)(128)(2,1)}, u32[]{:S(2)}) copy-start(bf16[128]{0:T(256)(128)(2,1)} %param.25) | copy-start | bytes 772
  84.7 15.6 %copy-start.10 = (bf16[256,128]{1,0:T(8,128)(2,1)S(1)}, bf16[256,128]{1,0:T(8,128)(2,1)}, u32[]{:S(2)}) copy-start(bf16[256,128]{1,0:T(8,128)(2,1)} %constant.22.clone.order_ref) | copy-start | bytes 196612
  89.5 10.7 %all-to-all-start = ((bf16[8,16,128]{2,1,0:T(8,128)(2,1)}), bf16[8,16,128]{2,1,0:T(8,128)(2,1)S(1)}, u32[]{:S(2)}, u32[]{:S(2)}) async-start(bf16[8,16,128]{2,1,0:T(8,128)(2,1)} %bitcast.8), calls=%async_computation | async-start | bytes 65536 | tf_op jit(solution)/shard_map/all_to_all | solution.py:392

commit v9 on v8

--- a/solution.py
+++ b/solution.py
@@ -11,7 +11,7 @@
 
 NZ, NY, NC, NX = 16, 4, 2, 4
 PLANE = ("z", "y", "c")
-CLASS_STEPS = (6, -6, 2, -2)
+CLASS_STEPS = (6, 2)
 
 
 def device_at(z, y, c):
@@ -38,8 +38,10 @@
 def gather_classes(block):
     regions, width = block.shape
     flat = block.reshape(regions, width // 128, 128)
-    four = [send(flat, lambda z, y: (z + d, y), lambda z, y: (z + d, y)) for d in CLASS_STEPS]
-    return jnp.stack([v.reshape(regions, width) for v in four], axis=1)
+    other = lax.ppermute(flat, "c", [(0, 1), (1, 0)])
+    both = jnp.stack([flat, other])
+    four = [send(both, lambda z, y: (z + d, y), lambda z, y: (z - d, y)) for d in CLASS_STEPS]
+    return jnp.concatenate(four, axis=0).reshape(4, regions, width).transpose(1, 0, 2)
 
 
 def best_means(regions, frames, corpus_ref, clip, rows, count):
@@ -76,21 +78,18 @@
 
 
 def column_places(z, y, c):
-    shape = (NZ * NY, NZ * NY)
+    shape = (2 * NZ * NY, NZ * NY)
     col = lax.broadcasted_iota(jnp.int32, shape, 1)
     row = lax.broadcasted_iota(jnp.int32, shape, 0)
-
-    def back(k):
-        return jnp.where(k == 2, -1, jnp.where(k == 3, 2, k))
-
-    far, step = back(col // 16), col // 4 % 4
+    far, step = col // 16, col // 4 % 4
+    far = jnp.where(far == 2, -1, jnp.where(far == 3, 2, far))
     near = jnp.where(step == 1, 2, jnp.where(step == 2, 1, jnp.where(step == 3, -1, 0)))
-    far_z = jnp.where((far == 2) & (step >= 2), -2, far)
-    kind = col % 4
-    first = jnp.where(kind < 2, 6, 2) * (1 - kind % 2 * 2)
-    from_z = (z + NZ - jnp.where(c == 0, near, far_z) - first) % NZ
-    from_y = (y + NY - jnp.where(c == 0, far, near)) % NY
-    return jnp.where(from_z * NY + from_y == row, 1.0, 0.0).astype(jnp.bfloat16)
+    first = jnp.where(col % 4 < 2, 6, 2)
+    from_z = jnp.where(c == 0, z - near - first, z - far + first)
+    from_y = jnp.where(c == 0, y - far, y - near)
+    parity = (c + col % 2) % 2
+    place = ((from_z + NZ) % NZ * NY + (from_y + NY) % NY) * 2 + parity
+    return jnp.where(place == row, 1.0, 0.0).astype(jnp.bfloat16)
 
 
 def table_body(regions, frames, at_ref, own_ref, other_ref, prev_ref, *refs):
@@ -144,7 +143,7 @@
     total = count * len(pieces)
     return kernel_call(
         functools.partial(table_body, regions, frames),
-        [((NC * NZ * NY, 2 * clips * frames), jnp.bfloat16)],
+        [((2 * NC * NZ * NY, 2 * clips * frames), jnp.bfloat16)],
         [at, own, other, prev, *pieces],
         [pltpu.VMEM((2 * clips * frames, total), jnp.float32)],
         4 * clips * rows * regions * total * width,
@@ -154,13 +153,13 @@
 
 def row_order():
     group = 4
-    order = np.zeros((4, 2, group, 8, NC, NX, group, NY), np.float32)
+    order = np.zeros((4, 2, group, 8, NX, group, NY, 2), np.float32)
     for k in range(4):
         for f in range(16):
             frame = 2 * f - 1 + k
             if 0 <= frame < 32:
                 for q in range(group):
-                    order[k, f % 2, q, f // 2, frame % 2, frame // 8, q, frame % 8 // 2] = 1
+                    order[k, f % 2, q, f // 2, frame // 8, q, frame % 8 // 2, frame % 2] = 1
     return order.reshape(4 * 64, 128)
 
 
@@ -185,7 +184,7 @@
         names_q = jnp.sum(jnp.where(line == query, names, 0), axis=0, keepdims=True)
         names_q = jnp.where(slot < count_ref[query], names_q, -1).astype(f32)
         spread = jnp.where(of_slot // 4 == to_chip, names_q, 0.0).astype(bf16)
-        pick = jnp.where((pick_to // 2 == q) & (pick_slot == core * 2 + pick_to % 2), 1.0, 0.0)
+        pick = jnp.where((pick_to % group == q) & (pick_slot == core * 2 + pick_to // group), 1.0, 0.0)
         listed = listed + dot(spread, pick.astype(bf16))
     listed_ref[...] = listed.astype(jnp.int32)
 
@@ -279,9 +278,11 @@
     even_row = lax.broadcasted_iota(jnp.int32, (128, 256), 0) % 2
     weight = jnp.where(lane == even_row, weight, 0.0).astype(jnp.bfloat16)
     bf16 = jnp.bfloat16
-    maps = dot(order_ref[...], parts_ref[...])
-    x = [maps[k * 64 : (k + 1) * 64] for k in range(4)]
-    x = [(pltpu.roll(v, 64, 1) if k % 2 == 0 else v).astype(bf16) for k, v in enumerate(x)]
+    parts = parts_ref[...].astype(jnp.float32)
+    half = parts.shape[0] // 2
+    parts = (parts[:half] + pltpu.roll(parts[half:], 64, 1)).astype(bf16)
+    maps = dot(order_ref[...], parts)
+    x = [maps[k * 64 : (k + 1) * 64].astype(bf16) for k in range(4)]
     both = jnp.concatenate(
         [jnp.concatenate(x[0:3], axis=1), jnp.concatenate(x[1:4], axis=1)], axis=0
     )
@@ -318,7 +319,7 @@
     score = jnp.max(score, axis=1, keepdims=True) + jnp.broadcast_to(bias_ref[0], (1, 128))
     score = score.reshape(16, 8, score.shape[1]).sum(axis=1) * 0.125
     listed = listed_ref[...]
-    slot_query = lax.broadcasted_iota(jnp.int32, (1, listed.shape[1]), 1) // 2
+    slot_query = lax.broadcasted_iota(jnp.int32, (1, listed.shape[1]), 1) % 4
     total = jnp.zeros(listed.shape, jnp.float32)
     for k in range(4):
         line = jnp.zeros((1, listed.shape[1]), jnp.float32)
@@ -382,7 +383,7 @@
     two_first = shift(behind_first, 1)
     behind_last = shift(last, 1)
     ahead_last = shift(last, -1)
-    two_last = shift(ahead_last, -1)
+    two_last = shift(behind_last, 1)
 
     near = [first, last, behind_first, behind_last, ahead_first, ahead_last]
     prev = frame_sims(own, other, near)
@@ -394,7 +395,7 @@
         parts, listed, spread, first_bias, second_bias, third_bias, score_weight, score_bias
     )
     values = lax.all_to_all(values, ("z", "y"), 0, 0, tiled=True)
-    return values.sum(axis=0).reshape(group, -1)
+    return values.sum(axis=0).reshape(-1, group).T
 
 
 def solution(mesh):

time: 126 us -> 125 us (level)
  starting transfers between devices: 68.3 us -> 60.6 us
  waiting for transfers between devices: 16 us -> 23 us
    ppermute x13 -> x11, starting transfers between devices: 55.7 us -> 41.4 us  [send(): return lax.ppermute(values, PLANE, pairs)]
    ppermute x0 -> x1, starting transfers between devices: none -> 8.79 us  [gather_classes(): other = lax.ppermute(flat, 'c', [(0, 1), (1, 0)])]
    ppermute x13 -> x11, waiting for transfers between devices: 11.8 us -> 18.7 us  [send(): return lax.ppermute(values, PLANE, pairs)]
    ppermute x1, starting transfers between devices: 6.83 us -> 4.41 us  [on_device(): other = lax.ppermute(own, 'c', [(0, 1), (1, 0)])]
  transfers between devices with their start and end apart: 15 -> 14, of which waited for: 6 -> 8; matrix products, arithmetic and copies ran while one was open for 1% -> 1% of each run, Pallas kernels for 5% -> 5%
where the time goes in v9:
time: 125 us; the launch traced here: 124 us
  starting transfers between devices  60.6 us (48%)
  waiting for transfers between devices  23 us (18%)
  blocking collectives  21.8 us (17%)
  Pallas kernels  13.3 us (11%)
  local copies, waits for them, and re-layouts  2.79 us (2%)
  other arithmetic  1.72 us (1%)
    ppermute x11, starting transfers between devices, send(): return lax.ppermute(values, PLANE, pairs)  41.4 us
    all_to_all x1, blocking collectives, on_device(): values = lax.all_to_all(values, ('z', 'y'), 0, 0, tiled=True)  21.8 us
    ppermute x11, waiting for transfers between devices, send(): return lax.ppermute(values, PLANE, pairs)  18.7 us
    pallas_call x4, Pallas kernels, kernel_call(): pl.pallas_call(body, in_specs=[pl.BlockSpec(memory_space=space) for space...  13.3 us
    ppermute x1, starting transfers between devices, gather_classes(): other = lax.ppermute(flat, 'c', [(0, 1), (1, 0)])  8.79 us
    all_to_all x1, starting transfers between devices, on_device(): parts = lax.all_to_all(table, ('c', 'x'), 0, 0, tiled=True)  5.99 us
    ppermute x1, starting transfers between devices, on_device(): other = lax.ppermute(own, 'c', [(0, 1), (1, 0)])  4.41 us
    all_to_all x1, waiting for transfers between devices, on_device(): parts = lax.all_to_all(table, ('c', 'x'), 0, 0, tiled=True)  4.32 us
  transfers between devices with their start and end apart: 14, of which 8 were waited for; matrix products, arithmetic and copies ran while one was open for 1% of the time, Pallas kernels for 5%

profile of v9, /device:TPU:1, one launch (start us, length us, event | category | flops | bytes accessed | tf_op | source)
XLA Modules:
  0.0 124.2 jit_solution(13146991153800591783)
XLA Ops:
  0.0 1.0 reshape_squeeze.3
  1.0 8.8 %collective-permute-start = (bf16[9,30,128]{2,1,0:T(8,128)(2,1)S(1)}, bf16[9,30,128]{2,1,0:T(8,128)(2,1)S(1)}, u32[]{:S(2)}, u32[]{:S(2)}) collective-permute-start(bf16[9,30,128]{2,1,0:T(8,128)(2,1)S(1)} %reshape_squeeze.3), channel_id=1, source_target_pairs={{0,4},{4,0},{1,5},{5,1},{2,6},{6,2},{3,7},{7,3},{8,12},{12,8},{9,1... | collective-permute-start | bytes 207368 | tf_op jit(solution)/shard_map/ppermute | solution.py:41
  9.8 1.0 stack_reshape_squeeze.3
  10.8 0.0 collective-permute-done
  10.8 0.0 copy-start.11
  10.8 0.0 copy-start.1
  10.8 0.0 copy-start.2
  10.8 0.0 copy-start.3
  10.8 0.0 copy-start.4
  10.8 0.0 copy-start.5
  10.9 9.3 %collective-permute-start.1 = (bf16[2,9,30,128]{3,2,0,1:T(8,128)(2,1)S(1)}, bf16[2,9,30,128]{3,2,0,1:T(8,128)(2,1)S(1)}, u32[]{:S(2)}, u32[]{:S(2)}) collective-permute-start(bf16[2,9,30,128]{3,2,0,1:T(8,128)(2,1)S(1)} %pad_maximum_fusion.3), channel_id=1, source_target_pairs={{0,192},{4,324},{8,200},{12,332},{16,208},{20,340},{24,216},{28,34... | collective-permute-start | bytes 414728 | tf_op jit(solution)/shard_map/ppermute | solution.py:27
  20.2 3.1 %collective-permute-start.2 = (bf16[2,9,30,128]{3,2,0,1:T(8,128)(2,1)S(1)}, bf16[2,9,30,128]{3,2,0,1:T(8,128)(2,1)S(1)}, u32[]{:S(2)}, u32[]{:S(2)}) collective-permute-start(bf16[2,9,30,128]{3,2,0,1:T(8,128)(2,1)S(1)} %pad_maximum_fusion.3), channel_id=1, source_target_pairs={{0,64},{4,452},{8,72},{12,460},{16,80},{20,468},{24,88},{28,476},{... | collective-permute-start | bytes 414728 | tf_op jit(solution)/shard_map/ppermute | solution.py:27
  23.3 6.1 %collective-permute-done.1 = bf16[2,9,30,128]{3,2,0,1:T(8,128)(2,1)S(1)} collective-permute-done((bf16[2,9,30,128]{3,2,0,1:T(8,128)(2,1)S(1)}, bf16[2,9,30,128]{3,2,0,1:T(8,128)(2,1)S(1)}, u32[]{:S(2)}, u32[]{:S(2)}) %collective-permute-start.1) | collective-permute-done | bytes 138272 | tf_op jit(solution)/shard_map/ppermute | solution.py:27
  29.4 4.0 %collective-permute-done.2 = bf16[2,9,30,128]{3,2,0,1:T(8,128)(2,1)S(1)} collective-permute-done((bf16[2,9,30,128]{3,2,0,1:T(8,128)(2,1)S(1)}, bf16[2,9,30,128]{3,2,0,1:T(8,128)(2,1)S(1)}, u32[]{:S(2)}, u32[]{:S(2)}) %collective-permute-start.2) | collective-permute-done | bytes 138272 | tf_op jit(solution)/shard_map/ppermute | solution.py:27
  33.4 0.1 reshape.23
  33.5 4.7 %collective-permute-start.3 = (bf16[9,4,3840]{2,1,0:T(4,128)(2,1)S(1)}, bf16[9,4,3840]{2,1,0:T(4,128)(2,1)S(1)}, u32[]{:S(2)}, u32[]{:S(2)}) collective-permute-start(bf16[9,4,3840]{2,1,0:T(4,128)(2,1)S(1)} %bitcast.37), channel_id=1, source_target_pairs={{0,64},{4,20},{8,72},{12,28},{16,80},{20,4},{24,88},{28,12},{32,96... | collective-permute-start | bytes 829448 | tf_op jit(solution)/shard_map/ppermute | solution.py:27
  38.2 0.1 pad_add_fusion.at_ref
  38.3 2.3 %collective-permute-start.4 = (bf16[9,4,3840]{2,1,0:T(4,128)(2,1)S(1)}, bf16[9,4,3840]{2,1,0:T(4,128)(2,1)S(1)}, u32[]{:S(2)}, u32[]{:S(2)}) collective-permute-start(bf16[9,4,3840]{2,1,0:T(4,128)(2,1)S(1)} %bitcast.38), channel_id=1, source_target_pairs={{0,32},{4,12},{8,40},{12,20},{16,48},{20,28},{24,56},{28,4},{32,64... | collective-permute-start | bytes 829448 | tf_op jit(solution)/shard_map/ppermute | solution.py:27
  40.6 4.2 %collective-permute-start.5 = (bf16[9,4,3840]{2,1,0:T(4,128)(2,1)S(1)}, bf16[9,4,3840]{2,1,0:T(4,128)(2,1)}, u32[]{:S(2)}, u32[]{:S(2)}) collective-permute-start(bf16[9,4,3840]{2,1,0:T(4,128)(2,1)S(1)} %bitcast.39), channel_id=1, source_target_pairs={{0,480},{4,28},{8,488},{12,4},{16,496},{20,12},{24,504},{28,20},{3... | collective-permute-start | bytes 829448 | tf_op jit(solution)/shard_map/ppermute | solution.py:27
  44.8 0.0 collective-permute-done.3
  44.8 0.3 pad_maximum_fusion.refs_0_
  45.1 0.0 copy-done.11
  45.1 0.0 copy-done.1
  45.1 0.0 copy-done.2
  45.2 0.0 copy-done.3
  45.2 0.0 copy-done.4
  45.2 0.0 copy-done.5
  45.2 0.0 copy-start
  45.2 1.3 %shard_map.136 = (s32[64,8]{1,0:T(8,128)S(1)}, bf16[384,1024]{1,0:T(8,128)(2,1)S(1)}, bf16[1152,256]{1,0:T(8,128)(2,1)S(1)}, bf16[1152,256]{1,0:T(8,128)(2,1)S(1)}) custom-call(s32[4]{0:T(128)S(1)} %pad_add_fusion.at_ref, s32[16]{0:T(128)S(1)} %copy-done.5, s32[16,256]{1,0:T(8,128)S(1)} %copy-done.3, s32[16,256]{1,0:T(8,128)S(1)} %copy-done.4, ...), custom_call_target="tpu_custom_call" | custom-call | flops 1000000000 | bytes 217744 | tf_op jit(solution)/shard_map/pallas_call | solution.py:113
  46.5 0.3 collective-permute-done.4
  46.8 1.5 %collective-permute-done.5 = bf16[9,4,3840]{2,1,0:T(4,128)(2,1)} collective-permute-done((bf16[9,4,3840]{2,1,0:T(4,128)(2,1)S(1)}, bf16[9,4,3840]{2,1,0:T(4,128)(2,1)}, u32[]{:S(2)}, u32[]{:S(2)}) %collective-permute-start.5) | collective-permute-done | bytes 276512 | tf_op jit(solution)/shard_map/ppermute | solution.py:27
  48.3 1.2 pad_maximum_fusion.1.refs_1_
  49.5 0.0 copy-done
  49.5 4.4 %collective-permute-start.6 = (bf16[2,288,3840]{2,1,0:T(8,128)(2,1)S(1)}, bf16[2,288,3840]{2,1,0:T(8,128)(2,1)S(1)}, u32[]{:S(2)}, u32[]{:S(2)}) collective-permute-start(bf16[2,288,3840]{2,1,0:T(8,128)(2,1)S(1)} %bitcast.26), channel_id=1, source_target_pairs={{0,4},{4,0},{1,5},{5,1},{2,6},{6,2},{3,7},{7,3},{8,12},{12,8},{9,1... | collective-permute-start | bytes 13271048 | tf_op jit(solution)/shard_map/ppermute | solution.py:380
  54.0 3.6 %collective-permute-start.9 = (bf16[9,8,3840]{2,1,0:T(8,128)(2,1)S(1)}, bf16[9,8,3840]{2,1,0:T(8,128)(2,1)S(1)}, u32[]{:S(2)}, u32[]{:S(2)}) collective-permute-start(bf16[9,8,3840]{2,1,0:T(8,128)(2,1)S(1)} %pad_maximum_fusion.1.refs_1_), channel_id=1, source_target_pairs={{0,8},{4,36},{8,16},{12,44},{16,24},{20,52},{24,0},{28,60},{32,40}... | collective-permute-start | bytes 1658888 | tf_op jit(solution)/shard_map/ppermute | solution.py:27
  57.6 3.1 %collective-permute-start.7 = (bf16[9,8,3840]{2,1,0:T(8,128)(2,1)S(1)}, bf16[9,8,3840]{2,1,0:T(8,128)(2,1)S(1)}, u32[]{:S(2)}, u32[]{:S(2)}) collective-permute-start(bf16[9,8,3840]{2,1,0:T(8,128)(2,1)S(1)} %pad_maximum_fusion.refs_0_), channel_id=1, source_target_pairs={{0,8},{4,36},{8,16},{12,44},{16,24},{20,52},{24,0},{28,60},{32,40}... | collective-permute-start | bytes 1658888 | tf_op jit(solution)/shard_map/ppermute | solution.py:27
  60.7 3.4 %collective-permute-start.11 = (bf16[9,8,3840]{2,1,0:T(8,128)(2,1)S(1)}, bf16[9,8,3840]{2,1,0:T(8,128)(2,1)S(1)}, u32[]{:S(2)}, u32[]{:S(2)}) collective-permute-start(bf16[9,8,3840]{2,1,0:T(8,128)(2,1)S(1)} %pad_maximum_fusion.refs_0_), channel_id=1, source_target_pairs={{0,24},{4,484},{8,0},{12,492},{16,8},{20,500},{24,16},{28,508},{32... | collective-permute-start | bytes 1658888 | tf_op jit(solution)/shard_map/ppermute | solution.py:27
  64.1 1.9 %collective-permute-start.12 = (bf16[9,8,3840]{2,1,0:T(8,128)(2,1)S(1)}, bf16[9,8,3840]{2,1,0:T(8,128)(2,1)S(1)}, u32[]{:S(2)}, u32[]{:S(2)}) collective-permute-start(bf16[9,8,3840]{2,1,0:T(8,128)(2,1)S(1)} %pad_maximum_fusion.1.refs_1_), channel_id=1, source_target_pairs={{0,24},{4,484},{8,0},{12,492},{16,8},{20,500},{24,16},{28,508},{32... | collective-permute-start | bytes 1658888 | tf_op jit(solution)/shard_map/ppermute | solution.py:27
  66.0 0.0 collective-permute-done.9.refs_3_
  66.1 3.4 %collective-permute-start.10 = (bf16[9,8,3840]{2,1,0:T(8,128)(2,1)S(1)}, bf16[9,8,3840]{2,1,0:T(8,128)(2,1)S(1)}, u32[]{:S(2)}, u32[]{:S(2)}) collective-permute-start(bf16[9,8,3840]{2,1,0:T(8,128)(2,1)S(1)} %collective-permute-done.9.refs_3_), channel_id=1, source_target_pairs={{0,8},{4,36},{8,16},{12,44},{16,24},{20,52},{24,0},{28,60},{32,40}... | collective-permute-start | bytes 1658888 | tf_op jit(solution)/shard_map/ppermute | solution.py:27
  69.4 2.2 %collective-permute-done.7.refs_2_ = bf16[9,8,3840]{2,1,0:T(8,128)(2,1)S(1)} collective-permute-done((bf16[9,8,3840]{2,1,0:T(8,128)(2,1)S(1)}, bf16[9,8,3840]{2,1,0:T(8,128)(2,1)S(1)}, u32[]{:S(2)}, u32[]{:S(2)}) %collective-permute-start.7) | collective-permute-done | bytes 552992 | tf_op jit(solution)/shard_map/ppermute | solution.py:27
  71.6 2.4 %collective-permute-start.8 = (bf16[9,8,3840]{2,1,0:T(8,128)(2,1)S(1)}, bf16[9,8,3840]{2,1,0:T(8,128)(2,1)S(1)}, u32[]{:S(2)}, u32[]{:S(2)}) collective-permute-start(bf16[9,8,3840]{2,1,0:T(8,128)(2,1)S(1)} %collective-permute-done.7.refs_2_), channel_id=1, source_target_pairs={{0,8},{4,36},{8,16},{12,44},{16,24},{20,52},{24,0},{28,60},{32,40}... | collective-permute-start | bytes 1658888 | tf_op jit(solution)/shard_map/ppermute | solution.py:27
  74.0 0.0 collective-permute-done.11.refs_4_
  74.1 3.1 %collective-permute-done.12.refs_5_ = bf16[9,8,3840]{2,1,0:T(8,128)(2,1)S(1)} collective-permute-done((bf16[9,8,3840]{2,1,0:T(8,128)(2,1)S(1)}, bf16[9,8,3840]{2,1,0:T(8,128)(2,1)S(1)}, u32[]{:S(2)}, u32[]{:S(2)}) %collective-permute-start.12) | collective-permute-done | bytes 552992 | tf_op jit(solution)/shard_map/ppermute | solution.py:27
  77.2 0.0 collective-permute-done.6.other_ref
  77.2 5.0 %shard_map.137.prev_ref = f32[128,48]{1,0:T(8,128)S(1)} custom-call(bf16[2,288,3840]{2,1,0:T(8,128)(2,1)S(1)} %bitcast.27, bf16[2,288,3840]{2,1,0:T(8,128)(2,1)S(1)} %collective-permute-done.6.other_ref, bf16[9,8,3840]{2,1,0:T(8,128)(2,1)S(1)} %pad_maximum_fusion.refs_0_, bf16[9,8,3840]{2,1,0:T(8,128)(2,1)S(1)} %pad_maximum_fusion.1.refs_1_, ...), custom_call_target="tpu_custom_call" | custom-call | flops 3822059520 | bytes 12165120 | tf_op jit(solution)/shard_map/pallas_call | solution.py:113
  82.2 0.0 copy-start.6
  82.2 0.0 copy-start.8
  82.2 0.0 copy-start.9
  82.2 0.0 copy-start.10
  82.2 0.0 collective-permute-done.10.refs_1_
  82.2 1.5 %collective-permute-done.8.refs_0_ = bf16[9,8,3840]{2,1,0:T(8,128)(2,1)S(1)} collective-permute-done((bf16[9,8,3840]{2,1,0:T(8,128)(2,1)S(1)}, bf16[9,8,3840]{2,1,0:T(8,128)(2,1)S(1)}, u32[]{:S(2)}, u32[]{:S(2)}) %collective-permute-start.8) | collective-permute-done | bytes 552992 | tf_op jit(solution)/shard_map/ppermute | solution.py:27
  83.7 4.0 %shard_map.138 = bf16[256,128]{1,0:T(8,128)(2,1)} custom-call(s32[4]{0:T(128)S(1)} %pad_add_fusion.at_ref, bf16[2,288,3840]{2,1,0:T(8,128)(2,1)S(1)} %bitcast.28, bf16[2,288,3840]{2,1,0:T(8,128)(2,1)S(1)} %collective-permute-done.6.other_ref, f32[128,48]{1,0:T(8,128)S(1)} %shard_map.137.prev_ref, bf16[9,8,3840]{2,1,0:T(8,128)(2,1)S(1)} %collective-permute-done.8.refs_0_, ...), custom_call_target="tpu_custom_call" | custom-call | flops 1274019840 | bytes 9977872 | tf_op jit(solution)/shard_map/pallas_call | solution.py:113
  87.7 6.0 %all-to-all-start = ((bf16[8,32,128]{2,1,0:T(8,128)(2,1)}), bf16[8,32,128]{2,1,0:T(8,128)(2,1)S(1)}, u32[]{:S(2)}, u32[]{:S(2)}) async-start(bf16[8,32,128]{2,1,0:T(8,128)(2,1)} %bitcast.11), calls=%async_computation | async-start | bytes 131072 | tf_op jit(solution)/shard_map/all_to_all | solution.py:393
  94.3 4.3 %all-to-all-done = bf16[8,32,128]{2,1,0:T(8,128)(2,1)S(1)} async-done(((bf16[8,32,128]{2,1,0:T(8,128)(2,1)}), bf16[8,32,128]{2,1,0:T(8,128)(2,1)S(1)}, u32[]{:S(2)}, u32[]{:S(2)}) %all-to-all-start) | async-done | bytes 65568 | tf_op jit(solution)/shard_map/all_to_all | solution.py:393
  98.6 0.0 copy-done.6
  98.6 0.0 copy-done.7
  98.6 0.0 copy-done.8
  98.6 0.0 copy-done.9
  98.6 0.0 copy-done.10
  98.7 3.0 %shard_map.139 = f32[64,8]{1,0:T(8,128)S(1)} custom-call(f32[1]{0:T(128)S(6)} %copy.19.bias_ref, bf16[256,128]{1,0:T(8,128)(2,1)S(1)} %bitcast.29, bf16[256,128]{1,0:T(8,128)(2,1)S(1)} %copy-done.10, bf16[384,1024]{1,0:T(8,128)(2,1)S(1)} %get-tuple-element.31.t1_ref, f32[1,32]{1,0:T(1,128)S(1)} %bitcast.33, bf16[1152,256]{1,0:T(8,128)(2,1)S(1)} %get-tuple-element.32.t2_ref, ...), custom_call_target="tpu_custom_call" | custom-call | flops 2000000000 | bytes 2100356 | tf_op jit(solution)/shard_map/pallas_call | solution.py:113
  101.7 21.8 %all_to_all.20 = f32[64,1,8]{2,1,0:T(1,128)S(1)} all-to-all(f32[64,1,8]{2,1,0:T(1,128)S(1)} %bitcast.30), channel_id=1, replica_groups=mesh['z'=16,'y'=4,'c'=2,'x'=4] {'z','y'}, dimensions={0} | all-to-all | bytes 4096 | tf_op jit(solution)/shard_map/all_to_all | solution.py:397
  123.5 0.1 reduce_sum.9
  123.6 0.6 reshape.27
  (4 shorter events, 0.1 us)
Async XLA Ops:
  1.0 9.8 %collective-permute-start = (bf16[9,30,128]{2,1,0:T(8,128)(2,1)S(1)}, bf16[9,30,128]{2,1,0:T(8,128)(2,1)S(1)}, u32[]{:S(2)}, u32[]{:S(2)}) collective-permute-start(bf16[9,30,128]{2,1,0:T(8,128)(2,1)S(1)} %reshape_squeeze.3), channel_id=1, source_target_pairs={{0,4},{4,0},{1,5},{5,1},{2,6},{6,2},{3,7},{7,3},{8,12},{12,8},{9,1... | collective-permute-start | bytes 207368 | tf_op jit(solution)/shard_map/ppermute | solution.py:41
  10.8 34.3 %copy-start.11 = (bf16[3,3,1,32]{3,1,2,0:T(4,128)(2,1)S(1)}, bf16[3,3,1,32]{3,1,2,0:T(4,128)(2,1)}, u32[]{:S(2)}) copy-start(bf16[3,3,1,32]{3,1,2,0:T(4,128)(2,1)} %param.19) | copy-start | bytes 1732
  10.8 34.3 %copy-start.1 = (bf16[3,3,64,128]{3,2,1,0:T(8,128)(2,1)S(1)}, bf16[3,3,64,128]{3,2,1,0:T(8,128)(2,1)}, u32[]{:S(2)}) copy-start(bf16[3,3,64,128]{3,2,1,0:T(8,128)(2,1)} %param.23) | copy-start | bytes 442372
  10.8 34.3 %copy-start.2 = (bf16[3,3,32,64]{3,2,1,0:T(8,128)(2,1)S(1)}, bf16[3,3,32,64]{3,2,1,0:T(8,128)(2,1)}, u32[]{:S(2)}) copy-start(bf16[3,3,32,64]{3,2,1,0:T(8,128)(2,1)} %param.21) | copy-start | bytes 110596
  10.8 34.3 %copy-start.3 = (s32[16,256]{1,0:T(8,128)S(1)}, s32[16,256]{1,0:T(8,128)}, u32[]{:S(2)}) copy-start(s32[16,256]{1,0:T(8,128)} %shard_ref.1) | copy-start | bytes 49156
  10.8 34.3 %copy-start.4 = (s32[16,256]{1,0:T(8,128)S(1)}, s32[16,256]{1,0:T(8,128)}, u32[]{:S(2)}) copy-start(s32[16,256]{1,0:T(8,128)} %clip_ref.1) | copy-start | bytes 49156
  10.8 34.3 %copy-start.5 = (s32[16]{0:T(128)S(1)}, s32[16]{0:T(128)}, u32[]{:S(2)}) copy-start(s32[16]{0:T(128)} %count_ref.1) | copy-start | bytes 196
  10.9 18.5 %collective-permute-start.1 = (bf16[2,9,30,128]{3,2,0,1:T(8,128)(2,1)S(1)}, bf16[2,9,30,128]{3,2,0,1:T(8,128)(2,1)S(1)}, u32[]{:S(2)}, u32[]{:S(2)}) collective-permute-start(bf16[2,9,30,128]{3,2,0,1:T(8,128)(2,1)S(1)} %pad_maximum_fusion.3), channel_id=1, source_target_pairs={{0,192},{4,324},{8,200},{12,332},{16,208},{20,340},{24,216},{28,34... | collective-permute-start | bytes 414728 | tf_op jit(solution)/shard_map/ppermute | solution.py:27
  20.2 13.2 %collective-permute-start.2 = (bf16[2,9,30,128]{3,2,0,1:T(8,128)(2,1)S(1)}, bf16[2,9,30,128]{3,2,0,1:T(8,128)(2,1)S(1)}, u32[]{:S(2)}, u32[]{:S(2)}) collective-permute-start(bf16[2,9,30,128]{3,2,0,1:T(8,128)(2,1)S(1)} %pad_maximum_fusion.3), channel_id=1, source_target_pairs={{0,64},{4,452},{8,72},{12,460},{16,80},{20,468},{24,88},{28,476},{... | collective-permute-start | bytes 414728 | tf_op jit(solution)/shard_map/ppermute | solution.py:27
  33.5 11.3 %collective-permute-start.3 = (bf16[9,4,3840]{2,1,0:T(4,128)(2,1)S(1)}, bf16[9,4,3840]{2,1,0:T(4,128)(2,1)S(1)}, u32[]{:S(2)}, u32[]{:S(2)}) collective-permute-start(bf16[9,4,3840]{2,1,0:T(4,128)(2,1)S(1)} %bitcast.37), channel_id=1, source_target_pairs={{0,64},{4,20},{8,72},{12,28},{16,80},{20,4},{24,88},{28,12},{32,96... | collective-permute-start | bytes 829448 | tf_op jit(solution)/shard_map/ppermute | solution.py:27
  38.3 8.5 %collective-permute-start.4 = (bf16[9,4,3840]{2,1,0:T(4,128)(2,1)S(1)}, bf16[9,4,3840]{2,1,0:T(4,128)(2,1)S(1)}, u32[]{:S(2)}, u32[]{:S(2)}) collective-permute-start(bf16[9,4,3840]{2,1,0:T(4,128)(2,1)S(1)} %bitcast.38), channel_id=1, source_target_pairs={{0,32},{4,12},{8,40},{12,20},{16,48},{20,28},{24,56},{28,4},{32,64... | collective-permute-start | bytes 829448 | tf_op jit(solution)/shard_map/ppermute | solution.py:27
  40.6 7.7 %collective-permute-start.5 = (bf16[9,4,3840]{2,1,0:T(4,128)(2,1)S(1)}, bf16[9,4,3840]{2,1,0:T(4,128)(2,1)}, u32[]{:S(2)}, u32[]{:S(2)}) collective-permute-start(bf16[9,4,3840]{2,1,0:T(4,128)(2,1)S(1)} %bitcast.39), channel_id=1, source_target_pairs={{0,480},{4,28},{8,488},{12,4},{16,496},{20,12},{24,504},{28,20},{3... | collective-permute-start | bytes 829448 | tf_op jit(solution)/shard_map/ppermute | solution.py:27
  45.2 4.3 %copy-start = (bf16[2,32,9,3840]{3,1,2,0:T(8,128)(2,1)S(1)}, bf16[2,32,9,3840]{3,1,2,0:T(8,128)(2,1)}, u32[]{:S(2)}) copy-start(bf16[2,32,9,3840]{3,1,2,0:T(8,128)(2,1)} %param.15) | copy-start | bytes 13271044
  49.5 27.6 %collective-permute-start.6 = (bf16[2,288,3840]{2,1,0:T(8,128)(2,1)S(1)}, bf16[2,288,3840]{2,1,0:T(8,128)(2,1)S(1)}, u32[]{:S(2)}, u32[]{:S(2)}) collective-permute-start(bf16[2,288,3840]{2,1,0:T(8,128)(2,1)S(1)} %bitcast.26), channel_id=1, source_target_pairs={{0,4},{4,0},{1,5},{5,1},{2,6},{6,2},{3,7},{7,3},{8,12},{12,8},{9,1... | collective-permute-start | bytes 13271048 | tf_op jit(solution)/shard_map/ppermute | solution.py:380
  54.0 12.1 %collective-permute-start.9 = (bf16[9,8,3840]{2,1,0:T(8,128)(2,1)S(1)}, bf16[9,8,3840]{2,1,0:T(8,128)(2,1)S(1)}, u32[]{:S(2)}, u32[]{:S(2)}) collective-permute-start(bf16[9,8,3840]{2,1,0:T(8,128)(2,1)S(1)} %pad_maximum_fusion.1.refs_1_), channel_id=1, source_target_pairs={{0,8},{4,36},{8,16},{12,44},{16,24},{20,52},{24,0},{28,60},{32,40}... | collective-permute-start | bytes 1658888 | tf_op jit(solution)/shard_map/ppermute | solution.py:27
  57.6 14.0 %collective-permute-start.7 = (bf16[9,8,3840]{2,1,0:T(8,128)(2,1)S(1)}, bf16[9,8,3840]{2,1,0:T(8,128)(2,1)S(1)}, u32[]{:S(2)}, u32[]{:S(2)}) collective-permute-start(bf16[9,8,3840]{2,1,0:T(8,128)(2,1)S(1)} %pad_maximum_fusion.refs_0_), channel_id=1, source_target_pairs={{0,8},{4,36},{8,16},{12,44},{16,24},{20,52},{24,0},{28,60},{32,40}... | collective-permute-start | bytes 1658888 | tf_op jit(solution)/shard_map/ppermute | solution.py:27
  60.7 13.3 %collective-permute-start.11 = (bf16[9,8,3840]{2,1,0:T(8,128)(2,1)S(1)}, bf16[9,8,3840]{2,1,0:T(8,128)(2,1)S(1)}, u32[]{:S(2)}, u32[]{:S(2)}) collective-permute-start(bf16[9,8,3840]{2,1,0:T(8,128)(2,1)S(1)} %pad_maximum_fusion.refs_0_), channel_id=1, source_target_pairs={{0,24},{4,484},{8,0},{12,492},{16,8},{20,500},{24,16},{28,508},{32... | collective-permute-start | bytes 1658888 | tf_op jit(solution)/shard_map/ppermute | solution.py:27
  64.1 13.1 %collective-permute-start.12 = (bf16[9,8,3840]{2,1,0:T(8,128)(2,1)S(1)}, bf16[9,8,3840]{2,1,0:T(8,128)(2,1)S(1)}, u32[]{:S(2)}, u32[]{:S(2)}) collective-permute-start(bf16[9,8,3840]{2,1,0:T(8,128)(2,1)S(1)} %pad_maximum_fusion.1.refs_1_), channel_id=1, source_target_pairs={{0,24},{4,484},{8,0},{12,492},{16,8},{20,500},{24,16},{28,508},{32... | collective-permute-start | bytes 1658888 | tf_op jit(solution)/shard_map/ppermute | solution.py:27
  66.1 16.1 %collective-permute-start.10 = (bf16[9,8,3840]{2,1,0:T(8,128)(2,1)S(1)}, bf16[9,8,3840]{2,1,0:T(8,128)(2,1)S(1)}, u32[]{:S(2)}, u32[]{:S(2)}) collective-permute-start(bf16[9,8,3840]{2,1,0:T(8,128)(2,1)S(1)} %collective-permute-done.9.refs_3_), channel_id=1, source_target_pairs={{0,8},{4,36},{8,16},{12,44},{16,24},{20,52},{24,0},{28,60},{32,40}... | collective-permute-start | bytes 1658888 | tf_op jit(solution)/shard_map/ppermute | solution.py:27
  71.6 12.1 %collective-permute-start.8 = (bf16[9,8,3840]{2,1,0:T(8,128)(2,1)S(1)}, bf16[9,8,3840]{2,1,0:T(8,128)(2,1)S(1)}, u32[]{:S(2)}, u32[]{:S(2)}) collective-permute-start(bf16[9,8,3840]{2,1,0:T(8,128)(2,1)S(1)} %collective-permute-done.7.refs_2_), channel_id=1, source_target_pairs={{0,8},{4,36},{8,16},{12,44},{16,24},{20,52},{24,0},{28,60},{32,40}... | collective-permute-start | bytes 1658888 | tf_op jit(solution)/shard_map/ppermute | solution.py:27
  82.2 16.5 %copy-start.6 = (f32[32]{0:T(128)S(1)}, f32[32]{0:T(128)}, u32[]{:S(2)}) copy-start(f32[32]{0:T(128)} %param.20) | copy-start | bytes 388
  82.2 16.5 %copy-start.7 = (f32[64]{0:T(128)S(1)}, f32[64]{0:T(128)}, u32[]{:S(2)}) copy-start(f32[64]{0:T(128)} %param.22) | copy-start | bytes 772
  82.2 16.5 %copy-start.8 = (f32[128]{0:T(128)S(1)}, f32[128]{0:T(128)}, u32[]{:S(2)}) copy-start(f32[128]{0:T(128)} %param.24) | copy-start | bytes 1540
  82.2 16.5 %copy-start.9 = (bf16[128]{0:T(256)(128)(2,1)S(1)}, bf16[128]{0:T(256)(128)(2,1)}, u32[]{:S(2)}) copy-start(bf16[128]{0:T(256)(128)(2,1)} %param.25) | copy-start | bytes 772
  82.2 16.5 %copy-start.10 = (bf16[256,128]{1,0:T(8,128)(2,1)S(1)}, bf16[256,128]{1,0:T(8,128)(2,1)}, u32[]{:S(2)}) copy-start(bf16[256,128]{1,0:T(8,128)(2,1)} %constant.22.clone.order_ref) | copy-start | bytes 196612
  87.7 11.0 %all-to-all-start = ((bf16[8,32,128]{2,1,0:T(8,128)(2,1)}), bf16[8,32,128]{2,1,0:T(8,128)(2,1)S(1)}, u32[]{:S(2)}, u32[]{:S(2)}) async-start(bf16[8,32,128]{2,1,0:T(8,128)(2,1)} %bitcast.11), calls=%async_computation | async-start | bytes 131072 | tf_op jit(solution)/shard_map/all_to_all | solution.py:393

commit v10 on v9

--- a/solution.py
+++ b/solution.py
@@ -36,12 +36,10 @@
 
 
 def gather_classes(block):
-    regions, width = block.shape
-    flat = block.reshape(regions, width // 128, 128)
-    other = lax.ppermute(flat, "c", [(0, 1), (1, 0)])
-    both = jnp.stack([flat, other])
+    other = lax.ppermute(block, "c", [(0, 1), (1, 0)])
+    both = jnp.stack([block, other], axis=1)
     four = [send(both, lambda z, y: (z + d, y), lambda z, y: (z - d, y)) for d in CLASS_STEPS]
-    return jnp.concatenate(four, axis=0).reshape(4, regions, width).transpose(1, 0, 2)
+    return jnp.concatenate(four, axis=1)
 
 
 def best_means(regions, frames, corpus_ref, clip, rows, count):
@@ -92,9 +90,9 @@
     return jnp.where(place == row, 1.0, 0.0).astype(jnp.bfloat16)
 
 
-def table_body(regions, frames, at_ref, own_ref, other_ref, prev_ref, *refs):
+def table_body(regions, frames, own_ref, other_ref, prev_ref, place_ref, *refs):
     out_ref, last_ref = refs[-2:]
-    place = column_places(at_ref[0], at_ref[1], at_ref[2])
+    place = place_ref[...]
     sims_body(regions, frames, own_ref, other_ref, *refs[:-2], last_ref)
     prev = prev_ref[...].astype(jnp.bfloat16)
     last = last_ref[...].astype(jnp.bfloat16)
@@ -136,7 +134,7 @@
     return kernel_call(body, outs, [own, other, *pieces], [], flops)[0]
 
 
-def frame_table(at, own, other, prev, pieces):
+def frame_table(own, other, prev, place, pieces):
     clips, rows, width = own.shape
     regions, count = pieces[0].shape[:2]
     frames = rows // regions
@@ -144,10 +142,9 @@
     return kernel_call(
         functools.partial(table_body, regions, frames),
         [((2 * NC * NZ * NY, 2 * clips * frames), jnp.bfloat16)],
-        [at, own, other, prev, *pieces],
+        [own, other, prev, place, *pieces],
         [pltpu.VMEM((2 * clips * frames, total), jnp.float32)],
         4 * clips * rows * regions * total * width,
-        scalars=1,
     )[0]
 
 
@@ -164,7 +161,7 @@
 
 
 def prepare_body(
-    at_ref, count_ref, shard_ref, clip_ref, first_ref, second_ref, third_ref, listed_ref, t1_ref, t2_ref, t3_ref
+    at_ref, count_ref, shard_ref, clip_ref, first_ref, second_ref, third_ref, listed_ref, place_ref, t1_ref, t2_ref, t3_ref
 ):
     f32, bf16 = jnp.float32, jnp.bfloat16
     group, slots = 4, shard_ref.shape[1]
@@ -187,6 +184,7 @@
         pick = jnp.where((pick_to % group == q) & (pick_slot == core * 2 + pick_to // group), 1.0, 0.0)
         listed = listed + dot(spread, pick.astype(bf16))
     listed_ref[...] = listed.astype(jnp.int32)
+    place_ref[...] = column_places(at_ref[0], at_ref[1], core)
 
     lanes = t1_ref.shape[1]
     row = lax.broadcasted_iota(jnp.int32, (128, lanes), 0) % 32
@@ -236,6 +234,7 @@
     ]
     outs = [
         ((cand_shard.shape[1] // 4, 8), jnp.int32),
+        ((2 * NZ * NY, NZ * NY), jnp.bfloat16),
         ((384, 1024), jnp.bfloat16),
         ((1152, 256), jnp.bfloat16),
         ((1152, 256), jnp.bfloat16),
@@ -373,7 +372,7 @@
     behind = near_shift(four, 1)
     kernels = (first_kernel, second_kernel, third_kernel)
     kernels, two = lax.optimization_barrier((kernels, two))
-    listed, *spread = prepare(at, cand_count, cand_shard, cand_clip, *kernels)
+    listed, place, *spread = prepare(at, cand_count, cand_shard, cand_clip, *kernels)
     first = jnp.concatenate([four, two], axis=1)
     last = jnp.concatenate([behind, ahead], axis=1)
     own, listed, first, last = lax.optimization_barrier((own, listed, first, last))
@@ -388,7 +387,7 @@
     near = [first, last, behind_first, behind_last, ahead_first, ahead_last]
     prev = frame_sims(own, other, near)
     two, prev = lax.optimization_barrier(((two_first, two_last), prev))
-    table = frame_table(at, own, other, prev, two)
+    table = frame_table(own, other, prev, place, two)
 
     parts = lax.all_to_all(table, ("c", "x"), 0, 0, tiled=True)
     values = slot_scores(

time: 125 us -> 124 us (level)
  transfers between devices with their start and end apart: 14 -> 14, of which waited for: 8 -> 9; matrix products, arithmetic and copies ran while one was open for 1% -> 1% of each run, Pallas kernels for 5% -> 5%
where the time goes in v10:
time: 124 us; the launch traced here: 123 us
  starting transfers between devices  60.6 us (49%)
  waiting for transfers between devices  22.2 us (18%)
  blocking collectives  22.1 us (18%)
  Pallas kernels  12.8 us (10%)
  other arithmetic  2.45 us (2%)
  local copies, waits for them, and re-layouts  1.85 us (1%)
    ppermute x11, starting transfers between devices, send(): return lax.ppermute(values, PLANE, pairs)  41.3 us
    all_to_all x1, blocking collectives, on_device(): values = lax.all_to_all(values, ('z', 'y'), 0, 0, tiled=True)  22.1 us
    ppermute x11, waiting for transfers between devices, send(): return lax.ppermute(values, PLANE, pairs)  17.7 us
    pallas_call x4, Pallas kernels, kernel_call(): pl.pallas_call(body, in_specs=[pl.BlockSpec(memory_space=space) for space...  12.8 us
    ppermute x1, starting transfers between devices, gather_classes(): other = lax.ppermute(block, 'c', [(0, 1), (1, 0)])  8.77 us
    all_to_all x1, starting transfers between devices, on_device(): parts = lax.all_to_all(table, ('c', 'x'), 0, 0, tiled=True)  6.01 us
    ppermute x1, starting transfers between devices, on_device(): other = lax.ppermute(own, 'c', [(0, 1), (1, 0)])  4.57 us
    all_to_all x1, waiting for transfers between devices, on_device(): parts = lax.all_to_all(table, ('c', 'x'), 0, 0, tiled=True)  4.32 us
  transfers between devices with their start and end apart: 14, of which 9 were waited for; matrix products, arithmetic and copies ran while one was open for 1% of the time, Pallas kernels for 5%

profile of v10, /device:TPU:1, one launch (start us, length us, event | category | flops | bytes accessed | tf_op | source)
XLA Modules:
  0.0 122.9 jit_solution(16294154181702577736)
XLA Ops:
  0.0 8.8 %collective-permute-start = (bf16[9,3840]{1,0:T(8,128)(2,1)}, bf16[9,3840]{1,0:T(8,128)(2,1)S(1)}, u32[]{:S(2)}, u32[]{:S(2)}) collective-permute-start(bf16[9,3840]{1,0:T(8,128)(2,1)} %bitcast.35), channel_id=1, source_target_pairs={{0,4},{4,0},{1,5},{5,1},{2,6},{6,2},{3,7},{7,3},{8,12},{12,8},{9,1... | collective-permute-start | bytes 207368 | tf_op jit(solution)/shard_map/ppermute | solution.py:39
  8.8 1.0 copy.17
  9.8 0.1 collective-permute-done
  9.9 0.1 copy.18
  10.1 0.0 copy-start.11
  10.1 0.0 copy-start.1
  10.1 0.0 copy-start.2
  10.1 0.0 copy-start.3
  10.1 0.0 copy-start.4
  10.1 0.0 copy-start.5
  10.1 0.3 pad_maximum_fusion.3
  10.5 9.2 %collective-permute-start.1 = (bf16[9,2,3840]{2,1,0:T(2,128)(2,1)S(1)}, bf16[9,2,3840]{2,1,0:T(2,128)(2,1)S(1)}, u32[]{:S(2)}, u32[]{:S(2)}) collective-permute-start(bf16[9,2,3840]{2,1,0:T(2,128)(2,1)S(1)} %pad_maximum_fusion.3), channel_id=1, source_target_pairs={{0,192},{4,324},{8,200},{12,332},{16,208},{20,340},{24,216},{28,34... | collective-permute-start | bytes 414728 | tf_op jit(solution)/shard_map/ppermute | solution.py:27
  19.7 3.1 %collective-permute-start.2 = (bf16[9,2,3840]{2,1,0:T(2,128)(2,1)S(1)}, bf16[9,2,3840]{2,1,0:T(2,128)(2,1)S(1)}, u32[]{:S(2)}, u32[]{:S(2)}) collective-permute-start(bf16[9,2,3840]{2,1,0:T(2,128)(2,1)S(1)} %pad_maximum_fusion.3), channel_id=1, source_target_pairs={{0,64},{4,452},{8,72},{12,460},{16,80},{20,468},{24,88},{28,476},{... | collective-permute-start | bytes 414728 | tf_op jit(solution)/shard_map/ppermute | solution.py:27
  22.7 5.6 %collective-permute-done.1 = bf16[9,2,3840]{2,1,0:T(2,128)(2,1)S(1)} collective-permute-done((bf16[9,2,3840]{2,1,0:T(2,128)(2,1)S(1)}, bf16[9,2,3840]{2,1,0:T(2,128)(2,1)S(1)}, u32[]{:S(2)}, u32[]{:S(2)}) %collective-permute-start.1) | collective-permute-done | bytes 138272 | tf_op jit(solution)/shard_map/ppermute | solution.py:27
  28.4 3.6 %collective-permute-done.2 = bf16[9,2,3840]{2,1,0:T(2,128)(2,1)S(1)} collective-permute-done((bf16[9,2,3840]{2,1,0:T(2,128)(2,1)S(1)}, bf16[9,2,3840]{2,1,0:T(2,128)(2,1)S(1)}, u32[]{:S(2)}, u32[]{:S(2)}) %collective-permute-start.2) | collective-permute-done | bytes 138272 | tf_op jit(solution)/shard_map/ppermute | solution.py:27
  32.0 0.3 pad_maximum_fusion.2
  32.3 4.7 %collective-permute-start.3 = (bf16[9,4,3840]{2,1,0:T(4,128)(2,1)S(1)}, bf16[9,4,3840]{2,1,0:T(4,128)(2,1)S(1)}, u32[]{:S(2)}, u32[]{:S(2)}) collective-permute-start(bf16[9,4,3840]{2,1,0:T(4,128)(2,1)S(1)} %pad_maximum_fusion.2), channel_id=1, source_target_pairs={{0,64},{4,20},{8,72},{12,28},{16,80},{20,4},{24,88},{28,12},{32,96... | collective-permute-start | bytes 829448 | tf_op jit(solution)/shard_map/ppermute | solution.py:27
  37.0 0.1 pad_add_fusion.at_ref
  37.0 2.3 %collective-permute-start.4 = (bf16[9,4,3840]{2,1,0:T(4,128)(2,1)S(1)}, bf16[9,4,3840]{2,1,0:T(4,128)(2,1)S(1)}, u32[]{:S(2)}, u32[]{:S(2)}) collective-permute-start(bf16[9,4,3840]{2,1,0:T(4,128)(2,1)S(1)} %pad_maximum_fusion.2), channel_id=1, source_target_pairs={{0,32},{4,12},{8,40},{12,20},{16,48},{20,28},{24,56},{28,4},{32,64... | collective-permute-start | bytes 829448 | tf_op jit(solution)/shard_map/ppermute | solution.py:27
  39.4 4.2 %collective-permute-start.5 = (bf16[9,4,3840]{2,1,0:T(4,128)(2,1)S(1)}, bf16[9,4,3840]{2,1,0:T(4,128)(2,1)}, u32[]{:S(2)}, u32[]{:S(2)}) collective-permute-start(bf16[9,4,3840]{2,1,0:T(4,128)(2,1)S(1)} %pad_maximum_fusion.2), channel_id=1, source_target_pairs={{0,480},{4,28},{8,488},{12,4},{16,496},{20,12},{24,504},{28,20},{3... | collective-permute-start | bytes 829448 | tf_op jit(solution)/shard_map/ppermute | solution.py:27
  43.5 0.0 collective-permute-done.3
  43.6 0.5 pad_maximum_fusion.refs_0_
  44.0 0.0 copy-done.11
  44.0 0.0 copy-done.1
  44.1 0.0 copy-done.2
  44.1 0.0 copy-done.3
  44.1 0.0 copy-done.4
  44.1 0.0 copy-done.5
  44.1 0.0 copy-start
  44.1 1.3 %shard_map.136 = (s32[64,8]{1,0:T(8,128)S(1)}, bf16[128,64]{1,0:T(8,128)(2,1)S(1)}, bf16[384,1024]{1,0:T(8,128)(2,1)S(1)}, bf16[1152,256]{1,0:T(8,128)(2,1)S(1)}, bf16[1152,256]{1,0:T(8,128)(2,1)S(1)}) custom-call(s32[4]{0:T(128)S(1)} %pad_add_fusion.at_ref, s32[16]{0:T(128)S(1)} %copy-done.5, s32[16,256]{1,0:T(8,128)S(1)} %copy-done.3, ...), custom_call_target="tpu_custom_call" | custom-call | flops 1000000000 | bytes 217744 | tf_op jit(solution)/shard_map/pallas_call | solution.py:111
  45.4 0.4 collective-permute-done.4
  45.8 1.2 collective-permute-done.5
  47.0 1.2 pad_maximum_fusion.1.refs_1_
  48.3 0.0 copy-done
  48.3 4.6 %collective-permute-start.6 = (bf16[2,288,3840]{2,1,0:T(8,128)(2,1)S(1)}, bf16[2,288,3840]{2,1,0:T(8,128)(2,1)S(1)}, u32[]{:S(2)}, u32[]{:S(2)}) collective-permute-start(bf16[2,288,3840]{2,1,0:T(8,128)(2,1)S(1)} %bitcast.24), channel_id=1, source_target_pairs={{0,4},{4,0},{1,5},{5,1},{2,6},{6,2},{3,7},{7,3},{8,12},{12,8},{9,1... | collective-permute-start | bytes 13271048 | tf_op jit(solution)/shard_map/ppermute | solution.py:379
  52.8 3.6 %collective-permute-start.9 = (bf16[9,8,3840]{2,1,0:T(8,128)(2,1)S(1)}, bf16[9,8,3840]{2,1,0:T(8,128)(2,1)S(1)}, u32[]{:S(2)}, u32[]{:S(2)}) collective-permute-start(bf16[9,8,3840]{2,1,0:T(8,128)(2,1)S(1)} %pad_maximum_fusion.1.refs_1_), channel_id=1, source_target_pairs={{0,8},{4,36},{8,16},{12,44},{16,24},{20,52},{24,0},{28,60},{32,40}... | collective-permute-start | bytes 1658888 | tf_op jit(solution)/shard_map/ppermute | solution.py:27
  56.5 3.1 %collective-permute-start.7 = (bf16[9,8,3840]{2,1,0:T(8,128)(2,1)S(1)}, bf16[9,8,3840]{2,1,0:T(8,128)(2,1)S(1)}, u32[]{:S(2)}, u32[]{:S(2)}) collective-permute-start(bf16[9,8,3840]{2,1,0:T(8,128)(2,1)S(1)} %pad_maximum_fusion.refs_0_), channel_id=1, source_target_pairs={{0,8},{4,36},{8,16},{12,44},{16,24},{20,52},{24,0},{28,60},{32,40}... | collective-permute-start | bytes 1658888 | tf_op jit(solution)/shard_map/ppermute | solution.py:27
  59.6 3.4 %collective-permute-start.11 = (bf16[9,8,3840]{2,1,0:T(8,128)(2,1)S(1)}, bf16[9,8,3840]{2,1,0:T(8,128)(2,1)S(1)}, u32[]{:S(2)}, u32[]{:S(2)}) collective-permute-start(bf16[9,8,3840]{2,1,0:T(8,128)(2,1)S(1)} %pad_maximum_fusion.refs_0_), channel_id=1, source_target_pairs={{0,24},{4,484},{8,0},{12,492},{16,8},{20,500},{24,16},{28,508},{32... | collective-permute-start | bytes 1658888 | tf_op jit(solution)/shard_map/ppermute | solution.py:27
  63.0 1.9 %collective-permute-start.12 = (bf16[9,8,3840]{2,1,0:T(8,128)(2,1)S(1)}, bf16[9,8,3840]{2,1,0:T(8,128)(2,1)S(1)}, u32[]{:S(2)}, u32[]{:S(2)}) collective-permute-start(bf16[9,8,3840]{2,1,0:T(8,128)(2,1)S(1)} %pad_maximum_fusion.1.refs_1_), channel_id=1, source_target_pairs={{0,24},{4,484},{8,0},{12,492},{16,8},{20,500},{24,16},{28,508},{32... | collective-permute-start | bytes 1658888 | tf_op jit(solution)/shard_map/ppermute | solution.py:27
  64.9 0.0 collective-permute-done.9.refs_3_
  64.9 3.4 %collective-permute-start.10 = (bf16[9,8,3840]{2,1,0:T(8,128)(2,1)S(1)}, bf16[9,8,3840]{2,1,0:T(8,128)(2,1)S(1)}, u32[]{:S(2)}, u32[]{:S(2)}) collective-permute-start(bf16[9,8,3840]{2,1,0:T(8,128)(2,1)S(1)} %collective-permute-done.9.refs_3_), channel_id=1, source_target_pairs={{0,8},{4,36},{8,16},{12,44},{16,24},{20,52},{24,0},{28,60},{32,40}... | collective-permute-start | bytes 1658888 | tf_op jit(solution)/shard_map/ppermute | solution.py:27
  68.3 2.2 %collective-permute-done.7.refs_2_ = bf16[9,8,3840]{2,1,0:T(8,128)(2,1)S(1)} collective-permute-done((bf16[9,8,3840]{2,1,0:T(8,128)(2,1)S(1)}, bf16[9,8,3840]{2,1,0:T(8,128)(2,1)S(1)}, u32[]{:S(2)}, u32[]{:S(2)}) %collective-permute-start.7) | collective-permute-done | bytes 552992 | tf_op jit(solution)/shard_map/ppermute | solution.py:27
  70.5 2.4 %collective-permute-start.8 = (bf16[9,8,3840]{2,1,0:T(8,128)(2,1)S(1)}, bf16[9,8,3840]{2,1,0:T(8,128)(2,1)S(1)}, u32[]{:S(2)}, u32[]{:S(2)}) collective-permute-start(bf16[9,8,3840]{2,1,0:T(8,128)(2,1)S(1)} %collective-permute-done.7.refs_2_), channel_id=1, source_target_pairs={{0,8},{4,36},{8,16},{12,44},{16,24},{20,52},{24,0},{28,60},{32,40}... | collective-permute-start | bytes 1658888 | tf_op jit(solution)/shard_map/ppermute | solution.py:27
  72.9 0.0 collective-permute-done.11.refs_4_
  72.9 3.1 %collective-permute-done.12.refs_5_ = bf16[9,8,3840]{2,1,0:T(8,128)(2,1)S(1)} collective-permute-done((bf16[9,8,3840]{2,1,0:T(8,128)(2,1)S(1)}, bf16[9,8,3840]{2,1,0:T(8,128)(2,1)S(1)}, u32[]{:S(2)}, u32[]{:S(2)}) %collective-permute-start.12) | collective-permute-done | bytes 552992 | tf_op jit(solution)/shard_map/ppermute | solution.py:27
  76.1 0.0 collective-permute-done.6.other_ref
  76.1 5.0 %shard_map.137.prev_ref = f32[128,48]{1,0:T(8,128)S(1)} custom-call(bf16[2,288,3840]{2,1,0:T(8,128)(2,1)S(1)} %bitcast.25, bf16[2,288,3840]{2,1,0:T(8,128)(2,1)S(1)} %collective-permute-done.6.other_ref, bf16[9,8,3840]{2,1,0:T(8,128)(2,1)S(1)} %pad_maximum_fusion.refs_0_, bf16[9,8,3840]{2,1,0:T(8,128)(2,1)S(1)} %pad_maximum_fusion.1.refs_1_, ...), custom_call_target="tpu_custom_call" | custom-call | flops 3822059520 | bytes 12165120 | tf_op jit(solution)/shard_map/pallas_call | solution.py:111
  81.0 0.0 collective-permute-done.10.refs_1_
  81.0 1.6 %collective-permute-done.8.refs_0_ = bf16[9,8,3840]{2,1,0:T(8,128)(2,1)S(1)} collective-permute-done((bf16[9,8,3840]{2,1,0:T(8,128)(2,1)S(1)}, bf16[9,8,3840]{2,1,0:T(8,128)(2,1)S(1)}, u32[]{:S(2)}, u32[]{:S(2)}) %collective-permute-start.8) | collective-permute-done | bytes 552992 | tf_op jit(solution)/shard_map/ppermute | solution.py:27
  82.6 0.0 copy-start.6
  82.6 0.0 copy-start.7
  82.6 0.0 copy-start.10
  82.6 3.4 %shard_map.138 = bf16[256,128]{1,0:T(8,128)(2,1)} custom-call(bf16[2,288,3840]{2,1,0:T(8,128)(2,1)S(1)} %bitcast.26, bf16[2,288,3840]{2,1,0:T(8,128)(2,1)S(1)} %collective-permute-done.6.other_ref, f32[128,48]{1,0:T(8,128)S(1)} %shard_map.137.prev_ref, bf16[128,64]{1,0:T(8,128)(2,1)S(1)} %get-tuple-element.30.place_ref, ...), custom_call_target="tpu_custom_call" | custom-call | flops 1274019840 | bytes 9994240 | tf_op jit(solution)/shard_map/pallas_call | solution.py:111
  86.0 6.0 %all-to-all-start = ((bf16[8,32,128]{2,1,0:T(8,128)(2,1)}), bf16[8,32,128]{2,1,0:T(8,128)(2,1)S(1)}, u32[]{:S(2)}, u32[]{:S(2)}) async-start(bf16[8,32,128]{2,1,0:T(8,128)(2,1)} %bitcast.11), calls=%async_computation | async-start | bytes 131072 | tf_op jit(solution)/shard_map/all_to_all | solution.py:392
  92.7 4.3 %all-to-all-done = bf16[8,32,128]{2,1,0:T(8,128)(2,1)S(1)} async-done(((bf16[8,32,128]{2,1,0:T(8,128)(2,1)}), bf16[8,32,128]{2,1,0:T(8,128)(2,1)S(1)}, u32[]{:S(2)}, u32[]{:S(2)}) %all-to-all-start) | async-done | bytes 65568 | tf_op jit(solution)/shard_map/all_to_all | solution.py:392
  97.0 0.0 copy-done.6
  97.0 0.0 copy-done.7
  97.0 0.0 copy-done.8
  97.0 0.0 copy-done.9
  97.0 0.0 copy-done.10
  97.0 3.1 %shard_map.139 = f32[64,8]{1,0:T(8,128)S(1)} custom-call(f32[1]{0:T(128)S(6)} %copy.20.bias_ref, bf16[256,128]{1,0:T(8,128)(2,1)S(1)} %bitcast.27, bf16[256,128]{1,0:T(8,128)(2,1)S(1)} %copy-done.10, bf16[384,1024]{1,0:T(8,128)(2,1)S(1)} %get-tuple-element.33.t1_ref, f32[1,32]{1,0:T(1,128)S(1)} %bitcast.31, bf16[1152,256]{1,0:T(8,128)(2,1)S(1)} %get-tuple-element.34.t2_ref, ...), custom_call_target="tpu_custom_call" | custom-call | flops 2000000000 | bytes 2100356 | tf_op jit(solution)/shard_map/pallas_call | solution.py:111
  100.1 22.1 %all_to_all.20 = f32[64,1,8]{2,1,0:T(1,128)S(1)} all-to-all(f32[64,1,8]{2,1,0:T(1,128)S(1)} %bitcast.28), channel_id=1, replica_groups=mesh['z'=16,'y'=4,'c'=2,'x'=4] {'z','y'}, dimensions={0} | all-to-all | bytes 4096 | tf_op jit(solution)/shard_map/all_to_all | solution.py:396
  122.2 0.1 reduce_sum.9
  122.3 0.6 reshape.23
  (3 shorter events, 0.0 us)
Async XLA Ops:
  0.0 9.9 %collective-permute-start = (bf16[9,3840]{1,0:T(8,128)(2,1)}, bf16[9,3840]{1,0:T(8,128)(2,1)S(1)}, u32[]{:S(2)}, u32[]{:S(2)}) collective-permute-start(bf16[9,3840]{1,0:T(8,128)(2,1)} %bitcast.35), channel_id=1, source_target_pairs={{0,4},{4,0},{1,5},{5,1},{2,6},{6,2},{3,7},{7,3},{8,12},{12,8},{9,1... | collective-permute-start | bytes 207368 | tf_op jit(solution)/shard_map/ppermute | solution.py:39
  10.1 34.0 %copy-start.11 = (bf16[3,3,1,32]{3,1,2,0:T(4,128)(2,1)S(1)}, bf16[3,3,1,32]{3,1,2,0:T(4,128)(2,1)}, u32[]{:S(2)}) copy-start(bf16[3,3,1,32]{3,1,2,0:T(4,128)(2,1)} %param.19) | copy-start | bytes 1732
  10.1 34.0 %copy-start.1 = (bf16[3,3,64,128]{3,2,1,0:T(8,128)(2,1)S(1)}, bf16[3,3,64,128]{3,2,1,0:T(8,128)(2,1)}, u32[]{:S(2)}) copy-start(bf16[3,3,64,128]{3,2,1,0:T(8,128)(2,1)} %param.23) | copy-start | bytes 442372
  10.1 34.0 %copy-start.2 = (bf16[3,3,32,64]{3,2,1,0:T(8,128)(2,1)S(1)}, bf16[3,3,32,64]{3,2,1,0:T(8,128)(2,1)}, u32[]{:S(2)}) copy-start(bf16[3,3,32,64]{3,2,1,0:T(8,128)(2,1)} %param.21) | copy-start | bytes 110596
  10.1 34.0 %copy-start.3 = (s32[16,256]{1,0:T(8,128)S(1)}, s32[16,256]{1,0:T(8,128)}, u32[]{:S(2)}) copy-start(s32[16,256]{1,0:T(8,128)} %shard_ref.1) | copy-start | bytes 49156
  10.1 34.0 %copy-start.4 = (s32[16,256]{1,0:T(8,128)S(1)}, s32[16,256]{1,0:T(8,128)}, u32[]{:S(2)}) copy-start(s32[16,256]{1,0:T(8,128)} %clip_ref.1) | copy-start | bytes 49156
  10.1 34.0 %copy-start.5 = (s32[16]{0:T(128)S(1)}, s32[16]{0:T(128)}, u32[]{:S(2)}) copy-start(s32[16]{0:T(128)} %count_ref.1) | copy-start | bytes 196
  10.5 17.9 %collective-permute-start.1 = (bf16[9,2,3840]{2,1,0:T(2,128)(2,1)S(1)}, bf16[9,2,3840]{2,1,0:T(2,128)(2,1)S(1)}, u32[]{:S(2)}, u32[]{:S(2)}) collective-permute-start(bf16[9,2,3840]{2,1,0:T(2,128)(2,1)S(1)} %pad_maximum_fusion.3), channel_id=1, source_target_pairs={{0,192},{4,324},{8,200},{12,332},{16,208},{20,340},{24,216},{28,34... | collective-permute-start | bytes 414728 | tf_op jit(solution)/shard_map/ppermute | solution.py:27
  19.7 12.3 %collective-permute-start.2 = (bf16[9,2,3840]{2,1,0:T(2,128)(2,1)S(1)}, bf16[9,2,3840]{2,1,0:T(2,128)(2,1)S(1)}, u32[]{:S(2)}, u32[]{:S(2)}) collective-permute-start(bf16[9,2,3840]{2,1,0:T(2,128)(2,1)S(1)} %pad_maximum_fusion.3), channel_id=1, source_target_pairs={{0,64},{4,452},{8,72},{12,460},{16,80},{20,468},{24,88},{28,476},{... | collective-permute-start | bytes 414728 | tf_op jit(solution)/shard_map/ppermute | solution.py:27
  32.3 11.3 %collective-permute-start.3 = (bf16[9,4,3840]{2,1,0:T(4,128)(2,1)S(1)}, bf16[9,4,3840]{2,1,0:T(4,128)(2,1)S(1)}, u32[]{:S(2)}, u32[]{:S(2)}) collective-permute-start(bf16[9,4,3840]{2,1,0:T(4,128)(2,1)S(1)} %pad_maximum_fusion.2), channel_id=1, source_target_pairs={{0,64},{4,20},{8,72},{12,28},{16,80},{20,4},{24,88},{28,12},{32,96... | collective-permute-start | bytes 829448 | tf_op jit(solution)/shard_map/ppermute | solution.py:27
  37.0 8.8 %collective-permute-start.4 = (bf16[9,4,3840]{2,1,0:T(4,128)(2,1)S(1)}, bf16[9,4,3840]{2,1,0:T(4,128)(2,1)S(1)}, u32[]{:S(2)}, u32[]{:S(2)}) collective-permute-start(bf16[9,4,3840]{2,1,0:T(4,128)(2,1)S(1)} %pad_maximum_fusion.2), channel_id=1, source_target_pairs={{0,32},{4,12},{8,40},{12,20},{16,48},{20,28},{24,56},{28,4},{32,64... | collective-permute-start | bytes 829448 | tf_op jit(solution)/shard_map/ppermute | solution.py:27
  39.4 7.7 %collective-permute-start.5 = (bf16[9,4,3840]{2,1,0:T(4,128)(2,1)S(1)}, bf16[9,4,3840]{2,1,0:T(4,128)(2,1)}, u32[]{:S(2)}, u32[]{:S(2)}) collective-permute-start(bf16[9,4,3840]{2,1,0:T(4,128)(2,1)S(1)} %pad_maximum_fusion.2), channel_id=1, source_target_pairs={{0,480},{4,28},{8,488},{12,4},{16,496},{20,12},{24,504},{28,20},{3... | collective-permute-start | bytes 829448 | tf_op jit(solution)/shard_map/ppermute | solution.py:27
  44.1 4.2 %copy-start = (bf16[2,32,9,3840]{3,1,2,0:T(8,128)(2,1)S(1)}, bf16[2,32,9,3840]{3,1,2,0:T(8,128)(2,1)}, u32[]{:S(2)}) copy-start(bf16[2,32,9,3840]{3,1,2,0:T(8,128)(2,1)} %param.15) | copy-start | bytes 13271044
  48.3 27.8 %collective-permute-start.6 = (bf16[2,288,3840]{2,1,0:T(8,128)(2,1)S(1)}, bf16[2,288,3840]{2,1,0:T(8,128)(2,1)S(1)}, u32[]{:S(2)}, u32[]{:S(2)}) collective-permute-start(bf16[2,288,3840]{2,1,0:T(8,128)(2,1)S(1)} %bitcast.24), channel_id=1, source_target_pairs={{0,4},{4,0},{1,5},{5,1},{2,6},{6,2},{3,7},{7,3},{8,12},{12,8},{9,1... | collective-permute-start | bytes 13271048 | tf_op jit(solution)/shard_map/ppermute | solution.py:379
  52.8 12.1 %collective-permute-start.9 = (bf16[9,8,3840]{2,1,0:T(8,128)(2,1)S(1)}, bf16[9,8,3840]{2,1,0:T(8,128)(2,1)S(1)}, u32[]{:S(2)}, u32[]{:S(2)}) collective-permute-start(bf16[9,8,3840]{2,1,0:T(8,128)(2,1)S(1)} %pad_maximum_fusion.1.refs_1_), channel_id=1, source_target_pairs={{0,8},{4,36},{8,16},{12,44},{16,24},{20,52},{24,0},{28,60},{32,40}... | collective-permute-start | bytes 1658888 | tf_op jit(solution)/shard_map/ppermute | solution.py:27
  56.5 14.0 %collective-permute-start.7 = (bf16[9,8,3840]{2,1,0:T(8,128)(2,1)S(1)}, bf16[9,8,3840]{2,1,0:T(8,128)(2,1)S(1)}, u32[]{:S(2)}, u32[]{:S(2)}) collective-permute-start(bf16[9,8,3840]{2,1,0:T(8,128)(2,1)S(1)} %pad_maximum_fusion.refs_0_), channel_id=1, source_target_pairs={{0,8},{4,36},{8,16},{12,44},{16,24},{20,52},{24,0},{28,60},{32,40}... | collective-permute-start | bytes 1658888 | tf_op jit(solution)/shard_map/ppermute | solution.py:27
  59.6 13.3 %collective-permute-start.11 = (bf16[9,8,3840]{2,1,0:T(8,128)(2,1)S(1)}, bf16[9,8,3840]{2,1,0:T(8,128)(2,1)S(1)}, u32[]{:S(2)}, u32[]{:S(2)}) collective-permute-start(bf16[9,8,3840]{2,1,0:T(8,128)(2,1)S(1)} %pad_maximum_fusion.refs_0_), channel_id=1, source_target_pairs={{0,24},{4,484},{8,0},{12,492},{16,8},{20,500},{24,16},{28,508},{32... | collective-permute-start | bytes 1658888 | tf_op jit(solution)/shard_map/ppermute | solution.py:27
  63.0 13.1 %collective-permute-start.12 = (bf16[9,8,3840]{2,1,0:T(8,128)(2,1)S(1)}, bf16[9,8,3840]{2,1,0:T(8,128)(2,1)S(1)}, u32[]{:S(2)}, u32[]{:S(2)}) collective-permute-start(bf16[9,8,3840]{2,1,0:T(8,128)(2,1)S(1)} %pad_maximum_fusion.1.refs_1_), channel_id=1, source_target_pairs={{0,24},{4,484},{8,0},{12,492},{16,8},{20,500},{24,16},{28,508},{32... | collective-permute-start | bytes 1658888 | tf_op jit(solution)/shard_map/ppermute | solution.py:27
  64.9 16.1 %collective-permute-start.10 = (bf16[9,8,3840]{2,1,0:T(8,128)(2,1)S(1)}, bf16[9,8,3840]{2,1,0:T(8,128)(2,1)S(1)}, u32[]{:S(2)}, u32[]{:S(2)}) collective-permute-start(bf16[9,8,3840]{2,1,0:T(8,128)(2,1)S(1)} %collective-permute-done.9.refs_3_), channel_id=1, source_target_pairs={{0,8},{4,36},{8,16},{12,44},{16,24},{20,52},{24,0},{28,60},{32,40}... | collective-permute-start | bytes 1658888 | tf_op jit(solution)/shard_map/ppermute | solution.py:27
  70.5 12.1 %collective-permute-start.8 = (bf16[9,8,3840]{2,1,0:T(8,128)(2,1)S(1)}, bf16[9,8,3840]{2,1,0:T(8,128)(2,1)S(1)}, u32[]{:S(2)}, u32[]{:S(2)}) collective-permute-start(bf16[9,8,3840]{2,1,0:T(8,128)(2,1)S(1)} %collective-permute-done.7.refs_2_), channel_id=1, source_target_pairs={{0,8},{4,36},{8,16},{12,44},{16,24},{20,52},{24,0},{28,60},{32,40}... | collective-permute-start | bytes 1658888 | tf_op jit(solution)/shard_map/ppermute | solution.py:27
  82.6 14.4 %copy-start.6 = (f32[32]{0:T(128)S(1)}, f32[32]{0:T(128)}, u32[]{:S(2)}) copy-start(f32[32]{0:T(128)} %param.20) | copy-start | bytes 388
  82.6 14.4 %copy-start.7 = (f32[64]{0:T(128)S(1)}, f32[64]{0:T(128)}, u32[]{:S(2)}) copy-start(f32[64]{0:T(128)} %param.22) | copy-start | bytes 772
  82.6 14.4 %copy-start.8 = (f32[128]{0:T(128)S(1)}, f32[128]{0:T(128)}, u32[]{:S(2)}) copy-start(f32[128]{0:T(128)} %param.24) | copy-start | bytes 1540
  82.6 14.4 %copy-start.9 = (bf16[128]{0:T(256)(128)(2,1)S(1)}, bf16[128]{0:T(256)(128)(2,1)}, u32[]{:S(2)}) copy-start(bf16[128]{0:T(256)(128)(2,1)} %param.25) | copy-start | bytes 772
  82.6 14.4 %copy-start.10 = (bf16[256,128]{1,0:T(8,128)(2,1)S(1)}, bf16[256,128]{1,0:T(8,128)(2,1)}, u32[]{:S(2)}) copy-start(bf16[256,128]{1,0:T(8,128)(2,1)} %constant.22.clone.order_ref) | copy-start | bytes 196612
  86.0 11.0 %all-to-all-start = ((bf16[8,32,128]{2,1,0:T(8,128)(2,1)}), bf16[8,32,128]{2,1,0:T(8,128)(2,1)S(1)}, u32[]{:S(2)}, u32[]{:S(2)}) async-start(bf16[8,32,128]{2,1,0:T(8,128)(2,1)} %bitcast.11), calls=%async_computation | async-start | bytes 131072 | tf_op jit(solution)/shard_map/all_to_all | solution.py:392

commit v11 on v10

--- a/solution.py
+++ b/solution.py
@@ -39,7 +39,7 @@
     other = lax.ppermute(block, "c", [(0, 1), (1, 0)])
     both = jnp.stack([block, other], axis=1)
     four = [send(both, lambda z, y: (z + d, y), lambda z, y: (z - d, y)) for d in CLASS_STEPS]
-    return jnp.concatenate(four, axis=1)
+    return four
 
 
 def best_means(regions, frames, corpus_ref, clip, rows, count):
@@ -366,17 +366,18 @@
     group = cand_shard.shape[0] // NX
 
     own = corpus.transpose(0, 2, 1, 3).reshape(clip_dev, regions * frames, width)
-    four = gather_classes(queries[0, 0])
+    head, tail = gather_classes(queries[0, 0])
+    kernels = (first_kernel, second_kernel, third_kernel)
+    kernels, head = lax.optimization_barrier((kernels, head))
+    listed, place, *spread = prepare(at, cand_count, cand_shard, cand_clip, *kernels)
+    own, listed, tail = lax.optimization_barrier((own, listed, tail))
+    other = lax.ppermute(own, "c", [(0, 1), (1, 0)])
+    four = jnp.concatenate([head, tail], axis=1)
     ahead = near_shift(four, -1)
     two = near_shift(four, 2)
     behind = near_shift(four, 1)
-    kernels = (first_kernel, second_kernel, third_kernel)
-    kernels, two = lax.optimization_barrier((kernels, two))
-    listed, place, *spread = prepare(at, cand_count, cand_shard, cand_clip, *kernels)
     first = jnp.concatenate([four, two], axis=1)
     last = jnp.concatenate([behind, ahead], axis=1)
-    own, listed, first, last = lax.optimization_barrier((own, listed, first, last))
-    other = lax.ppermute(own, "c", [(0, 1), (1, 0)])
     behind_first = shift(first, 1)
     ahead_first = shift(first, -1)
     two_first = shift(behind_first, 1)

time: 124 us -> 133 us (1.073)
  local copies, waits for them, and re-layouts: 1.85 us -> 6.38 us
  blocking collectives: 22.1 us -> 25.9 us
  starting transfers between devices: 60.6 us -> 63.4 us
    all_to_all x1, starting transfers between devices: 6.01 us -> 10.7 us  [on_device(): parts = lax.all_to_all(table, ('c', 'x'), 0, 0, tiled=True)]
    unnamed x24 -> x22, local copies, waits for them, and re-layouts: 0.07 us -> 3.91 us
    all_to_all x1, blocking collectives: 22.1 us -> 25.9 us  [on_device(): values = lax.all_to_all(values, ('z', 'y'), 0, 0, tiled=True)]
    ppermute x1, starting transfers between devices: 4.57 us -> 1.92 us  [on_device(): other = lax.ppermute(own, 'c', [(0, 1), (1, 0)])]
  transfers between devices with their start and end apart: 14 -> 14, of which waited for: 9 -> 8; matrix products, arithmetic and copies ran while one was open for 1% -> 2% of each run, Pallas kernels for 5% -> 5%
where the time goes in v11:
time: 133 us; the launch traced here: 132 us
  starting transfers between devices  63.4 us (48%)
  blocking collectives  25.9 us (19%)
  waiting for transfers between devices  21.3 us (16%)
  Pallas kernels  12.8 us (10%)
  local copies, waits for them, and re-layouts  6.38 us (5%)
  other arithmetic  1.5 us (1%)
    ppermute x11, starting transfers between devices, send(): return lax.ppermute(values, PLANE, pairs)  42 us
    all_to_all x1, blocking collectives, on_device(): values = lax.all_to_all(values, ('z', 'y'), 0, 0, tiled=True)  25.9 us
    ppermute x11, waiting for transfers between devices, send(): return lax.ppermute(values, PLANE, pairs)  16.9 us
    pallas_call x4, Pallas kernels, kernel_call(): pl.pallas_call(body, in_specs=[pl.BlockSpec(memory_space=space) for space...  12.8 us
    all_to_all x1, starting transfers between devices, on_device(): parts = lax.all_to_all(table, ('c', 'x'), 0, 0, tiled=True)  10.7 us
    ppermute x1, starting transfers between devices, gather_classes(): other = lax.ppermute(block, 'c', [(0, 1), (1, 0)])  8.77 us
    all_to_all x1, waiting for transfers between devices, on_device(): parts = lax.all_to_all(table, ('c', 'x'), 0, 0, tiled=True)  4.32 us
    unnamed x22, local copies, waits for them, and re-layouts  3.91 us
  transfers between devices with their start and end apart: 14, of which 8 were waited for; matrix products, arithmetic and copies ran while one was open for 2% of the time, Pallas kernels for 5%

profile of v11, /device:TPU:1, one launch (start us, length us, event | category | flops | bytes accessed | tf_op | source)
XLA Modules:
  0.0 132.2 jit_solution(468421365916995904)
XLA Ops:
  0.0 8.8 %collective-permute-start = (bf16[9,3840]{1,0:T(8,128)(2,1)}, bf16[9,3840]{1,0:T(8,128)(2,1)S(1)}, u32[]{:S(2)}, u32[]{:S(2)}) collective-permute-start(bf16[9,3840]{1,0:T(8,128)(2,1)} %bitcast.35), channel_id=1, source_target_pairs={{0,4},{4,0},{1,5},{5,1},{2,6},{6,2},{3,7},{7,3},{8,12},{12,8},{9,1... | collective-permute-start | bytes 207368 | tf_op jit(solution)/shard_map/ppermute | solution.py:39
  8.8 1.0 copy.17
  9.8 0.1 collective-permute-done
  9.9 0.1 copy.18
  10.1 0.3 pad_maximum_fusion.3
  10.4 9.2 %collective-permute-start.1 = (bf16[9,2,3840]{2,1,0:T(2,128)(2,1)S(1)}, bf16[9,2,3840]{2,1,0:T(2,128)(2,1)S(1)}, u32[]{:S(2)}, u32[]{:S(2)}) collective-permute-start(bf16[9,2,3840]{2,1,0:T(2,128)(2,1)S(1)} %pad_maximum_fusion.3), channel_id=1, source_target_pairs={{0,192},{4,324},{8,200},{12,332},{16,208},{20,340},{24,216},{28,34... | collective-permute-start | bytes 414728 | tf_op jit(solution)/shard_map/ppermute | solution.py:27
  19.6 3.1 %collective-permute-start.2 = (bf16[9,2,3840]{2,1,0:T(2,128)(2,1)S(1)}, bf16[9,2,3840]{2,1,0:T(2,128)(2,1)S(1)}, u32[]{:S(2)}, u32[]{:S(2)}) collective-permute-start(bf16[9,2,3840]{2,1,0:T(2,128)(2,1)S(1)} %pad_maximum_fusion.3), channel_id=1, source_target_pairs={{0,64},{4,452},{8,72},{12,460},{16,80},{20,468},{24,88},{28,476},{... | collective-permute-start | bytes 414728 | tf_op jit(solution)/shard_map/ppermute | solution.py:27
  22.7 0.1 pad_add_fusion.at_ref
  22.8 5.6 %collective-permute-done.1 = bf16[9,2,3840]{2,1,0:T(2,128)(2,1)S(1)} collective-permute-done((bf16[9,2,3840]{2,1,0:T(2,128)(2,1)S(1)}, bf16[9,2,3840]{2,1,0:T(2,128)(2,1)S(1)}, u32[]{:S(2)}, u32[]{:S(2)}) %collective-permute-start.1) | collective-permute-done | bytes 138272 | tf_op jit(solution)/shard_map/ppermute | solution.py:27
  28.3 0.7 reshape.20.first_ref
  29.0 0.9 copy-done.1
  29.9 0.0 copy-start.2
  29.9 0.9 copy-done.2
  30.8 0.0 copy-start.3
  30.8 0.7 copy-done.3
  31.5 0.0 copy-start.4
  31.5 0.7 copy-done.4
  32.2 0.0 copy-start.5
  32.2 0.7 copy-done.5
  32.9 0.0 copy-start
  32.9 1.3 shard_map.136
  34.2 0.0 collective-permute-done.2
  34.2 1.9 %collective-permute-start.3 = (bf16[2,288,3840]{2,1,0:T(8,128)(2,1)}, bf16[2,288,3840]{2,1,0:T(8,128)(2,1)S(1)}, u32[]{:S(2)}, u32[]{:S(2)}) collective-permute-start(bf16[2,288,3840]{2,1,0:T(8,128)(2,1)} %bitcast.24), channel_id=1, source_target_pairs={{0,4},{4,0},{1,5},{5,1},{2,6},{6,2},{3,7},{7,3},{8,12},{12,8},{9,1... | collective-permute-start | bytes 13271048 | tf_op jit(solution)/shard_map/ppermute | solution.py:374
  36.2 0.3 pad_maximum_fusion.2
  36.5 3.4 %collective-permute-start.7 = (bf16[9,4,3840]{2,1,0:T(4,128)(2,1)S(1)}, bf16[9,4,3840]{2,1,0:T(4,128)(2,1)S(1)}, u32[]{:S(2)}, u32[]{:S(2)}) collective-permute-start(bf16[9,4,3840]{2,1,0:T(4,128)(2,1)S(1)} %pad_maximum_fusion.2), channel_id=1, source_target_pairs={{0,32},{4,12},{8,40},{12,20},{16,48},{20,28},{24,56},{28,4},{32,64... | collective-permute-start | bytes 829448 | tf_op jit(solution)/shard_map/ppermute | solution.py:27
  39.9 3.4 %collective-permute-start.8 = (bf16[9,4,3840]{2,1,0:T(4,128)(2,1)S(1)}, bf16[9,4,3840]{2,1,0:T(4,128)(2,1)S(1)}, u32[]{:S(2)}, u32[]{:S(2)}) collective-permute-start(bf16[9,4,3840]{2,1,0:T(4,128)(2,1)S(1)} %pad_maximum_fusion.2), channel_id=1, source_target_pairs={{0,480},{4,28},{8,488},{12,4},{16,496},{20,12},{24,504},{28,20},{3... | collective-permute-start | bytes 829448 | tf_op jit(solution)/shard_map/ppermute | solution.py:27
  43.3 3.5 %collective-permute-start.4 = (bf16[9,4,3840]{2,1,0:T(4,128)(2,1)S(1)}, bf16[9,4,3840]{2,1,0:T(4,128)(2,1)S(1)}, u32[]{:S(2)}, u32[]{:S(2)}) collective-permute-start(bf16[9,4,3840]{2,1,0:T(4,128)(2,1)S(1)} %pad_maximum_fusion.2), channel_id=1, source_target_pairs={{0,64},{4,20},{8,72},{12,28},{16,80},{20,4},{24,88},{28,12},{32,96... | collective-permute-start | bytes 829448 | tf_op jit(solution)/shard_map/ppermute | solution.py:27
  46.8 0.0 collective-permute-done.7
  46.8 0.6 collective-permute-done.8
  47.5 0.3 pad_maximum_fusion.1.refs_1_
  47.7 2.5 %collective-permute-start.9 = (bf16[9,8,3840]{2,1,0:T(8,128)(2,1)S(1)}, bf16[9,8,3840]{2,1,0:T(8,128)(2,1)S(1)}, u32[]{:S(2)}, u32[]{:S(2)}) collective-permute-start(bf16[9,8,3840]{2,1,0:T(8,128)(2,1)S(1)} %pad_maximum_fusion.1.refs_1_), channel_id=1, source_target_pairs={{0,8},{4,36},{8,16},{12,44},{16,24},{20,52},{24,0},{28,60},{32,40}... | collective-permute-start | bytes 1658888 | tf_op jit(solution)/shard_map/ppermute | solution.py:27
  50.2 1.8 %collective-permute-done.4 = bf16[9,4,3840]{2,1,0:T(4,128)(2,1)S(1)} collective-permute-done((bf16[9,4,3840]{2,1,0:T(4,128)(2,1)S(1)}, bf16[9,4,3840]{2,1,0:T(4,128)(2,1)S(1)}, u32[]{:S(2)}, u32[]{:S(2)}) %collective-permute-start.4) | collective-permute-done | bytes 276512 | tf_op jit(solution)/shard_map/ppermute | solution.py:27
  52.0 0.5 pad_maximum_fusion.refs_0_
  52.5 3.2 %collective-permute-start.5 = (bf16[9,8,3840]{2,1,0:T(8,128)(2,1)S(1)}, bf16[9,8,3840]{2,1,0:T(8,128)(2,1)S(1)}, u32[]{:S(2)}, u32[]{:S(2)}) collective-permute-start(bf16[9,8,3840]{2,1,0:T(8,128)(2,1)S(1)} %pad_maximum_fusion.refs_0_), channel_id=1, source_target_pairs={{0,8},{4,36},{8,16},{12,44},{16,24},{20,52},{24,0},{28,60},{32,40}... | collective-permute-start | bytes 1658888 | tf_op jit(solution)/shard_map/ppermute | solution.py:27
  55.7 6.6 %collective-permute-start.12 = (bf16[9,8,3840]{2,1,0:T(8,128)(2,1)S(1)}, bf16[9,8,3840]{2,1,0:T(8,128)(2,1)S(1)}, u32[]{:S(2)}, u32[]{:S(2)}) collective-permute-start(bf16[9,8,3840]{2,1,0:T(8,128)(2,1)S(1)} %pad_maximum_fusion.1.refs_1_), channel_id=1, source_target_pairs={{0,24},{4,484},{8,0},{12,492},{16,8},{20,500},{24,16},{28,508},{32... | collective-permute-start | bytes 1658888 | tf_op jit(solution)/shard_map/ppermute | solution.py:27
  62.3 3.4 %collective-permute-start.11 = (bf16[9,8,3840]{2,1,0:T(8,128)(2,1)S(1)}, bf16[9,8,3840]{2,1,0:T(8,128)(2,1)S(1)}, u32[]{:S(2)}, u32[]{:S(2)}) collective-permute-start(bf16[9,8,3840]{2,1,0:T(8,128)(2,1)S(1)} %pad_maximum_fusion.refs_0_), channel_id=1, source_target_pairs={{0,24},{4,484},{8,0},{12,492},{16,8},{20,500},{24,16},{28,508},{32... | collective-permute-start | bytes 1658888 | tf_op jit(solution)/shard_map/ppermute | solution.py:27
  65.7 0.0 collective-permute-done.9.refs_3_
  65.7 1.9 %collective-permute-start.10 = (bf16[9,8,3840]{2,1,0:T(8,128)(2,1)S(1)}, bf16[9,8,3840]{2,1,0:T(8,128)(2,1)S(1)}, u32[]{:S(2)}, u32[]{:S(2)}) collective-permute-start(bf16[9,8,3840]{2,1,0:T(8,128)(2,1)S(1)} %collective-permute-done.9.refs_3_), channel_id=1, source_target_pairs={{0,8},{4,36},{8,16},{12,44},{16,24},{20,52},{24,0},{28,60},{32,40}... | collective-permute-start | bytes 1658888 | tf_op jit(solution)/shard_map/ppermute | solution.py:27
  67.6 1.9 %collective-permute-done.5.refs_2_ = bf16[9,8,3840]{2,1,0:T(8,128)(2,1)S(1)} collective-permute-done((bf16[9,8,3840]{2,1,0:T(8,128)(2,1)S(1)}, bf16[9,8,3840]{2,1,0:T(8,128)(2,1)S(1)}, u32[]{:S(2)}, u32[]{:S(2)}) %collective-permute-start.5) | collective-permute-done | bytes 552992 | tf_op jit(solution)/shard_map/ppermute | solution.py:27
  69.6 1.9 %collective-permute-start.6 = (bf16[9,8,3840]{2,1,0:T(8,128)(2,1)S(1)}, bf16[9,8,3840]{2,1,0:T(8,128)(2,1)S(1)}, u32[]{:S(2)}, u32[]{:S(2)}) collective-permute-start(bf16[9,8,3840]{2,1,0:T(8,128)(2,1)S(1)} %collective-permute-done.5.refs_2_), channel_id=1, source_target_pairs={{0,8},{4,36},{8,16},{12,44},{16,24},{20,52},{24,0},{28,60},{32,40}... | collective-permute-start | bytes 1658888 | tf_op jit(solution)/shard_map/ppermute | solution.py:27
  71.5 0.0 collective-permute-done.12.refs_5_
  71.5 3.2 %collective-permute-done.11.refs_4_ = bf16[9,8,3840]{2,1,0:T(8,128)(2,1)S(1)} collective-permute-done((bf16[9,8,3840]{2,1,0:T(8,128)(2,1)S(1)}, bf16[9,8,3840]{2,1,0:T(8,128)(2,1)S(1)}, u32[]{:S(2)}, u32[]{:S(2)}) %collective-permute-start.11) | collective-permute-done | bytes 552992 | tf_op jit(solution)/shard_map/ppermute | solution.py:27
  74.7 0.0 collective-permute-done.3.other_ref
  74.7 0.0 copy-done
  74.7 5.0 %shard_map.137.prev_ref = f32[128,48]{1,0:T(8,128)S(1)} custom-call(bf16[2,288,3840]{2,1,0:T(8,128)(2,1)S(1)} %bitcast.25, bf16[2,288,3840]{2,1,0:T(8,128)(2,1)S(1)} %collective-permute-done.3.other_ref, bf16[9,8,3840]{2,1,0:T(8,128)(2,1)S(1)} %pad_maximum_fusion.refs_0_, bf16[9,8,3840]{2,1,0:T(8,128)(2,1)S(1)} %pad_maximum_fusion.1.refs_1_, ...), custom_call_target="tpu_custom_call" | custom-call | flops 3822059520 | bytes 12165120 | tf_op jit(solution)/shard_map/pallas_call | solution.py:111
  79.7 0.0 collective-permute-done.10.refs_1_
  79.7 3.7 %collective-permute-done.6.refs_0_ = bf16[9,8,3840]{2,1,0:T(8,128)(2,1)S(1)} collective-permute-done((bf16[9,8,3840]{2,1,0:T(8,128)(2,1)S(1)}, bf16[9,8,3840]{2,1,0:T(8,128)(2,1)S(1)}, u32[]{:S(2)}, u32[]{:S(2)}) %collective-permute-start.6) | collective-permute-done | bytes 552992 | tf_op jit(solution)/shard_map/ppermute | solution.py:27
  83.4 0.0 copy-start.6
  83.4 0.0 copy-start.7
  83.4 0.0 copy-start.8
  83.4 0.0 copy-start.9
  83.4 0.0 copy-start.10
  83.4 3.4 %shard_map.138 = bf16[256,128]{1,0:T(8,128)(2,1)} custom-call(bf16[2,288,3840]{2,1,0:T(8,128)(2,1)S(1)} %bitcast.26, bf16[2,288,3840]{2,1,0:T(8,128)(2,1)S(1)} %collective-permute-done.3.other_ref, f32[128,48]{1,0:T(8,128)S(1)} %shard_map.137.prev_ref, bf16[128,64]{1,0:T(8,128)(2,1)S(1)} %get-tuple-element.28.place_ref, ...), custom_call_target="tpu_custom_call" | custom-call | flops 1274019840 | bytes 9994240 | tf_op jit(solution)/shard_map/pallas_call | solution.py:111
  86.8 10.7 %all-to-all-start = ((bf16[8,32,128]{2,1,0:T(8,128)(2,1)}), bf16[8,32,128]{2,1,0:T(8,128)(2,1)S(1)}, u32[]{:S(2)}, u32[]{:S(2)}) async-start(bf16[8,32,128]{2,1,0:T(8,128)(2,1)} %bitcast.11), calls=%async_computation | async-start | bytes 131072 | tf_op jit(solution)/shard_map/all_to_all | solution.py:393
  98.1 4.3 %all-to-all-done = bf16[8,32,128]{2,1,0:T(8,128)(2,1)S(1)} async-done(((bf16[8,32,128]{2,1,0:T(8,128)(2,1)}), bf16[8,32,128]{2,1,0:T(8,128)(2,1)S(1)}, u32[]{:S(2)}, u32[]{:S(2)}) %all-to-all-start) | async-done | bytes 65568 | tf_op jit(solution)/shard_map/all_to_all | solution.py:393
  102.4 0.0 copy-done.6
  102.5 0.0 copy-done.7
  102.5 0.0 copy-done.8
  102.5 0.0 copy-done.9
  102.5 0.0 copy-done.10
  102.5 3.0 %shard_map.139 = f32[64,8]{1,0:T(8,128)S(1)} custom-call(f32[1]{0:T(128)S(6)} %copy.20.bias_ref, bf16[256,128]{1,0:T(8,128)(2,1)S(1)} %bitcast.27, bf16[256,128]{1,0:T(8,128)(2,1)S(1)} %copy-done.10, bf16[384,1024]{1,0:T(8,128)(2,1)S(1)} %get-tuple-element.31.t1_ref, f32[1,32]{1,0:T(1,128)S(1)} %bitcast.31, bf16[1152,256]{1,0:T(8,128)(2,1)S(1)} %get-tuple-element.32.t2_ref, ...), custom_call_target="tpu_custom_call" | custom-call | flops 2000000000 | bytes 2100356 | tf_op jit(solution)/shard_map/pallas_call | solution.py:111
  105.5 25.9 %all_to_all.20 = f32[64,1,8]{2,1,0:T(1,128)S(1)} all-to-all(f32[64,1,8]{2,1,0:T(1,128)S(1)} %bitcast.28), channel_id=1, replica_groups=mesh['z'=16,'y'=4,'c'=2,'x'=4] {'z','y'}, dimensions={0} | all-to-all | bytes 4096 | tf_op jit(solution)/shard_map/all_to_all | solution.py:397
  131.4 0.1 reduce_sum.9
  131.5 0.6 reshape.23
  (1 shorter events, 0.0 us)
Async XLA Ops:
  0.0 9.9 %collective-permute-start = (bf16[9,3840]{1,0:T(8,128)(2,1)}, bf16[9,3840]{1,0:T(8,128)(2,1)S(1)}, u32[]{:S(2)}, u32[]{:S(2)}) collective-permute-start(bf16[9,3840]{1,0:T(8,128)(2,1)} %bitcast.35), channel_id=1, source_target_pairs={{0,4},{4,0},{1,5},{5,1},{2,6},{6,2},{3,7},{7,3},{8,12},{12,8},{9,1... | collective-permute-start | bytes 207368 | tf_op jit(solution)/shard_map/ppermute | solution.py:39
  10.4 17.9 %collective-permute-start.1 = (bf16[9,2,3840]{2,1,0:T(2,128)(2,1)S(1)}, bf16[9,2,3840]{2,1,0:T(2,128)(2,1)S(1)}, u32[]{:S(2)}, u32[]{:S(2)}) collective-permute-start(bf16[9,2,3840]{2,1,0:T(2,128)(2,1)S(1)} %pad_maximum_fusion.3), channel_id=1, source_target_pairs={{0,192},{4,324},{8,200},{12,332},{16,208},{20,340},{24,216},{28,34... | collective-permute-start | bytes 414728 | tf_op jit(solution)/shard_map/ppermute | solution.py:27
  19.6 14.6 %collective-permute-start.2 = (bf16[9,2,3840]{2,1,0:T(2,128)(2,1)S(1)}, bf16[9,2,3840]{2,1,0:T(2,128)(2,1)S(1)}, u32[]{:S(2)}, u32[]{:S(2)}) collective-permute-start(bf16[9,2,3840]{2,1,0:T(2,128)(2,1)S(1)} %pad_maximum_fusion.3), channel_id=1, source_target_pairs={{0,64},{4,452},{8,72},{12,460},{16,80},{20,468},{24,88},{28,476},{... | collective-permute-start | bytes 414728 | tf_op jit(solution)/shard_map/ppermute | solution.py:27
  29.0 0.9 copy-start.1
  29.9 0.9 copy-start.2
  30.8 0.7 copy-start.3
  31.5 0.7 copy-start.4
  32.2 0.7 copy-start.5
  32.9 41.8 %copy-start = (bf16[2,32,9,3840]{3,1,2,0:T(8,128)(2,1)S(1)}, bf16[2,32,9,3840]{3,1,2,0:T(8,128)(2,1)}, u32[]{:S(2)}) copy-start(bf16[2,32,9,3840]{3,1,2,0:T(8,128)(2,1)} %param.15) | copy-start | bytes 13271044
  34.2 40.4 %collective-permute-start.3 = (bf16[2,288,3840]{2,1,0:T(8,128)(2,1)}, bf16[2,288,3840]{2,1,0:T(8,128)(2,1)S(1)}, u32[]{:S(2)}, u32[]{:S(2)}) collective-permute-start(bf16[2,288,3840]{2,1,0:T(8,128)(2,1)} %bitcast.24), channel_id=1, source_target_pairs={{0,4},{4,0},{1,5},{5,1},{2,6},{6,2},{3,7},{7,3},{8,12},{12,8},{9,1... | collective-permute-start | bytes 13271048 | tf_op jit(solution)/shard_map/ppermute | solution.py:374
  36.5 10.4 %collective-permute-start.7 = (bf16[9,4,3840]{2,1,0:T(4,128)(2,1)S(1)}, bf16[9,4,3840]{2,1,0:T(4,128)(2,1)S(1)}, u32[]{:S(2)}, u32[]{:S(2)}) collective-permute-start(bf16[9,4,3840]{2,1,0:T(4,128)(2,1)S(1)} %pad_maximum_fusion.2), channel_id=1, source_target_pairs={{0,32},{4,12},{8,40},{12,20},{16,48},{20,28},{24,56},{28,4},{32,64... | collective-permute-start | bytes 829448 | tf_op jit(solution)/shard_map/ppermute | solution.py:27
  39.9 7.6 %collective-permute-start.8 = (bf16[9,4,3840]{2,1,0:T(4,128)(2,1)S(1)}, bf16[9,4,3840]{2,1,0:T(4,128)(2,1)S(1)}, u32[]{:S(2)}, u32[]{:S(2)}) collective-permute-start(bf16[9,4,3840]{2,1,0:T(4,128)(2,1)S(1)} %pad_maximum_fusion.2), channel_id=1, source_target_pairs={{0,480},{4,28},{8,488},{12,4},{16,496},{20,12},{24,504},{28,20},{3... | collective-permute-start | bytes 829448 | tf_op jit(solution)/shard_map/ppermute | solution.py:27
  43.3 8.8 %collective-permute-start.4 = (bf16[9,4,3840]{2,1,0:T(4,128)(2,1)S(1)}, bf16[9,4,3840]{2,1,0:T(4,128)(2,1)S(1)}, u32[]{:S(2)}, u32[]{:S(2)}) collective-permute-start(bf16[9,4,3840]{2,1,0:T(4,128)(2,1)S(1)} %pad_maximum_fusion.2), channel_id=1, source_target_pairs={{0,64},{4,20},{8,72},{12,28},{16,80},{20,4},{24,88},{28,12},{32,96... | collective-permute-start | bytes 829448 | tf_op jit(solution)/shard_map/ppermute | solution.py:27
  47.7 18.0 %collective-permute-start.9 = (bf16[9,8,3840]{2,1,0:T(8,128)(2,1)S(1)}, bf16[9,8,3840]{2,1,0:T(8,128)(2,1)S(1)}, u32[]{:S(2)}, u32[]{:S(2)}) collective-permute-start(bf16[9,8,3840]{2,1,0:T(8,128)(2,1)S(1)} %pad_maximum_fusion.1.refs_1_), channel_id=1, source_target_pairs={{0,8},{4,36},{8,16},{12,44},{16,24},{20,52},{24,0},{28,60},{32,40}... | collective-permute-start | bytes 1658888 | tf_op jit(solution)/shard_map/ppermute | solution.py:27
  52.5 17.1 %collective-permute-start.5 = (bf16[9,8,3840]{2,1,0:T(8,128)(2,1)S(1)}, bf16[9,8,3840]{2,1,0:T(8,128)(2,1)S(1)}, u32[]{:S(2)}, u32[]{:S(2)}) collective-permute-start(bf16[9,8,3840]{2,1,0:T(8,128)(2,1)S(1)} %pad_maximum_fusion.refs_0_), channel_id=1, source_target_pairs={{0,8},{4,36},{8,16},{12,44},{16,24},{20,52},{24,0},{28,60},{32,40}... | collective-permute-start | bytes 1658888 | tf_op jit(solution)/shard_map/ppermute | solution.py:27
  55.7 15.8 %collective-permute-start.12 = (bf16[9,8,3840]{2,1,0:T(8,128)(2,1)S(1)}, bf16[9,8,3840]{2,1,0:T(8,128)(2,1)S(1)}, u32[]{:S(2)}, u32[]{:S(2)}) collective-permute-start(bf16[9,8,3840]{2,1,0:T(8,128)(2,1)S(1)} %pad_maximum_fusion.1.refs_1_), channel_id=1, source_target_pairs={{0,24},{4,484},{8,0},{12,492},{16,8},{20,500},{24,16},{28,508},{32... | collective-permute-start | bytes 1658888 | tf_op jit(solution)/shard_map/ppermute | solution.py:27
  62.3 12.3 %collective-permute-start.11 = (bf16[9,8,3840]{2,1,0:T(8,128)(2,1)S(1)}, bf16[9,8,3840]{2,1,0:T(8,128)(2,1)S(1)}, u32[]{:S(2)}, u32[]{:S(2)}) collective-permute-start(bf16[9,8,3840]{2,1,0:T(8,128)(2,1)S(1)} %pad_maximum_fusion.refs_0_), channel_id=1, source_target_pairs={{0,24},{4,484},{8,0},{12,492},{16,8},{20,500},{24,16},{28,508},{32... | collective-permute-start | bytes 1658888 | tf_op jit(solution)/shard_map/ppermute | solution.py:27
  65.7 13.9 %collective-permute-start.10 = (bf16[9,8,3840]{2,1,0:T(8,128)(2,1)S(1)}, bf16[9,8,3840]{2,1,0:T(8,128)(2,1)S(1)}, u32[]{:S(2)}, u32[]{:S(2)}) collective-permute-start(bf16[9,8,3840]{2,1,0:T(8,128)(2,1)S(1)} %collective-permute-done.9.refs_3_), channel_id=1, source_target_pairs={{0,8},{4,36},{8,16},{12,44},{16,24},{20,52},{24,0},{28,60},{32,40}... | collective-permute-start | bytes 1658888 | tf_op jit(solution)/shard_map/ppermute | solution.py:27
  69.6 13.8 %collective-permute-start.6 = (bf16[9,8,3840]{2,1,0:T(8,128)(2,1)S(1)}, bf16[9,8,3840]{2,1,0:T(8,128)(2,1)S(1)}, u32[]{:S(2)}, u32[]{:S(2)}) collective-permute-start(bf16[9,8,3840]{2,1,0:T(8,128)(2,1)S(1)} %collective-permute-done.5.refs_2_), channel_id=1, source_target_pairs={{0,8},{4,36},{8,16},{12,44},{16,24},{20,52},{24,0},{28,60},{32,40}... | collective-permute-start | bytes 1658888 | tf_op jit(solution)/shard_map/ppermute | solution.py:27
  83.4 19.1 %copy-start.6 = (f32[32]{0:T(128)S(1)}, f32[32]{0:T(128)}, u32[]{:S(2)}) copy-start(f32[32]{0:T(128)} %param.20) | copy-start | bytes 388
  83.4 19.1 %copy-start.7 = (f32[64]{0:T(128)S(1)}, f32[64]{0:T(128)}, u32[]{:S(2)}) copy-start(f32[64]{0:T(128)} %param.22) | copy-start | bytes 772
  83.4 19.1 %copy-start.8 = (f32[128]{0:T(128)S(1)}, f32[128]{0:T(128)}, u32[]{:S(2)}) copy-start(f32[128]{0:T(128)} %param.24) | copy-start | bytes 1540
  83.4 19.1 %copy-start.9 = (bf16[128]{0:T(256)(128)(2,1)S(1)}, bf16[128]{0:T(256)(128)(2,1)}, u32[]{:S(2)}) copy-start(bf16[128]{0:T(256)(128)(2,1)} %param.25) | copy-start | bytes 772
  83.4 19.1 %copy-start.10 = (bf16[256,128]{1,0:T(8,128)(2,1)S(1)}, bf16[256,128]{1,0:T(8,128)(2,1)}, u32[]{:S(2)}) copy-start(bf16[256,128]{1,0:T(8,128)(2,1)} %constant.22.clone.order_ref) | copy-start | bytes 196612
  86.8 15.6 %all-to-all-start = ((bf16[8,32,128]{2,1,0:T(8,128)(2,1)}), bf16[8,32,128]{2,1,0:T(8,128)(2,1)S(1)}, u32[]{:S(2)}, u32[]{:S(2)}) async-start(bf16[8,32,128]{2,1,0:T(8,128)(2,1)} %bitcast.11), calls=%async_computation | async-start | bytes 131072 | tf_op jit(solution)/shard_map/all_to_all | solution.py:393

commit v12 on v10

--- a/solution.py
+++ b/solution.py
@@ -325,7 +325,8 @@
         for q in range(4):
             line = jnp.where(slot_query == q, score[k * 4 + q : k * 4 + q + 1, : listed.shape[1]], line)
         total = jnp.where(listed == k, line, total)
-    out_ref[...] = total
+    out_ref[:, 0, :] = total[:, :4]
+    out_ref[:, 1, :] = total[:, 4:]
 
 
 def slot_scores(parts, listed, spread, first_bias, second_bias, third_bias, score_weight, score_bias):
@@ -342,7 +343,7 @@
         score_weight[None, :],
         listed,
     ]
-    outs = [(listed.shape, jnp.float32)]
+    outs = [((listed.shape[0], 2, listed.shape[1] // 2), jnp.float32)]
     return kernel_call(score_body, outs, operands, [], 2 * 10**9, scalars=1)[0]
 
 
@@ -394,7 +395,7 @@
         parts, listed, spread, first_bias, second_bias, third_bias, score_weight, score_bias
     )
     values = lax.all_to_all(values, ("z", "y"), 0, 0, tiled=True)
-    return values.sum(axis=0).reshape(-1, group).T
+    return values.sum(axis=0).T
 
 
 def solution(mesh):

time: 124 us -> 124 us (level)
  no operation moved by 1% of the time
where the time goes in v12:
time: 124 us; the launch traced here: 123 us
  starting transfers between devices  60.6 us (49%)
  blocking collectives  22.6 us (18%)
  waiting for transfers between devices  22.2 us (18%)
  Pallas kernels  12.9 us (10%)
  other arithmetic  3 us (2%)
    ppermute x11, starting transfers between devices, send(): return lax.ppermute(values, PLANE, pairs)  41.3 us
    all_to_all x1, blocking collectives, on_device(): values = lax.all_to_all(values, ('z', 'y'), 0, 0, tiled=True)  22.6 us
    ppermute x11, waiting for transfers between devices, send(): return lax.ppermute(values, PLANE, pairs)  17.7 us
    pallas_call x4, Pallas kernels, kernel_call(): pl.pallas_call(body, in_specs=[pl.BlockSpec(memory_space=space) for space...  12.9 us
    ppermute x1, starting transfers between devices, gather_classes(): other = lax.ppermute(block, 'c', [(0, 1), (1, 0)])  8.77 us
    all_to_all x1, starting transfers between devices, on_device(): parts = lax.all_to_all(table, ('c', 'x'), 0, 0, tiled=True)  6.01 us
    ppermute x1, starting transfers between devices, on_device(): other = lax.ppermute(own, 'c', [(0, 1), (1, 0)])  4.57 us
    all_to_all x1, waiting for transfers between devices, on_device(): parts = lax.all_to_all(table, ('c', 'x'), 0, 0, tiled=True)  4.32 us
  transfers between devices with their start and end apart: 14, of which 9 were waited for; matrix products, arithmetic and copies ran while one was open for 1% of the time, Pallas kernels for 5%

profile of v12, /device:TPU:1, one launch (start us, length us, event | category | flops | bytes accessed | tf_op | source)
XLA Modules:
  0.0 123.5 jit_solution(11804697557950546433)
XLA Ops:
  0.0 8.8 %collective-permute-start = (bf16[9,3840]{1,0:T(8,128)(2,1)}, bf16[9,3840]{1,0:T(8,128)(2,1)S(1)}, u32[]{:S(2)}, u32[]{:S(2)}) collective-permute-start(bf16[9,3840]{1,0:T(8,128)(2,1)} %bitcast.31), channel_id=1, source_target_pairs={{0,4},{4,0},{1,5},{5,1},{2,6},{6,2},{3,7},{7,3},{8,12},{12,8},{9,1... | collective-permute-start | bytes 207368 | tf_op jit(solution)/shard_map/ppermute | solution.py:39
  8.8 1.0 copy.15
  9.8 0.1 collective-permute-done
  9.9 0.1 copy.16
  10.1 0.0 copy-start.11
  10.1 0.0 copy-start.1
  10.1 0.0 copy-start.2
  10.1 0.0 copy-start.3
  10.1 0.0 copy-start.4
  10.1 0.0 copy-start.5
  10.1 0.3 pad_maximum_fusion.3
  10.5 9.2 %collective-permute-start.1 = (bf16[9,2,3840]{2,1,0:T(2,128)(2,1)S(1)}, bf16[9,2,3840]{2,1,0:T(2,128)(2,1)S(1)}, u32[]{:S(2)}, u32[]{:S(2)}) collective-permute-start(bf16[9,2,3840]{2,1,0:T(2,128)(2,1)S(1)} %pad_maximum_fusion.3), channel_id=1, source_target_pairs={{0,192},{4,324},{8,200},{12,332},{16,208},{20,340},{24,216},{28,34... | collective-permute-start | bytes 414728 | tf_op jit(solution)/shard_map/ppermute | solution.py:27
  19.7 3.1 %collective-permute-start.2 = (bf16[9,2,3840]{2,1,0:T(2,128)(2,1)S(1)}, bf16[9,2,3840]{2,1,0:T(2,128)(2,1)S(1)}, u32[]{:S(2)}, u32[]{:S(2)}) collective-permute-start(bf16[9,2,3840]{2,1,0:T(2,128)(2,1)S(1)} %pad_maximum_fusion.3), channel_id=1, source_target_pairs={{0,64},{4,452},{8,72},{12,460},{16,80},{20,468},{24,88},{28,476},{... | collective-permute-start | bytes 414728 | tf_op jit(solution)/shard_map/ppermute | solution.py:27
  22.7 5.6 %collective-permute-done.1 = bf16[9,2,3840]{2,1,0:T(2,128)(2,1)S(1)} collective-permute-done((bf16[9,2,3840]{2,1,0:T(2,128)(2,1)S(1)}, bf16[9,2,3840]{2,1,0:T(2,128)(2,1)S(1)}, u32[]{:S(2)}, u32[]{:S(2)}) %collective-permute-start.1) | collective-permute-done | bytes 138272 | tf_op jit(solution)/shard_map/ppermute | solution.py:27
  28.4 3.6 %collective-permute-done.2 = bf16[9,2,3840]{2,1,0:T(2,128)(2,1)S(1)} collective-permute-done((bf16[9,2,3840]{2,1,0:T(2,128)(2,1)S(1)}, bf16[9,2,3840]{2,1,0:T(2,128)(2,1)S(1)}, u32[]{:S(2)}, u32[]{:S(2)}) %collective-permute-start.2) | collective-permute-done | bytes 138272 | tf_op jit(solution)/shard_map/ppermute | solution.py:27
  32.0 0.3 pad_maximum_fusion.2
  32.3 4.7 %collective-permute-start.3 = (bf16[9,4,3840]{2,1,0:T(4,128)(2,1)S(1)}, bf16[9,4,3840]{2,1,0:T(4,128)(2,1)S(1)}, u32[]{:S(2)}, u32[]{:S(2)}) collective-permute-start(bf16[9,4,3840]{2,1,0:T(4,128)(2,1)S(1)} %pad_maximum_fusion.2), channel_id=1, source_target_pairs={{0,64},{4,20},{8,72},{12,28},{16,80},{20,4},{24,88},{28,12},{32,96... | collective-permute-start | bytes 829448 | tf_op jit(solution)/shard_map/ppermute | solution.py:27
  37.0 0.1 pad_add_fusion.at_ref
  37.0 2.3 %collective-permute-start.4 = (bf16[9,4,3840]{2,1,0:T(4,128)(2,1)S(1)}, bf16[9,4,3840]{2,1,0:T(4,128)(2,1)S(1)}, u32[]{:S(2)}, u32[]{:S(2)}) collective-permute-start(bf16[9,4,3840]{2,1,0:T(4,128)(2,1)S(1)} %pad_maximum_fusion.2), channel_id=1, source_target_pairs={{0,32},{4,12},{8,40},{12,20},{16,48},{20,28},{24,56},{28,4},{32,64... | collective-permute-start | bytes 829448 | tf_op jit(solution)/shard_map/ppermute | solution.py:27
  39.4 4.2 %collective-permute-start.5 = (bf16[9,4,3840]{2,1,0:T(4,128)(2,1)S(1)}, bf16[9,4,3840]{2,1,0:T(4,128)(2,1)}, u32[]{:S(2)}, u32[]{:S(2)}) collective-permute-start(bf16[9,4,3840]{2,1,0:T(4,128)(2,1)S(1)} %pad_maximum_fusion.2), channel_id=1, source_target_pairs={{0,480},{4,28},{8,488},{12,4},{16,496},{20,12},{24,504},{28,20},{3... | collective-permute-start | bytes 829448 | tf_op jit(solution)/shard_map/ppermute | solution.py:27
  43.5 0.0 collective-permute-done.3
  43.6 0.5 pad_maximum_fusion.refs_0_
  44.0 0.0 copy-done.11
  44.0 0.0 copy-done.1
  44.1 0.0 copy-done.2
  44.1 0.0 copy-done.3
  44.1 0.0 copy-done.4
  44.1 0.0 copy-done.5
  44.1 0.0 copy-start
  44.1 1.3 %shard_map.136 = (s32[64,8]{1,0:T(8,128)S(1)}, bf16[128,64]{1,0:T(8,128)(2,1)S(1)}, bf16[384,1024]{1,0:T(8,128)(2,1)S(1)}, bf16[1152,256]{1,0:T(8,128)(2,1)S(1)}, bf16[1152,256]{1,0:T(8,128)(2,1)S(1)}) custom-call(s32[4]{0:T(128)S(1)} %pad_add_fusion.at_ref, s32[16]{0:T(128)S(1)} %copy-done.5, s32[16,256]{1,0:T(8,128)S(1)} %copy-done.3, ...), custom_call_target="tpu_custom_call" | custom-call | flops 1000000000 | bytes 217744 | tf_op jit(solution)/shard_map/pallas_call | solution.py:111
  45.4 0.4 collective-permute-done.4
  45.8 1.2 collective-permute-done.5
  47.0 1.2 pad_maximum_fusion.1.refs_1_
  48.3 0.0 copy-done
  48.3 4.6 %collective-permute-start.6 = (bf16[2,288,3840]{2,1,0:T(8,128)(2,1)S(1)}, bf16[2,288,3840]{2,1,0:T(8,128)(2,1)S(1)}, u32[]{:S(2)}, u32[]{:S(2)}) collective-permute-start(bf16[2,288,3840]{2,1,0:T(8,128)(2,1)S(1)} %bitcast.21), channel_id=1, source_target_pairs={{0,4},{4,0},{1,5},{5,1},{2,6},{6,2},{3,7},{7,3},{8,12},{12,8},{9,1... | collective-permute-start | bytes 13271048 | tf_op jit(solution)/shard_map/ppermute | solution.py:380
  52.8 3.6 %collective-permute-start.9 = (bf16[9,8,3840]{2,1,0:T(8,128)(2,1)S(1)}, bf16[9,8,3840]{2,1,0:T(8,128)(2,1)S(1)}, u32[]{:S(2)}, u32[]{:S(2)}) collective-permute-start(bf16[9,8,3840]{2,1,0:T(8,128)(2,1)S(1)} %pad_maximum_fusion.1.refs_1_), channel_id=1, source_target_pairs={{0,8},{4,36},{8,16},{12,44},{16,24},{20,52},{24,0},{28,60},{32,40}... | collective-permute-start | bytes 1658888 | tf_op jit(solution)/shard_map/ppermute | solution.py:27
  56.5 3.1 %collective-permute-start.7 = (bf16[9,8,3840]{2,1,0:T(8,128)(2,1)S(1)}, bf16[9,8,3840]{2,1,0:T(8,128)(2,1)S(1)}, u32[]{:S(2)}, u32[]{:S(2)}) collective-permute-start(bf16[9,8,3840]{2,1,0:T(8,128)(2,1)S(1)} %pad_maximum_fusion.refs_0_), channel_id=1, source_target_pairs={{0,8},{4,36},{8,16},{12,44},{16,24},{20,52},{24,0},{28,60},{32,40}... | collective-permute-start | bytes 1658888 | tf_op jit(solution)/shard_map/ppermute | solution.py:27
  59.6 3.4 %collective-permute-start.11 = (bf16[9,8,3840]{2,1,0:T(8,128)(2,1)S(1)}, bf16[9,8,3840]{2,1,0:T(8,128)(2,1)S(1)}, u32[]{:S(2)}, u32[]{:S(2)}) collective-permute-start(bf16[9,8,3840]{2,1,0:T(8,128)(2,1)S(1)} %pad_maximum_fusion.refs_0_), channel_id=1, source_target_pairs={{0,24},{4,484},{8,0},{12,492},{16,8},{20,500},{24,16},{28,508},{32... | collective-permute-start | bytes 1658888 | tf_op jit(solution)/shard_map/ppermute | solution.py:27
  63.0 1.9 %collective-permute-start.12 = (bf16[9,8,3840]{2,1,0:T(8,128)(2,1)S(1)}, bf16[9,8,3840]{2,1,0:T(8,128)(2,1)S(1)}, u32[]{:S(2)}, u32[]{:S(2)}) collective-permute-start(bf16[9,8,3840]{2,1,0:T(8,128)(2,1)S(1)} %pad_maximum_fusion.1.refs_1_), channel_id=1, source_target_pairs={{0,24},{4,484},{8,0},{12,492},{16,8},{20,500},{24,16},{28,508},{32... | collective-permute-start | bytes 1658888 | tf_op jit(solution)/shard_map/ppermute | solution.py:27
  64.9 0.0 collective-permute-done.9.refs_3_
  64.9 3.4 %collective-permute-start.10 = (bf16[9,8,3840]{2,1,0:T(8,128)(2,1)S(1)}, bf16[9,8,3840]{2,1,0:T(8,128)(2,1)S(1)}, u32[]{:S(2)}, u32[]{:S(2)}) collective-permute-start(bf16[9,8,3840]{2,1,0:T(8,128)(2,1)S(1)} %collective-permute-done.9.refs_3_), channel_id=1, source_target_pairs={{0,8},{4,36},{8,16},{12,44},{16,24},{20,52},{24,0},{28,60},{32,40}... | collective-permute-start | bytes 1658888 | tf_op jit(solution)/shard_map/ppermute | solution.py:27
  68.3 2.2 %collective-permute-done.7.refs_2_ = bf16[9,8,3840]{2,1,0:T(8,128)(2,1)S(1)} collective-permute-done((bf16[9,8,3840]{2,1,0:T(8,128)(2,1)S(1)}, bf16[9,8,3840]{2,1,0:T(8,128)(2,1)S(1)}, u32[]{:S(2)}, u32[]{:S(2)}) %collective-permute-start.7) | collective-permute-done | bytes 552992 | tf_op jit(solution)/shard_map/ppermute | solution.py:27
  70.5 2.4 %collective-permute-start.8 = (bf16[9,8,3840]{2,1,0:T(8,128)(2,1)S(1)}, bf16[9,8,3840]{2,1,0:T(8,128)(2,1)S(1)}, u32[]{:S(2)}, u32[]{:S(2)}) collective-permute-start(bf16[9,8,3840]{2,1,0:T(8,128)(2,1)S(1)} %collective-permute-done.7.refs_2_), channel_id=1, source_target_pairs={{0,8},{4,36},{8,16},{12,44},{16,24},{20,52},{24,0},{28,60},{32,40}... | collective-permute-start | bytes 1658888 | tf_op jit(solution)/shard_map/ppermute | solution.py:27
  72.9 0.0 collective-permute-done.11.refs_4_
  72.9 3.1 %collective-permute-done.12.refs_5_ = bf16[9,8,3840]{2,1,0:T(8,128)(2,1)S(1)} collective-permute-done((bf16[9,8,3840]{2,1,0:T(8,128)(2,1)S(1)}, bf16[9,8,3840]{2,1,0:T(8,128)(2,1)S(1)}, u32[]{:S(2)}, u32[]{:S(2)}) %collective-permute-start.12) | collective-permute-done | bytes 552992 | tf_op jit(solution)/shard_map/ppermute | solution.py:27
  76.1 0.0 collective-permute-done.6.other_ref
  76.1 5.0 %shard_map.137.prev_ref = f32[128,48]{1,0:T(8,128)S(1)} custom-call(bf16[2,288,3840]{2,1,0:T(8,128)(2,1)S(1)} %bitcast.22, bf16[2,288,3840]{2,1,0:T(8,128)(2,1)S(1)} %collective-permute-done.6.other_ref, bf16[9,8,3840]{2,1,0:T(8,128)(2,1)S(1)} %pad_maximum_fusion.refs_0_, bf16[9,8,3840]{2,1,0:T(8,128)(2,1)S(1)} %pad_maximum_fusion.1.refs_1_, ...), custom_call_target="tpu_custom_call" | custom-call | flops 3822059520 | bytes 12165120 | tf_op jit(solution)/shard_map/pallas_call | solution.py:111
  81.0 0.0 collective-permute-done.10.refs_1_
  81.0 1.6 %collective-permute-done.8.refs_0_ = bf16[9,8,3840]{2,1,0:T(8,128)(2,1)S(1)} collective-permute-done((bf16[9,8,3840]{2,1,0:T(8,128)(2,1)S(1)}, bf16[9,8,3840]{2,1,0:T(8,128)(2,1)S(1)}, u32[]{:S(2)}, u32[]{:S(2)}) %collective-permute-start.8) | collective-permute-done | bytes 552992 | tf_op jit(solution)/shard_map/ppermute | solution.py:27
  82.6 0.0 copy-start.7
  82.6 0.0 copy-start.8
  82.6 0.0 copy-start.9
  82.6 0.0 copy-start.10
  82.6 3.4 %shard_map.138 = bf16[256,128]{1,0:T(8,128)(2,1)} custom-call(bf16[2,288,3840]{2,1,0:T(8,128)(2,1)S(1)} %bitcast.23, bf16[2,288,3840]{2,1,0:T(8,128)(2,1)S(1)} %collective-permute-done.6.other_ref, f32[128,48]{1,0:T(8,128)S(1)} %shard_map.137.prev_ref, bf16[128,64]{1,0:T(8,128)(2,1)S(1)} %get-tuple-element.30.place_ref, ...), custom_call_target="tpu_custom_call" | custom-call | flops 1274019840 | bytes 9994240 | tf_op jit(solution)/shard_map/pallas_call | solution.py:111
  86.0 6.0 %all-to-all-start = ((bf16[8,32,128]{2,1,0:T(8,128)(2,1)}), bf16[8,32,128]{2,1,0:T(8,128)(2,1)S(1)}, u32[]{:S(2)}, u32[]{:S(2)}) async-start(bf16[8,32,128]{2,1,0:T(8,128)(2,1)} %bitcast.11), calls=%async_computation | async-start | bytes 131072 | tf_op jit(solution)/shard_map/all_to_all | solution.py:393
  92.7 4.3 %all-to-all-done = bf16[8,32,128]{2,1,0:T(8,128)(2,1)S(1)} async-done(((bf16[8,32,128]{2,1,0:T(8,128)(2,1)}), bf16[8,32,128]{2,1,0:T(8,128)(2,1)S(1)}, u32[]{:S(2)}, u32[]{:S(2)}) %all-to-all-start) | async-done | bytes 65568 | tf_op jit(solution)/shard_map/all_to_all | solution.py:393
  97.0 0.0 copy-done.6
  97.0 0.0 copy-done.7
  97.0 0.0 copy-done.8
  97.0 0.0 copy-done.9
  97.0 0.0 copy-done.10
  97.0 3.2 %shard_map.139 = f32[64,2,4]{2,1,0:T(2,128)S(1)} custom-call(f32[1]{0:T(128)S(6)} %copy.17.bias_ref, bf16[256,128]{1,0:T(8,128)(2,1)S(1)} %bitcast.24, bf16[256,128]{1,0:T(8,128)(2,1)S(1)} %copy-done.10, bf16[384,1024]{1,0:T(8,128)(2,1)S(1)} %get-tuple-element.33.t1_ref, f32[1,32]{1,0:T(1,128)S(1)} %bitcast.27, ...), custom_call_target="tpu_custom_call" | custom-call | flops 2000000000 | bytes 2100356 | tf_op jit(solution)/shard_map/pallas_call | solution.py:111
  100.2 22.6 %all_to_all.16 = f32[64,2,4]{2,1,0:T(2,128)S(1)} all-to-all(f32[64,2,4]{2,1,0:T(2,128)S(1)} %shard_map.139), channel_id=1, replica_groups=mesh['z'=16,'y'=4,'c'=2,'x'=4] {'z','y'}, dimensions={0} | all-to-all | bytes 4096 | tf_op jit(solution)/shard_map/all_to_all | solution.py:397
  122.8 0.6 reduce_sum.9
  (2 shorter events, 0.0 us)
Async XLA Ops:
  0.0 9.9 %collective-permute-start = (bf16[9,3840]{1,0:T(8,128)(2,1)}, bf16[9,3840]{1,0:T(8,128)(2,1)S(1)}, u32[]{:S(2)}, u32[]{:S(2)}) collective-permute-start(bf16[9,3840]{1,0:T(8,128)(2,1)} %bitcast.31), channel_id=1, source_target_pairs={{0,4},{4,0},{1,5},{5,1},{2,6},{6,2},{3,7},{7,3},{8,12},{12,8},{9,1... | collective-permute-start | bytes 207368 | tf_op jit(solution)/shard_map/ppermute | solution.py:39
  10.1 34.0 %copy-start.11 = (bf16[3,3,1,32]{3,1,2,0:T(4,128)(2,1)S(1)}, bf16[3,3,1,32]{3,1,2,0:T(4,128)(2,1)}, u32[]{:S(2)}) copy-start(bf16[3,3,1,32]{3,1,2,0:T(4,128)(2,1)} %param.19) | copy-start | bytes 1732
  10.1 34.0 %copy-start.1 = (bf16[3,3,64,128]{3,2,1,0:T(8,128)(2,1)S(1)}, bf16[3,3,64,128]{3,2,1,0:T(8,128)(2,1)}, u32[]{:S(2)}) copy-start(bf16[3,3,64,128]{3,2,1,0:T(8,128)(2,1)} %param.23) | copy-start | bytes 442372
  10.1 34.0 %copy-start.2 = (bf16[3,3,32,64]{3,2,1,0:T(8,128)(2,1)S(1)}, bf16[3,3,32,64]{3,2,1,0:T(8,128)(2,1)}, u32[]{:S(2)}) copy-start(bf16[3,3,32,64]{3,2,1,0:T(8,128)(2,1)} %param.21) | copy-start | bytes 110596
  10.1 34.0 %copy-start.3 = (s32[16,256]{1,0:T(8,128)S(1)}, s32[16,256]{1,0:T(8,128)}, u32[]{:S(2)}) copy-start(s32[16,256]{1,0:T(8,128)} %shard_ref.1) | copy-start | bytes 49156
  10.1 34.0 %copy-start.4 = (s32[16,256]{1,0:T(8,128)S(1)}, s32[16,256]{1,0:T(8,128)}, u32[]{:S(2)}) copy-start(s32[16,256]{1,0:T(8,128)} %clip_ref.1) | copy-start | bytes 49156
  10.1 34.0 %copy-start.5 = (s32[16]{0:T(128)S(1)}, s32[16]{0:T(128)}, u32[]{:S(2)}) copy-start(s32[16]{0:T(128)} %count_ref.1) | copy-start | bytes 196
  10.5 17.9 %collective-permute-start.1 = (bf16[9,2,3840]{2,1,0:T(2,128)(2,1)S(1)}, bf16[9,2,3840]{2,1,0:T(2,128)(2,1)S(1)}, u32[]{:S(2)}, u32[]{:S(2)}) collective-permute-start(bf16[9,2,3840]{2,1,0:T(2,128)(2,1)S(1)} %pad_maximum_fusion.3), channel_id=1, source_target_pairs={{0,192},{4,324},{8,200},{12,332},{16,208},{20,340},{24,216},{28,34... | collective-permute-start | bytes 414728 | tf_op jit(solution)/shard_map/ppermute | solution.py:27
  19.7 12.3 %collective-permute-start.2 = (bf16[9,2,3840]{2,1,0:T(2,128)(2,1)S(1)}, bf16[9,2,3840]{2,1,0:T(2,128)(2,1)S(1)}, u32[]{:S(2)}, u32[]{:S(2)}) collective-permute-start(bf16[9,2,3840]{2,1,0:T(2,128)(2,1)S(1)} %pad_maximum_fusion.3), channel_id=1, source_target_pairs={{0,64},{4,452},{8,72},{12,460},{16,80},{20,468},{24,88},{28,476},{... | collective-permute-start | bytes 414728 | tf_op jit(solution)/shard_map/ppermute | solution.py:27
  32.3 11.3 %collective-permute-start.3 = (bf16[9,4,3840]{2,1,0:T(4,128)(2,1)S(1)}, bf16[9,4,3840]{2,1,0:T(4,128)(2,1)S(1)}, u32[]{:S(2)}, u32[]{:S(2)}) collective-permute-start(bf16[9,4,3840]{2,1,0:T(4,128)(2,1)S(1)} %pad_maximum_fusion.2), channel_id=1, source_target_pairs={{0,64},{4,20},{8,72},{12,28},{16,80},{20,4},{24,88},{28,12},{32,96... | collective-permute-start | bytes 829448 | tf_op jit(solution)/shard_map/ppermute | solution.py:27
  37.0 8.8 %collective-permute-start.4 = (bf16[9,4,3840]{2,1,0:T(4,128)(2,1)S(1)}, bf16[9,4,3840]{2,1,0:T(4,128)(2,1)S(1)}, u32[]{:S(2)}, u32[]{:S(2)}) collective-permute-start(bf16[9,4,3840]{2,1,0:T(4,128)(2,1)S(1)} %pad_maximum_fusion.2), channel_id=1, source_target_pairs={{0,32},{4,12},{8,40},{12,20},{16,48},{20,28},{24,56},{28,4},{32,64... | collective-permute-start | bytes 829448 | tf_op jit(solution)/shard_map/ppermute | solution.py:27
  39.4 7.7 %collective-permute-start.5 = (bf16[9,4,3840]{2,1,0:T(4,128)(2,1)S(1)}, bf16[9,4,3840]{2,1,0:T(4,128)(2,1)}, u32[]{:S(2)}, u32[]{:S(2)}) collective-permute-start(bf16[9,4,3840]{2,1,0:T(4,128)(2,1)S(1)} %pad_maximum_fusion.2), channel_id=1, source_target_pairs={{0,480},{4,28},{8,488},{12,4},{16,496},{20,12},{24,504},{28,20},{3... | collective-permute-start | bytes 829448 | tf_op jit(solution)/shard_map/ppermute | solution.py:27
  44.1 4.2 %copy-start = (bf16[2,32,9,3840]{3,1,2,0:T(8,128)(2,1)S(1)}, bf16[2,32,9,3840]{3,1,2,0:T(8,128)(2,1)}, u32[]{:S(2)}) copy-start(bf16[2,32,9,3840]{3,1,2,0:T(8,128)(2,1)} %param.15) | copy-start | bytes 13271044
  48.3 27.8 %collective-permute-start.6 = (bf16[2,288,3840]{2,1,0:T(8,128)(2,1)S(1)}, bf16[2,288,3840]{2,1,0:T(8,128)(2,1)S(1)}, u32[]{:S(2)}, u32[]{:S(2)}) collective-permute-start(bf16[2,288,3840]{2,1,0:T(8,128)(2,1)S(1)} %bitcast.21), channel_id=1, source_target_pairs={{0,4},{4,0},{1,5},{5,1},{2,6},{6,2},{3,7},{7,3},{8,12},{12,8},{9,1... | collective-permute-start | bytes 13271048 | tf_op jit(solution)/shard_map/ppermute | solution.py:380
  52.8 12.1 %collective-permute-start.9 = (bf16[9,8,3840]{2,1,0:T(8,128)(2,1)S(1)}, bf16[9,8,3840]{2,1,0:T(8,128)(2,1)S(1)}, u32[]{:S(2)}, u32[]{:S(2)}) collective-permute-start(bf16[9,8,3840]{2,1,0:T(8,128)(2,1)S(1)} %pad_maximum_fusion.1.refs_1_), channel_id=1, source_target_pairs={{0,8},{4,36},{8,16},{12,44},{16,24},{20,52},{24,0},{28,60},{32,40}... | collective-permute-start | bytes 1658888 | tf_op jit(solution)/shard_map/ppermute | solution.py:27
  56.5 14.0 %collective-permute-start.7 = (bf16[9,8,3840]{2,1,0:T(8,128)(2,1)S(1)}, bf16[9,8,3840]{2,1,0:T(8,128)(2,1)S(1)}, u32[]{:S(2)}, u32[]{:S(2)}) collective-permute-start(bf16[9,8,3840]{2,1,0:T(8,128)(2,1)S(1)} %pad_maximum_fusion.refs_0_), channel_id=1, source_target_pairs={{0,8},{4,36},{8,16},{12,44},{16,24},{20,52},{24,0},{28,60},{32,40}... | collective-permute-start | bytes 1658888 | tf_op jit(solution)/shard_map/ppermute | solution.py:27
  59.6 13.3 %collective-permute-start.11 = (bf16[9,8,3840]{2,1,0:T(8,128)(2,1)S(1)}, bf16[9,8,3840]{2,1,0:T(8,128)(2,1)S(1)}, u32[]{:S(2)}, u32[]{:S(2)}) collective-permute-start(bf16[9,8,3840]{2,1,0:T(8,128)(2,1)S(1)} %pad_maximum_fusion.refs_0_), channel_id=1, source_target_pairs={{0,24},{4,484},{8,0},{12,492},{16,8},{20,500},{24,16},{28,508},{32... | collective-permute-start | bytes 1658888 | tf_op jit(solution)/shard_map/ppermute | solution.py:27
  63.0 13.1 %collective-permute-start.12 = (bf16[9,8,3840]{2,1,0:T(8,128)(2,1)S(1)}, bf16[9,8,3840]{2,1,0:T(8,128)(2,1)S(1)}, u32[]{:S(2)}, u32[]{:S(2)}) collective-permute-start(bf16[9,8,3840]{2,1,0:T(8,128)(2,1)S(1)} %pad_maximum_fusion.1.refs_1_), channel_id=1, source_target_pairs={{0,24},{4,484},{8,0},{12,492},{16,8},{20,500},{24,16},{28,508},{32... | collective-permute-start | bytes 1658888 | tf_op jit(solution)/shard_map/ppermute | solution.py:27
  64.9 16.1 %collective-permute-start.10 = (bf16[9,8,3840]{2,1,0:T(8,128)(2,1)S(1)}, bf16[9,8,3840]{2,1,0:T(8,128)(2,1)S(1)}, u32[]{:S(2)}, u32[]{:S(2)}) collective-permute-start(bf16[9,8,3840]{2,1,0:T(8,128)(2,1)S(1)} %collective-permute-done.9.refs_3_), channel_id=1, source_target_pairs={{0,8},{4,36},{8,16},{12,44},{16,24},{20,52},{24,0},{28,60},{32,40}... | collective-permute-start | bytes 1658888 | tf_op jit(solution)/shard_map/ppermute | solution.py:27
  70.5 12.1 %collective-permute-start.8 = (bf16[9,8,3840]{2,1,0:T(8,128)(2,1)S(1)}, bf16[9,8,3840]{2,1,0:T(8,128)(2,1)S(1)}, u32[]{:S(2)}, u32[]{:S(2)}) collective-permute-start(bf16[9,8,3840]{2,1,0:T(8,128)(2,1)S(1)} %collective-permute-done.7.refs_2_), channel_id=1, source_target_pairs={{0,8},{4,36},{8,16},{12,44},{16,24},{20,52},{24,0},{28,60},{32,40}... | collective-permute-start | bytes 1658888 | tf_op jit(solution)/shard_map/ppermute | solution.py:27
  82.6 14.4 %copy-start.6 = (f32[32]{0:T(128)S(1)}, f32[32]{0:T(128)}, u32[]{:S(2)}) copy-start(f32[32]{0:T(128)} %param.20) | copy-start | bytes 388
  82.6 14.4 %copy-start.7 = (f32[64]{0:T(128)S(1)}, f32[64]{0:T(128)}, u32[]{:S(2)}) copy-start(f32[64]{0:T(128)} %param.22) | copy-start | bytes 772
  82.6 14.4 %copy-start.8 = (f32[128]{0:T(128)S(1)}, f32[128]{0:T(128)}, u32[]{:S(2)}) copy-start(f32[128]{0:T(128)} %param.24) | copy-start | bytes 1540
  82.6 14.4 %copy-start.9 = (bf16[128]{0:T(256)(128)(2,1)S(1)}, bf16[128]{0:T(256)(128)(2,1)}, u32[]{:S(2)}) copy-start(bf16[128]{0:T(256)(128)(2,1)} %param.25) | copy-start | bytes 772
  82.6 14.4 %copy-start.10 = (bf16[256,128]{1,0:T(8,128)(2,1)S(1)}, bf16[256,128]{1,0:T(8,128)(2,1)}, u32[]{:S(2)}) copy-start(bf16[256,128]{1,0:T(8,128)(2,1)} %constant.22.clone.order_ref) | copy-start | bytes 196612
  86.0 11.0 %all-to-all-start = ((bf16[8,32,128]{2,1,0:T(8,128)(2,1)}), bf16[8,32,128]{2,1,0:T(8,128)(2,1)S(1)}, u32[]{:S(2)}, u32[]{:S(2)}) async-start(bf16[8,32,128]{2,1,0:T(8,128)(2,1)} %bitcast.11), calls=%async_computation | async-start | bytes 131072 | tf_op jit(solution)/shard_map/all_to_all | solution.py:393
